TPU v7x, 256 devices: a whole 4x4x8 slice. The times are simulated.
256 devices in a mesh: section: 16 (over y, z_hi), dp: 16 (over z_lo, x, core).
Axes of the slice: x: 4, y: 4, z: 8 (z_hi: 4, z_lo: 2; z = z_hi * 2 + z_lo), core: 2. Of those that a mesh axis runs over, the one named last changes fastest.
Arguments:
- inputs_down: bfloat16 [48, 24, 5120], P('dp'), may hold values from -6 to 6
- inputs_up: bfloat16 [48, 24, 5120], P('dp'), may hold values from -6 to 6
- w_in: bfloat16 [16, 2, 5120, 256], P('section'), as said below
- w_out: bfloat16 [16, 2, 5120, 256], P('section'), as said below
Outputs:
- grad_w_out: float32 [16, 5120, 256], P('section', 'dp')
Inputs may be any that keep to these rules, and one draw needn't show every extreme that they name: w_in[s, 1] equals w_in[15 - s, 0] for every s: both directions use the same layers. w_out[s, 1] equals w_out[15 - s, 0] for every s: both directions use the same layers.
All inputs are finite; a program needn't handle non-finite values.
Results may differ from a plain program's by a relative error of at most 0.015.
Values may be sent and summed in bfloat16 or wider, within the bound.
No kernel may reach another device: no remote copies, remote signals or barrier semaphores. Data moves between devices by JAX's collectives and lax.ppermute only.
A program may use at most 128 MiB of HBM per device.

v0:
```python
import jax
import jax.numpy as jnp
from jax import lax
from jax.sharding import PartitionSpec as P

epsilon = 1e-06
cot_weight = 0.0625


def passed_along(value, axis, steps):
    count = lax.axis_size(axis)
    first, last = (max(0, -steps), min(count, count - steps))
    return lax.ppermute(value, axis, [(source, source + steps) for source in range(first, last)])


def partner(block, axis, apart):
    count = lax.axis_size(axis)
    route = []
    for low in range(count):
        high = low | 1 << apart
        if high != low and high < count:
            route += [(low, high), (high, low)]
    return lax.ppermute(block, axis, route)


def forward_layer(hidden, w_one, w_two):
    widened = hidden.astype(jnp.float32)
    inv_rms = lax.rsqrt(jnp.mean(widened * widened, axis=-1, keepdims=True) + epsilon)
    normed = (widened * inv_rms).astype(jnp.bfloat16)
    pre_act = jnp.dot(normed, w_one, preferred_element_type=jnp.float32)
    active = jax.nn.silu(pre_act).astype(jnp.bfloat16)
    branch = lax.dot_general(
        active, w_two, (((1,), (1,)), ((), ())), preferred_element_type=jnp.float32
    )
    return (widened + branch).astype(jnp.bfloat16)


def backward_layer(hidden, upstream, w_one, w_two):
    widened = hidden.astype(jnp.float32)
    inv_rms = lax.rsqrt(jnp.mean(widened * widened, axis=-1, keepdims=True) + epsilon)
    unit_rows = widened * inv_rms
    normed = unit_rows.astype(jnp.bfloat16)
    pre_act = jnp.dot(normed, w_one, preferred_element_type=jnp.float32)
    active = jax.nn.silu(pre_act).astype(jnp.bfloat16)
    d_active = jnp.dot(upstream, w_two, preferred_element_type=jnp.float32)
    sigma = jax.nn.sigmoid(pre_act)
    d_pre = (d_active * sigma * (1.0 + pre_act * (1.0 - sigma))).astype(jnp.bfloat16)
    d_normed = lax.dot_general(
        d_pre, w_one, (((1,), (1,)), ((), ())), preferred_element_type=jnp.float32
    )
    d_hidden = inv_rms * (
        d_normed - unit_rows * jnp.mean(d_normed * unit_rows, axis=-1, keepdims=True)
    )
    return ((upstream.astype(jnp.float32) + d_hidden).astype(jnp.bfloat16), active)


def seed_rows(final_rows):
    return (final_rows.astype(jnp.float32) * cot_weight).astype(jnp.bfloat16)


def outer_grad(cot_store, act_store):
    width = cot_store.shape[-1]
    inner = act_store.shape[-1]
    return lax.dot_general(
        cot_store.reshape(-1, width),
        act_store.reshape(-1, inner),
        (((0,), (0,)), ((), ())),
        preferred_element_type=jnp.float32,
    )


def shards(inputs_down, inputs_up, w_in, w_out):
    section_count = lax.axis_size("section")
    section_pos = lax.axis_index("section")
    micro_count = inputs_down.shape[0]
    step_count = section_count + micro_count - 1
    bit_count = section_count.bit_length() - 1
    down_one, up_one = (w_in[0, 0], w_in[0, 1])
    down_two, up_two = (w_out[0, 0], w_out[0, 1])
    is_first = section_pos == 0
    is_last = section_pos == section_count - 1
    zero_rows = jnp.zeros_like(inputs_down[0])
    zero_stash = jnp.zeros_like(inputs_down)
    zero_act_rows = jnp.zeros((inputs_down.shape[1], down_one.shape[1]), jnp.bfloat16)
    zero_act = jnp.zeros((micro_count, inputs_down.shape[1], down_one.shape[1]), jnp.bfloat16)
    ticks = jnp.arange(step_count, dtype=jnp.int32)

    def pass_through(rows_now):
        return rows_now

    def layer_down(rows_now):
        return forward_layer(rows_now, down_one, down_two)

    def layer_up(rows_now):
        return forward_layer(rows_now, up_one, up_two)

    def forward_pass(run_down, run_up):

        def advance(state_now, tick_num):
            down_buf, up_buf, stash_down, stash_up, final_down, final_up = state_now
            if run_down:
                mb_slot = tick_num - section_pos
                active_now = (mb_slot >= 0) & (mb_slot < micro_count)
                slot_index = jnp.clip(mb_slot, 0, micro_count - 1)
                fed_rows = jnp.where(is_first, inputs_down[slot_index], down_buf)
                result = lax.cond(active_now, layer_down, pass_through, fed_rows)
                stash_down = lax.dynamic_update_index_in_dim(
                    stash_down,
                    jnp.where(active_now, fed_rows, stash_down[slot_index]),
                    slot_index,
                    0,
                )
                final_down = lax.dynamic_update_index_in_dim(
                    final_down,
                    jnp.where(active_now & is_last, result, final_down[slot_index]),
                    slot_index,
                    0,
                )
                down_buf = passed_along(result, "section", 1)
            if run_up:
                mb_slot = tick_num - (section_count - 1 - section_pos)
                active_now = (mb_slot >= 0) & (mb_slot < micro_count)
                slot_index = jnp.clip(mb_slot, 0, micro_count - 1)
                fed_rows = jnp.where(is_last, inputs_up[slot_index], up_buf)
                result = lax.cond(active_now, layer_up, pass_through, fed_rows)
                stash_up = lax.dynamic_update_index_in_dim(
                    stash_up, jnp.where(active_now, fed_rows, stash_up[slot_index]), slot_index, 0
                )
                final_up = lax.dynamic_update_index_in_dim(
                    final_up,
                    jnp.where(active_now & is_first, result, final_up[slot_index]),
                    slot_index,
                    0,
                )
                up_buf = passed_along(result, "section", -1)
            return ((down_buf, up_buf, stash_down, stash_up, final_down, final_up), None)

        start = (zero_rows, zero_rows, zero_stash, zero_stash, zero_stash, zero_stash)
        state_end, unused = lax.scan(advance, start, ticks)
        return state_end

    def skip_back(packed):
        return (packed[1], zero_act_rows)

    def back_down(packed):
        return backward_layer(packed[0], packed[1], down_one, down_two)

    def back_up(packed):
        return backward_layer(packed[0], packed[1], up_one, up_two)

    def backward_pass(run_down, run_up, stash_down, stash_up, final_down, final_up):

        def retreat(state_now, tick_num):
            down_buf, up_buf, cot_down, act_down, cot_up, act_up = state_now
            if run_down:
                mb_slot = tick_num - (section_count - 1 - section_pos)
                active_now = (mb_slot >= 0) & (mb_slot < micro_count)
                slot_index = jnp.clip(mb_slot, 0, micro_count - 1)
                fed_rows = jnp.where(is_last, seed_rows(final_down[slot_index]), down_buf)
                sent_rows, act_rows = lax.cond(
                    active_now, back_down, skip_back, (stash_down[slot_index], fed_rows)
                )
                cot_down = lax.dynamic_update_index_in_dim(
                    cot_down, jnp.where(active_now, fed_rows, cot_down[slot_index]), slot_index, 0
                )
                act_down = lax.dynamic_update_index_in_dim(
                    act_down, jnp.where(active_now, act_rows, act_down[slot_index]), slot_index, 0
                )
                down_buf = passed_along(sent_rows, "section", -1)
            if run_up:
                mb_slot = tick_num - section_pos
                active_now = (mb_slot >= 0) & (mb_slot < micro_count)
                slot_index = jnp.clip(mb_slot, 0, micro_count - 1)
                fed_rows = jnp.where(is_first, seed_rows(final_up[slot_index]), up_buf)
                sent_rows, act_rows = lax.cond(
                    active_now, back_up, skip_back, (stash_up[slot_index], fed_rows)
                )
                cot_up = lax.dynamic_update_index_in_dim(
                    cot_up, jnp.where(active_now, fed_rows, cot_up[slot_index]), slot_index, 0
                )
                act_up = lax.dynamic_update_index_in_dim(
                    act_up, jnp.where(active_now, act_rows, act_up[slot_index]), slot_index, 0
                )
                up_buf = passed_along(sent_rows, "section", 1)
            return ((down_buf, up_buf, cot_down, act_down, cot_up, act_up), None)

        start = (zero_rows, zero_rows, zero_stash, zero_act, zero_stash, zero_act)
        state_end, unused = lax.scan(retreat, start, ticks)
        return (state_end[2], state_end[3], state_end[4], state_end[5])

    down_state = forward_pass(True, False)
    up_state = forward_pass(False, True)
    cot_down, act_down, unused_a, unused_b = backward_pass(
        True, False, down_state[2], up_state[3], down_state[4], up_state[5]
    )
    unused_c, unused_d, cot_up, act_up = backward_pass(
        False, True, down_state[2], up_state[3], down_state[4], up_state[5]
    )
    part_down = outer_grad(cot_down, act_down).astype(jnp.bfloat16)
    part_up = outer_grad(cot_up, act_up).astype(jnp.bfloat16)
    bit_order = list(range(bit_count))
    received = part_up
    for bit_num in bit_order:
        received = partner(received, "section", bit_num)
    summed = (
        lax.psum_scatter(
            part_down.astype(jnp.float32).astype(jnp.bfloat16),
            "dp",
            scatter_dimension=0,
            tiled=True,
        ).astype(jnp.float32),
        lax.psum_scatter(
            received.astype(jnp.float32).astype(jnp.bfloat16), "dp", scatter_dimension=0, tiled=True
        ).astype(jnp.float32),
    )
    own_share = lax.optimization_barrier(summed[0].astype(jnp.bfloat16)).astype(jnp.float32)
    far_share = lax.optimization_barrier(summed[1].astype(jnp.bfloat16)).astype(jnp.float32)
    total = own_share + far_share
    return total[None]


def solution(mesh):
    placed = (
        P("dp", None, None),
        P("dp", None, None),
        P("section", None, None, None),
        P("section", None, None, None),
    )
    return jax.shard_map(
        shards, mesh=mesh, in_specs=placed, out_specs=P("section", "dp", None), check_vma=False
    )
```

profile of v0, /device:TPU:2, one launch (start us, length us, event | category | flops | bytes accessed | tf_op | source)
XLA Modules:
  0.0 1990.8 jit_solution(3466535035934635851)
XLA Ops:
  15.5 361.9 %while.62 = (s32[]{:T(128)}, bf16[24,5120]{1,0:T(8,128)(2,1)}, bf16[3,24,5120]{2,1,0:T(8,128)(2,1)S(1)}, bf16[3,24,5120]{2,1,0:T(8,128)(2,1)}, s32[18]{0:T(128)S...) while((s32[]{:T(128)}, bf16[24,5120]{1,0:T(8,128)(2,1)}, ...), condition=%wide.region_16.17_spmd, body=%wide.region_12.16_spmd.sunk | while | flops 127334432 | bytes 11387601 | solution.py:139
  21.7 13.7 collective-permute-done.2
  90.1 11.8 collective-permute-done.2
  108.1 15.7 collective-permute-done.2
  145.4 12.1 collective-permute-done.2
  194.4 12.1 collective-permute-done.2
  258.4 56.0 %collective-permute-done.2 = bf16[24,5120]{1,0:T(8,128)(2,1)} collective-permute-done((bf16[24,5120]{1,0:T(8,128)(2,1)}, bf16[24,5120]{1,0:T(8,128)(2,1)}, u32[]{:S(2)}, u32[]{:S(2)}) %collective-permute-start.2) | collective-permute-done | bytes 245792 | tf_op jit(solution)/shard_map/while/body/eval_jaxpr/ppermute | solution.py:13
  379.1 417.2 %while.63 = (s32[]{:T(128)}, bf16[24,5120]{1,0:T(8,128)(2,1)}, bf16[3,24,5120]{2,1,0:T(8,128)(2,1)}, bf16[3,24,256]{2,1,0:T(8,128)(2,1)S(1)}, s32[18]{0:T(128)S(...) while((s32[]{:T(128)}, bf16[24,5120]{1,0:T(8,128)(2,1)}, ...), condition=%wide.region_22.23_spmd, body=%wide.region_17.22_spmd.sunk | while | flops 191662112 | bytes 13396661 | solution.py:188
  455.2 15.9 collective-permute-start.3
  530.7 15.1 collective-permute-start.3
  611.5 13.5 collective-permute-start.3
  650.7 13.0 collective-permute-start.3
  718.1 72.2 %collective-permute-start.3 = (bf16[24,5120]{1,0:T(8,128)(2,1)}, bf16[24,5120]{1,0:T(8,128)(2,1)}, u32[]{:S(2)}, u32[]{:S(2)}) collective-permute-start(bf16[24,5120]{1,0:T(8,128)(2,1)} %get-tuple-element.874), channel_id=1, source_target_pairs={{0,16},{16,32},{32,48},{48,64},{64,80},{80,96},{96,112},{112,128},... | collective-permute-start | bytes 737288 | tf_op jit(solution)/shard_map/while/body/eval_jaxpr/ppermute | solution.py:13
  798.4 19.1 collective-permute-start.4
  817.4 102.3 %collective-permute-done.4 = bf16[5120,256]{1,0:T(8,128)(2,1)} collective-permute-done((bf16[5120,256]{1,0:T(8,128)(2,1)S(1)}, bf16[5120,256]{1,0:T(8,128)(2,1)}, u32[]{:S(2)}, u32[]{:S(2)}) %collective-permute-start.4) | collective-permute-done | bytes 2621472 | tf_op jit(solution)/shard_map/ppermute | solution.py:23
  919.7 34.4 %collective-permute-start.5 = (bf16[5120,256]{1,0:T(8,128)(2,1)}, bf16[5120,256]{1,0:T(8,128)(2,1)}, u32[]{:S(2)}, u32[]{:S(2)}) collective-permute-start(bf16[5120,256]{1,0:T(8,128)(2,1)} %collective-permute-done.4), channel_id=1, source_target_pairs={{0,32},{32,0},{16,48},{48,16},{64,96},{96,64},{80,112},{112,80},{1... | collective-permute-start | bytes 7864328 | tf_op jit(solution)/shard_map/ppermute | solution.py:23
  954.1 117.2 %collective-permute-done.5 = bf16[5120,256]{1,0:T(8,128)(2,1)} collective-permute-done((bf16[5120,256]{1,0:T(8,128)(2,1)}, bf16[5120,256]{1,0:T(8,128)(2,1)}, u32[]{:S(2)}, u32[]{:S(2)}) %collective-permute-start.5) | collective-permute-done | bytes 2621472 | tf_op jit(solution)/shard_map/ppermute | solution.py:23
  1071.4 23.8 %collective-permute-start.6 = (bf16[5120,256]{1,0:T(8,128)(2,1)}, bf16[5120,256]{1,0:T(8,128)(2,1)}, u32[]{:S(2)}, u32[]{:S(2)}) collective-permute-start(bf16[5120,256]{1,0:T(8,128)(2,1)} %collective-permute-done.5), channel_id=1, source_target_pairs={{0,64},{64,0},{16,80},{80,16},{32,96},{96,32},{48,112},{112,48},{1... | collective-permute-start | bytes 7864328 | tf_op jit(solution)/shard_map/ppermute | solution.py:23
  1096.9 325.7 %while.60 = (s32[]{:T(128)}, bf16[24,5120]{1,0:T(8,128)(2,1)}, bf16[3,24,5120]{2,1,0:T(8,128)(2,1)S(1)}, bf16[3,24,5120]{2,1,0:T(8,128)(2,1)}, s32[18]{0:T(128)S...) while((s32[]{:T(128)}, bf16[24,5120]{1,0:T(8,128)(2,1)}, ...), condition=%wide.region_4.5_spmd, body=%wide.region_0.4_spmd.sunk | while | flops 127334432 | bytes 11387601 | solution.py:139
  1161.0 12.4 collective-permute-start
  1196.5 13.9 collective-permute-start
  1306.4 12.2 collective-permute-start
  1424.3 419.1 %while.61 = (s32[]{:T(128)}, bf16[24,5120]{1,0:T(8,128)(2,1)}, bf16[3,24,5120]{2,1,0:T(8,128)(2,1)}, bf16[3,24,256]{2,1,0:T(8,128)(2,1)S(1)}, s32[18]{0:T(128)S(...) while((s32[]{:T(128)}, bf16[24,5120]{1,0:T(8,128)(2,1)}, ...), condition=%wide.region_10.11_spmd, body=%wide.region_5.10_spmd.sunk | while | flops 191662112 | bytes 13396661 | solution.py:188
  1492.3 13.6 collective-permute-done.1
  1511.4 11.9 collective-permute-done.1
  1543.4 14.3 collective-permute-done.1
  1595.9 22.2 %collective-permute-done.1 = bf16[24,5120]{1,0:T(8,128)(2,1)} collective-permute-done((bf16[24,5120]{1,0:T(8,128)(2,1)}, bf16[24,5120]{1,0:T(8,128)(2,1)}, u32[]{:S(2)}, u32[]{:S(2)}) %collective-permute-start.1) | collective-permute-done | bytes 245792 | tf_op jit(solution)/shard_map/while/body/eval_jaxpr/ppermute | solution.py:13
  1667.7 99.9 %collective-permute-done.1 = bf16[24,5120]{1,0:T(8,128)(2,1)} collective-permute-done((bf16[24,5120]{1,0:T(8,128)(2,1)}, bf16[24,5120]{1,0:T(8,128)(2,1)}, u32[]{:S(2)}, u32[]{:S(2)}) %collective-permute-start.1) | collective-permute-done | bytes 245792 | tf_op jit(solution)/shard_map/while/body/eval_jaxpr/ppermute | solution.py:13
  1780.5 17.9 collective-permute-done.1
  1850.3 30.1 %collective-permute-done.7 = bf16[5120,256]{1,0:T(8,128)(2,1)S(1)} collective-permute-done((bf16[5120,256]{1,0:T(8,128)(2,1)}, bf16[5120,256]{1,0:T(8,128)(2,1)S(1)}, u32[]{:S(2)}, u32[]{:S(2)}) %collective-permute-start.7) | collective-permute-done | bytes 2621472 | tf_op jit(solution)/shard_map/ppermute | solution.py:23
  1882.0 32.9 %reduce-scatter.3.cloned.1.call-done = bf16[320,256]{1,0:T(8,128)(2,1)} async-done(((bf16[5120,256]{1,0:T(8,128)(2,1)}), bf16[320,256]{1,0:T(8,128)(2,1)}) %reduce-scatter.3.cloned.1.call-update) | async-done | bytes 163856 | tf_op jit(solution)/shard_map/reduce_scatter | solution.py:206
  1914.9 67.3 %reduce-scatter.5.cloned.1.call-done = bf16[320,256]{1,0:T(8,128)(2,1)} async-done(((bf16[5120,256]{1,0:T(8,128)(2,1)}), bf16[320,256]{1,0:T(8,128)(2,1)}) %reduce-scatter.5.cloned.1.call-update) | async-done | bytes 163856 | tf_op jit(solution)/shard_map/reduce_scatter | solution.py:212
  (686 shorter events, 1123.6 us)
Async XLA Ops:
  6.5 1908.4 %reduce-scatter.3.cloned.1.call-start = ((), (), s32[]{:S(2)}) async-start(), calls=%async_computation.2 | async-start | bytes 2785280 | tf_op jit(solution)/shard_map/reduce_scatter | solution.py:206
  18.7 16.7 collective-permute-start.2
  87.0 14.8 collective-permute-start.2
  105.0 18.8 collective-permute-start.2
  142.3 15.1 collective-permute-start.2
  191.3 15.1 collective-permute-start.2
  255.3 59.0 %collective-permute-start.2 = (bf16[24,5120]{1,0:T(8,128)(2,1)}, bf16[24,5120]{1,0:T(8,128)(2,1)}, u32[]{:S(2)}, u32[]{:S(2)}) collective-permute-start(bf16[24,5120]{1,0:T(8,128)(2,1)} %get-tuple-element.1066), channel_id=1, source_target_pairs={{16,0},{32,16},{48,32},{64,48},{80,64},{96,80},{112,96},{128,112},... | collective-permute-start | bytes 737288 | tf_op jit(solution)/shard_map/while/body/eval_jaxpr/ppermute | solution.py:13
  455.2 20.4 %collective-permute-start.3 = (bf16[24,5120]{1,0:T(8,128)(2,1)}, bf16[24,5120]{1,0:T(8,128)(2,1)}, u32[]{:S(2)}, u32[]{:S(2)}) collective-permute-start(bf16[24,5120]{1,0:T(8,128)(2,1)} %get-tuple-element.874), channel_id=1, source_target_pairs={{0,16},{16,32},{32,48},{48,64},{64,80},{80,96},{96,112},{112,128},... | collective-permute-start | bytes 737288 | tf_op jit(solution)/shard_map/while/body/eval_jaxpr/ppermute | solution.py:13
  530.7 20.2 %collective-permute-start.3 = (bf16[24,5120]{1,0:T(8,128)(2,1)}, bf16[24,5120]{1,0:T(8,128)(2,1)}, u32[]{:S(2)}, u32[]{:S(2)}) collective-permute-start(bf16[24,5120]{1,0:T(8,128)(2,1)} %get-tuple-element.874), channel_id=1, source_target_pairs={{0,16},{16,32},{32,48},{48,64},{64,80},{80,96},{96,112},{112,128},... | collective-permute-start | bytes 737288 | tf_op jit(solution)/shard_map/while/body/eval_jaxpr/ppermute | solution.py:13
  554.9 15.1 collective-permute-start.3
  592.5 15.0 collective-permute-start.3
  611.5 18.5 collective-permute-start.3
  650.7 19.2 collective-permute-start.3
  718.1 78.2 %collective-permute-start.3 = (bf16[24,5120]{1,0:T(8,128)(2,1)}, bf16[24,5120]{1,0:T(8,128)(2,1)}, u32[]{:S(2)}, u32[]{:S(2)}) collective-permute-start(bf16[24,5120]{1,0:T(8,128)(2,1)} %get-tuple-element.874), channel_id=1, source_target_pairs={{0,16},{16,32},{32,48},{48,64},{64,80},{80,96},{96,112},{112,128},... | collective-permute-start | bytes 737288 | tf_op jit(solution)/shard_map/while/body/eval_jaxpr/ppermute | solution.py:13
  798.4 121.4 %collective-permute-start.4 = (bf16[5120,256]{1,0:T(8,128)(2,1)S(1)}, bf16[5120,256]{1,0:T(8,128)(2,1)}, u32[]{:S(2)}, u32[]{:S(2)}) collective-permute-start(bf16[5120,256]{1,0:T(8,128)(2,1)S(1)} %fusion.75), channel_id=1, source_target_pairs={{0,16},{16,0},{32,48},{48,32},{64,80},{80,64},{96,112},{112,96},{1... | collective-permute-start | bytes 7864328 | tf_op jit(solution)/shard_map/ppermute | solution.py:23
  919.7 151.6 %collective-permute-start.5 = (bf16[5120,256]{1,0:T(8,128)(2,1)}, bf16[5120,256]{1,0:T(8,128)(2,1)}, u32[]{:S(2)}, u32[]{:S(2)}) collective-permute-start(bf16[5120,256]{1,0:T(8,128)(2,1)} %collective-permute-done.4), channel_id=1, source_target_pairs={{0,32},{32,0},{16,48},{48,16},{64,96},{96,64},{80,112},{112,80},{1... | collective-permute-start | bytes 7864328 | tf_op jit(solution)/shard_map/ppermute | solution.py:23
  1071.4 775.6 %collective-permute-start.6 = (bf16[5120,256]{1,0:T(8,128)(2,1)}, bf16[5120,256]{1,0:T(8,128)(2,1)}, u32[]{:S(2)}, u32[]{:S(2)}) collective-permute-start(bf16[5120,256]{1,0:T(8,128)(2,1)} %collective-permute-done.5), channel_id=1, source_target_pairs={{0,64},{64,0},{16,80},{80,16},{32,96},{96,32},{48,112},{112,48},{1... | collective-permute-start | bytes 7864328 | tf_op jit(solution)/shard_map/ppermute | solution.py:23
  1122.4 15.2 collective-permute-start
  1161.0 16.4 collective-permute-start
  1196.5 19.2 collective-permute-start
  1233.8 17.9 collective-permute-start
  1254.7 16.0 collective-permute-start
  1306.4 15.7 collective-permute-start
  1325.1 16.9 collective-permute-start
  1345.0 15.6 collective-permute-start
  1490.9 14.9 collective-permute-start.1
  1542.1 15.6 collective-permute-start.1
  1594.6 23.5 %collective-permute-start.1 = (bf16[24,5120]{1,0:T(8,128)(2,1)}, bf16[24,5120]{1,0:T(8,128)(2,1)}, u32[]{:S(2)}, u32[]{:S(2)}) collective-permute-start(bf16[24,5120]{1,0:T(8,128)(2,1)} %get-tuple-element.846), channel_id=1, source_target_pairs={{16,0},{32,16},{48,32},{64,48},{80,64},{96,80},{112,96},{128,112},... | collective-permute-start | bytes 737288 | tf_op jit(solution)/shard_map/while/body/eval_jaxpr/ppermute | solution.py:13
  1666.4 101.3 %collective-permute-start.1 = (bf16[24,5120]{1,0:T(8,128)(2,1)}, bf16[24,5120]{1,0:T(8,128)(2,1)}, u32[]{:S(2)}, u32[]{:S(2)}) collective-permute-start(bf16[24,5120]{1,0:T(8,128)(2,1)} %get-tuple-element.846), channel_id=1, source_target_pairs={{16,0},{32,16},{48,32},{64,48},{80,64},{96,80},{112,96},{128,112},... | collective-permute-start | bytes 737288 | tf_op jit(solution)/shard_map/while/body/eval_jaxpr/ppermute | solution.py:13
  1779.2 19.2 collective-permute-start.1
  1846.9 135.3 %reduce-scatter.5.cloned.1.call-start = ((), (), s32[]{:S(2)}) async-start(), calls=%async_computation.3 | async-start | bytes 2785280 | tf_op jit(solution)/shard_map/reduce_scatter | solution.py:212
  1847.0 33.5 %collective-permute-start.7 = (bf16[5120,256]{1,0:T(8,128)(2,1)}, bf16[5120,256]{1,0:T(8,128)(2,1)S(1)}, u32[]{:S(2)}, u32[]{:S(2)}) collective-permute-start(bf16[5120,256]{1,0:T(8,128)(2,1)} %collective-permute-done.6), channel_id=1, source_target_pairs={{0,128},{128,0},{16,144},{144,16},{32,160},{160,32},{48,176},{176,... | collective-permute-start | bytes 7864328 | tf_op jit(solution)/shard_map/ppermute | solution.py:23
  (53 other events, 544.1 us)
Sparse Core Ops, SparseCore 0:
  1847.1 67.7 reduce-scatter.2
  1917.4 64.7 reduce-scatter.4
where the time goes:
time: 2000 us; the launch traced here: 1990 us
  waiting for transfers between devices  1030 us (52%)
  starting transfers between devices  504 us (25%)
  other arithmetic  182 us (9%)
  local copies, waits for them, and re-layouts  138 us (7%)
  matrix products  73 us (4%)
  loops' own time  49.1 us (2%)
    ppermute x72, waiting for transfers between devices, passed_along(): lax.ppermute(value, axis, [(source, source + steps) for source in range(f...  681 us
    ppermute x72, starting transfers between devices, passed_along(): lax.ppermute(value, axis, [(source, source + steps) for source in range(f...  424 us
    ppermute x4, waiting for transfers between devices, partner(): return lax.ppermute(block, axis, route)  250 us
    ppermute x4, starting transfers between devices, partner(): return lax.ppermute(block, axis, route)  80.6 us
    reduce_scatter x1, waiting for transfers between devices, shards(): lax.psum_scatter(received.astype(jnp.float32).astype(jnp.bfloat16), 'dp',...  67.3 us
    dynamic_slice x72, local copies, waits for them, and re-layouts, forward_pass(): state_end, unused = lax.scan(advance, start, ticks)  41.9 us
  transfers between devices with their start and end apart: 78, of which 77 were waited for; matrix products, arithmetic and copies ran while one was open for 11% of the time, Pallas kernels for 0%

commit v1 on v0

v1 whole, which is shorter than its diff:
```python
import jax
import jax.numpy as jnp
from jax import lax
from jax.experimental import pallas as pl
from jax.experimental.pallas import tpu as pltpu
from jax.sharding import Mesh, PartitionSpec as P

EPS = 1e-06
COT = 0.0625
D, R = 5120, 256
REAL, ROWS = 18, 24
SET = 4
CH = 4
CW = D // CH
DP = ("zl", "x", "core")
GRID_AXES = ("y", "zh", "zl", "x", "core")
ANY = pl.BlockSpec(memory_space=pl.ANY)
VM = pl.BlockSpec(memory_space=pltpu.VMEM)
SM = pl.BlockSpec(memory_space=pltpu.SMEM)


def weight_copy(w_ref, wbuf, sem, flags, layer, which):
    held = jnp.where(flags[1] == 1, SET - 1 - layer, layer)
    slot = lax.rem(layer, 2)
    return pltpu.make_async_copy(
        w_ref.at[held, :, which], wbuf.at[slot, which], sem.at[slot, which]
    )


def chunk(wbuf, slot, which, c):
    per = 16 // CH
    return wbuf[slot, which, c * per : (c + 1) * per].reshape(CW, R)


def columns(c):
    return slice(c * CW, (c + 1) * CW)


def inverse_rms(hbuf, layer):
    total = jnp.zeros((ROWS, 1), jnp.float32)
    for c in range(CH):
        v = hbuf[layer, :, columns(c)].astype(jnp.float32)
        total = total + jnp.sum(v * v, axis=-1, keepdims=True)
    return lax.rsqrt(total * (1.0 / D) + EPS)


def forward_kernel(*refs, aliased):
    flags, x_ref, w_ref = refs[:3]
    refs = refs[3 + (3 if aliased else 0) :]
    y_ref, h_out, pre_out, act_out = refs[:4]
    wbuf, hbuf, prebuf, actbuf, sem_w, sem_h, sem_p, sem_a = refs[4:]

    @pl.when(flags[0] == 1)
    def _():
        for which in range(2):
            weight_copy(w_ref, wbuf, sem_w, flags, 0, which).start()
        hbuf[0] = x_ref[...]

        def step(layer, carry):
            slot = lax.rem(layer, 2)

            @pl.when(layer + 1 < SET)
            def _():
                for which in range(2):
                    weight_copy(w_ref, wbuf, sem_w, flags, layer + 1, which).start()

            pltpu.make_async_copy(hbuf.at[layer], h_out.at[layer], sem_h.at[layer]).start()
            inv = inverse_rms(hbuf, layer)
            weight_copy(w_ref, wbuf, sem_w, flags, layer, 0).wait()
            pre = jnp.zeros((ROWS, R), jnp.float32)
            for c in range(CH):
                normed = (hbuf[layer, :, columns(c)].astype(jnp.float32) * inv).astype(jnp.bfloat16)
                pre = pre + jnp.dot(
                    normed, chunk(wbuf, slot, 0, c), preferred_element_type=jnp.float32
                )
            active = (pre / (1.0 + jnp.exp(-pre))).astype(jnp.bfloat16)
            prebuf[layer] = pre
            actbuf[layer] = active
            weight_copy(w_ref, wbuf, sem_w, flags, layer, 1).wait()
            for c in range(CH):
                branch = lax.dot_general(
                    active,
                    chunk(wbuf, slot, 1, c),
                    (((1,), (1,)), ((), ())),
                    preferred_element_type=jnp.float32,
                )
                before = hbuf[layer, :, columns(c)].astype(jnp.float32)
                hbuf[layer + 1, :, columns(c)] = (before + branch).astype(jnp.bfloat16)
            return carry

        lax.fori_loop(0, SET, step, 0)
        y_ref[...] = hbuf[SET]
        copies = [
            pltpu.make_async_copy(prebuf, pre_out, sem_p.at[0]),
            pltpu.make_async_copy(actbuf, act_out, sem_a.at[0]),
        ]
        for one in copies:
            one.start()
        for layer in range(SET):
            copies.append(
                pltpu.make_async_copy(hbuf.at[layer], h_out.at[layer], sem_h.at[layer])
            )
        for one in copies:
            one.wait()


def run_forward(flags, rows, weights, held=None):
    outs = (
        jax.ShapeDtypeStruct((ROWS, D), jnp.bfloat16),
        jax.ShapeDtypeStruct((SET, ROWS, D), jnp.bfloat16),
        jax.ShapeDtypeStruct((SET, ROWS, R), jnp.float32),
        jax.ShapeDtypeStruct((SET, ROWS, R), jnp.bfloat16),
    )
    aliased = held is not None
    return pl.pallas_call(
        lambda *refs: forward_kernel(*refs, aliased=aliased),
        out_shape=outs,
        in_specs=[SM, VM, ANY] + ([ANY] * 3 if aliased else []),
        out_specs=(VM, ANY, ANY, ANY),
        scratch_shapes=[
            pltpu.VMEM((2, 2, 16, D // 16, R), jnp.bfloat16),
            pltpu.VMEM((SET + 1, ROWS, D), jnp.bfloat16),
            pltpu.VMEM((SET, ROWS, R), jnp.float32),
            pltpu.VMEM((SET, ROWS, R), jnp.bfloat16),
            pltpu.SemaphoreType.DMA((2, 2)),
            pltpu.SemaphoreType.DMA((SET,)),
            pltpu.SemaphoreType.DMA((1,)),
            pltpu.SemaphoreType.DMA((1,)),
        ],
        input_output_aliases={3: 1, 4: 2, 5: 3} if aliased else {},
        compiler_params=pltpu.CompilerParams(vmem_limit_bytes=40 * 2**20),
        cost_estimate=pl.CostEstimate(
            flops=4 * SET * ROWS * D * R, bytes_accessed=SET * 4 * D * R, transcendentals=0
        ),
        name="forward_set",
    )(flags, rows, weights, *(held or ()))


def backward_kernel(*refs, aliased, from_final, last):
    flags, g_ref, w_ref, h_in, pre_in = refs[:5]
    refs = refs[5 + (1 if aliased else 0) :]
    y_ref, g_out = refs[:2]
    wbuf, hbuf, prebuf, gbuf, dnbuf, sem_w, sem_h, sem_p, sem_g = refs[2:]

    @pl.when(flags[0] == 1)
    def _():
        def wanted(step, which):
            held = jnp.where(flags[1] == 1, step, SET - 1 - step)
            slot = lax.rem(step, 2)
            return pltpu.make_async_copy(
                w_ref.at[held, :, which], wbuf.at[slot, which], sem_w.at[slot, which]
            )

        wanted(0, 1).start()
        wanted(0, 0).start()
        pre_copy = pltpu.make_async_copy(pre_in, prebuf, sem_p.at[0])
        pre_copy.start()
        for layer in range(SET - 1, -1, -1):
            pltpu.make_async_copy(h_in.at[layer], hbuf.at[layer], sem_h.at[layer]).start()
        if from_final:
            gbuf[0] = (g_ref[...].astype(jnp.float32) * COT).astype(jnp.bfloat16)
        else:
            gbuf[0] = g_ref[...]
        pre_copy.wait()
        steps = SET - 1 if last else SET

        def one_layer(step, carry):
            layer = SET - 1 - step
            slot = lax.rem(step, 2)

            @pl.when(step + 1 < steps)
            def _():
                wanted(step + 1, 1).start()
                wanted(step + 1, 0).start()

            pltpu.make_async_copy(gbuf.at[step], g_out.at[layer], sem_g.at[step]).start()
            pltpu.make_async_copy(h_in.at[layer], hbuf.at[layer], sem_h.at[layer]).wait()
            inv = inverse_rms(hbuf, layer)
            pre = prebuf[layer]
            sigma = 1.0 / (1.0 + jnp.exp(-pre))
            slope = sigma * (1.0 + pre * (1.0 - sigma))
            wanted(step, 1).wait()
            d_active = jnp.zeros((ROWS, R), jnp.float32)
            for c in range(CH):
                d_active = d_active + jnp.dot(
                    gbuf[step, :, columns(c)],
                    chunk(wbuf, slot, 1, c),
                    preferred_element_type=jnp.float32,
                )
            d_pre = (d_active * slope).astype(jnp.bfloat16)
            wanted(step, 0).wait()
            total = jnp.zeros((ROWS, 1), jnp.float32)
            for c in range(CH):
                d_normed = lax.dot_general(
                    d_pre,
                    chunk(wbuf, slot, 0, c),
                    (((1,), (1,)), ((), ())),
                    preferred_element_type=jnp.float32,
                )
                unit = hbuf[layer, :, columns(c)].astype(jnp.float32) * inv
                total = total + jnp.sum(d_normed * unit, axis=-1, keepdims=True)
                dnbuf[:, columns(c)] = d_normed
            mean = total * (1.0 / D)
            for c in range(CH):
                unit = hbuf[layer, :, columns(c)].astype(jnp.float32) * inv
                moved = inv * (dnbuf[:, columns(c)] - unit * mean)
                before = gbuf[step, :, columns(c)].astype(jnp.float32)
                gbuf[step + 1, :, columns(c)] = (before + moved).astype(jnp.bfloat16)
            return carry

        lax.fori_loop(0, steps, one_layer, 0)
        if last:
            pltpu.make_async_copy(gbuf.at[SET - 1], g_out.at[0], sem_g.at[SET - 1]).start()
            pltpu.make_async_copy(h_in.at[0], hbuf.at[0], sem_h.at[0]).wait()
        y_ref[...] = gbuf[steps]
        for step in range(SET):
            pltpu.make_async_copy(
                gbuf.at[step], g_out.at[SET - 1 - step], sem_g.at[step]
            ).wait()


def run_backward(flags, g_rows, weights, h_held, pre_held, held=None, from_final=False, last=False):
    outs = (
        jax.ShapeDtypeStruct((ROWS, D), jnp.bfloat16),
        jax.ShapeDtypeStruct((SET, ROWS, D), jnp.bfloat16),
    )
    aliased = held is not None
    return pl.pallas_call(
        lambda *refs: backward_kernel(*refs, aliased=aliased, from_final=from_final, last=last),
        out_shape=outs,
        in_specs=[SM, VM, ANY, ANY, ANY] + ([ANY] if aliased else []),
        out_specs=(VM, ANY),
        scratch_shapes=[
            pltpu.VMEM((2, 2, 16, D // 16, R), jnp.bfloat16),
            pltpu.VMEM((SET, ROWS, D), jnp.bfloat16),
            pltpu.VMEM((SET, ROWS, R), jnp.float32),
            pltpu.VMEM((SET + 1, ROWS, D), jnp.bfloat16),
            pltpu.VMEM((ROWS, D), jnp.float32),
            pltpu.SemaphoreType.DMA((2, 2)),
            pltpu.SemaphoreType.DMA((SET,)),
            pltpu.SemaphoreType.DMA((1,)),
            pltpu.SemaphoreType.DMA((SET,)),
        ],
        input_output_aliases={5: 1} if aliased else {},
        compiler_params=pltpu.CompilerParams(vmem_limit_bytes=40 * 2**20),
        cost_estimate=pl.CostEstimate(
            flops=4 * SET * ROWS * D * R, bytes_accessed=SET * 4 * D * R, transcendentals=0
        ),
        name="backward_set",
    )(flags, g_rows, weights, h_held, pre_held, *((held,) if aliased else ()))


def grad_kernel(g_ref, act_ref, out_ref, *, first):
    for layer in range(SET):
        g = g_ref[:, layer].reshape(16 * ROWS, D // 16)
        act = act_ref[:, first + layer].reshape(16 * ROWS, R)
        out_ref[layer] = lax.dot_general(
            g, act, (((0,), (0,)), ((), ())), preferred_element_type=jnp.float32
        ).astype(jnp.bfloat16)


def run_grad(g_all, act_all, first):
    return pl.pallas_call(
        lambda *refs: grad_kernel(*refs, first=first),
        out_shape=jax.ShapeDtypeStruct((SET, D // 16, R), jnp.bfloat16),
        in_specs=[VM, VM],
        out_specs=VM,
        compiler_params=pltpu.CompilerParams(vmem_limit_bytes=40 * 2**20),
        name="grad_set",
    )(g_all, act_all)


def hop(rows):
    return lax.ppermute(rows, "y", [(0, 1), (1, 0), (2, 3), (3, 2)])


def spread(g_set):
    cut = g_set.reshape(SET, ROWS, 16, D // 16).transpose(2, 0, 1, 3)
    return lax.all_to_all(cut, DP, 0, 0)


def shards(inputs_down, inputs_up, w_in, w_out):
    y, zh, dp = lax.axis_index("y"), lax.axis_index("zh"), lax.axis_index(DP)
    low_half = y < 2
    stage_p = (y == 0) | (y == 3)

    def own(layer_slot):
        parts = [
            lax.dynamic_slice(w, (0, layer_slot, dp * (D // 16), 0), (1, 1, D // 16, R))[0, 0]
            for w in (w_in, w_out)
        ]
        return jnp.stack(parts)

    def gathered(own_part):
        return lax.all_gather(own_part, ("zh",) + DP).reshape(SET, 16, 2, D // 16, R)

    first_slot = jnp.where(low_half, 0, 1)
    own_a, own_b = own(first_slot), own(1 - first_slot)
    w_a = gathered(own_a)
    own_b, w_a = lax.optimization_barrier((own_b, w_a))
    w_b = gathered(own_b)

    def flag(active, reverse):
        return jnp.stack([active.astype(jnp.int32), reverse.astype(jnp.int32)])

    p_a, p_b = flag(stage_p, ~low_half), flag(stage_p, low_half)
    q_a, q_b = flag(~stage_p, ~low_half), flag(~stage_p, low_half)

    mine = jnp.where(low_half, inputs_down, inputs_up).reshape(-1, D)
    mine = lax.dynamic_slice(mine, (zh * REAL, 0), (REAL, D))
    rows = jnp.pad(mine, ((0, ROWS - REAL), (0, 0)))

    rows, h_a, pre_a, act_a = run_forward(p_a, rows, w_a)
    rows = hop(rows)
    rows, h_a, pre_a, act_a = run_forward(q_a, rows, w_a, (h_a, pre_a, act_a))
    rows, h_b, pre_b, act_b = run_forward(q_b, rows, w_b)
    rows = hop(rows)
    rows, h_b, pre_b, act_b = run_forward(p_b, rows, w_b, (h_b, pre_b, act_b))
    act_all = lax.all_gather(jnp.concatenate([act_a, act_b], axis=0), DP)
    rows, g_b = run_backward(p_b, rows, w_b, h_b, pre_b, from_final=True)
    rows = hop(rows)
    rows, g_b = run_backward(q_b, rows, w_b, h_b, pre_b, held=g_b)
    rows, g_a = run_backward(q_a, rows, w_a, h_a, pre_a)
    rows = hop(rows)
    rows, g_a = run_backward(p_a, rows, w_a, h_a, pre_a, held=g_a, last=True)
    part_b = run_grad(spread(g_b), act_all, SET)
    sum_b = lax.psum_scatter(part_b, "zh", scatter_dimension=0, tiled=True)[0]
    part_a = run_grad(spread(g_a), act_all, 0)
    sum_a = lax.psum_scatter(part_a, "zh", scatter_dimension=0, tiled=True)[0]
    kept = jnp.where(low_half, sum_a, sum_b)
    other = jnp.where(low_half, sum_b, sum_a)
    received = lax.ppermute(other, "y", [(0, 3), (3, 0), (1, 2), (2, 1)])
    return (kept.astype(jnp.float32) + received.astype(jnp.float32))[None]


def solution(mesh):
    fine = Mesh(mesh.devices.reshape(4, 4, 2, 4, 2), GRID_AXES)
    section = ("y", "zh")
    placed = (
        P(DP, None, None),
        P(DP, None, None),
        P(section, None, None, None),
        P(section, None, None, None),
    )
    return jax.shard_map(
        shards, mesh=fine, in_specs=placed, out_specs=P(section, DP, None), check_vma=False
    )
```

time: 2000 us -> 436 us (0.22)
  waiting for transfers between devices: 1030 us -> 299 us
  starting transfers between devices: 504 us -> 51.9 us
  other arithmetic: 182 us -> 5.19 us
  local copies, waits for them, and re-layouts: 138 us -> 12.8 us
  matrix products: 73 us -> 0 us
  Pallas kernels: 0 us -> 53.1 us
  loops' own time: 49.1 us -> 0 us
    ppermute x76 -> x5, waiting for transfers between devices: 931 us -> 30.5 us  [the longest x4 26.7 us: hop(): return lax.ppermute(rows, 'y', [(0, 1), (1, 0), (2, 3), (3, 2)])]
    ppermute x76 -> x5, starting transfers between devices: 504 us -> 39.7 us  [the longest x4 36.8 us: hop(): return lax.ppermute(rows, 'y', [(0, 1), (1, 0), (2, 3), (3, 2)])]
    all_gather x0 -> x3, waiting for transfers between devices: none -> 202 us  [the longest x2 202 us: gathered(): lax.all_gather(own_part, ('zh',) + DP).reshape(SET, 16, 2, D // 16, R)]
    dynamic_update_slice x144 -> x0, other arithmetic: 166 us -> none  [the longest x18 35.5 us: retreat(): lax.dynamic_update_index_in_dim(cot_down, jnp.where(active_now, fed_rows,...]
    dynamic_slice x216 -> x1, local copies, waits for them, and re-layouts: 112 us -> 0.07 us  [shards(): mine = lax.dynamic_slice(mine, (zh * REAL, 0), (REAL, D))]
    dot_general x20 -> x0, matrix products: 73 us -> none  [the longest x6 30.1 us: backward_layer(): lax.dot_general(d_pre, w_one, (((1,), (1,)), ((), ())), preferred_element...]
    reduce_scatter x2, waiting for transfers between devices: 100 us -> 45.3 us  [the longest x1 30.9 us: shards(): sum_b = lax.psum_scatter(part_b, 'zh', scatter_dimension=0, tiled=True)[0]]
    pallas_call x0 -> x10, Pallas kernels: none -> 53.1 us  [the longest x4 25.6 us: run_backward(): pl.pallas_call(lambda *refs: backward_kernel(*refs, aliased=aliased, from...]
  transfers between devices with their start and end apart: 78 -> 12, of which waited for: 77 -> 11; matrix products, arithmetic and copies ran while one was open for 11% -> 2% of each run, Pallas kernels for 0% -> 6%
where the time goes in v1:
time: 436 us
  waiting for transfers between devices  299 us (69%)
  Pallas kernels  53.1 us (12%)
  starting transfers between devices  51.9 us (12%)
  between operations  13.3 us (3%)
  local copies, waits for them, and re-layouts  12.8 us (3%)
  other arithmetic  5.19 us (1%)
    all_gather x2, waiting for transfers between devices, gathered(): lax.all_gather(own_part, ('zh',) + DP).reshape(SET, 16, 2, D // 16, R)  202 us
    ppermute x4, starting transfers between devices, hop(): return lax.ppermute(rows, 'y', [(0, 1), (1, 0), (2, 3), (3, 2)])  36.8 us
    reduce_scatter x1, waiting for transfers between devices, shards(): sum_b = lax.psum_scatter(part_b, 'zh', scatter_dimension=0, tiled=True)[0]  30.9 us
    ppermute x4, waiting for transfers between devices, hop(): return lax.ppermute(rows, 'y', [(0, 1), (1, 0), (2, 3), (3, 2)])  26.7 us
    pallas_call x4, Pallas kernels, run_backward(): pl.pallas_call(lambda *refs: backward_kernel(*refs, aliased=aliased, from...  25.6 us
    pallas_call x4, Pallas kernels, run_forward(): pl.pallas_call(lambda *refs: forward_kernel(*refs, aliased=aliased), out_...  24.7 us
    all_to_all x2, waiting for transfers between devices, spread(): return lax.all_to_all(cut, DP, 0, 0)  21.4 us
    reduce_scatter x1, waiting for transfers between devices, shards(): sum_a = lax.psum_scatter(part_a, 'zh', scatter_dimension=0, tiled=True)[0]  14.4 us
  transfers between devices with their start and end apart: 12, of which 11 were waited for; matrix products, arithmetic and copies ran while one was open for 2% of the time, Pallas kernels for 6%

profile of v1, /device:TPU:2, one launch (start us, length us, event | category | flops | bytes accessed | tf_op | source)
XLA Modules:
  0.0 435.8 jit_solution(484874443999680112)
XLA Ops:
  6.5 1.3 dynamic-slice_bitcast_fusion
  7.9 0.8 pad_maximum_fusion.1
  9.4 112.9 %all-gather.7.cloned.1.call-done = bf16[128,320,256]{2,1,0:T(8,128)(2,1)} async-done(((bf16[2,320,256]{2,1,0:T(8,128)(2,1)}), bf16[128,320,256]{2,1,0:T(8,128)(2,1)}) %all-gather.7.cloned.1.call-update) | async-done | bytes 20971536 | tf_op jit(solution)/shard_map/all_gather | solution.py:295
  122.7 11.7 %forward_set.4 = (bf16[24,5120]{1,0:T(8,128)(2,1)S(1)}, bf16[4,24,5120]{2,1,0:T(8,128)(2,1)S(1)}, f32[4,24,256]{2,1,0:T(8,128)S(1)}, bf16[4,24,256]{2,1,0:T(8,128)(2,1)S(1)}) custom-call(s32[2]{0:T(128)S(1)} %pad_add_fusion.1.refs_0_, bf16[24,5120]{1,0:T(8,128)(2,1)S(1)} %pad.4.refs_1_, bf16[4,16,2,320,256]{4,3,2,1,0:T(8,128)(2,1)} %bitcast.31), custom_call_target="tpu_custom_call" | custom-call | flops 503316480 | bytes 20971520 | tf_op jit(solution)/shard_map/forward_set/pallas_call | solution.py:115
  134.7 7.9 %collective-permute-done.refs_1_ = bf16[24,5120]{1,0:T(8,128)(2,1)S(1)} collective-permute-done((bf16[24,5120]{1,0:T(8,128)(2,1)S(1)}, bf16[24,5120]{1,0:T(8,128)(2,1)S(1)}, u32[]{:S(2)}, u32[]{:S(2)}) %collective-permute-start) | collective-permute-done | bytes 245792 | tf_op jit(solution)/shard_map/ppermute | solution.py:274
  143.3 89.3 %all-gather.9.cloned.1.call-done = bf16[128,320,256]{2,1,0:T(8,128)(2,1)} async-done(((bf16[2,320,256]{2,1,0:T(8,128)(2,1)}), bf16[128,320,256]{2,1,0:T(8,128)(2,1)}) %all-gather.9.cloned.1.call-update) | async-done | bytes 20971536 | tf_op jit(solution)/shard_map/all_gather | solution.py:295
  233.3 12.6 %collective-permute-start.1 = (bf16[24,5120]{1,0:T(8,128)(2,1)S(1)}, bf16[24,5120]{1,0:T(8,128)(2,1)S(1)}, u32[]{:S(2)}, u32[]{:S(2)}) collective-permute-start(bf16[24,5120]{1,0:T(8,128)(2,1)S(1)} %get-tuple-element.37), channel_id=1, source_target_pairs={{0,64},{64,0},{128,192},{192,128},{1,65},{65,1},{129,193},{193,129... | collective-permute-start | bytes 737288 | tf_op jit(solution)/shard_map/ppermute | solution.py:274
  246.0 6.3 %collective-permute-done.1.refs_1_ = bf16[24,5120]{1,0:T(8,128)(2,1)S(1)} collective-permute-done((bf16[24,5120]{1,0:T(8,128)(2,1)S(1)}, bf16[24,5120]{1,0:T(8,128)(2,1)S(1)}, u32[]{:S(2)}, u32[]{:S(2)}) %collective-permute-start.1) | collective-permute-done | bytes 245792 | tf_op jit(solution)/shard_map/ppermute | solution.py:274
  252.3 11.7 %forward_set.7 = (bf16[24,5120]{1,0:T(8,128)(2,1)S(1)}, bf16[4,24,5120]{2,1,0:T(8,128)(2,1)S(1)}, f32[4,24,256]{2,1,0:T(8,128)S(1)}, bf16[4,24,256]{2,1,0:T(8,128)(2,1)S(1)}) custom-call(s32[2]{0:T(128)S(1)} %pad_add_fusion.2.refs_0_, ...), custom_call_target="tpu_custom_call", output_to_operand_aliasing={{1}: (3, {}), {2}: (4, {}), {3}: (5, {})} | custom-call | flops 503316480 | bytes 20971520 | tf_op jit(solution)/shard_map/forward_set/pallas_call | solution.py:115
  264.0 13.2 %backward_set.4 = (bf16[24,5120]{1,0:T(8,128)(2,1)}, bf16[4,24,5120]{2,1,0:T(8,128)(2,1)S(1)}) custom-call(s32[2]{0:T(128)S(1)} %pad_add_fusion.2.refs_0_, bf16[24,5120]{1,0:T(8,128)(2,1)S(1)} %get-tuple-element.41.refs_1_, bf16[4,16,2,320,256]{4,3,2,1,0:T(8,128)(2,1)} %bitcast.37, bf16[4,24,5120]{2,1,0:T(8,128)(2,1)S(1)} %get-tuple-element.42.refs_3_, ...), custom_call_target="tpu_custom_call" | custom-call | flops 503316480 | bytes 20971520 | tf_op jit(solution)/shard_map/backward_set/pallas_call | solution.py:228
  278.0 7.1 %collective-permute-done.2.refs_1_ = bf16[24,5120]{1,0:T(8,128)(2,1)S(1)} collective-permute-done((bf16[24,5120]{1,0:T(8,128)(2,1)}, bf16[24,5120]{1,0:T(8,128)(2,1)S(1)}, u32[]{:S(2)}, u32[]{:S(2)}) %collective-permute-start.2) | collective-permute-done | bytes 245792 | tf_op jit(solution)/shard_map/ppermute | solution.py:274
  286.5 24.0 %collective-permute-start.3 = (bf16[24,5120]{1,0:T(8,128)(2,1)S(1)}, bf16[24,5120]{1,0:T(8,128)(2,1)S(1)}, u32[]{:S(2)}, u32[]{:S(2)}) collective-permute-start(bf16[24,5120]{1,0:T(8,128)(2,1)S(1)} %get-tuple-element.49), channel_id=1, source_target_pairs={{0,64},{64,0},{128,192},{192,128},{1,65},{65,1},{129,193},{193,129... | collective-permute-start | bytes 737288 | tf_op jit(solution)/shard_map/ppermute | solution.py:274
  310.5 5.3 %collective-permute-done.3.refs_1_ = bf16[24,5120]{1,0:T(8,128)(2,1)S(1)} collective-permute-done((bf16[24,5120]{1,0:T(8,128)(2,1)S(1)}, bf16[24,5120]{1,0:T(8,128)(2,1)S(1)}, u32[]{:S(2)}, u32[]{:S(2)}) %collective-permute-start.3) | collective-permute-done | bytes 245792 | tf_op jit(solution)/shard_map/ppermute | solution.py:274
  315.8 11.1 %backward_set.7 = (bf16[24,5120]{1,0:T(8,128)(2,1)}, bf16[4,24,5120]{2,1,0:T(8,128)(2,1)S(1)}) custom-call(s32[2]{0:T(128)S(1)} %pad_add_fusion.1.refs_0_, bf16[24,5120]{1,0:T(8,128)(2,1)S(1)} %collective-permute-done.3.refs_1_, bf16[4,16,2,320,256]{4,3,2,1,0:T(8,128)(2,1)} %bitcast.34, ...), custom_call_target="tpu_custom_call", output_to_operand_aliasing={{1}: (5, {})} | custom-call | flops 503316480 | bytes 20971520 | tf_op jit(solution)/shard_map/backward_set/pallas_call | solution.py:228
  326.9 1.8 reshape.24
  328.7 2.6 copy.20
  331.3 5.3 %all-to-all-start = ((bf16[16,4,24,320]{3,2,1,0:T(8,128)(2,1)}), bf16[16,4,24,320]{3,2,1,0:T(8,128)(2,1)S(1)}, u32[]{:S(2)}, u32[]{:S(2)}) async-start(bf16[16,4,24,320]{3,2,1,0:T(8,128)(2,1)} %bitcast.40), calls=%async_computation | async-start | bytes 2359296 | tf_op jit(solution)/shard_map/all_to_all | solution.py:279
  336.6 1.8 reshape.25
  338.3 2.5 copy.19
  340.9 10.7 %all-to-all-done.refs_0_ = bf16[16,4,24,320]{3,2,1,0:T(8,128)(2,1)S(1)} async-done(((bf16[16,4,24,320]{3,2,1,0:T(8,128)(2,1)}), bf16[16,4,24,320]{3,2,1,0:T(8,128)(2,1)S(1)}, u32[]{:S(2)}, u32[]{:S(2)}) %all-to-all-start) | async-done | bytes 983072 | tf_op jit(solution)/shard_map/all_to_all | solution.py:279
  351.6 6.7 %all-to-all-start.1 = ((bf16[16,4,24,320]{3,2,1,0:T(8,128)(2,1)}), bf16[16,4,24,320]{3,2,1,0:T(8,128)(2,1)S(1)}, u32[]{:S(2)}, u32[]{:S(2)}) async-start(bf16[16,4,24,320]{3,2,1,0:T(8,128)(2,1)} %bitcast.39), calls=%async_computation.2 | async-start | bytes 2359296 | tf_op jit(solution)/shard_map/all_to_all | solution.py:279
  358.4 1.4 copy-done
  359.8 1.3 copy-done.3
  361.0 1.4 grad_set.2
  362.5 10.7 %all-to-all-done.1.refs_0_ = bf16[16,4,24,320]{3,2,1,0:T(8,128)(2,1)S(1)} async-done(((bf16[16,4,24,320]{3,2,1,0:T(8,128)(2,1)}), bf16[16,4,24,320]{3,2,1,0:T(8,128)(2,1)S(1)}, u32[]{:S(2)}, u32[]{:S(2)}) %all-to-all-start.1) | async-done | bytes 983072 | tf_op jit(solution)/shard_map/all_to_all | solution.py:279
  373.3 1.4 grad_set.3
  374.7 14.4 %reduce-scatter.3.cloned.1.call-done = bf16[1,320,256]{2,1,0:T(8,128)(2,1)} async-done(((bf16[4,320,256]{2,1,0:T(8,128)(2,1)}), bf16[1,320,256]{2,1,0:T(8,128)(2,1)}) %reduce-scatter.3.cloned.1.call-update) | async-done | bytes 163856 | tf_op jit(solution)/shard_map/reduce_scatter | solution.py:329
  389.1 30.9 %reduce-scatter.5.cloned.1.call-done = bf16[1,320,256]{2,1,0:T(8,128)(2,1)} async-done(((bf16[4,320,256]{2,1,0:T(8,128)(2,1)}), bf16[1,320,256]{2,1,0:T(8,128)(2,1)}) %reduce-scatter.5.cloned.1.call-update) | async-done | bytes 163856 | tf_op jit(solution)/shard_map/reduce_scatter | solution.py:327
  420.0 0.9 select_bitcast_fusion
  420.9 2.8 collective-permute-start.4
  423.8 3.8 collective-permute-done.4
  427.5 1.7 fusion
  (36 shorter events, 5.0 us)
Async XLA Ops:
  6.5 115.8 %all-gather.7.cloned.1.call-start = ((), (), s32[]{:S(2)}) async-start(), calls=%async_computation.6 | async-start | bytes 21299200 | tf_op jit(solution)/shard_map/all_gather | solution.py:295
  6.5 115.9 %copy-start.4 = (bf16[3,24,5120]{2,1,0:T(8,128)(2,1)S(1)}, bf16[3,24,5120]{2,1,0:T(8,128)(2,1)}, u32[]{:S(2)}) copy-start(bf16[3,24,5120]{2,1,0:T(8,128)(2,1)} %param.4) | copy-start | bytes 2211844
  6.5 115.9 %copy-start.5 = (bf16[3,24,5120]{2,1,0:T(8,128)(2,1)S(1)}, bf16[3,24,5120]{2,1,0:T(8,128)(2,1)}, u32[]{:S(2)}) copy-start(bf16[3,24,5120]{2,1,0:T(8,128)(2,1)} %param.5) | copy-start | bytes 2211844
  8.6 224.0 %all-gather.9.cloned.1.call-start = ((), (), s32[]{:S(2)}) async-start(), calls=%async_computation.7 | async-start | bytes 21299200 | tf_op jit(solution)/shard_map/all_gather | solution.py:295
  122.4 236.0 %all-gather.11.cloned.1.call-start = ((), (), s32[]{:S(2)}) async-start(), calls=%async_computation.8 | async-start | bytes 1671168 | tf_op jit(solution)/shard_map/all_gather | solution.py:319
  134.4 8.2 %collective-permute-start = (bf16[24,5120]{1,0:T(8,128)(2,1)S(1)}, bf16[24,5120]{1,0:T(8,128)(2,1)S(1)}, u32[]{:S(2)}, u32[]{:S(2)}) collective-permute-start(bf16[24,5120]{1,0:T(8,128)(2,1)S(1)} %get-tuple-element.31), channel_id=1, source_target_pairs={{0,64},{64,0},{128,192},{192,128},{1,65},{65,1},{129,193},{193,129... | collective-permute-start | bytes 737288 | tf_op jit(solution)/shard_map/ppermute | solution.py:274
  233.3 19.0 %collective-permute-start.1 = (bf16[24,5120]{1,0:T(8,128)(2,1)S(1)}, bf16[24,5120]{1,0:T(8,128)(2,1)S(1)}, u32[]{:S(2)}, u32[]{:S(2)}) collective-permute-start(bf16[24,5120]{1,0:T(8,128)(2,1)S(1)} %get-tuple-element.37), channel_id=1, source_target_pairs={{0,64},{64,0},{128,192},{192,128},{1,65},{65,1},{129,193},{193,129... | collective-permute-start | bytes 737288 | tf_op jit(solution)/shard_map/ppermute | solution.py:274
  277.2 7.9 %collective-permute-start.2 = (bf16[24,5120]{1,0:T(8,128)(2,1)}, bf16[24,5120]{1,0:T(8,128)(2,1)S(1)}, u32[]{:S(2)}, u32[]{:S(2)}) collective-permute-start(bf16[24,5120]{1,0:T(8,128)(2,1)} %get-tuple-element.44), channel_id=1, source_target_pairs={{0,64},{64,0},{128,192},{192,128},{1,65},{65,1},{129,193},{193,129... | collective-permute-start | bytes 737288 | tf_op jit(solution)/shard_map/ppermute | solution.py:274
  286.5 29.3 %collective-permute-start.3 = (bf16[24,5120]{1,0:T(8,128)(2,1)S(1)}, bf16[24,5120]{1,0:T(8,128)(2,1)S(1)}, u32[]{:S(2)}, u32[]{:S(2)}) collective-permute-start(bf16[24,5120]{1,0:T(8,128)(2,1)S(1)} %get-tuple-element.49), channel_id=1, source_target_pairs={{0,64},{64,0},{128,192},{192,128},{1,65},{65,1},{129,193},{193,129... | collective-permute-start | bytes 737288 | tf_op jit(solution)/shard_map/ppermute | solution.py:274
  331.3 20.3 %all-to-all-start = ((bf16[16,4,24,320]{3,2,1,0:T(8,128)(2,1)}), bf16[16,4,24,320]{3,2,1,0:T(8,128)(2,1)S(1)}, u32[]{:S(2)}, u32[]{:S(2)}) async-start(bf16[16,4,24,320]{3,2,1,0:T(8,128)(2,1)} %bitcast.40), calls=%async_computation | async-start | bytes 2359296 | tf_op jit(solution)/shard_map/all_to_all | solution.py:279
  351.6 6.8 %copy-start.2 = (bf16[16,4,24,320]{3,2,1,0:T(8,128)(2,1)}, bf16[16,4,24,320]{3,2,1,0:T(8,128)(2,1)S(1)}, u32[]{:S(2)}) copy-start(bf16[16,4,24,320]{3,2,1,0:T(8,128)(2,1)S(1)} %all-to-all-done.refs_0_) | copy-start | bytes 2949124
  351.6 21.7 %all-to-all-start.1 = ((bf16[16,4,24,320]{3,2,1,0:T(8,128)(2,1)}), bf16[16,4,24,320]{3,2,1,0:T(8,128)(2,1)S(1)}, u32[]{:S(2)}, u32[]{:S(2)}) async-start(bf16[16,4,24,320]{3,2,1,0:T(8,128)(2,1)} %bitcast.39), calls=%async_computation.2 | async-start | bytes 2359296 | tf_op jit(solution)/shard_map/all_to_all | solution.py:279
  358.3 30.8 %reduce-scatter.3.cloned.1.call-start = ((), (), s32[]{:S(2)}) async-start(), calls=%async_computation.4 | async-start | bytes 819200 | tf_op jit(solution)/shard_map/reduce_scatter | solution.py:329
  358.4 1.4 copy-start
  359.8 1.3 copy-start.3
  361.0 12.2 %copy-start.1 = (bf16[128,24,256]{2,1,0:T(8,128)(2,1)S(1)}, bf16[128,24,256]{2,1,0:T(8,128)(2,1)}, u32[]{:S(2)}) copy-start(bf16[128,24,256]{2,1,0:T(8,128)(2,1)} %all-gather.11.cloned.1.call-done) | copy-start | bytes 4718596
  362.5 57.5 %reduce-scatter.5.cloned.1.call-start = ((), (), s32[]{:S(2)}) async-start(), calls=%async_computation.5 | async-start | bytes 819200 | tf_op jit(solution)/shard_map/reduce_scatter | solution.py:327
  420.9 6.6 %collective-permute-start.4 = (bf16[320,256]{1,0:T(8,128)(2,1)S(1)}, bf16[320,256]{1,0:T(8,128)(2,1)S(1)}, u32[]{:S(2)}, u32[]{:S(2)}) collective-permute-start(bf16[320,256]{1,0:T(8,128)(2,1)S(1)} %select_bitcast_fusion), channel_id=1, source_target_pairs={{0,192},{192,0},{64,128},{128,64},{1,193},{193,1},{65,129},{129,65... | collective-permute-start | bytes 491528 | tf_op jit(solution)/shard_map/ppermute | solution.py:332
Sparse Core Ops, SparseCore 0:
  10.1 112.1 all-gather.6
  125.1 107.4 all-gather.8
  278.1 34.1 all-gather.10
  362.6 26.4 reduce-scatter.2
  391.4 28.4 reduce-scatter.4

commit v2 on v1

--- a/solution.py
+++ b/solution.py
@@ -11,6 +11,7 @@
 REAL, ROWS = 18, 24
 SET = 4
 CH = 4
+PIECES = 1
 CW = D // CH
 DP = ("zl", "x", "core")
 GRID_AXES = ("y", "zh", "zl", "x", "core")
@@ -19,11 +20,11 @@
 SM = pl.BlockSpec(memory_space=pltpu.SMEM)
 
 
-def weight_copy(w_ref, wbuf, sem, flags, layer, which):
-    held = jnp.where(flags[1] == 1, SET - 1 - layer, layer)
-    slot = lax.rem(layer, 2)
+def weight_copy(w_ref, wbuf, sem, held, slot, which, c):
+    per = 16 // PIECES
+    piece = pl.ds(c * per, per)
     return pltpu.make_async_copy(
-        w_ref.at[held, :, which], wbuf.at[slot, which], sem.at[slot, which]
+        w_ref.at[held, piece, which], wbuf.at[slot, which, piece], sem.at[slot, which, c]
     )
 
 
@@ -52,32 +53,39 @@
 
     @pl.when(flags[0] == 1)
     def _():
+        def wanted(layer, which, c):
+            held = jnp.where(flags[1] == 1, SET - 1 - layer, layer)
+            return weight_copy(w_ref, wbuf, sem_w, held, layer % 2, which, c)
+
         for which in range(2):
-            weight_copy(w_ref, wbuf, sem_w, flags, 0, which).start()
+            for c in range(PIECES):
+                wanted(0, which, c).start()
         hbuf[0] = x_ref[...]
 
-        def step(layer, carry):
-            slot = lax.rem(layer, 2)
-
-            @pl.when(layer + 1 < SET)
-            def _():
-                for which in range(2):
-                    weight_copy(w_ref, wbuf, sem_w, flags, layer + 1, which).start()
+        def step(layer):
+            slot = layer % 2
+
+            def arrive(which, c):
+                if c % (CH // PIECES) == 0:
+                    c = c // (CH // PIECES)
+                    wanted(layer, which, c).wait()
+                    if layer + 1 < SET:
+                        wanted(layer + 1, which, c).start()
 
             pltpu.make_async_copy(hbuf.at[layer], h_out.at[layer], sem_h.at[layer]).start()
             inv = inverse_rms(hbuf, layer)
-            weight_copy(w_ref, wbuf, sem_w, flags, layer, 0).wait()
             pre = jnp.zeros((ROWS, R), jnp.float32)
             for c in range(CH):
                 normed = (hbuf[layer, :, columns(c)].astype(jnp.float32) * inv).astype(jnp.bfloat16)
+                arrive(0, c)
                 pre = pre + jnp.dot(
                     normed, chunk(wbuf, slot, 0, c), preferred_element_type=jnp.float32
                 )
             active = (pre / (1.0 + jnp.exp(-pre))).astype(jnp.bfloat16)
             prebuf[layer] = pre
             actbuf[layer] = active
-            weight_copy(w_ref, wbuf, sem_w, flags, layer, 1).wait()
-            for c in range(CH):
+            for c in range(CH):
+                arrive(1, c)
                 branch = lax.dot_general(
                     active,
                     chunk(wbuf, slot, 1, c),
@@ -86,9 +94,9 @@
                 )
                 before = hbuf[layer, :, columns(c)].astype(jnp.float32)
                 hbuf[layer + 1, :, columns(c)] = (before + branch).astype(jnp.bfloat16)
-            return carry
-
-        lax.fori_loop(0, SET, step, 0)
+
+        for layer in range(SET):
+            step(layer)
         y_ref[...] = hbuf[SET]
         copies = [
             pltpu.make_async_copy(prebuf, pre_out, sem_p.at[0]),
@@ -122,7 +130,7 @@
             pltpu.VMEM((SET + 1, ROWS, D), jnp.bfloat16),
             pltpu.VMEM((SET, ROWS, R), jnp.float32),
             pltpu.VMEM((SET, ROWS, R), jnp.bfloat16),
-            pltpu.SemaphoreType.DMA((2, 2)),
+            pltpu.SemaphoreType.DMA((2, 2, PIECES)),
             pltpu.SemaphoreType.DMA((SET,)),
             pltpu.SemaphoreType.DMA((1,)),
             pltpu.SemaphoreType.DMA((1,)),
@@ -130,7 +138,7 @@
         input_output_aliases={3: 1, 4: 2, 5: 3} if aliased else {},
         compiler_params=pltpu.CompilerParams(vmem_limit_bytes=40 * 2**20),
         cost_estimate=pl.CostEstimate(
-            flops=4 * SET * ROWS * D * R, bytes_accessed=SET * 4 * D * R, transcendentals=0
+            flops=SET * ROWS * D * R, bytes_accessed=SET * D * R, transcendentals=0
         ),
         name="forward_set",
     )(flags, rows, weights, *(held or ()))
@@ -140,23 +148,35 @@
     flags, g_ref, w_ref, h_in, pre_in = refs[:5]
     refs = refs[5 + (1 if aliased else 0) :]
     y_ref, g_out = refs[:2]
-    wbuf, hbuf, prebuf, gbuf, dnbuf, sem_w, sem_h, sem_p, sem_g = refs[2:]
+    wbuf, hbuf, prebuf, gbuf, dnbuf, gcut, sem_w, sem_h, sem_p, sem_g = refs[2:]
 
     @pl.when(flags[0] == 1)
     def _():
-        def wanted(step, which):
+        def wanted(step, which, c):
             held = jnp.where(flags[1] == 1, step, SET - 1 - step)
-            slot = lax.rem(step, 2)
+            return weight_copy(w_ref, wbuf, sem_w, held, step % 2, which, c)
+
+        def g_copy(step):
             return pltpu.make_async_copy(
-                w_ref.at[held, :, which], wbuf.at[slot, which], sem_w.at[slot, which]
+                gcut.at[:, step], g_out.at[:, SET - 1 - step], sem_g.at[step]
             )
 
-        wanted(0, 1).start()
-        wanted(0, 0).start()
+        def g_send(step):
+            for r in range(16):
+                gcut[r, step] = gbuf[step, :, r * (D // 16) : (r + 1) * (D // 16)]
+            g_copy(step).start()
+
+        def h_copy(layer):
+            return pltpu.make_async_copy(h_in.at[layer], hbuf.at[layer], sem_h.at[layer])
+
         pre_copy = pltpu.make_async_copy(pre_in, prebuf, sem_p.at[0])
         pre_copy.start()
-        for layer in range(SET - 1, -1, -1):
-            pltpu.make_async_copy(h_in.at[layer], hbuf.at[layer], sem_h.at[layer]).start()
+        h_copy(SET - 1).start()
+        for which in (1, 0):
+            for c in range(PIECES):
+                wanted(0, which, c).start()
+        for layer in range(SET - 2, -1, -1):
+            h_copy(layer).start()
         if from_final:
             gbuf[0] = (g_ref[...].astype(jnp.float32) * COT).astype(jnp.bfloat16)
         else:
@@ -164,33 +184,35 @@
         pre_copy.wait()
         steps = SET - 1 if last else SET
 
-        def one_layer(step, carry):
+        def one_layer(step):
             layer = SET - 1 - step
-            slot = lax.rem(step, 2)
-
-            @pl.when(step + 1 < steps)
-            def _():
-                wanted(step + 1, 1).start()
-                wanted(step + 1, 0).start()
-
-            pltpu.make_async_copy(gbuf.at[step], g_out.at[layer], sem_g.at[step]).start()
-            pltpu.make_async_copy(h_in.at[layer], hbuf.at[layer], sem_h.at[layer]).wait()
+            slot = step % 2
+
+            def arrive(which, c):
+                if c % (CH // PIECES) == 0:
+                    c = c // (CH // PIECES)
+                    wanted(step, which, c).wait()
+                    if step + 1 < steps:
+                        wanted(step + 1, which, c).start()
+
+            g_send(step)
+            h_copy(layer).wait()
             inv = inverse_rms(hbuf, layer)
             pre = prebuf[layer]
             sigma = 1.0 / (1.0 + jnp.exp(-pre))
             slope = sigma * (1.0 + pre * (1.0 - sigma))
-            wanted(step, 1).wait()
             d_active = jnp.zeros((ROWS, R), jnp.float32)
             for c in range(CH):
+                arrive(1, c)
                 d_active = d_active + jnp.dot(
                     gbuf[step, :, columns(c)],
                     chunk(wbuf, slot, 1, c),
                     preferred_element_type=jnp.float32,
                 )
             d_pre = (d_active * slope).astype(jnp.bfloat16)
-            wanted(step, 0).wait()
             total = jnp.zeros((ROWS, 1), jnp.float32)
             for c in range(CH):
+                arrive(0, c)
                 d_normed = lax.dot_general(
                     d_pre,
                     chunk(wbuf, slot, 0, c),
@@ -206,23 +228,21 @@
                 moved = inv * (dnbuf[:, columns(c)] - unit * mean)
                 before = gbuf[step, :, columns(c)].astype(jnp.float32)
                 gbuf[step + 1, :, columns(c)] = (before + moved).astype(jnp.bfloat16)
-            return carry
-
-        lax.fori_loop(0, steps, one_layer, 0)
+
+        for step in range(steps):
+            one_layer(step)
         if last:
-            pltpu.make_async_copy(gbuf.at[SET - 1], g_out.at[0], sem_g.at[SET - 1]).start()
-            pltpu.make_async_copy(h_in.at[0], hbuf.at[0], sem_h.at[0]).wait()
+            g_send(SET - 1)
+            h_copy(0).wait()
         y_ref[...] = gbuf[steps]
         for step in range(SET):
-            pltpu.make_async_copy(
-                gbuf.at[step], g_out.at[SET - 1 - step], sem_g.at[step]
-            ).wait()
+            g_copy(step).wait()
 
 
 def run_backward(flags, g_rows, weights, h_held, pre_held, held=None, from_final=False, last=False):
     outs = (
         jax.ShapeDtypeStruct((ROWS, D), jnp.bfloat16),
-        jax.ShapeDtypeStruct((SET, ROWS, D), jnp.bfloat16),
+        jax.ShapeDtypeStruct((16, SET, ROWS, D // 16), jnp.bfloat16),
     )
     aliased = held is not None
     return pl.pallas_call(
@@ -236,7 +256,8 @@
             pltpu.VMEM((SET, ROWS, R), jnp.float32),
             pltpu.VMEM((SET + 1, ROWS, D), jnp.bfloat16),
             pltpu.VMEM((ROWS, D), jnp.float32),
-            pltpu.SemaphoreType.DMA((2, 2)),
+            pltpu.VMEM((16, SET, ROWS, D // 16), jnp.bfloat16),
+            pltpu.SemaphoreType.DMA((2, 2, PIECES)),
             pltpu.SemaphoreType.DMA((SET,)),
             pltpu.SemaphoreType.DMA((1,)),
             pltpu.SemaphoreType.DMA((SET,)),
@@ -244,30 +265,40 @@
         input_output_aliases={5: 1} if aliased else {},
         compiler_params=pltpu.CompilerParams(vmem_limit_bytes=40 * 2**20),
         cost_estimate=pl.CostEstimate(
-            flops=4 * SET * ROWS * D * R, bytes_accessed=SET * 4 * D * R, transcendentals=0
+            flops=SET * ROWS * D * R, bytes_accessed=SET * D * R, transcendentals=0
         ),
         name="backward_set",
     )(flags, g_rows, weights, h_held, pre_held, *((held,) if aliased else ()))
 
 
-def grad_kernel(g_ref, act_ref, out_ref, *, first):
-    for layer in range(SET):
+def grad_kernel(place, g_ref, act_ref, *out_refs, first):
+    for k in range(SET):
+        layer = lax.rem(place[0] + k, SET)
         g = g_ref[:, layer].reshape(16 * ROWS, D // 16)
         act = act_ref[:, first + layer].reshape(16 * ROWS, R)
-        out_ref[layer] = lax.dot_general(
+        out_refs[k][...] = lax.dot_general(
             g, act, (((0,), (0,)), ((), ())), preferred_element_type=jnp.float32
         ).astype(jnp.bfloat16)
 
 
-def run_grad(g_all, act_all, first):
+def run_grad(place, g_all, act_all, first):
     return pl.pallas_call(
         lambda *refs: grad_kernel(*refs, first=first),
-        out_shape=jax.ShapeDtypeStruct((SET, D // 16, R), jnp.bfloat16),
-        in_specs=[VM, VM],
-        out_specs=VM,
+        out_shape=(jax.ShapeDtypeStruct((D // 16, R), jnp.bfloat16),) * SET,
+        in_specs=[SM, VM, VM],
+        out_specs=(VM,) * SET,
         compiler_params=pltpu.CompilerParams(vmem_limit_bytes=40 * 2**20),
         name="grad_set",
-    )(g_all, act_all)
+    )(place, g_all, act_all)
+
+
+def summed_over_zh(place, g_all, act_all, first):
+    parts = run_grad(place, g_all, act_all, first)
+    total = parts[0].astype(jnp.float32)
+    for k in range(1, SET):
+        route = [(source, (source + k) % SET) for source in range(SET)]
+        total = total + lax.ppermute(parts[k], "zh", route).astype(jnp.float32)
+    return total.astype(jnp.bfloat16)
 
 
 def hop(rows):
@@ -275,8 +306,7 @@
 
 
 def spread(g_set):
-    cut = g_set.reshape(SET, ROWS, 16, D // 16).transpose(2, 0, 1, 3)
-    return lax.all_to_all(cut, DP, 0, 0)
+    return lax.all_to_all(g_set, DP, 0, 0)
 
 
 def shards(inputs_down, inputs_up, w_in, w_out):
@@ -323,10 +353,12 @@
     rows, g_a = run_backward(q_a, rows, w_a, h_a, pre_a)
     rows = hop(rows)
     rows, g_a = run_backward(p_a, rows, w_a, h_a, pre_a, held=g_a, last=True)
-    part_b = run_grad(spread(g_b), act_all, SET)
-    sum_b = lax.psum_scatter(part_b, "zh", scatter_dimension=0, tiled=True)[0]
-    part_a = run_grad(spread(g_a), act_all, 0)
-    sum_a = lax.psum_scatter(part_a, "zh", scatter_dimension=0, tiled=True)[0]
+    place = zh.astype(jnp.int32)[None]
+    far_b = spread(g_b)
+    g_a, far_b = lax.optimization_barrier((g_a, far_b))
+    far_a = spread(g_a)
+    sum_b = summed_over_zh(place, far_b, act_all, SET)
+    sum_a = summed_over_zh(place, far_a, act_all, 0)
     kept = jnp.where(low_half, sum_a, sum_b)
     other = jnp.where(low_half, sum_b, sum_a)
     received = lax.ppermute(other, "y", [(0, 3), (3, 0), (1, 2), (2, 1)])

time: 436 us -> 408 us (0.936); the launches traced: 436 us -> 401 us
  waiting for transfers between devices: 299 us -> 263 us
  starting transfers between devices: 51.9 us -> 65 us
  local copies, waits for them, and re-layouts: 12.8 us -> 2.81 us
    reduce_scatter x2 -> x0, waiting for transfers between devices: 45.3 us -> none  [the longest x1 30.9 us: shards(): sum_b = lax.psum_scatter(part_b, 'zh', scatter_dimension=0, tiled=True)[0]]
    ppermute x0 -> x6, waiting for transfers between devices: none -> 19 us  [summed_over_zh(): total = total + lax.ppermute(parts[k], 'zh', route).astype(jnp.float32)]
    ppermute x0 -> x6, starting transfers between devices: none -> 14.9 us  [summed_over_zh(): total = total + lax.ppermute(parts[k], 'zh', route).astype(jnp.float32)]
    all_to_all x2, waiting for transfers between devices: 21.4 us -> 7.78 us  [spread(): return lax.all_to_all(g_set, DP, 0, 0)]
    reshape x4 -> x0, local copies, waits for them, and re-layouts: 8.69 us -> none  [spread(): cut = g_set.reshape(SET, ROWS, 16, D // 16).transpose(2, 0, 1, 3)]
  transfers between devices with their start and end apart: 12 -> 16, of which waited for: 11 -> 12; matrix products, arithmetic and copies ran while one was open for 2% -> 0% of each run, Pallas kernels for 6% -> 7%
where the time goes in v2:
time: 408 us; the launch traced here: 401 us
  waiting for transfers between devices  263 us (64%)
  starting transfers between devices  65 us (16%)
  Pallas kernels  53.3 us (13%)
  between operations  13.5 us (3%)
    all_gather x2, waiting for transfers between devices, gathered(): lax.all_gather(own_part, ('zh',) + DP).reshape(SET, 16, 2, D // 16, R)  202 us
    ppermute x4, starting transfers between devices, hop(): return lax.ppermute(rows, 'y', [(0, 1), (1, 0), (2, 3), (3, 2)])  36.7 us
    ppermute x4, waiting for transfers between devices, hop(): return lax.ppermute(rows, 'y', [(0, 1), (1, 0), (2, 3), (3, 2)])  28.1 us
    pallas_call x4, Pallas kernels, run_backward(): pl.pallas_call(lambda *refs: backward_kernel(*refs, aliased=aliased, from...  26 us
    pallas_call x4, Pallas kernels, run_forward(): pl.pallas_call(lambda *refs: forward_kernel(*refs, aliased=aliased), out_...  24.9 us
    ppermute x6, waiting for transfers between devices, summed_over_zh(): total = total + lax.ppermute(parts[k], 'zh', route).astype(jnp.float32)  19 us
    ppermute x6, starting transfers between devices, summed_over_zh(): total = total + lax.ppermute(parts[k], 'zh', route).astype(jnp.float32)  14.9 us
    all_to_all x2, starting transfers between devices, spread(): return lax.all_to_all(g_set, DP, 0, 0)  11.1 us
  transfers between devices with their start and end apart: 16, of which 12 were waited for; matrix products, arithmetic and copies ran while one was open for 0% of the time, Pallas kernels for 7%

profile of v2, /device:TPU:2, one launch (start us, length us, event | category | flops | bytes accessed | tf_op | source)
XLA Modules:
  0.0 400.7 jit_solution(8165616481503415735)
XLA Ops:
  6.5 1.3 dynamic-slice_bitcast_fusion
  9.4 112.9 %all-gather.7.cloned.1.call-done = bf16[128,320,256]{2,1,0:T(8,128)(2,1)} async-done(((bf16[2,320,256]{2,1,0:T(8,128)(2,1)}), bf16[128,320,256]{2,1,0:T(8,128)(2,1)}) %all-gather.7.cloned.1.call-update) | async-done | bytes 20971536 | tf_op jit(solution)/shard_map/all_gather | solution.py:325
  122.7 11.7 %forward_set.4 = (bf16[24,5120]{1,0:T(8,128)(2,1)S(1)}, bf16[4,24,5120]{2,1,0:T(8,128)(2,1)S(1)}, f32[4,24,256]{2,1,0:T(8,128)S(1)}, bf16[4,24,256]{2,1,0:T(8,128)(2,1)S(1)}) custom-call(s32[2]{0:T(128)S(1)} %pad_add_fusion.1.refs_0_, bf16[24,5120]{1,0:T(8,128)(2,1)S(1)} %pad.4.refs_1_, bf16[4,16,2,320,256]{4,3,2,1,0:T(8,128)(2,1)} %bitcast.21), custom_call_target="tpu_custom_call" | custom-call | flops 125829120 | bytes 5242880 | tf_op jit(solution)/shard_map/forward_set/pallas_call | solution.py:123
  134.6 7.9 %collective-permute-done.refs_1_ = bf16[24,5120]{1,0:T(8,128)(2,1)S(1)} collective-permute-done((bf16[24,5120]{1,0:T(8,128)(2,1)S(1)}, bf16[24,5120]{1,0:T(8,128)(2,1)S(1)}, u32[]{:S(2)}, u32[]{:S(2)}) %collective-permute-start) | collective-permute-done | bytes 245792 | tf_op jit(solution)/shard_map/ppermute | solution.py:305
  143.2 89.4 %all-gather.9.cloned.1.call-done = bf16[128,320,256]{2,1,0:T(8,128)(2,1)} async-done(((bf16[2,320,256]{2,1,0:T(8,128)(2,1)}), bf16[128,320,256]{2,1,0:T(8,128)(2,1)}) %all-gather.9.cloned.1.call-update) | async-done | bytes 20971536 | tf_op jit(solution)/shard_map/all_gather | solution.py:325
  232.6 0.8 forward_set.6
  233.5 12.6 %collective-permute-start.1 = (bf16[24,5120]{1,0:T(8,128)(2,1)S(1)}, bf16[24,5120]{1,0:T(8,128)(2,1)S(1)}, u32[]{:S(2)}, u32[]{:S(2)}) collective-permute-start(bf16[24,5120]{1,0:T(8,128)(2,1)S(1)} %get-tuple-element.47), channel_id=1, source_target_pairs={{0,64},{64,0},{128,192},{192,128},{1,65},{65,1},{129,193},{193,129... | collective-permute-start | bytes 737288 | tf_op jit(solution)/shard_map/ppermute | solution.py:305
  246.2 6.3 %collective-permute-done.1.refs_1_ = bf16[24,5120]{1,0:T(8,128)(2,1)S(1)} collective-permute-done((bf16[24,5120]{1,0:T(8,128)(2,1)S(1)}, bf16[24,5120]{1,0:T(8,128)(2,1)S(1)}, u32[]{:S(2)}, u32[]{:S(2)}) %collective-permute-start.1) | collective-permute-done | bytes 245792 | tf_op jit(solution)/shard_map/ppermute | solution.py:305
  252.5 11.7 %forward_set.7 = (bf16[24,5120]{1,0:T(8,128)(2,1)S(1)}, bf16[4,24,5120]{2,1,0:T(8,128)(2,1)S(1)}, f32[4,24,256]{2,1,0:T(8,128)S(1)}, bf16[4,24,256]{2,1,0:T(8,128)(2,1)S(1)}) custom-call(s32[2]{0:T(128)S(1)} %pad_add_fusion.2.refs_0_, ...), custom_call_target="tpu_custom_call", output_to_operand_aliasing={{1}: (3, {}), {2}: (4, {}), {3}: (5, {})} | custom-call | flops 125829120 | bytes 5242880 | tf_op jit(solution)/shard_map/forward_set/pallas_call | solution.py:123
  264.2 12.9 %backward_set.4 = (bf16[24,5120]{1,0:T(8,128)(2,1)S(1)}, bf16[16,4,24,320]{3,2,1,0:T(8,128)(2,1)}) custom-call(s32[2]{0:T(128)S(1)} %pad_add_fusion.2.refs_0_, bf16[24,5120]{1,0:T(8,128)(2,1)S(1)} %get-tuple-element.51.refs_1_, bf16[4,16,2,320,256]{4,3,2,1,0:T(8,128)(2,1)} %bitcast.27, bf16[4,24,5120]{2,1,0:T(8,128)(2,1)S(1)} %get-tuple-element.52.refs_3_, ...), custom_call_target="tpu_custom_call" | custom-call | flops 125829120 | bytes 5242880 | tf_op jit(solution)/shard_map/backward_set/pallas_call | solution.py:248
  277.1 7.6 %collective-permute-done.2.refs_1_ = bf16[24,5120]{1,0:T(8,128)(2,1)S(1)} collective-permute-done((bf16[24,5120]{1,0:T(8,128)(2,1)S(1)}, bf16[24,5120]{1,0:T(8,128)(2,1)S(1)}, u32[]{:S(2)}, u32[]{:S(2)}) %collective-permute-start.2) | collective-permute-done | bytes 245792 | tf_op jit(solution)/shard_map/ppermute | solution.py:305
  285.4 5.3 %all-to-all-start = ((bf16[16,4,24,320]{3,2,1,0:T(8,128)(2,1)}), bf16[16,4,24,320]{3,2,1,0:T(8,128)(2,1)S(1)}, u32[]{:S(2)}, u32[]{:S(2)}) async-start(bf16[16,4,24,320]{3,2,1,0:T(8,128)(2,1)} %get-tuple-element.62), calls=%async_computation | async-start | bytes 2359296 | tf_op jit(solution)/shard_map/all_to_all | solution.py:309
  291.5 0.8 backward_set.6
  292.3 23.9 %collective-permute-start.3 = (bf16[24,5120]{1,0:T(8,128)(2,1)S(1)}, bf16[24,5120]{1,0:T(8,128)(2,1)S(1)}, u32[]{:S(2)}, u32[]{:S(2)}) collective-permute-start(bf16[24,5120]{1,0:T(8,128)(2,1)S(1)} %get-tuple-element.59), channel_id=1, source_target_pairs={{0,64},{64,0},{128,192},{192,128},{1,65},{65,1},{129,193},{193,129... | collective-permute-start | bytes 737288 | tf_op jit(solution)/shard_map/ppermute | solution.py:305
  316.2 6.3 %collective-permute-done.3.refs_1_ = bf16[24,5120]{1,0:T(8,128)(2,1)S(1)} collective-permute-done((bf16[24,5120]{1,0:T(8,128)(2,1)S(1)}, bf16[24,5120]{1,0:T(8,128)(2,1)S(1)}, u32[]{:S(2)}, u32[]{:S(2)}) %collective-permute-start.3) | collective-permute-done | bytes 245792 | tf_op jit(solution)/shard_map/ppermute | solution.py:305
  322.5 11.6 %backward_set.7 = (bf16[24,5120]{1,0:T(8,128)(2,1)}, bf16[16,4,24,320]{3,2,1,0:T(8,128)(2,1)}) custom-call(s32[2]{0:T(128)S(1)} %pad_add_fusion.1.refs_0_, bf16[24,5120]{1,0:T(8,128)(2,1)S(1)} %collective-permute-done.3.refs_1_, bf16[4,16,2,320,256]{4,3,2,1,0:T(8,128)(2,1)} %bitcast.24, ...), custom_call_target="tpu_custom_call", output_to_operand_aliasing={{1}: (5, {})} | custom-call | flops 125829120 | bytes 5242880 | tf_op jit(solution)/shard_map/backward_set/pallas_call | solution.py:248
  334.2 5.8 %all-to-all-start.1 = ((bf16[16,4,24,320]{3,2,1,0:T(8,128)(2,1)}), bf16[16,4,24,320]{3,2,1,0:T(8,128)(2,1)}, u32[]{:S(2)}, u32[]{:S(2)}) async-start(bf16[16,4,24,320]{3,2,1,0:T(8,128)(2,1)} %get-tuple-element.63), calls=%async_computation.1 | async-start | bytes 2359296 | tf_op jit(solution)/shard_map/all_to_all | solution.py:309
  340.0 1.4 copy-done
  341.9 2.2 collective-permute-start.7
  344.1 2.5 collective-permute-start.8
  346.6 3.0 collective-permute-start.9
  349.6 7.8 %all-to-all-done.1.refs_1_ = bf16[16,4,24,320]{3,2,1,0:T(8,128)(2,1)} async-done(((bf16[16,4,24,320]{3,2,1,0:T(8,128)(2,1)}), bf16[16,4,24,320]{3,2,1,0:T(8,128)(2,1)}, u32[]{:S(2)}, u32[]{:S(2)}) %all-to-all-start.1) | async-done | bytes 983072 | tf_op jit(solution)/shard_map/all_to_all | solution.py:309
  357.4 1.8 grad_set.2
  359.3 2.2 collective-permute-start.4
  361.4 2.5 collective-permute-start.5
  363.9 2.6 collective-permute-start.6
  366.5 2.3 collective-permute-done.8
  368.9 5.3 %collective-permute-done.4 = bf16[320,256]{1,0:T(8,128)(2,1)S(1)} collective-permute-done((bf16[320,256]{1,0:T(8,128)(2,1)S(1)}, bf16[320,256]{1,0:T(8,128)(2,1)S(1)}, u32[]{:S(2)}, u32[]{:S(2)}) %collective-permute-start.4) | collective-permute-done | bytes 163872 | tf_op jit(solution)/shard_map/ppermute | solution.py:300
  374.2 4.5 %collective-permute-done.5 = bf16[320,256]{1,0:T(8,128)(2,1)S(1)} collective-permute-done((bf16[320,256]{1,0:T(8,128)(2,1)S(1)}, bf16[320,256]{1,0:T(8,128)(2,1)S(1)}, u32[]{:S(2)}, u32[]{:S(2)}) %collective-permute-start.5) | collective-permute-done | bytes 163872 | tf_op jit(solution)/shard_map/ppermute | solution.py:300
  378.7 6.9 %collective-permute-done.6 = bf16[320,256]{1,0:T(8,128)(2,1)S(1)} collective-permute-done((bf16[320,256]{1,0:T(8,128)(2,1)S(1)}, bf16[320,256]{1,0:T(8,128)(2,1)S(1)}, u32[]{:S(2)}, u32[]{:S(2)}) %collective-permute-start.6) | collective-permute-done | bytes 163872 | tf_op jit(solution)/shard_map/ppermute | solution.py:300
  385.7 2.2 collective-permute-start.10
  387.9 5.2 %collective-permute-done.10 = bf16[320,256]{1,0:T(8,128)(2,1)S(1)} collective-permute-done((bf16[320,256]{1,0:T(8,128)(2,1)S(1)}, bf16[320,256]{1,0:T(8,128)(2,1)S(1)}, u32[]{:S(2)}, u32[]{:S(2)}) %collective-permute-start.10) | collective-permute-done | bytes 163872 | tf_op jit(solution)/shard_map/ppermute | solution.py:364
  (34 shorter events, 5.8 us)
Async XLA Ops:
  6.5 115.8 %all-gather.7.cloned.1.call-start = ((), (), s32[]{:S(2)}) async-start(), calls=%async_computation.2 | async-start | bytes 21299200 | tf_op jit(solution)/shard_map/all_gather | solution.py:325
  6.5 115.9 %copy-start.2 = (bf16[3,24,5120]{2,1,0:T(8,128)(2,1)S(1)}, bf16[3,24,5120]{2,1,0:T(8,128)(2,1)}, u32[]{:S(2)}) copy-start(bf16[3,24,5120]{2,1,0:T(8,128)(2,1)} %param.4) | copy-start | bytes 2211844
  6.5 115.9 %copy-start.3 = (bf16[3,24,5120]{2,1,0:T(8,128)(2,1)S(1)}, bf16[3,24,5120]{2,1,0:T(8,128)(2,1)}, u32[]{:S(2)}) copy-start(bf16[3,24,5120]{2,1,0:T(8,128)(2,1)} %param.5) | copy-start | bytes 2211844
  8.6 224.0 %all-gather.9.cloned.1.call-start = ((), (), s32[]{:S(2)}) async-start(), calls=%async_computation.3 | async-start | bytes 21299200 | tf_op jit(solution)/shard_map/all_gather | solution.py:325
  134.4 8.2 %collective-permute-start = (bf16[24,5120]{1,0:T(8,128)(2,1)S(1)}, bf16[24,5120]{1,0:T(8,128)(2,1)S(1)}, u32[]{:S(2)}, u32[]{:S(2)}) collective-permute-start(bf16[24,5120]{1,0:T(8,128)(2,1)S(1)} %get-tuple-element.41), channel_id=1, source_target_pairs={{0,64},{64,0},{128,192},{192,128},{1,65},{65,1},{129,193},{193,129... | collective-permute-start | bytes 737288 | tf_op jit(solution)/shard_map/ppermute | solution.py:305
  233.5 19.0 %collective-permute-start.1 = (bf16[24,5120]{1,0:T(8,128)(2,1)S(1)}, bf16[24,5120]{1,0:T(8,128)(2,1)S(1)}, u32[]{:S(2)}, u32[]{:S(2)}) collective-permute-start(bf16[24,5120]{1,0:T(8,128)(2,1)S(1)} %get-tuple-element.47), channel_id=1, source_target_pairs={{0,64},{64,0},{128,192},{192,128},{1,65},{65,1},{129,193},{193,129... | collective-permute-start | bytes 737288 | tf_op jit(solution)/shard_map/ppermute | solution.py:305
  277.0 7.7 %collective-permute-start.2 = (bf16[24,5120]{1,0:T(8,128)(2,1)S(1)}, bf16[24,5120]{1,0:T(8,128)(2,1)S(1)}, u32[]{:S(2)}, u32[]{:S(2)}) collective-permute-start(bf16[24,5120]{1,0:T(8,128)(2,1)S(1)} %get-tuple-element.54), channel_id=1, source_target_pairs={{0,64},{64,0},{128,192},{192,128},{1,65},{65,1},{129,193},{193,129... | collective-permute-start | bytes 737288 | tf_op jit(solution)/shard_map/ppermute | solution.py:305
  285.4 48.7 %all-to-all-start = ((bf16[16,4,24,320]{3,2,1,0:T(8,128)(2,1)}), bf16[16,4,24,320]{3,2,1,0:T(8,128)(2,1)S(1)}, u32[]{:S(2)}, u32[]{:S(2)}) async-start(bf16[16,4,24,320]{3,2,1,0:T(8,128)(2,1)} %get-tuple-element.62), calls=%async_computation | async-start | bytes 2359296 | tf_op jit(solution)/shard_map/all_to_all | solution.py:309
  290.7 49.2 %all-gather.11.cloned.1.call-start = ((), (), s32[]{:S(2)}) async-start(), calls=%async_computation.4 | async-start | bytes 1671168 | tf_op jit(solution)/shard_map/all_gather | solution.py:349
  292.3 30.2 %collective-permute-start.3 = (bf16[24,5120]{1,0:T(8,128)(2,1)S(1)}, bf16[24,5120]{1,0:T(8,128)(2,1)S(1)}, u32[]{:S(2)}, u32[]{:S(2)}) collective-permute-start(bf16[24,5120]{1,0:T(8,128)(2,1)S(1)} %get-tuple-element.59), channel_id=1, source_target_pairs={{0,64},{64,0},{128,192},{192,128},{1,65},{65,1},{129,193},{193,129... | collective-permute-start | bytes 737288 | tf_op jit(solution)/shard_map/ppermute | solution.py:305
  334.2 23.2 %all-to-all-start.1 = ((bf16[16,4,24,320]{3,2,1,0:T(8,128)(2,1)}), bf16[16,4,24,320]{3,2,1,0:T(8,128)(2,1)}, u32[]{:S(2)}, u32[]{:S(2)}) async-start(bf16[16,4,24,320]{3,2,1,0:T(8,128)(2,1)} %get-tuple-element.63), calls=%async_computation.1 | async-start | bytes 2359296 | tf_op jit(solution)/shard_map/all_to_all | solution.py:309
  340.0 1.4 copy-start
  341.4 16.0 %copy-start.1 = (bf16[128,24,256]{2,1,0:T(8,128)(2,1)S(1)}, bf16[128,24,256]{2,1,0:T(8,128)(2,1)}, u32[]{:S(2)}) copy-start(bf16[128,24,256]{2,1,0:T(8,128)(2,1)} %all-gather.11.cloned.1.call-done) | copy-start | bytes 4718596
  341.9 22.0 %collective-permute-start.7 = (bf16[320,256]{1,0:T(8,128)(2,1)S(1)}, bf16[320,256]{1,0:T(8,128)(2,1)S(1)}, u32[]{:S(2)}, u32[]{:S(2)}) collective-permute-start(bf16[320,256]{1,0:T(8,128)(2,1)S(1)} %get-tuple-element.72), channel_id=1, source_target_pairs={{0,16},{16,32},{32,48},{48,0},{1,17},{17,33},{33,49},{49,1},{2,18}... | collective-permute-start | bytes 491528 | tf_op jit(solution)/shard_map/ppermute | solution.py:300
  344.1 24.8 %collective-permute-start.8 = (bf16[320,256]{1,0:T(8,128)(2,1)S(1)}, bf16[320,256]{1,0:T(8,128)(2,1)S(1)}, u32[]{:S(2)}, u32[]{:S(2)}) collective-permute-start(bf16[320,256]{1,0:T(8,128)(2,1)S(1)} %get-tuple-element.73), channel_id=1, source_target_pairs={{0,32},{16,48},{32,0},{48,16},{1,33},{17,49},{33,1},{49,17},{2,34}... | collective-permute-start | bytes 491528 | tf_op jit(solution)/shard_map/ppermute | solution.py:300
  346.6 22.3 %collective-permute-start.9 = (bf16[320,256]{1,0:T(8,128)(2,1)S(1)}, bf16[320,256]{1,0:T(8,128)(2,1)S(1)}, u32[]{:S(2)}, u32[]{:S(2)}) collective-permute-start(bf16[320,256]{1,0:T(8,128)(2,1)S(1)} %get-tuple-element.74), channel_id=1, source_target_pairs={{0,48},{16,0},{32,16},{48,32},{1,49},{17,1},{33,17},{49,33},{2,50}... | collective-permute-start | bytes 491528 | tf_op jit(solution)/shard_map/ppermute | solution.py:300
  359.3 14.9 %collective-permute-start.4 = (bf16[320,256]{1,0:T(8,128)(2,1)S(1)}, bf16[320,256]{1,0:T(8,128)(2,1)S(1)}, u32[]{:S(2)}, u32[]{:S(2)}) collective-permute-start(bf16[320,256]{1,0:T(8,128)(2,1)S(1)} %get-tuple-element.67), channel_id=1, source_target_pairs={{0,16},{16,32},{32,48},{48,0},{1,17},{17,33},{33,49},{49,1},{2,18}... | collective-permute-start | bytes 491528 | tf_op jit(solution)/shard_map/ppermute | solution.py:300
  361.4 17.2 %collective-permute-start.5 = (bf16[320,256]{1,0:T(8,128)(2,1)S(1)}, bf16[320,256]{1,0:T(8,128)(2,1)S(1)}, u32[]{:S(2)}, u32[]{:S(2)}) collective-permute-start(bf16[320,256]{1,0:T(8,128)(2,1)S(1)} %get-tuple-element.68), channel_id=1, source_target_pairs={{0,32},{16,48},{32,0},{48,16},{1,33},{17,49},{33,1},{49,17},{2,34}... | collective-permute-start | bytes 491528 | tf_op jit(solution)/shard_map/ppermute | solution.py:300
  363.9 21.7 %collective-permute-start.6 = (bf16[320,256]{1,0:T(8,128)(2,1)S(1)}, bf16[320,256]{1,0:T(8,128)(2,1)S(1)}, u32[]{:S(2)}, u32[]{:S(2)}) collective-permute-start(bf16[320,256]{1,0:T(8,128)(2,1)S(1)} %get-tuple-element.69), channel_id=1, source_target_pairs={{0,48},{16,0},{32,16},{48,32},{1,49},{17,1},{33,17},{49,33},{2,50}... | collective-permute-start | bytes 491528 | tf_op jit(solution)/shard_map/ppermute | solution.py:300
  385.7 7.4 %collective-permute-start.10 = (bf16[320,256]{1,0:T(8,128)(2,1)S(1)}, bf16[320,256]{1,0:T(8,128)(2,1)S(1)}, u32[]{:S(2)}, u32[]{:S(2)}) collective-permute-start(bf16[320,256]{1,0:T(8,128)(2,1)S(1)} %get-tuple-element.75), channel_id=1, source_target_pairs={{0,192},{192,0},{64,128},{128,64},{1,193},{193,1},{65,129},{129,65... | collective-permute-start | bytes 491528 | tf_op jit(solution)/shard_map/ppermute | solution.py:364
Sparse Core Ops, SparseCore 0:
  10.1 112.1 all-gather.6
  125.1 107.4 all-gather.8
  293.4 44.7 all-gather.10

commit v3 on v2

--- a/solution.py
+++ b/solution.py
@@ -11,7 +11,6 @@
 REAL, ROWS = 18, 24
 SET = 4
 CH = 4
-PIECES = 1
 CW = D // CH
 DP = ("zl", "x", "core")
 GRID_AXES = ("y", "zh", "zl", "x", "core")
@@ -20,17 +19,81 @@
 SM = pl.BlockSpec(memory_space=pltpu.SMEM)
 
 
-def weight_copy(w_ref, wbuf, sem, held, slot, which, c):
-    per = 16 // PIECES
-    piece = pl.ds(c * per, per)
-    return pltpu.make_async_copy(
-        w_ref.at[held, piece, which], wbuf.at[slot, which, piece], sem.at[slot, which, c]
-    )
+class Gathered:
+    count = 1
+
+    def __init__(self, refs, flags, wbuf, sem):
+        self.w, self.flags, self.wbuf, self.sem = refs[0], flags, wbuf, sem
+
+    def copy(self, layer, slot, which):
+        held = jnp.where(self.flags[1] == 1, SET - 1 - layer, layer)
+        return pltpu.make_async_copy(
+            self.w.at[held, :, which], self.wbuf.at[slot, :, which], self.sem.at[slot, which]
+        )
+
+    def first(self, layer, order):
+        for which in order:
+            self.copy(layer, 0, which).start()
+
+    def begin(self, layer, slot):
+        pass
+
+    def arrive(self, layer, slot, which, following):
+        self.copy(layer, slot, which).wait()
+        if following is not None:
+            self.copy(following, 1 - slot, which).start()
+
+
+class Scattered:
+    count = 18
+
+    def __init__(self, refs, flags, wbuf, sem):
+        self.own, self.parts = refs[:2], refs[2:]
+        self.flags, self.wbuf, self.sem = flags, wbuf, sem
+
+    def fetch(self, layer, slot):
+        flags = self.flags
+        held = jnp.where(flags[1] == 1, SET - 1 - layer, layer)
+        away = lax.rem(held + SET - flags[3], SET)
+
+        @pl.when(away == 0)
+        def _():
+            for which in range(2):
+                pltpu.make_async_copy(
+                    self.own[which].at[flags[2]], self.wbuf.at[slot, :, which], self.sem.at[slot, 0]
+                ).start()
+
+        @pl.when(away > 0)
+        def _():
+            for n in range(16):
+                zl_off, x_off, core_off = n // 8, (n // 2) % 4, n % 2
+                zl = lax.rem(flags[4] + zl_off, 2)
+                x = lax.rem(flags[5] + x_off, 4)
+                core = lax.rem(flags[6] + core_off, 2)
+                pltpu.make_async_copy(
+                    self.parts[n].at[away - 1],
+                    self.wbuf.at[slot, zl * 8 + x * 2 + core],
+                    self.sem.at[slot, 0],
+                ).start()
+
+    def first(self, layer, order):
+        self.leading = order[0]
+        self.fetch(layer, 0)
+
+    def begin(self, following, slot):
+        if following is not None:
+            self.fetch(following, 1 - slot)
+
+    def arrive(self, layer, slot, which, following):
+        if which == self.leading:
+            pltpu.make_async_copy(
+                self.wbuf.at[1 - slot], self.wbuf.at[slot], self.sem.at[slot, 0]
+            ).wait()
 
 
 def chunk(wbuf, slot, which, c):
     per = 16 // CH
-    return wbuf[slot, which, c * per : (c + 1) * per].reshape(CW, R)
+    return wbuf[slot, c * per : (c + 1) * per, which].reshape(CW, R)
 
 
 def columns(c):
@@ -45,47 +108,38 @@
     return lax.rsqrt(total * (1.0 / D) + EPS)
 
 
-def forward_kernel(*refs, aliased):
-    flags, x_ref, w_ref = refs[:3]
-    refs = refs[3 + (3 if aliased else 0) :]
+def forward_kernel(*refs, source, aliased):
+    flags, x_ref = refs[:2]
+    w_refs = refs[2 : 2 + source.count]
+    refs = refs[2 + source.count + (3 if aliased else 0) :]
     y_ref, h_out, pre_out, act_out = refs[:4]
     wbuf, hbuf, prebuf, actbuf, sem_w, sem_h, sem_p, sem_a = refs[4:]
 
     @pl.when(flags[0] == 1)
     def _():
-        def wanted(layer, which, c):
-            held = jnp.where(flags[1] == 1, SET - 1 - layer, layer)
-            return weight_copy(w_ref, wbuf, sem_w, held, layer % 2, which, c)
-
-        for which in range(2):
-            for c in range(PIECES):
-                wanted(0, which, c).start()
+        weights = source(w_refs, flags, wbuf, sem_w)
+        weights.first(0, (0, 1))
         hbuf[0] = x_ref[...]
 
         def step(layer):
             slot = layer % 2
 
-            def arrive(which, c):
-                if c % (CH // PIECES) == 0:
-                    c = c // (CH // PIECES)
-                    wanted(layer, which, c).wait()
-                    if layer + 1 < SET:
-                        wanted(layer + 1, which, c).start()
-
+            following = layer + 1 if layer + 1 < SET else None
+            weights.begin(following, slot)
             pltpu.make_async_copy(hbuf.at[layer], h_out.at[layer], sem_h.at[layer]).start()
             inv = inverse_rms(hbuf, layer)
             pre = jnp.zeros((ROWS, R), jnp.float32)
+            weights.arrive(layer, slot, 0, following)
             for c in range(CH):
                 normed = (hbuf[layer, :, columns(c)].astype(jnp.float32) * inv).astype(jnp.bfloat16)
-                arrive(0, c)
                 pre = pre + jnp.dot(
                     normed, chunk(wbuf, slot, 0, c), preferred_element_type=jnp.float32
                 )
             active = (pre / (1.0 + jnp.exp(-pre))).astype(jnp.bfloat16)
             prebuf[layer] = pre
             actbuf[layer] = active
+            weights.arrive(layer, slot, 1, following)
             for c in range(CH):
-                arrive(1, c)
                 branch = lax.dot_general(
                     active,
                     chunk(wbuf, slot, 1, c),
@@ -113,6 +167,8 @@
 
 
 def run_forward(flags, rows, weights, held=None):
+    source = Gathered if len(weights) == 1 else Scattered
+    first = 2 + source.count
     outs = (
         jax.ShapeDtypeStruct((ROWS, D), jnp.bfloat16),
         jax.ShapeDtypeStruct((SET, ROWS, D), jnp.bfloat16),
@@ -121,40 +177,39 @@
     )
     aliased = held is not None
     return pl.pallas_call(
-        lambda *refs: forward_kernel(*refs, aliased=aliased),
+        lambda *refs: forward_kernel(*refs, source=source, aliased=aliased),
         out_shape=outs,
-        in_specs=[SM, VM, ANY] + ([ANY] * 3 if aliased else []),
+        in_specs=[SM, VM] + [ANY] * (source.count + (3 if aliased else 0)),
         out_specs=(VM, ANY, ANY, ANY),
         scratch_shapes=[
-            pltpu.VMEM((2, 2, 16, D // 16, R), jnp.bfloat16),
+            pltpu.VMEM((2, 16, 2, D // 16, R), jnp.bfloat16),
             pltpu.VMEM((SET + 1, ROWS, D), jnp.bfloat16),
             pltpu.VMEM((SET, ROWS, R), jnp.float32),
             pltpu.VMEM((SET, ROWS, R), jnp.bfloat16),
-            pltpu.SemaphoreType.DMA((2, 2, PIECES)),
+            pltpu.SemaphoreType.DMA((2, 2)),
             pltpu.SemaphoreType.DMA((SET,)),
             pltpu.SemaphoreType.DMA((1,)),
             pltpu.SemaphoreType.DMA((1,)),
         ],
-        input_output_aliases={3: 1, 4: 2, 5: 3} if aliased else {},
-        compiler_params=pltpu.CompilerParams(vmem_limit_bytes=40 * 2**20),
+        input_output_aliases={first: 1, first + 1: 2, first + 2: 3} if aliased else {},
+        compiler_params=pltpu.CompilerParams(vmem_limit_bytes=52 * 2**20),
         cost_estimate=pl.CostEstimate(
             flops=SET * ROWS * D * R, bytes_accessed=SET * D * R, transcendentals=0
         ),
         name="forward_set",
-    )(flags, rows, weights, *(held or ()))
-
-
-def backward_kernel(*refs, aliased, from_final, last):
-    flags, g_ref, w_ref, h_in, pre_in = refs[:5]
-    refs = refs[5 + (1 if aliased else 0) :]
+    )(flags, rows, *weights, *(held or ()))
+
+
+def backward_kernel(*refs, source, aliased, from_final, last):
+    flags, g_ref, h_in, pre_in = refs[:4]
+    w_refs = refs[4 : 4 + source.count]
+    refs = refs[4 + source.count + (1 if aliased else 0) :]
     y_ref, g_out = refs[:2]
     wbuf, hbuf, prebuf, gbuf, dnbuf, gcut, sem_w, sem_h, sem_p, sem_g = refs[2:]
 
     @pl.when(flags[0] == 1)
     def _():
-        def wanted(step, which, c):
-            held = jnp.where(flags[1] == 1, step, SET - 1 - step)
-            return weight_copy(w_ref, wbuf, sem_w, held, step % 2, which, c)
+        weights = source(w_refs, flags, wbuf, sem_w)
 
         def g_copy(step):
             return pltpu.make_async_copy(
@@ -172,9 +227,7 @@
         pre_copy = pltpu.make_async_copy(pre_in, prebuf, sem_p.at[0])
         pre_copy.start()
         h_copy(SET - 1).start()
-        for which in (1, 0):
-            for c in range(PIECES):
-                wanted(0, which, c).start()
+        weights.first(SET - 1, (1, 0))
         for layer in range(SET - 2, -1, -1):
             h_copy(layer).start()
         if from_final:
@@ -188,13 +241,8 @@
             layer = SET - 1 - step
             slot = step % 2
 
-            def arrive(which, c):
-                if c % (CH // PIECES) == 0:
-                    c = c // (CH // PIECES)
-                    wanted(step, which, c).wait()
-                    if step + 1 < steps:
-                        wanted(step + 1, which, c).start()
-
+            following = layer - 1 if step + 1 < steps else None
+            weights.begin(following, slot)
             g_send(step)
             h_copy(layer).wait()
             inv = inverse_rms(hbuf, layer)
@@ -202,8 +250,8 @@
             sigma = 1.0 / (1.0 + jnp.exp(-pre))
             slope = sigma * (1.0 + pre * (1.0 - sigma))
             d_active = jnp.zeros((ROWS, R), jnp.float32)
+            weights.arrive(layer, slot, 1, following)
             for c in range(CH):
-                arrive(1, c)
                 d_active = d_active + jnp.dot(
                     gbuf[step, :, columns(c)],
                     chunk(wbuf, slot, 1, c),
@@ -211,8 +259,8 @@
                 )
             d_pre = (d_active * slope).astype(jnp.bfloat16)
             total = jnp.zeros((ROWS, 1), jnp.float32)
+            weights.arrive(layer, slot, 0, following)
             for c in range(CH):
-                arrive(0, c)
                 d_normed = lax.dot_general(
                     d_pre,
                     chunk(wbuf, slot, 0, c),
@@ -240,35 +288,38 @@
 
 
 def run_backward(flags, g_rows, weights, h_held, pre_held, held=None, from_final=False, last=False):
+    source = Gathered if len(weights) == 1 else Scattered
     outs = (
         jax.ShapeDtypeStruct((ROWS, D), jnp.bfloat16),
         jax.ShapeDtypeStruct((16, SET, ROWS, D // 16), jnp.bfloat16),
     )
     aliased = held is not None
     return pl.pallas_call(
-        lambda *refs: backward_kernel(*refs, aliased=aliased, from_final=from_final, last=last),
+        lambda *refs: backward_kernel(
+            *refs, source=source, aliased=aliased, from_final=from_final, last=last
+        ),
         out_shape=outs,
-        in_specs=[SM, VM, ANY, ANY, ANY] + ([ANY] if aliased else []),
+        in_specs=[SM, VM, ANY, ANY] + [ANY] * (source.count + (1 if aliased else 0)),
         out_specs=(VM, ANY),
         scratch_shapes=[
-            pltpu.VMEM((2, 2, 16, D // 16, R), jnp.bfloat16),
+            pltpu.VMEM((2, 16, 2, D // 16, R), jnp.bfloat16),
             pltpu.VMEM((SET, ROWS, D), jnp.bfloat16),
             pltpu.VMEM((SET, ROWS, R), jnp.float32),
             pltpu.VMEM((SET + 1, ROWS, D), jnp.bfloat16),
             pltpu.VMEM((ROWS, D), jnp.float32),
             pltpu.VMEM((16, SET, ROWS, D // 16), jnp.bfloat16),
-            pltpu.SemaphoreType.DMA((2, 2, PIECES)),
+            pltpu.SemaphoreType.DMA((2, 2)),
             pltpu.SemaphoreType.DMA((SET,)),
             pltpu.SemaphoreType.DMA((1,)),
             pltpu.SemaphoreType.DMA((SET,)),
         ],
-        input_output_aliases={5: 1} if aliased else {},
-        compiler_params=pltpu.CompilerParams(vmem_limit_bytes=40 * 2**20),
+        input_output_aliases={4 + source.count: 1} if aliased else {},
+        compiler_params=pltpu.CompilerParams(vmem_limit_bytes=52 * 2**20),
         cost_estimate=pl.CostEstimate(
             flops=SET * ROWS * D * R, bytes_accessed=SET * D * R, transcendentals=0
         ),
         name="backward_set",
-    )(flags, g_rows, weights, h_held, pre_held, *((held,) if aliased else ()))
+    )(flags, g_rows, h_held, pre_held, *weights, *((held,) if aliased else ()))
 
 
 def grad_kernel(place, g_ref, act_ref, *out_refs, first):
@@ -287,7 +338,7 @@
         out_shape=(jax.ShapeDtypeStruct((D // 16, R), jnp.bfloat16),) * SET,
         in_specs=[SM, VM, VM],
         out_specs=(VM,) * SET,
-        compiler_params=pltpu.CompilerParams(vmem_limit_bytes=40 * 2**20),
+        compiler_params=pltpu.CompilerParams(vmem_limit_bytes=52 * 2**20),
         name="grad_set",
     )(place, g_all, act_all)
 
@@ -309,6 +360,24 @@
     return lax.all_to_all(g_set, DP, 0, 0)
 
 
+def from_ring(block, axis, away):
+    count = lax.axis_size(axis)
+    return lax.ppermute(block, axis, [((d + away) % count, d) for d in range(count)])
+
+
+def passed_round(own_part):
+    near = jnp.stack([from_ring(own_part, "zh", away) for away in (1, 2, 3)])
+    far = from_ring(near, "zl", 1)
+    near_up, near_down = from_ring(near, "x", 1), from_ring(near, "x", -1)
+    near_across = from_ring(near_up, "x", 1)
+    far_up, far_down = from_ring(far, "x", 1), from_ring(far, "x", -1)
+    far_across = from_ring(far_down, "x", -1)
+    parts = []
+    for one in (near, near_up, near_across, near_down, far, far_up, far_across, far_down):
+        parts += [one, from_ring(one, "core", 1)]
+    return tuple(parts)
+
+
 def shards(inputs_down, inputs_up, w_in, w_out):
     y, zh, dp = lax.axis_index("y"), lax.axis_index("zh"), lax.axis_index(DP)
     low_half = y < 2
@@ -325,13 +394,15 @@
         return lax.all_gather(own_part, ("zh",) + DP).reshape(SET, 16, 2, D // 16, R)
 
     first_slot = jnp.where(low_half, 0, 1)
-    own_a, own_b = own(first_slot), own(1 - first_slot)
-    w_a = gathered(own_a)
-    own_b, w_a = lax.optimization_barrier((own_b, w_a))
-    w_b = gathered(own_b)
+    w_a = (gathered(own(first_slot)),)
+    w_b = tuple(w[0].reshape(2, 16, D // 16, R) for w in (w_in, w_out)) + passed_round(
+        own(1 - first_slot)
+    )
+    place_flags = jnp.stack([1 - first_slot, zh] + [lax.axis_index(name) for name in DP])
 
     def flag(active, reverse):
-        return jnp.stack([active.astype(jnp.int32), reverse.astype(jnp.int32)])
+        both = jnp.stack([active.astype(jnp.int32), reverse.astype(jnp.int32)])
+        return jnp.concatenate([both, place_flags.astype(jnp.int32)])
 
     p_a, p_b = flag(stage_p, ~low_half), flag(stage_p, low_half)
     q_a, q_b = flag(~stage_p, ~low_half), flag(~stage_p, low_half)

time: 408 us -> 388 us (0.951)
  waiting for transfers between devices: 263 us -> 193 us
  starting transfers between devices: 65 us -> 95.5 us
  Pallas kernels: 53.3 us -> 72.8 us
    all_gather x2 -> x1, waiting for transfers between devices: 202 us -> 39.3 us  [gathered(): lax.all_gather(own_part, ('zh',) + DP).reshape(SET, 16, 2, D // 16, R)]
    ppermute x0 -> x18, waiting for transfers between devices: none -> 98.3 us  [from_ring(): lax.ppermute(block, axis, [((d + away) % count, d) for d in range(count)])]
    ppermute x0 -> x18, starting transfers between devices: none -> 24.1 us  [from_ring(): lax.ppermute(block, axis, [((d + away) % count, d) for d in range(count)])]
    pallas_call x8, Pallas kernels: 50.9 us -> 68.9 us  [the longest x4 34.7 us: run_backward(): pl.pallas_call(lambda *refs: backward_kernel(*refs, source=source, aliase...]
  transfers between devices with their start and end apart: 16 -> 33, of which waited for: 12 -> 17; matrix products, arithmetic and copies ran while one was open for 0% -> 1% of each run, Pallas kernels for 7% -> 8%
where the time goes in v3:
time: 388 us; the launch traced here: 381 us
  waiting for transfers between devices  193 us (50%)
  starting transfers between devices  95.5 us (25%)
  Pallas kernels  72.8 us (19%)
  between operations  14.2 us (4%)
    ppermute x18, waiting for transfers between devices, from_ring(): lax.ppermute(block, axis, [((d + away) % count, d) for d in range(count)])  98.3 us
    ppermute x4, starting transfers between devices, hop(): return lax.ppermute(rows, 'y', [(0, 1), (1, 0), (2, 3), (3, 2)])  39.9 us
    all_gather x1, waiting for transfers between devices, gathered(): lax.all_gather(own_part, ('zh',) + DP).reshape(SET, 16, 2, D // 16, R)  39.3 us
    pallas_call x4, Pallas kernels, run_backward(): pl.pallas_call(lambda *refs: backward_kernel(*refs, source=source, aliase...  34.7 us
    pallas_call x4, Pallas kernels, run_forward(): pl.pallas_call(lambda *refs: forward_kernel(*refs, source=source, aliased...  34.2 us
    ppermute x4, waiting for transfers between devices, hop(): return lax.ppermute(rows, 'y', [(0, 1), (1, 0), (2, 3), (3, 2)])  27.5 us
    ppermute x18, starting transfers between devices, from_ring(): lax.ppermute(block, axis, [((d + away) % count, d) for d in range(count)])  24.1 us
    ppermute x6, starting transfers between devices, summed_over_zh(): total = total + lax.ppermute(parts[k], 'zh', route).astype(jnp.float32)  18.8 us
  transfers between devices with their start and end apart: 33, of which 17 were waited for; matrix products, arithmetic and copies ran while one was open for 1% of the time, Pallas kernels for 8%

profile of v3, /device:TPU:2, one launch (start us, length us, event | category | flops | bytes accessed | tf_op | source)
XLA Modules:
  0.0 381.2 jit_solution(7791992515442856621)
XLA Ops:
  8.6 6.4 %collective-permute-start.1 = (bf16[2,320,256]{2,1,0:T(8,128)(2,1)S(1)}, bf16[2,320,256]{2,1,0:T(8,128)(2,1)S(1)}, u32[]{:S(2)}, u32[]{:S(2)}) collective-permute-start(bf16[2,320,256]{2,1,0:T(8,128)(2,1)S(1)} %pad_maximum_fusion.2), channel_id=1, source_target_pairs={{16,0},{32,16},{48,32},{0,48},{17,1},{33,17},{49,33},{1,49},{18,2}... | collective-permute-start | bytes 983048 | tf_op jit(solution)/shard_map/ppermute | solution.py:365
  15.9 2.8 collective-permute-start.3
  18.7 21.4 %collective-permute-done.1 = bf16[2,320,256]{2,1,0:T(8,128)(2,1)S(1)} collective-permute-done((bf16[2,320,256]{2,1,0:T(8,128)(2,1)S(1)}, bf16[2,320,256]{2,1,0:T(8,128)(2,1)S(1)}, u32[]{:S(2)}, u32[]{:S(2)}) %collective-permute-start.1) | collective-permute-done | bytes 327712 | tf_op jit(solution)/shard_map/ppermute | solution.py:365
  40.2 7.2 %collective-permute-done.3 = bf16[2,320,256]{2,1,0:T(8,128)(2,1)S(1)} collective-permute-done((bf16[2,320,256]{2,1,0:T(8,128)(2,1)S(1)}, bf16[2,320,256]{2,1,0:T(8,128)(2,1)S(1)}, u32[]{:S(2)}, u32[]{:S(2)}) %collective-permute-start.3) | collective-permute-done | bytes 327712 | tf_op jit(solution)/shard_map/ppermute | solution.py:365
  47.5 4.9 %collective-permute-start.11 = (bf16[3,2,320,256]{3,2,1,0:T(8,128)(2,1)S(1)}, bf16[3,2,320,256]{3,2,1,0:T(8,128)(2,1)S(1)}, u32[]{:S(2)}, u32[]{:S(2)}) collective-permute-start(bf16[3,2,320,256]{3,2,1,0:T(8,128)(2,1)S(1)} %pad_maximum_fusion.refs_4_.refs_6_), channel_id=1, source_target_pairs={{8,0},{0,8},{9,1},{1,9},{10,2},{2,10},{11,3},{3,11},{12,4},{4,12},... | collective-permute-start | bytes 2949128 | tf_op jit(solution)/shard_map/ppermute | solution.py:365
  54.4 26.9 %collective-permute-done.11.refs_12_.refs_14_ = bf16[3,2,320,256]{3,2,1,0:T(8,128)(2,1)S(1)} collective-permute-done((bf16[3,2,320,256]{3,2,1,0:T(8,128)(2,1)S(1)}, bf16[3,2,320,256]{3,2,1,0:T(8,128)(2,1)S(1)}, u32[]{:S(2)}, u32[]{:S(2)}) %collective-permute-start.11) | collective-permute-done | bytes 983072 | tf_op jit(solution)/shard_map/ppermute | solution.py:365
  85.6 40.8 %collective-permute-done.15.refs_18_.refs_20_ = bf16[3,2,320,256]{3,2,1,0:T(8,128)(2,1)} collective-permute-done((bf16[3,2,320,256]{3,2,1,0:T(8,128)(2,1)S(1)}, bf16[3,2,320,256]{3,2,1,0:T(8,128)(2,1)}, u32[]{:S(2)}, u32[]{:S(2)}) %collective-permute-start.15) | collective-permute-done | bytes 983072 | tf_op jit(solution)/shard_map/ppermute | solution.py:365
  129.4 39.3 %all-gather.5.cloned.1.call-done = bf16[128,320,256]{2,1,0:T(8,128)(2,1)} async-done(((bf16[2,320,256]{2,1,0:T(8,128)(2,1)}), bf16[128,320,256]{2,1,0:T(8,128)(2,1)}) %all-gather.5.cloned.1.call-update) | async-done | bytes 20971536 | tf_op jit(solution)/shard_map/all_gather | solution.py:394
  168.7 11.9 %forward_set.4 = (bf16[24,5120]{1,0:T(8,128)(2,1)S(1)}, bf16[4,24,5120]{2,1,0:T(8,128)(2,1)S(1)}, f32[4,24,256]{2,1,0:T(8,128)S(1)}, bf16[4,24,256]{2,1,0:T(8,128)(2,1)S(1)}) custom-call(s32[7]{0:T(128)S(1)} %concatenate.19.refs_0_, bf16[24,5120]{1,0:T(8,128)(2,1)S(1)} %pad.4.refs_1_, bf16[4,16,2,320,256]{4,3,2,1,0:T(8,128)(2,1)} %bitcast.27), custom_call_target="tpu_custom_call" | custom-call | flops 125829120 | bytes 5242880 | tf_op jit(solution)/shard_map/forward_set/pallas_call | solution.py:179
  181.8 7.0 %collective-permute-done.refs_1_ = bf16[24,5120]{1,0:T(8,128)(2,1)S(1)} collective-permute-done((bf16[24,5120]{1,0:T(8,128)(2,1)S(1)}, bf16[24,5120]{1,0:T(8,128)(2,1)S(1)}, u32[]{:S(2)}, u32[]{:S(2)}) %collective-permute-start) | collective-permute-done | bytes 245792 | tf_op jit(solution)/shard_map/ppermute | solution.py:356
  191.7 9.1 %forward_set.6 = (bf16[24,5120]{1,0:T(8,128)(2,1)S(1)}, bf16[4,24,5120]{2,1,0:T(8,128)(2,1)S(1)}, f32[4,24,256]{2,1,0:T(8,128)S(1)}, bf16[4,24,256]{2,1,0:T(8,128)(2,1)S(1)}) custom-call(s32[7]{0:T(128)S(1)} %concatenate.21.refs_0_, bf16[24,5120]{1,0:T(8,128)(2,1)S(1)} %get-tuple-element.42.refs_1_, bf16[2,16,320,256]{3,2,1,0:T(8,128)(2,1)} %bitcast.35, ...), custom_call_target="tpu_custom_call" | custom-call | flops 125829120 | bytes 5242880 | tf_op jit(solution)/shard_map/forward_set/pallas_call | solution.py:179
  200.8 22.2 %collective-permute-start.19 = (bf16[24,5120]{1,0:T(8,128)(2,1)S(1)}, bf16[24,5120]{1,0:T(8,128)(2,1)S(1)}, u32[]{:S(2)}, u32[]{:S(2)}) collective-permute-start(bf16[24,5120]{1,0:T(8,128)(2,1)S(1)} %get-tuple-element.43), channel_id=1, source_target_pairs={{0,64},{64,0},{128,192},{192,128},{1,65},{65,1},{129,193},{193,129... | collective-permute-start | bytes 737288 | tf_op jit(solution)/shard_map/ppermute | solution.py:356
  223.1 6.5 %collective-permute-done.19.refs_1_ = bf16[24,5120]{1,0:T(8,128)(2,1)S(1)} collective-permute-done((bf16[24,5120]{1,0:T(8,128)(2,1)S(1)}, bf16[24,5120]{1,0:T(8,128)(2,1)S(1)}, u32[]{:S(2)}, u32[]{:S(2)}) %collective-permute-start.19) | collective-permute-done | bytes 245792 | tf_op jit(solution)/shard_map/ppermute | solution.py:356
  229.6 12.5 %forward_set.7 = (bf16[24,5120]{1,0:T(8,128)(2,1)S(1)}, bf16[4,24,5120]{2,1,0:T(8,128)(2,1)S(1)}, f32[4,24,256]{2,1,0:T(8,128)S(1)}, bf16[4,24,256]{2,1,0:T(8,128)(2,1)S(1)}) custom-call(s32[7]{0:T(128)S(1)} %concatenate.22.refs_0_, ...), custom_call_target="tpu_custom_call", output_to_operand_aliasing={{1}: (20, {}), {2}: (21, {}), {3}: (22, {})} | custom-call | flops 125829120 | bytes 5242880 | tf_op jit(solution)/shard_map/forward_set/pallas_call | solution.py:179
  242.1 13.0 %backward_set.4 = (bf16[24,5120]{1,0:T(8,128)(2,1)S(1)}, bf16[16,4,24,320]{3,2,1,0:T(8,128)(2,1)}) custom-call(s32[7]{0:T(128)S(1)} %concatenate.22.refs_0_, bf16[24,5120]{1,0:T(8,128)(2,1)S(1)} %get-tuple-element.47.refs_1_, bf16[4,24,5120]{2,1,0:T(8,128)(2,1)S(1)} %get-tuple-element.48.refs_2_, f32[4,24,256]{2,1,0:T(8,128)S(1)} %get-tuple-element.49.refs_3_, ...), custom_call_target="tpu_custom_call" | custom-call | flops 125829120 | bytes 5242880 | tf_op jit(solution)/shard_map/backward_set/pallas_call | solution.py:297
  255.2 7.8 %collective-permute-done.20.refs_1_ = bf16[24,5120]{1,0:T(8,128)(2,1)S(1)} collective-permute-done((bf16[24,5120]{1,0:T(8,128)(2,1)S(1)}, bf16[24,5120]{1,0:T(8,128)(2,1)S(1)}, u32[]{:S(2)}, u32[]{:S(2)}) %collective-permute-start.20) | collective-permute-done | bytes 245792 | tf_op jit(solution)/shard_map/ppermute | solution.py:356
  263.0 9.4 %backward_set.5 = (bf16[24,5120]{1,0:T(8,128)(2,1)S(1)}, bf16[16,4,24,320]{3,2,1,0:T(8,128)(2,1)}) custom-call(s32[7]{0:T(128)S(1)} %concatenate.21.refs_0_, bf16[24,5120]{1,0:T(8,128)(2,1)S(1)} %collective-permute-done.20.refs_1_, bf16[4,24,5120]{2,1,0:T(8,128)(2,1)S(1)} %get-tuple-element.48.refs_2_, ...), custom_call_target="tpu_custom_call", output_to_operand_aliasing={{1}: (22, {})} | custom-call | flops 125829120 | bytes 5242880 | tf_op jit(solution)/shard_map/backward_set/pallas_call | solution.py:297
  272.4 4.5 %all-to-all-start = ((bf16[16,4,24,320]{3,2,1,0:T(8,128)(2,1)}), bf16[16,4,24,320]{3,2,1,0:T(8,128)(2,1)S(1)}, u32[]{:S(2)}, u32[]{:S(2)}) async-start(bf16[16,4,24,320]{3,2,1,0:T(8,128)(2,1)} %get-tuple-element.58), calls=%async_computation | async-start | bytes 2359296 | tf_op jit(solution)/shard_map/all_to_all | solution.py:360
  278.4 17.6 %collective-permute-start.21 = (bf16[24,5120]{1,0:T(8,128)(2,1)S(1)}, bf16[24,5120]{1,0:T(8,128)(2,1)S(1)}, u32[]{:S(2)}, u32[]{:S(2)}) collective-permute-start(bf16[24,5120]{1,0:T(8,128)(2,1)S(1)} %get-tuple-element.55), channel_id=1, source_target_pairs={{0,64},{64,0},{128,192},{192,128},{1,65},{65,1},{129,193},{193,129... | collective-permute-start | bytes 737288 | tf_op jit(solution)/shard_map/ppermute | solution.py:356
  296.0 6.3 %collective-permute-done.21.refs_1_ = bf16[24,5120]{1,0:T(8,128)(2,1)S(1)} collective-permute-done((bf16[24,5120]{1,0:T(8,128)(2,1)S(1)}, bf16[24,5120]{1,0:T(8,128)(2,1)S(1)}, u32[]{:S(2)}, u32[]{:S(2)}) %collective-permute-start.21) | collective-permute-done | bytes 245792 | tf_op jit(solution)/shard_map/ppermute | solution.py:356
  302.2 11.6 %backward_set.7 = (bf16[24,5120]{1,0:T(8,128)(2,1)}, bf16[16,4,24,320]{3,2,1,0:T(8,128)(2,1)}) custom-call(s32[7]{0:T(128)S(1)} %concatenate.19.refs_0_, bf16[24,5120]{1,0:T(8,128)(2,1)S(1)} %collective-permute-done.21.refs_1_, bf16[4,24,5120]{2,1,0:T(8,128)(2,1)S(1)} %get-tuple-element.53.refs_2_, ...), custom_call_target="tpu_custom_call", output_to_operand_aliasing={{1}: (5, {})} | custom-call | flops 125829120 | bytes 5242880 | tf_op jit(solution)/shard_map/backward_set/pallas_call | solution.py:297
  313.8 5.7 %all-to-all-start.1 = ((bf16[16,4,24,320]{3,2,1,0:T(8,128)(2,1)}), bf16[16,4,24,320]{3,2,1,0:T(8,128)(2,1)S(1)}, u32[]{:S(2)}, u32[]{:S(2)}) async-start(bf16[16,4,24,320]{3,2,1,0:T(8,128)(2,1)} %get-tuple-element.59), calls=%async_computation.1 | async-start | bytes 2359296 | tf_op jit(solution)/shard_map/all_to_all | solution.py:360
  322.0 2.7 collective-permute-start.25
  324.7 3.6 collective-permute-start.26
  328.4 3.4 collective-permute-start.27
  331.8 5.3 %all-to-all-done.1.refs_1_ = bf16[16,4,24,320]{3,2,1,0:T(8,128)(2,1)S(1)} async-done(((bf16[16,4,24,320]{3,2,1,0:T(8,128)(2,1)}), bf16[16,4,24,320]{3,2,1,0:T(8,128)(2,1)S(1)}, u32[]{:S(2)}, u32[]{:S(2)}) %all-to-all-start.1) | async-done | bytes 983072 | tf_op jit(solution)/shard_map/all_to_all | solution.py:360
  341.4 4.4 %collective-permute-start.23 = (bf16[320,256]{1,0:T(8,128)(2,1)S(1)}, bf16[320,256]{1,0:T(8,128)(2,1)S(1)}, u32[]{:S(2)}, u32[]{:S(2)}) collective-permute-start(bf16[320,256]{1,0:T(8,128)(2,1)S(1)} %get-tuple-element.64), channel_id=1, source_target_pairs={{0,32},{16,48},{32,0},{48,16},{1,33},{17,49},{33,1},{49,17},{2,34}... | collective-permute-start | bytes 491528 | tf_op jit(solution)/shard_map/ppermute | solution.py:351
  348.2 4.4 %collective-permute-done.26 = bf16[320,256]{1,0:T(8,128)(2,1)S(1)} collective-permute-done((bf16[320,256]{1,0:T(8,128)(2,1)S(1)}, bf16[320,256]{1,0:T(8,128)(2,1)S(1)}, u32[]{:S(2)}, u32[]{:S(2)}) %collective-permute-start.26) | collective-permute-done | bytes 163872 | tf_op jit(solution)/shard_map/ppermute | solution.py:351
  352.6 3.8 collective-permute-done.22
  356.4 3.5 collective-permute-done.23
  359.9 5.6 %collective-permute-done.24 = bf16[320,256]{1,0:T(8,128)(2,1)S(1)} collective-permute-done((bf16[320,256]{1,0:T(8,128)(2,1)S(1)}, bf16[320,256]{1,0:T(8,128)(2,1)S(1)}, u32[]{:S(2)}, u32[]{:S(2)}) %collective-permute-start.24) | collective-permute-done | bytes 163872 | tf_op jit(solution)/shard_map/ppermute | solution.py:351
  368.0 5.0 %collective-permute-done.28 = bf16[320,256]{1,0:T(8,128)(2,1)S(1)} collective-permute-done((bf16[320,256]{1,0:T(8,128)(2,1)S(1)}, bf16[320,256]{1,0:T(8,128)(2,1)S(1)}, u32[]{:S(2)}, u32[]{:S(2)}) %collective-permute-start.28) | collective-permute-done | bytes 163872 | tf_op jit(solution)/shard_map/ppermute | solution.py:435
  (70 shorter events, 30.5 us)
Async XLA Ops:
  6.5 162.1 %all-gather.5.cloned.1.call-start = ((), (), s32[]{:S(2)}) async-start(), calls=%async_computation.2 | async-start | bytes 21299200 | tf_op jit(solution)/shard_map/all_gather | solution.py:394
  8.6 31.6 %collective-permute-start.1 = (bf16[2,320,256]{2,1,0:T(8,128)(2,1)S(1)}, bf16[2,320,256]{2,1,0:T(8,128)(2,1)S(1)}, u32[]{:S(2)}, u32[]{:S(2)}) collective-permute-start(bf16[2,320,256]{2,1,0:T(8,128)(2,1)S(1)} %pad_maximum_fusion.2), channel_id=1, source_target_pairs={{16,0},{32,16},{48,32},{0,48},{17,1},{33,17},{49,33},{1,49},{18,2}... | collective-permute-start | bytes 983048 | tf_op jit(solution)/shard_map/ppermute | solution.py:365
  14.9 25.2 %collective-permute-start.2 = (bf16[2,320,256]{2,1,0:T(8,128)(2,1)S(1)}, bf16[2,320,256]{2,1,0:T(8,128)(2,1)S(1)}, u32[]{:S(2)}, u32[]{:S(2)}) collective-permute-start(bf16[2,320,256]{2,1,0:T(8,128)(2,1)S(1)} %pad_maximum_fusion.2), channel_id=1, source_target_pairs={{32,0},{48,16},{0,32},{16,48},{33,1},{49,17},{1,33},{17,49},{34,2}... | collective-permute-start | bytes 983048 | tf_op jit(solution)/shard_map/ppermute | solution.py:365
  15.9 31.4 %collective-permute-start.3 = (bf16[2,320,256]{2,1,0:T(8,128)(2,1)S(1)}, bf16[2,320,256]{2,1,0:T(8,128)(2,1)S(1)}, u32[]{:S(2)}, u32[]{:S(2)}) collective-permute-start(bf16[2,320,256]{2,1,0:T(8,128)(2,1)S(1)} %pad_maximum_fusion.2), channel_id=1, source_target_pairs={{48,0},{0,16},{16,32},{32,48},{49,1},{1,17},{17,33},{33,49},{50,2}... | collective-permute-start | bytes 983048 | tf_op jit(solution)/shard_map/ppermute | solution.py:365
  47.5 33.8 %collective-permute-start.11 = (bf16[3,2,320,256]{3,2,1,0:T(8,128)(2,1)S(1)}, bf16[3,2,320,256]{3,2,1,0:T(8,128)(2,1)S(1)}, u32[]{:S(2)}, u32[]{:S(2)}) collective-permute-start(bf16[3,2,320,256]{3,2,1,0:T(8,128)(2,1)S(1)} %pad_maximum_fusion.refs_4_.refs_6_), channel_id=1, source_target_pairs={{8,0},{0,8},{9,1},{1,9},{10,2},{2,10},{11,3},{3,11},{12,4},{4,12},... | collective-permute-start | bytes 2949128 | tf_op jit(solution)/shard_map/ppermute | solution.py:365
  52.4 31.0 %collective-permute-start.5 = (bf16[3,2,320,256]{3,2,1,0:T(8,128)(2,1)S(1)}, bf16[3,2,320,256]{3,2,1,0:T(8,128)(2,1)S(1)}, u32[]{:S(2)}, u32[]{:S(2)}) collective-permute-start(bf16[3,2,320,256]{3,2,1,0:T(8,128)(2,1)S(1)} %pad_maximum_fusion.refs_4_.refs_6_), channel_id=1, source_target_pairs={{2,0},{4,2},{6,4},{0,6},{3,1},{5,3},{7,5},{1,7},{10,8},{12,10},{14... | collective-permute-start | bytes 2949128 | tf_op jit(solution)/shard_map/ppermute | solution.py:365
  52.9 30.4 %collective-permute-start.9 = (bf16[3,2,320,256]{3,2,1,0:T(8,128)(2,1)S(1)}, bf16[3,2,320,256]{3,2,1,0:T(8,128)(2,1)}, u32[]{:S(2)}, u32[]{:S(2)}) collective-permute-start(bf16[3,2,320,256]{3,2,1,0:T(8,128)(2,1)S(1)} %pad_maximum_fusion.refs_4_.refs_6_), channel_id=1, source_target_pairs={{6,0},{0,2},{2,4},{4,6},{7,1},{1,3},{3,5},{5,7},{14,8},{8,10},{10,... | collective-permute-start | bytes 2949128 | tf_op jit(solution)/shard_map/ppermute | solution.py:365
  54.4 31.1 %collective-permute-start.4 = (bf16[3,2,320,256]{3,2,1,0:T(8,128)(2,1)S(1)}, bf16[3,2,320,256]{3,2,1,0:T(8,128)(2,1)S(1)}, u32[]{:S(2)}, u32[]{:S(2)}) collective-permute-start(bf16[3,2,320,256]{3,2,1,0:T(8,128)(2,1)S(1)} %pad_maximum_fusion.refs_4_.refs_6_), channel_id=1, source_target_pairs={{1,0},{0,1},{3,2},{2,3},{5,4},{4,5},{7,6},{6,7},{9,8},{8,9},{11,10... | collective-permute-start | bytes 2949128 | tf_op jit(solution)/shard_map/ppermute | solution.py:365
  81.3 45.1 %collective-permute-start.15 = (bf16[3,2,320,256]{3,2,1,0:T(8,128)(2,1)S(1)}, bf16[3,2,320,256]{3,2,1,0:T(8,128)(2,1)}, u32[]{:S(2)}, u32[]{:S(2)}) collective-permute-start(bf16[3,2,320,256]{3,2,1,0:T(8,128)(2,1)S(1)} %collective-permute-done.11.refs_12_.refs_14_), channel_id=1, source_target_pairs={{6,0},{0,2},{2,4},{4,6},{7,1},{1,3},{3,5},{5,7},{14,8},{8,10},{10,... | collective-permute-start | bytes 2949128 | tf_op jit(solution)/shard_map/ppermute | solution.py:365
  82.8 97.8 %collective-permute-start.13 = (bf16[3,2,320,256]{3,2,1,0:T(8,128)(2,1)S(1)}, bf16[3,2,320,256]{3,2,1,0:T(8,128)(2,1)}, u32[]{:S(2)}, u32[]{:S(2)}) collective-permute-start(bf16[3,2,320,256]{3,2,1,0:T(8,128)(2,1)S(1)} %collective-permute-done.11.refs_12_.refs_14_), channel_id=1, source_target_pairs={{2,0},{4,2},{6,4},{0,6},{3,1},{5,3},{7,5},{1,7},{10,8},{12,10},{14... | collective-permute-start | bytes 2949128 | tf_op jit(solution)/shard_map/ppermute | solution.py:365
  83.3 98.0 %collective-permute-start.12 = (bf16[3,2,320,256]{3,2,1,0:T(8,128)(2,1)S(1)}, bf16[3,2,320,256]{3,2,1,0:T(8,128)(2,1)}, u32[]{:S(2)}, u32[]{:S(2)}) collective-permute-start(bf16[3,2,320,256]{3,2,1,0:T(8,128)(2,1)S(1)} %collective-permute-done.11.refs_12_.refs_14_), channel_id=1, source_target_pairs={{1,0},{0,1},{3,2},{2,3},{5,4},{4,5},{7,6},{6,7},{9,8},{8,9},{11,10... | collective-permute-start | bytes 2949128 | tf_op jit(solution)/shard_map/ppermute | solution.py:365
  83.3 97.4 %collective-permute-start.7 = (bf16[3,2,320,256]{3,2,1,0:T(8,128)(2,1)S(1)}, bf16[3,2,320,256]{3,2,1,0:T(8,128)(2,1)}, u32[]{:S(2)}, u32[]{:S(2)}) collective-permute-start(bf16[3,2,320,256]{3,2,1,0:T(8,128)(2,1)S(1)} %collective-permute-done.5.refs_6_.refs_8_), channel_id=1, source_target_pairs={{2,0},{4,2},{6,4},{0,6},{3,1},{5,3},{7,5},{1,7},{10,8},{12,10},{14... | collective-permute-start | bytes 2949128 | tf_op jit(solution)/shard_map/ppermute | solution.py:365
  85.5 95.6 %collective-permute-start.10 = (bf16[3,2,320,256]{3,2,1,0:T(8,128)(2,1)}, bf16[3,2,320,256]{3,2,1,0:T(8,128)(2,1)}, u32[]{:S(2)}, u32[]{:S(2)}) collective-permute-start(bf16[3,2,320,256]{3,2,1,0:T(8,128)(2,1)} %collective-permute-done.9.refs_10_.refs_12_), channel_id=1, source_target_pairs={{1,0},{0,1},{3,2},{2,3},{5,4},{4,5},{7,6},{6,7},{9,8},{8,9},{11,10... | collective-permute-start | bytes 2949128 | tf_op jit(solution)/shard_map/ppermute | solution.py:365
  126.4 55.2 %collective-permute-start.16 = (bf16[3,2,320,256]{3,2,1,0:T(8,128)(2,1)}, bf16[3,2,320,256]{3,2,1,0:T(8,128)(2,1)}, u32[]{:S(2)}, u32[]{:S(2)}) collective-permute-start(bf16[3,2,320,256]{3,2,1,0:T(8,128)(2,1)} %collective-permute-done.15.refs_18_.refs_20_), channel_id=1, source_target_pairs={{6,0},{0,2},{2,4},{4,6},{7,1},{1,3},{3,5},{5,7},{14,8},{8,10},{10,... | collective-permute-start | bytes 2949128 | tf_op jit(solution)/shard_map/ppermute | solution.py:365
  180.6 8.2 %collective-permute-start = (bf16[24,5120]{1,0:T(8,128)(2,1)S(1)}, bf16[24,5120]{1,0:T(8,128)(2,1)S(1)}, u32[]{:S(2)}, u32[]{:S(2)}) collective-permute-start(bf16[24,5120]{1,0:T(8,128)(2,1)S(1)} %get-tuple-element.38), channel_id=1, source_target_pairs={{0,64},{64,0},{128,192},{192,128},{1,65},{65,1},{129,193},{193,129... | collective-permute-start | bytes 737288 | tf_op jit(solution)/shard_map/ppermute | solution.py:356
  180.7 8.9 %collective-permute-start.6 = (bf16[3,2,320,256]{3,2,1,0:T(8,128)(2,1)S(1)}, bf16[3,2,320,256]{3,2,1,0:T(8,128)(2,1)}, u32[]{:S(2)}, u32[]{:S(2)}) collective-permute-start(bf16[3,2,320,256]{3,2,1,0:T(8,128)(2,1)S(1)} %collective-permute-done.5.refs_6_.refs_8_), channel_id=1, source_target_pairs={{1,0},{0,1},{3,2},{2,3},{5,4},{4,5},{7,6},{6,7},{9,8},{8,9},{11,10... | collective-permute-start | bytes 2949128 | tf_op jit(solution)/shard_map/ppermute | solution.py:365
  181.1 8.6 %collective-permute-start.18 = (bf16[3,2,320,256]{3,2,1,0:T(8,128)(2,1)}, bf16[3,2,320,256]{3,2,1,0:T(8,128)(2,1)}, u32[]{:S(2)}, u32[]{:S(2)}) collective-permute-start(bf16[3,2,320,256]{3,2,1,0:T(8,128)(2,1)} %collective-permute-done.15.refs_18_.refs_20_), channel_id=1, source_target_pairs={{1,0},{0,1},{3,2},{2,3},{5,4},{4,5},{7,6},{6,7},{9,8},{8,9},{11,10... | collective-permute-start | bytes 2949128 | tf_op jit(solution)/shard_map/ppermute | solution.py:365
  181.3 8.3 %collective-permute-start.14 = (bf16[3,2,320,256]{3,2,1,0:T(8,128)(2,1)}, bf16[3,2,320,256]{3,2,1,0:T(8,128)(2,1)S(1)}, u32[]{:S(2)}, u32[]{:S(2)}) collective-permute-start(bf16[3,2,320,256]{3,2,1,0:T(8,128)(2,1)} %collective-permute-done.13.refs_14_.refs_16_), channel_id=1, source_target_pairs={{1,0},{0,1},{3,2},{2,3},{5,4},{4,5},{7,6},{6,7},{9,8},{8,9},{11,10... | collective-permute-start | bytes 2949128 | tf_op jit(solution)/shard_map/ppermute | solution.py:365
  181.6 8.1 %collective-permute-start.8 = (bf16[3,2,320,256]{3,2,1,0:T(8,128)(2,1)}, bf16[3,2,320,256]{3,2,1,0:T(8,128)(2,1)}, u32[]{:S(2)}, u32[]{:S(2)}) collective-permute-start(bf16[3,2,320,256]{3,2,1,0:T(8,128)(2,1)} %collective-permute-done.7.refs_8_.refs_10_), channel_id=1, source_target_pairs={{1,0},{0,1},{3,2},{2,3},{5,4},{4,5},{7,6},{6,7},{9,8},{8,9},{11,10... | collective-permute-start | bytes 2949128 | tf_op jit(solution)/shard_map/ppermute | solution.py:365
  200.8 28.8 %collective-permute-start.19 = (bf16[24,5120]{1,0:T(8,128)(2,1)S(1)}, bf16[24,5120]{1,0:T(8,128)(2,1)S(1)}, u32[]{:S(2)}, u32[]{:S(2)}) collective-permute-start(bf16[24,5120]{1,0:T(8,128)(2,1)S(1)} %get-tuple-element.43), channel_id=1, source_target_pairs={{0,64},{64,0},{128,192},{192,128},{1,65},{65,1},{129,193},{193,129... | collective-permute-start | bytes 737288 | tf_op jit(solution)/shard_map/ppermute | solution.py:356
  255.1 7.9 %collective-permute-start.20 = (bf16[24,5120]{1,0:T(8,128)(2,1)S(1)}, bf16[24,5120]{1,0:T(8,128)(2,1)S(1)}, u32[]{:S(2)}, u32[]{:S(2)}) collective-permute-start(bf16[24,5120]{1,0:T(8,128)(2,1)S(1)} %get-tuple-element.50), channel_id=1, source_target_pairs={{0,64},{64,0},{128,192},{192,128},{1,65},{65,1},{129,193},{193,129... | collective-permute-start | bytes 737288 | tf_op jit(solution)/shard_map/ppermute | solution.py:356
  272.4 41.4 %all-to-all-start = ((bf16[16,4,24,320]{3,2,1,0:T(8,128)(2,1)}), bf16[16,4,24,320]{3,2,1,0:T(8,128)(2,1)S(1)}, u32[]{:S(2)}, u32[]{:S(2)}) async-start(bf16[16,4,24,320]{3,2,1,0:T(8,128)(2,1)} %get-tuple-element.58), calls=%async_computation | async-start | bytes 2359296 | tf_op jit(solution)/shard_map/all_to_all | solution.py:360
  276.9 43.1 %all-gather.7.cloned.1.call-start = ((), (), s32[]{:S(2)}) async-start(), calls=%async_computation.3 | async-start | bytes 1671168 | tf_op jit(solution)/shard_map/all_gather | solution.py:420
  278.4 23.9 %collective-permute-start.21 = (bf16[24,5120]{1,0:T(8,128)(2,1)S(1)}, bf16[24,5120]{1,0:T(8,128)(2,1)S(1)}, u32[]{:S(2)}, u32[]{:S(2)}) collective-permute-start(bf16[24,5120]{1,0:T(8,128)(2,1)S(1)} %get-tuple-element.55), channel_id=1, source_target_pairs={{0,64},{64,0},{128,192},{192,128},{1,65},{65,1},{129,193},{193,129... | collective-permute-start | bytes 737288 | tf_op jit(solution)/shard_map/ppermute | solution.py:356
  313.8 23.2 %all-to-all-start.1 = ((bf16[16,4,24,320]{3,2,1,0:T(8,128)(2,1)}), bf16[16,4,24,320]{3,2,1,0:T(8,128)(2,1)S(1)}, u32[]{:S(2)}, u32[]{:S(2)}) async-start(bf16[16,4,24,320]{3,2,1,0:T(8,128)(2,1)} %get-tuple-element.59), calls=%async_computation.1 | async-start | bytes 2359296 | tf_op jit(solution)/shard_map/all_to_all | solution.py:360
  322.0 23.8 %collective-permute-start.25 = (bf16[320,256]{1,0:T(8,128)(2,1)S(1)}, bf16[320,256]{1,0:T(8,128)(2,1)S(1)}, u32[]{:S(2)}, u32[]{:S(2)}) collective-permute-start(bf16[320,256]{1,0:T(8,128)(2,1)S(1)} %get-tuple-element.68), channel_id=1, source_target_pairs={{0,16},{16,32},{32,48},{48,0},{1,17},{17,33},{33,49},{49,1},{2,18}... | collective-permute-start | bytes 491528 | tf_op jit(solution)/shard_map/ppermute | solution.py:351
  324.7 27.8 %collective-permute-start.26 = (bf16[320,256]{1,0:T(8,128)(2,1)S(1)}, bf16[320,256]{1,0:T(8,128)(2,1)S(1)}, u32[]{:S(2)}, u32[]{:S(2)}) collective-permute-start(bf16[320,256]{1,0:T(8,128)(2,1)S(1)} %get-tuple-element.69), channel_id=1, source_target_pairs={{0,32},{16,48},{32,0},{48,16},{1,33},{17,49},{33,1},{49,17},{2,34}... | collective-permute-start | bytes 491528 | tf_op jit(solution)/shard_map/ppermute | solution.py:351
  328.4 24.2 %collective-permute-start.27 = (bf16[320,256]{1,0:T(8,128)(2,1)S(1)}, bf16[320,256]{1,0:T(8,128)(2,1)S(1)}, u32[]{:S(2)}, u32[]{:S(2)}) collective-permute-start(bf16[320,256]{1,0:T(8,128)(2,1)S(1)} %get-tuple-element.70), channel_id=1, source_target_pairs={{0,48},{16,0},{32,16},{48,32},{1,49},{17,1},{33,17},{49,33},{2,50}... | collective-permute-start | bytes 491528 | tf_op jit(solution)/shard_map/ppermute | solution.py:351
  339.0 17.3 %collective-permute-start.22 = (bf16[320,256]{1,0:T(8,128)(2,1)S(1)}, bf16[320,256]{1,0:T(8,128)(2,1)S(1)}, u32[]{:S(2)}, u32[]{:S(2)}) collective-permute-start(bf16[320,256]{1,0:T(8,128)(2,1)S(1)} %get-tuple-element.63), channel_id=1, source_target_pairs={{0,16},{16,32},{32,48},{48,0},{1,17},{17,33},{33,49},{49,1},{2,18}... | collective-permute-start | bytes 491528 | tf_op jit(solution)/shard_map/ppermute | solution.py:351
  341.4 18.5 %collective-permute-start.23 = (bf16[320,256]{1,0:T(8,128)(2,1)S(1)}, bf16[320,256]{1,0:T(8,128)(2,1)S(1)}, u32[]{:S(2)}, u32[]{:S(2)}) collective-permute-start(bf16[320,256]{1,0:T(8,128)(2,1)S(1)} %get-tuple-element.64), channel_id=1, source_target_pairs={{0,32},{16,48},{32,0},{48,16},{1,33},{17,49},{33,1},{49,17},{2,34}... | collective-permute-start | bytes 491528 | tf_op jit(solution)/shard_map/ppermute | solution.py:351
  345.8 19.7 %collective-permute-start.24 = (bf16[320,256]{1,0:T(8,128)(2,1)S(1)}, bf16[320,256]{1,0:T(8,128)(2,1)S(1)}, u32[]{:S(2)}, u32[]{:S(2)}) collective-permute-start(bf16[320,256]{1,0:T(8,128)(2,1)S(1)} %get-tuple-element.65), channel_id=1, source_target_pairs={{0,48},{16,0},{32,16},{48,32},{1,49},{17,1},{33,17},{49,33},{2,50}... | collective-permute-start | bytes 491528 | tf_op jit(solution)/shard_map/ppermute | solution.py:351
  365.6 7.4 %collective-permute-start.28 = (bf16[320,256]{1,0:T(8,128)(2,1)S(1)}, bf16[320,256]{1,0:T(8,128)(2,1)S(1)}, u32[]{:S(2)}, u32[]{:S(2)}) collective-permute-start(bf16[320,256]{1,0:T(8,128)(2,1)S(1)} %get-tuple-element.71), channel_id=1, source_target_pairs={{0,192},{192,0},{64,128},{128,64},{1,193},{193,1},{65,129},{129,65... | collective-permute-start | bytes 491528 | tf_op jit(solution)/shard_map/ppermute | solution.py:435
  (6 other events, 198.2 us)
Sparse Core Ops, SparseCore 0:
  10.1 158.5 all-gather.4
  279.6 40.3 all-gather.6

commit v4 on v3

--- a/solution.py
+++ b/solution.py
@@ -32,16 +32,15 @@
         )
 
     def first(self, layer, order):
-        for which in order:
-            self.copy(layer, 0, which).start()
+        self.order = order
+        self.begin(layer, 0)
 
     def begin(self, layer, slot):
-        pass
-
-    def arrive(self, layer, slot, which, following):
+        for which in self.order:
+            self.copy(layer, slot, which).start()
+
+    def arrive(self, layer, slot, which):
         self.copy(layer, slot, which).wait()
-        if following is not None:
-            self.copy(following, 1 - slot, which).start()
 
 
 class Scattered:
@@ -80,11 +79,10 @@
         self.leading = order[0]
         self.fetch(layer, 0)
 
-    def begin(self, following, slot):
-        if following is not None:
-            self.fetch(following, 1 - slot)
-
-    def arrive(self, layer, slot, which, following):
+    def begin(self, layer, slot):
+        self.fetch(layer, slot)
+
+    def arrive(self, layer, slot, which):
         if which == self.leading:
             pltpu.make_async_copy(
                 self.wbuf.at[1 - slot], self.wbuf.at[slot], self.sem.at[slot, 0]
@@ -121,15 +119,18 @@
         weights.first(0, (0, 1))
         hbuf[0] = x_ref[...]
 
-        def step(layer):
-            slot = layer % 2
-
-            following = layer + 1 if layer + 1 < SET else None
-            weights.begin(following, slot)
+        def step(layer, carry):
+            slot = lax.rem(layer, 2)
+
+
+            @pl.when(layer + 1 < SET)
+            def _():
+                weights.begin(layer + 1, 1 - slot)
+
             pltpu.make_async_copy(hbuf.at[layer], h_out.at[layer], sem_h.at[layer]).start()
             inv = inverse_rms(hbuf, layer)
             pre = jnp.zeros((ROWS, R), jnp.float32)
-            weights.arrive(layer, slot, 0, following)
+            weights.arrive(layer, slot, 0)
             for c in range(CH):
                 normed = (hbuf[layer, :, columns(c)].astype(jnp.float32) * inv).astype(jnp.bfloat16)
                 pre = pre + jnp.dot(
@@ -138,7 +139,7 @@
             active = (pre / (1.0 + jnp.exp(-pre))).astype(jnp.bfloat16)
             prebuf[layer] = pre
             actbuf[layer] = active
-            weights.arrive(layer, slot, 1, following)
+            weights.arrive(layer, slot, 1)
             for c in range(CH):
                 branch = lax.dot_general(
                     active,
@@ -148,9 +149,9 @@
                 )
                 before = hbuf[layer, :, columns(c)].astype(jnp.float32)
                 hbuf[layer + 1, :, columns(c)] = (before + branch).astype(jnp.bfloat16)
-
-        for layer in range(SET):
-            step(layer)
+            return carry
+
+        lax.fori_loop(0, SET, step, 0)
         y_ref[...] = hbuf[SET]
         copies = [
             pltpu.make_async_copy(prebuf, pre_out, sem_p.at[0]),
@@ -237,12 +238,15 @@
         pre_copy.wait()
         steps = SET - 1 if last else SET
 
-        def one_layer(step):
+        def one_layer(step, carry):
             layer = SET - 1 - step
-            slot = step % 2
-
-            following = layer - 1 if step + 1 < steps else None
-            weights.begin(following, slot)
+            slot = lax.rem(step, 2)
+
+
+            @pl.when(step + 1 < steps)
+            def _():
+                weights.begin(layer - 1, 1 - slot)
+
             g_send(step)
             h_copy(layer).wait()
             inv = inverse_rms(hbuf, layer)
@@ -250,7 +254,7 @@
             sigma = 1.0 / (1.0 + jnp.exp(-pre))
             slope = sigma * (1.0 + pre * (1.0 - sigma))
             d_active = jnp.zeros((ROWS, R), jnp.float32)
-            weights.arrive(layer, slot, 1, following)
+            weights.arrive(layer, slot, 1)
             for c in range(CH):
                 d_active = d_active + jnp.dot(
                     gbuf[step, :, columns(c)],
@@ -259,7 +263,7 @@
                 )
             d_pre = (d_active * slope).astype(jnp.bfloat16)
             total = jnp.zeros((ROWS, 1), jnp.float32)
-            weights.arrive(layer, slot, 0, following)
+            weights.arrive(layer, slot, 0)
             for c in range(CH):
                 d_normed = lax.dot_general(
                     d_pre,
@@ -276,9 +280,9 @@
                 moved = inv * (dnbuf[:, columns(c)] - unit * mean)
                 before = gbuf[step, :, columns(c)].astype(jnp.float32)
                 gbuf[step + 1, :, columns(c)] = (before + moved).astype(jnp.bfloat16)
-
-        for step in range(steps):
-            one_layer(step)
+            return carry
+
+        lax.fori_loop(0, steps, one_layer, 0)
         if last:
             g_send(SET - 1)
             h_copy(0).wait()
@@ -394,11 +398,11 @@
         return lax.all_gather(own_part, ("zh",) + DP).reshape(SET, 16, 2, D // 16, R)
 
     first_slot = jnp.where(low_half, 0, 1)
-    w_a = (gathered(own(first_slot)),)
-    w_b = tuple(w[0].reshape(2, 16, D // 16, R) for w in (w_in, w_out)) + passed_round(
-        own(1 - first_slot)
+    w_b = (gathered(own(1 - first_slot)),)
+    w_a = tuple(w[0].reshape(2, 16, D // 16, R) for w in (w_in, w_out)) + passed_round(
+        own(first_slot)
     )
-    place_flags = jnp.stack([1 - first_slot, zh] + [lax.axis_index(name) for name in DP])
+    place_flags = jnp.stack([first_slot, zh] + [lax.axis_index(name) for name in DP])
 
     def flag(active, reverse):
         both = jnp.stack([active.astype(jnp.int32), reverse.astype(jnp.int32)])

time: 388 us -> 368 us (0.948); the launches traced: 381 us -> 366 us
  Pallas kernels: 72.8 us -> 55.3 us
  starting transfers between devices: 95.5 us -> 99.4 us
    ppermute x18, waiting for transfers between devices: 98.3 us -> 138 us  [from_ring(): lax.ppermute(block, axis, [((d + away) % count, d) for d in range(count)])]
    all_gather x1, waiting for transfers between devices: 39.3 us -> 0.02 us  [gathered(): lax.all_gather(own_part, ('zh',) + DP).reshape(SET, 16, 2, D // 16, R)]
    pallas_call x4, Pallas kernels: 34.7 us -> 25.8 us  [run_backward(): pl.pallas_call(lambda *refs: backward_kernel(*refs, source=source, aliase...]
    pallas_call x4, Pallas kernels: 34.2 us -> 25.6 us  [run_forward(): pl.pallas_call(lambda *refs: forward_kernel(*refs, source=source, aliased...]
    ppermute x4, starting transfers between devices: 39.9 us -> 47.9 us  [hop(): return lax.ppermute(rows, 'y', [(0, 1), (1, 0), (2, 3), (3, 2)])]
  transfers between devices with their start and end apart: 33 -> 33, of which waited for: 17 -> 19; matrix products, arithmetic and copies ran while one was open for 1% -> 0% of each run, Pallas kernels for 8% -> 8%
where the time goes in v4:
time: 368 us; the launch traced here: 366 us
  waiting for transfers between devices  194 us (53%)
  starting transfers between devices  99.4 us (27%)
  Pallas kernels  55.3 us (15%)
  between operations  13.7 us (4%)
    ppermute x18, waiting for transfers between devices, from_ring(): lax.ppermute(block, axis, [((d + away) % count, d) for d in range(count)])  138 us
    ppermute x4, starting transfers between devices, hop(): return lax.ppermute(rows, 'y', [(0, 1), (1, 0), (2, 3), (3, 2)])  47.9 us
    ppermute x4, waiting for transfers between devices, hop(): return lax.ppermute(rows, 'y', [(0, 1), (1, 0), (2, 3), (3, 2)])  27.2 us
    pallas_call x4, Pallas kernels, run_backward(): pl.pallas_call(lambda *refs: backward_kernel(*refs, source=source, aliase...  25.8 us
    pallas_call x4, Pallas kernels, run_forward(): pl.pallas_call(lambda *refs: forward_kernel(*refs, source=source, aliased...  25.6 us
    ppermute x18, starting transfers between devices, from_ring(): lax.ppermute(block, axis, [((d + away) % count, d) for d in range(count)])  20.4 us
    ppermute x6, waiting for transfers between devices, summed_over_zh(): total = total + lax.ppermute(parts[k], 'zh', route).astype(jnp.float32)  16.5 us
    ppermute x6, starting transfers between devices, summed_over_zh(): total = total + lax.ppermute(parts[k], 'zh', route).astype(jnp.float32)  15.6 us
  transfers between devices with their start and end apart: 33, of which 19 were waited for; matrix products, arithmetic and copies ran while one was open for 0% of the time, Pallas kernels for 8%

profile of v4, /device:TPU:2, one launch (start us, length us, event | category | flops | bytes accessed | tf_op | source)
XLA Modules:
  0.0 366.3 jit_solution(2704329681533668362)
XLA Ops:
  8.6 3.3 collective-permute-start.2
  11.9 5.4 %collective-permute-start.1 = (bf16[2,320,256]{2,1,0:T(8,128)(2,1)S(1)}, bf16[2,320,256]{2,1,0:T(8,128)(2,1)S(1)}, u32[]{:S(2)}, u32[]{:S(2)}) collective-permute-start(bf16[2,320,256]{2,1,0:T(8,128)(2,1)S(1)} %pad_maximum_fusion.1), channel_id=1, source_target_pairs={{32,0},{48,16},{0,32},{16,48},{33,1},{49,17},{1,33},{17,49},{34,2}... | collective-permute-start | bytes 983048 | tf_op jit(solution)/shard_map/ppermute | solution.py:369
  17.3 2.7 collective-permute-start
  20.0 6.8 %collective-permute-done.2 = bf16[2,320,256]{2,1,0:T(8,128)(2,1)S(1)} collective-permute-done((bf16[2,320,256]{2,1,0:T(8,128)(2,1)S(1)}, bf16[2,320,256]{2,1,0:T(8,128)(2,1)S(1)}, u32[]{:S(2)}, u32[]{:S(2)}) %collective-permute-start.2) | collective-permute-done | bytes 327712 | tf_op jit(solution)/shard_map/ppermute | solution.py:369
  26.8 15.3 %collective-permute-done.1 = bf16[2,320,256]{2,1,0:T(8,128)(2,1)S(1)} collective-permute-done((bf16[2,320,256]{2,1,0:T(8,128)(2,1)S(1)}, bf16[2,320,256]{2,1,0:T(8,128)(2,1)S(1)}, u32[]{:S(2)}, u32[]{:S(2)}) %collective-permute-start.1) | collective-permute-done | bytes 327712 | tf_op jit(solution)/shard_map/ppermute | solution.py:369
  42.1 10.1 %collective-permute-done = bf16[2,320,256]{2,1,0:T(8,128)(2,1)S(1)} collective-permute-done((bf16[2,320,256]{2,1,0:T(8,128)(2,1)S(1)}, bf16[2,320,256]{2,1,0:T(8,128)(2,1)S(1)}, u32[]{:S(2)}, u32[]{:S(2)}) %collective-permute-start) | collective-permute-done | bytes 327712 | tf_op jit(solution)/shard_map/ppermute | solution.py:369
  54.7 29.3 %collective-permute-done.10.refs_12_.refs_14_ = bf16[3,2,320,256]{3,2,1,0:T(8,128)(2,1)S(1)} collective-permute-done((bf16[3,2,320,256]{3,2,1,0:T(8,128)(2,1)S(1)}, bf16[3,2,320,256]{3,2,1,0:T(8,128)(2,1)S(1)}, u32[]{:S(2)}, u32[]{:S(2)}) %collective-permute-start.10) | collective-permute-done | bytes 983072 | tf_op jit(solution)/shard_map/ppermute | solution.py:369
  88.1 41.2 %collective-permute-done.14.refs_18_.refs_20_ = bf16[3,2,320,256]{3,2,1,0:T(8,128)(2,1)} collective-permute-done((bf16[3,2,320,256]{3,2,1,0:T(8,128)(2,1)S(1)}, bf16[3,2,320,256]{3,2,1,0:T(8,128)(2,1)}, u32[]{:S(2)}, u32[]{:S(2)}) %collective-permute-start.14) | collective-permute-done | bytes 983072 | tf_op jit(solution)/shard_map/ppermute | solution.py:369
  132.0 29.6 %collective-permute-done.12.refs_14_.refs_16_ = bf16[3,2,320,256]{3,2,1,0:T(8,128)(2,1)} collective-permute-done((bf16[3,2,320,256]{3,2,1,0:T(8,128)(2,1)S(1)}, bf16[3,2,320,256]{3,2,1,0:T(8,128)(2,1)}, u32[]{:S(2)}, u32[]{:S(2)}) %collective-permute-start.12) | collective-permute-done | bytes 983072 | tf_op jit(solution)/shard_map/ppermute | solution.py:369
  164.6 2.8 collective-permute-done.16.refs_17_.refs_19_
  167.4 12.6 %forward_set.4 = (bf16[24,5120]{1,0:T(8,128)(2,1)S(1)}, bf16[4,24,5120]{2,1,0:T(8,128)(2,1)S(1)}, f32[4,24,256]{2,1,0:T(8,128)S(1)}, bf16[4,24,256]{2,1,0:T(8,128)(2,1)S(1)}) custom-call(s32[7]{0:T(128)S(1)} %concatenate.19.refs_0_, bf16[24,5120]{1,0:T(8,128)(2,1)S(1)} %pad.4.refs_1_, bf16[2,16,320,256]{3,2,1,0:T(8,128)(2,1)} %bitcast.31, ...), custom_call_target="tpu_custom_call" | custom-call | flops 125829120 | bytes 5242880 | tf_op jit(solution)/shard_map/forward_set/pallas_call | solution.py:180
  180.3 8.0 %collective-permute-done.18.refs_1_ = bf16[24,5120]{1,0:T(8,128)(2,1)S(1)} collective-permute-done((bf16[24,5120]{1,0:T(8,128)(2,1)S(1)}, bf16[24,5120]{1,0:T(8,128)(2,1)S(1)}, u32[]{:S(2)}, u32[]{:S(2)}) %collective-permute-start.18) | collective-permute-done | bytes 245792 | tf_op jit(solution)/shard_map/ppermute | solution.py:360
  189.7 23.4 %collective-permute-start.19 = (bf16[24,5120]{1,0:T(8,128)(2,1)S(1)}, bf16[24,5120]{1,0:T(8,128)(2,1)S(1)}, u32[]{:S(2)}, u32[]{:S(2)}) collective-permute-start(bf16[24,5120]{1,0:T(8,128)(2,1)S(1)} %get-tuple-element.43), channel_id=1, source_target_pairs={{0,64},{64,0},{128,192},{192,128},{1,65},{65,1},{129,193},{193,129... | collective-permute-start | bytes 737288 | tf_op jit(solution)/shard_map/ppermute | solution.py:360
  213.2 5.8 %collective-permute-done.19.refs_1_ = bf16[24,5120]{1,0:T(8,128)(2,1)S(1)} collective-permute-done((bf16[24,5120]{1,0:T(8,128)(2,1)S(1)}, bf16[24,5120]{1,0:T(8,128)(2,1)S(1)}, u32[]{:S(2)}, u32[]{:S(2)}) %collective-permute-start.19) | collective-permute-done | bytes 245792 | tf_op jit(solution)/shard_map/ppermute | solution.py:360
  219.0 11.7 %forward_set.7 = (bf16[24,5120]{1,0:T(8,128)(2,1)S(1)}, bf16[4,24,5120]{2,1,0:T(8,128)(2,1)S(1)}, f32[4,24,256]{2,1,0:T(8,128)S(1)}, bf16[4,24,256]{2,1,0:T(8,128)(2,1)S(1)}) custom-call(s32[7]{0:T(128)S(1)} %concatenate.22.refs_0_, bf16[24,5120]{1,0:T(8,128)(2,1)S(1)} %collective-permute-done.19.refs_1_, ...), custom_call_target="tpu_custom_call", output_to_operand_aliasing={{1}: (3, {}), {2}: (4, {}), {3}: (5, {})} | custom-call | flops 125829120 | bytes 5242880 | tf_op jit(solution)/shard_map/forward_set/pallas_call | solution.py:180
  230.7 12.3 %backward_set.4 = (bf16[24,5120]{1,0:T(8,128)(2,1)S(1)}, bf16[16,4,24,320]{3,2,1,0:T(8,128)(2,1)}) custom-call(s32[7]{0:T(128)S(1)} %concatenate.22.refs_0_, bf16[24,5120]{1,0:T(8,128)(2,1)S(1)} %get-tuple-element.47.refs_1_, bf16[4,24,5120]{2,1,0:T(8,128)(2,1)S(1)} %get-tuple-element.48.refs_2_, f32[4,24,256]{2,1,0:T(8,128)S(1)} %get-tuple-element.49.refs_3_, ...), custom_call_target="tpu_custom_call" | custom-call | flops 125829120 | bytes 5242880 | tf_op jit(solution)/shard_map/backward_set/pallas_call | solution.py:301
  243.1 7.1 %collective-permute-done.20.refs_1_ = bf16[24,5120]{1,0:T(8,128)(2,1)S(1)} collective-permute-done((bf16[24,5120]{1,0:T(8,128)(2,1)S(1)}, bf16[24,5120]{1,0:T(8,128)(2,1)S(1)}, u32[]{:S(2)}, u32[]{:S(2)}) %collective-permute-start.20) | collective-permute-done | bytes 245792 | tf_op jit(solution)/shard_map/ppermute | solution.py:360
  250.8 5.1 %all-to-all-start = ((bf16[16,4,24,320]{3,2,1,0:T(8,128)(2,1)}), bf16[16,4,24,320]{3,2,1,0:T(8,128)(2,1)S(1)}, u32[]{:S(2)}, u32[]{:S(2)}) async-start(bf16[16,4,24,320]{3,2,1,0:T(8,128)(2,1)} %get-tuple-element.58), calls=%async_computation | async-start | bytes 2359296 | tf_op jit(solution)/shard_map/all_to_all | solution.py:364
  257.4 24.3 %collective-permute-start.21 = (bf16[24,5120]{1,0:T(8,128)(2,1)S(1)}, bf16[24,5120]{1,0:T(8,128)(2,1)S(1)}, u32[]{:S(2)}, u32[]{:S(2)}) collective-permute-start(bf16[24,5120]{1,0:T(8,128)(2,1)S(1)} %get-tuple-element.55), channel_id=1, source_target_pairs={{0,64},{64,0},{128,192},{192,128},{1,65},{65,1},{129,193},{193,129... | collective-permute-start | bytes 737288 | tf_op jit(solution)/shard_map/ppermute | solution.py:360
  281.7 6.3 %collective-permute-done.21.refs_1_ = bf16[24,5120]{1,0:T(8,128)(2,1)S(1)} collective-permute-done((bf16[24,5120]{1,0:T(8,128)(2,1)S(1)}, bf16[24,5120]{1,0:T(8,128)(2,1)S(1)}, u32[]{:S(2)}, u32[]{:S(2)}) %collective-permute-start.21) | collective-permute-done | bytes 245792 | tf_op jit(solution)/shard_map/ppermute | solution.py:360
  288.0 12.1 %backward_set.7 = (bf16[24,5120]{1,0:T(8,128)(2,1)}, bf16[16,4,24,320]{3,2,1,0:T(8,128)(2,1)}) custom-call(s32[7]{0:T(128)S(1)} %concatenate.19.refs_0_, bf16[24,5120]{1,0:T(8,128)(2,1)S(1)} %collective-permute-done.21.refs_1_, bf16[4,24,5120]{2,1,0:T(8,128)(2,1)S(1)} %get-tuple-element.53.refs_2_, ...), custom_call_target="tpu_custom_call", output_to_operand_aliasing={{1}: (22, {})} | custom-call | flops 125829120 | bytes 5242880 | tf_op jit(solution)/shard_map/backward_set/pallas_call | solution.py:301
  300.2 5.8 %all-to-all-start.1 = ((bf16[16,4,24,320]{3,2,1,0:T(8,128)(2,1)}), bf16[16,4,24,320]{3,2,1,0:T(8,128)(2,1)S(1)}, u32[]{:S(2)}, u32[]{:S(2)}) async-start(bf16[16,4,24,320]{3,2,1,0:T(8,128)(2,1)} %get-tuple-element.59), calls=%async_computation.1 | async-start | bytes 2359296 | tf_op jit(solution)/shard_map/all_to_all | solution.py:364
  305.9 2.0 grad_set.3
  307.9 3.0 collective-permute-start.27
  310.9 3.0 collective-permute-start.26
  315.8 7.7 %all-to-all-done.1.refs_1_ = bf16[16,4,24,320]{3,2,1,0:T(8,128)(2,1)S(1)} async-done(((bf16[16,4,24,320]{3,2,1,0:T(8,128)(2,1)}), bf16[16,4,24,320]{3,2,1,0:T(8,128)(2,1)S(1)}, u32[]{:S(2)}, u32[]{:S(2)}) %all-to-all-start.1) | async-done | bytes 983072 | tf_op jit(solution)/shard_map/all_to_all | solution.py:364
  325.5 2.7 collective-permute-start.24
  328.2 4.9 %collective-permute-start.23 = (bf16[320,256]{1,0:T(8,128)(2,1)S(1)}, bf16[320,256]{1,0:T(8,128)(2,1)S(1)}, u32[]{:S(2)}, u32[]{:S(2)}) collective-permute-start(bf16[320,256]{1,0:T(8,128)(2,1)S(1)} %get-tuple-element.64), channel_id=1, source_target_pairs={{0,32},{16,48},{32,0},{48,16},{1,33},{17,49},{33,1},{49,17},{2,34}... | collective-permute-start | bytes 491528 | tf_op jit(solution)/shard_map/ppermute | solution.py:355
  333.3 2.1 collective-permute-done.26
  337.2 12.5 %collective-permute-done.24 = bf16[320,256]{1,0:T(8,128)(2,1)S(1)} collective-permute-done((bf16[320,256]{1,0:T(8,128)(2,1)S(1)}, bf16[320,256]{1,0:T(8,128)(2,1)S(1)}, u32[]{:S(2)}, u32[]{:S(2)}) %collective-permute-start.24) | collective-permute-done | bytes 163872 | tf_op jit(solution)/shard_map/ppermute | solution.py:355
  349.9 4.5 %collective-permute-start.28 = (bf16[320,256]{1,0:T(8,128)(2,1)S(1)}, bf16[320,256]{1,0:T(8,128)(2,1)S(1)}, u32[]{:S(2)}, u32[]{:S(2)}) collective-permute-start(bf16[320,256]{1,0:T(8,128)(2,1)S(1)} %get-tuple-element.71), channel_id=1, source_target_pairs={{0,192},{192,0},{64,128},{128,64},{1,193},{193,1},{65,129},{129,65... | collective-permute-start | bytes 491528 | tf_op jit(solution)/shard_map/ppermute | solution.py:439
  354.4 4.3 %collective-permute-done.28 = bf16[320,256]{1,0:T(8,128)(2,1)S(1)} collective-permute-done((bf16[320,256]{1,0:T(8,128)(2,1)S(1)}, bf16[320,256]{1,0:T(8,128)(2,1)S(1)}, u32[]{:S(2)}, u32[]{:S(2)}) %collective-permute-start.28) | collective-permute-done | bytes 163872 | tf_op jit(solution)/shard_map/ppermute | solution.py:439
  (76 shorter events, 24.8 us)
Async XLA Ops:
  6.5 182.5 %all-gather.5.cloned.1.call-start = ((), (), s32[]{:S(2)}) async-start(), calls=%async_computation.2 | async-start | bytes 21299200 | tf_op jit(solution)/shard_map/all_gather | solution.py:398
  8.6 18.2 %collective-permute-start.2 = (bf16[2,320,256]{2,1,0:T(8,128)(2,1)S(1)}, bf16[2,320,256]{2,1,0:T(8,128)(2,1)S(1)}, u32[]{:S(2)}, u32[]{:S(2)}) collective-permute-start(bf16[2,320,256]{2,1,0:T(8,128)(2,1)S(1)} %pad_maximum_fusion.1), channel_id=1, source_target_pairs={{48,0},{0,16},{16,32},{32,48},{49,1},{1,17},{17,33},{33,49},{50,2}... | collective-permute-start | bytes 983048 | tf_op jit(solution)/shard_map/ppermute | solution.py:369
  11.9 30.2 %collective-permute-start.1 = (bf16[2,320,256]{2,1,0:T(8,128)(2,1)S(1)}, bf16[2,320,256]{2,1,0:T(8,128)(2,1)S(1)}, u32[]{:S(2)}, u32[]{:S(2)}) collective-permute-start(bf16[2,320,256]{2,1,0:T(8,128)(2,1)S(1)} %pad_maximum_fusion.1), channel_id=1, source_target_pairs={{32,0},{48,16},{0,32},{16,48},{33,1},{49,17},{1,33},{17,49},{34,2}... | collective-permute-start | bytes 983048 | tf_op jit(solution)/shard_map/ppermute | solution.py:369
  17.3 35.0 %collective-permute-start = (bf16[2,320,256]{2,1,0:T(8,128)(2,1)S(1)}, bf16[2,320,256]{2,1,0:T(8,128)(2,1)S(1)}, u32[]{:S(2)}, u32[]{:S(2)}) collective-permute-start(bf16[2,320,256]{2,1,0:T(8,128)(2,1)S(1)} %pad_maximum_fusion.1), channel_id=1, source_target_pairs={{16,0},{32,16},{48,32},{0,48},{17,1},{33,17},{49,33},{1,49},{18,2}... | collective-permute-start | bytes 983048 | tf_op jit(solution)/shard_map/ppermute | solution.py:369
  52.4 31.6 %collective-permute-start.10 = (bf16[3,2,320,256]{3,2,1,0:T(8,128)(2,1)S(1)}, bf16[3,2,320,256]{3,2,1,0:T(8,128)(2,1)S(1)}, u32[]{:S(2)}, u32[]{:S(2)}) collective-permute-start(bf16[3,2,320,256]{3,2,1,0:T(8,128)(2,1)S(1)} %pad_maximum_fusion.refs_4_.refs_6_), channel_id=1, source_target_pairs={{8,0},{0,8},{9,1},{1,9},{10,2},{2,10},{11,3},{3,11},{12,4},{4,12},... | collective-permute-start | bytes 2949128 | tf_op jit(solution)/shard_map/ppermute | solution.py:369
  52.7 33.0 %collective-permute-start.4 = (bf16[3,2,320,256]{3,2,1,0:T(8,128)(2,1)S(1)}, bf16[3,2,320,256]{3,2,1,0:T(8,128)(2,1)S(1)}, u32[]{:S(2)}, u32[]{:S(2)}) collective-permute-start(bf16[3,2,320,256]{3,2,1,0:T(8,128)(2,1)S(1)} %pad_maximum_fusion.refs_4_.refs_6_), channel_id=1, source_target_pairs={{2,0},{4,2},{6,4},{0,6},{3,1},{5,3},{7,5},{1,7},{10,8},{12,10},{14... | collective-permute-start | bytes 2949128 | tf_op jit(solution)/shard_map/ppermute | solution.py:369
  53.2 33.0 %collective-permute-start.8 = (bf16[3,2,320,256]{3,2,1,0:T(8,128)(2,1)S(1)}, bf16[3,2,320,256]{3,2,1,0:T(8,128)(2,1)S(1)}, u32[]{:S(2)}, u32[]{:S(2)}) collective-permute-start(bf16[3,2,320,256]{3,2,1,0:T(8,128)(2,1)S(1)} %pad_maximum_fusion.refs_4_.refs_6_), channel_id=1, source_target_pairs={{6,0},{0,2},{2,4},{4,6},{7,1},{1,3},{3,5},{5,7},{14,8},{8,10},{10,... | collective-permute-start | bytes 2949128 | tf_op jit(solution)/shard_map/ppermute | solution.py:369
  54.7 31.6 %collective-permute-start.3 = (bf16[3,2,320,256]{3,2,1,0:T(8,128)(2,1)S(1)}, bf16[3,2,320,256]{3,2,1,0:T(8,128)(2,1)S(1)}, u32[]{:S(2)}, u32[]{:S(2)}) collective-permute-start(bf16[3,2,320,256]{3,2,1,0:T(8,128)(2,1)S(1)} %pad_maximum_fusion.refs_4_.refs_6_), channel_id=1, source_target_pairs={{1,0},{0,1},{3,2},{2,3},{5,4},{4,5},{7,6},{6,7},{9,8},{8,9},{11,10... | collective-permute-start | bytes 2949128 | tf_op jit(solution)/shard_map/ppermute | solution.py:369
  84.1 45.2 %collective-permute-start.14 = (bf16[3,2,320,256]{3,2,1,0:T(8,128)(2,1)S(1)}, bf16[3,2,320,256]{3,2,1,0:T(8,128)(2,1)}, u32[]{:S(2)}, u32[]{:S(2)}) collective-permute-start(bf16[3,2,320,256]{3,2,1,0:T(8,128)(2,1)S(1)} %collective-permute-done.10.refs_12_.refs_14_), channel_id=1, source_target_pairs={{6,0},{0,2},{2,4},{4,6},{7,1},{1,3},{3,5},{5,7},{14,8},{8,10},{10,... | collective-permute-start | bytes 2949128 | tf_op jit(solution)/shard_map/ppermute | solution.py:369
  85.6 45.1 %collective-permute-start.5 = (bf16[3,2,320,256]{3,2,1,0:T(8,128)(2,1)S(1)}, bf16[3,2,320,256]{3,2,1,0:T(8,128)(2,1)S(1)}, u32[]{:S(2)}, u32[]{:S(2)}) collective-permute-start(bf16[3,2,320,256]{3,2,1,0:T(8,128)(2,1)S(1)} %collective-permute-done.4.refs_6_.refs_8_), channel_id=1, source_target_pairs={{1,0},{0,1},{3,2},{2,3},{5,4},{4,5},{7,6},{6,7},{9,8},{8,9},{11,10... | collective-permute-start | bytes 2949128 | tf_op jit(solution)/shard_map/ppermute | solution.py:369
  85.7 45.8 %collective-permute-start.6 = (bf16[3,2,320,256]{3,2,1,0:T(8,128)(2,1)S(1)}, bf16[3,2,320,256]{3,2,1,0:T(8,128)(2,1)}, u32[]{:S(2)}, u32[]{:S(2)}) collective-permute-start(bf16[3,2,320,256]{3,2,1,0:T(8,128)(2,1)S(1)} %collective-permute-done.4.refs_6_.refs_8_), channel_id=1, source_target_pairs={{2,0},{4,2},{6,4},{0,6},{3,1},{5,3},{7,5},{1,7},{10,8},{12,10},{14... | collective-permute-start | bytes 2949128 | tf_op jit(solution)/shard_map/ppermute | solution.py:369
  86.2 45.3 %collective-permute-start.9 = (bf16[3,2,320,256]{3,2,1,0:T(8,128)(2,1)S(1)}, bf16[3,2,320,256]{3,2,1,0:T(8,128)(2,1)S(1)}, u32[]{:S(2)}, u32[]{:S(2)}) collective-permute-start(bf16[3,2,320,256]{3,2,1,0:T(8,128)(2,1)S(1)} %collective-permute-done.8.refs_10_.refs_12_), channel_id=1, source_target_pairs={{1,0},{0,1},{3,2},{2,3},{5,4},{4,5},{7,6},{6,7},{9,8},{8,9},{11,10... | collective-permute-start | bytes 2949128 | tf_op jit(solution)/shard_map/ppermute | solution.py:369
  86.3 75.2 %collective-permute-start.12 = (bf16[3,2,320,256]{3,2,1,0:T(8,128)(2,1)S(1)}, bf16[3,2,320,256]{3,2,1,0:T(8,128)(2,1)}, u32[]{:S(2)}, u32[]{:S(2)}) collective-permute-start(bf16[3,2,320,256]{3,2,1,0:T(8,128)(2,1)S(1)} %collective-permute-done.10.refs_12_.refs_14_), channel_id=1, source_target_pairs={{2,0},{4,2},{6,4},{0,6},{3,1},{5,3},{7,5},{1,7},{10,8},{12,10},{14... | collective-permute-start | bytes 2949128 | tf_op jit(solution)/shard_map/ppermute | solution.py:369
  129.3 32.4 %collective-permute-start.15 = (bf16[3,2,320,256]{3,2,1,0:T(8,128)(2,1)}, bf16[3,2,320,256]{3,2,1,0:T(8,128)(2,1)}, u32[]{:S(2)}, u32[]{:S(2)}) collective-permute-start(bf16[3,2,320,256]{3,2,1,0:T(8,128)(2,1)} %collective-permute-done.14.refs_18_.refs_20_), channel_id=1, source_target_pairs={{6,0},{0,2},{2,4},{4,6},{7,1},{1,3},{3,5},{5,7},{14,8},{8,10},{10,... | collective-permute-start | bytes 2949128 | tf_op jit(solution)/shard_map/ppermute | solution.py:369
  130.8 31.9 %collective-permute-start.11 = (bf16[3,2,320,256]{3,2,1,0:T(8,128)(2,1)S(1)}, bf16[3,2,320,256]{3,2,1,0:T(8,128)(2,1)}, u32[]{:S(2)}, u32[]{:S(2)}) collective-permute-start(bf16[3,2,320,256]{3,2,1,0:T(8,128)(2,1)S(1)} %collective-permute-done.10.refs_12_.refs_14_), channel_id=1, source_target_pairs={{1,0},{0,1},{3,2},{2,3},{5,4},{4,5},{7,6},{6,7},{9,8},{8,9},{11,10... | collective-permute-start | bytes 2949128 | tf_op jit(solution)/shard_map/ppermute | solution.py:369
  131.5 33.1 %collective-permute-start.17 = (bf16[3,2,320,256]{3,2,1,0:T(8,128)(2,1)}, bf16[3,2,320,256]{3,2,1,0:T(8,128)(2,1)}, u32[]{:S(2)}, u32[]{:S(2)}) collective-permute-start(bf16[3,2,320,256]{3,2,1,0:T(8,128)(2,1)} %collective-permute-done.14.refs_18_.refs_20_), channel_id=1, source_target_pairs={{1,0},{0,1},{3,2},{2,3},{5,4},{4,5},{7,6},{6,7},{9,8},{8,9},{11,10... | collective-permute-start | bytes 2949128 | tf_op jit(solution)/shard_map/ppermute | solution.py:369
  131.5 31.2 %collective-permute-start.7 = (bf16[3,2,320,256]{3,2,1,0:T(8,128)(2,1)}, bf16[3,2,320,256]{3,2,1,0:T(8,128)(2,1)}, u32[]{:S(2)}, u32[]{:S(2)}) collective-permute-start(bf16[3,2,320,256]{3,2,1,0:T(8,128)(2,1)} %collective-permute-done.6.refs_8_.refs_10_), channel_id=1, source_target_pairs={{1,0},{0,1},{3,2},{2,3},{5,4},{4,5},{7,6},{6,7},{9,8},{8,9},{11,10... | collective-permute-start | bytes 2949128 | tf_op jit(solution)/shard_map/ppermute | solution.py:369
  161.7 5.7 %collective-permute-start.16 = (bf16[3,2,320,256]{3,2,1,0:T(8,128)(2,1)}, bf16[3,2,320,256]{3,2,1,0:T(8,128)(2,1)}, u32[]{:S(2)}, u32[]{:S(2)}) collective-permute-start(bf16[3,2,320,256]{3,2,1,0:T(8,128)(2,1)} %collective-permute-done.15.refs_16_.refs_18_), channel_id=1, source_target_pairs={{1,0},{0,1},{3,2},{2,3},{5,4},{4,5},{7,6},{6,7},{9,8},{8,9},{11,10... | collective-permute-start | bytes 2949128 | tf_op jit(solution)/shard_map/ppermute | solution.py:369
  180.0 8.3 %collective-permute-start.18 = (bf16[24,5120]{1,0:T(8,128)(2,1)S(1)}, bf16[24,5120]{1,0:T(8,128)(2,1)S(1)}, u32[]{:S(2)}, u32[]{:S(2)}) collective-permute-start(bf16[24,5120]{1,0:T(8,128)(2,1)S(1)} %get-tuple-element.38), channel_id=1, source_target_pairs={{0,64},{64,0},{128,192},{192,128},{1,65},{65,1},{129,193},{193,129... | collective-permute-start | bytes 737288 | tf_op jit(solution)/shard_map/ppermute | solution.py:360
  189.7 29.3 %collective-permute-start.19 = (bf16[24,5120]{1,0:T(8,128)(2,1)S(1)}, bf16[24,5120]{1,0:T(8,128)(2,1)S(1)}, u32[]{:S(2)}, u32[]{:S(2)}) collective-permute-start(bf16[24,5120]{1,0:T(8,128)(2,1)S(1)} %get-tuple-element.43), channel_id=1, source_target_pairs={{0,64},{64,0},{128,192},{192,128},{1,65},{65,1},{129,193},{193,129... | collective-permute-start | bytes 737288 | tf_op jit(solution)/shard_map/ppermute | solution.py:360
  243.0 7.2 %collective-permute-start.20 = (bf16[24,5120]{1,0:T(8,128)(2,1)S(1)}, bf16[24,5120]{1,0:T(8,128)(2,1)S(1)}, u32[]{:S(2)}, u32[]{:S(2)}) collective-permute-start(bf16[24,5120]{1,0:T(8,128)(2,1)S(1)} %get-tuple-element.50), channel_id=1, source_target_pairs={{0,64},{64,0},{128,192},{192,128},{1,65},{65,1},{129,193},{193,129... | collective-permute-start | bytes 737288 | tf_op jit(solution)/shard_map/ppermute | solution.py:360
  250.8 49.3 %all-to-all-start = ((bf16[16,4,24,320]{3,2,1,0:T(8,128)(2,1)}), bf16[16,4,24,320]{3,2,1,0:T(8,128)(2,1)S(1)}, u32[]{:S(2)}, u32[]{:S(2)}) async-start(bf16[16,4,24,320]{3,2,1,0:T(8,128)(2,1)} %get-tuple-element.58), calls=%async_computation | async-start | bytes 2359296 | tf_op jit(solution)/shard_map/all_to_all | solution.py:364
  256.0 50.0 %all-gather.7.cloned.1.call-start = ((), (), s32[]{:S(2)}) async-start(), calls=%async_computation.3 | async-start | bytes 1671168 | tf_op jit(solution)/shard_map/all_gather | solution.py:424
  257.4 30.6 %collective-permute-start.21 = (bf16[24,5120]{1,0:T(8,128)(2,1)S(1)}, bf16[24,5120]{1,0:T(8,128)(2,1)S(1)}, u32[]{:S(2)}, u32[]{:S(2)}) collective-permute-start(bf16[24,5120]{1,0:T(8,128)(2,1)S(1)} %get-tuple-element.55), channel_id=1, source_target_pairs={{0,64},{64,0},{128,192},{192,128},{1,65},{65,1},{129,193},{193,129... | collective-permute-start | bytes 737288 | tf_op jit(solution)/shard_map/ppermute | solution.py:360
  300.2 23.4 %all-to-all-start.1 = ((bf16[16,4,24,320]{3,2,1,0:T(8,128)(2,1)}), bf16[16,4,24,320]{3,2,1,0:T(8,128)(2,1)S(1)}, u32[]{:S(2)}, u32[]{:S(2)}) async-start(bf16[16,4,24,320]{3,2,1,0:T(8,128)(2,1)} %get-tuple-element.59), calls=%async_computation.1 | async-start | bytes 2359296 | tf_op jit(solution)/shard_map/all_to_all | solution.py:364
  307.9 25.2 %collective-permute-start.27 = (bf16[320,256]{1,0:T(8,128)(2,1)S(1)}, bf16[320,256]{1,0:T(8,128)(2,1)S(1)}, u32[]{:S(2)}, u32[]{:S(2)}) collective-permute-start(bf16[320,256]{1,0:T(8,128)(2,1)S(1)} %get-tuple-element.70), channel_id=1, source_target_pairs={{0,48},{16,0},{32,16},{48,32},{1,49},{17,1},{33,17},{49,33},{2,50}... | collective-permute-start | bytes 491528 | tf_op jit(solution)/shard_map/ppermute | solution.py:355
  310.9 24.5 %collective-permute-start.26 = (bf16[320,256]{1,0:T(8,128)(2,1)S(1)}, bf16[320,256]{1,0:T(8,128)(2,1)S(1)}, u32[]{:S(2)}, u32[]{:S(2)}) collective-permute-start(bf16[320,256]{1,0:T(8,128)(2,1)S(1)} %get-tuple-element.69), channel_id=1, source_target_pairs={{0,32},{16,48},{32,0},{48,16},{1,33},{17,49},{33,1},{49,17},{2,34}... | collective-permute-start | bytes 491528 | tf_op jit(solution)/shard_map/ppermute | solution.py:355
  314.0 23.3 %collective-permute-start.25 = (bf16[320,256]{1,0:T(8,128)(2,1)S(1)}, bf16[320,256]{1,0:T(8,128)(2,1)S(1)}, u32[]{:S(2)}, u32[]{:S(2)}) collective-permute-start(bf16[320,256]{1,0:T(8,128)(2,1)S(1)} %get-tuple-element.68), channel_id=1, source_target_pairs={{0,16},{16,32},{32,48},{48,0},{1,17},{17,33},{33,49},{49,1},{2,18}... | collective-permute-start | bytes 491528 | tf_op jit(solution)/shard_map/ppermute | solution.py:355
  325.5 24.2 %collective-permute-start.24 = (bf16[320,256]{1,0:T(8,128)(2,1)S(1)}, bf16[320,256]{1,0:T(8,128)(2,1)S(1)}, u32[]{:S(2)}, u32[]{:S(2)}) collective-permute-start(bf16[320,256]{1,0:T(8,128)(2,1)S(1)} %get-tuple-element.65), channel_id=1, source_target_pairs={{0,48},{16,0},{32,16},{48,32},{1,49},{17,1},{33,17},{49,33},{2,50}... | collective-permute-start | bytes 491528 | tf_op jit(solution)/shard_map/ppermute | solution.py:355
  328.2 21.5 %collective-permute-start.23 = (bf16[320,256]{1,0:T(8,128)(2,1)S(1)}, bf16[320,256]{1,0:T(8,128)(2,1)S(1)}, u32[]{:S(2)}, u32[]{:S(2)}) collective-permute-start(bf16[320,256]{1,0:T(8,128)(2,1)S(1)} %get-tuple-element.64), channel_id=1, source_target_pairs={{0,32},{16,48},{32,0},{48,16},{1,33},{17,49},{33,1},{49,17},{2,34}... | collective-permute-start | bytes 491528 | tf_op jit(solution)/shard_map/ppermute | solution.py:355
  333.1 16.6 %collective-permute-start.22 = (bf16[320,256]{1,0:T(8,128)(2,1)S(1)}, bf16[320,256]{1,0:T(8,128)(2,1)S(1)}, u32[]{:S(2)}, u32[]{:S(2)}) collective-permute-start(bf16[320,256]{1,0:T(8,128)(2,1)S(1)} %get-tuple-element.63), channel_id=1, source_target_pairs={{0,16},{16,32},{32,48},{48,0},{1,17},{17,33},{33,49},{49,1},{2,18}... | collective-permute-start | bytes 491528 | tf_op jit(solution)/shard_map/ppermute | solution.py:355
  349.9 8.8 %collective-permute-start.28 = (bf16[320,256]{1,0:T(8,128)(2,1)S(1)}, bf16[320,256]{1,0:T(8,128)(2,1)S(1)}, u32[]{:S(2)}, u32[]{:S(2)}) collective-permute-start(bf16[320,256]{1,0:T(8,128)(2,1)S(1)} %get-tuple-element.71), channel_id=1, source_target_pairs={{0,192},{192,0},{64,128},{128,64},{1,193},{193,1},{65,129},{129,65... | collective-permute-start | bytes 491528 | tf_op jit(solution)/shard_map/ppermute | solution.py:439
  (9 other events, 633.6 us)
Sparse Core Ops, SparseCore 0:
  10.1 157.2 all-gather.4
  258.7 46.6 all-gather.6

commit v5 on v4

--- a/solution.py
+++ b/solution.py
@@ -19,41 +19,19 @@
 SM = pl.BlockSpec(memory_space=pltpu.SMEM)
 
 
-class Gathered:
-    count = 1
+class Scattered:
+    count = 20
 
     def __init__(self, refs, flags, wbuf, sem):
-        self.w, self.flags, self.wbuf, self.sem = refs[0], flags, wbuf, sem
-
-    def copy(self, layer, slot, which):
-        held = jnp.where(self.flags[1] == 1, SET - 1 - layer, layer)
-        return pltpu.make_async_copy(
-            self.w.at[held, :, which], self.wbuf.at[slot, :, which], self.sem.at[slot, which]
-        )
-
-    def first(self, layer, order):
-        self.order = order
-        self.begin(layer, 0)
-
-    def begin(self, layer, slot):
-        for which in self.order:
-            self.copy(layer, slot, which).start()
-
-    def arrive(self, layer, slot, which):
-        self.copy(layer, slot, which).wait()
-
-
-class Scattered:
-    count = 18
-
-    def __init__(self, refs, flags, wbuf, sem):
-        self.own, self.parts = refs[:2], refs[2:]
+        self.own, self.halves, self.parts = refs[:2], refs[2:4], refs[4:]
         self.flags, self.wbuf, self.sem = flags, wbuf, sem
 
     def fetch(self, layer, slot):
         flags = self.flags
         held = jnp.where(flags[1] == 1, SET - 1 - layer, layer)
-        away = lax.rem(held + SET - flags[3], SET)
+        zh = flags[3]
+        away = lax.rem(held + SET - zh, SET)
+        mirrored = held == SET - 1 - zh
 
         @pl.when(away == 0)
         def _():
@@ -62,15 +40,27 @@
                     self.own[which].at[flags[2]], self.wbuf.at[slot, :, which], self.sem.at[slot, 0]
                 ).start()
 
-        @pl.when(away > 0)
+        @pl.when(mirrored)
         def _():
+            for n in range(2):
+                half = lax.rem(flags[6] + n, 2)
+                for which in range(2):
+                    pltpu.make_async_copy(
+                        self.halves[n].at[which],
+                        self.wbuf.at[slot, pl.ds(half * 8, 8), which],
+                        self.sem.at[slot, 0],
+                    ).start()
+
+        @pl.when((away > 0) & jnp.logical_not(mirrored))
+        def _():
+            entry = jnp.where(away == 2, 1, 0)
             for n in range(16):
                 zl_off, x_off, core_off = n // 8, (n // 2) % 4, n % 2
                 zl = lax.rem(flags[4] + zl_off, 2)
                 x = lax.rem(flags[5] + x_off, 4)
                 core = lax.rem(flags[6] + core_off, 2)
                 pltpu.make_async_copy(
-                    self.parts[n].at[away - 1],
+                    self.parts[n].at[entry],
                     self.wbuf.at[slot, zl * 8 + x * 2 + core],
                     self.sem.at[slot, 0],
                 ).start()
@@ -168,7 +158,7 @@
 
 
 def run_forward(flags, rows, weights, held=None):
-    source = Gathered if len(weights) == 1 else Scattered
+    source = Scattered
     first = 2 + source.count
     outs = (
         jax.ShapeDtypeStruct((ROWS, D), jnp.bfloat16),
@@ -292,7 +282,7 @@
 
 
 def run_backward(flags, g_rows, weights, h_held, pre_held, held=None, from_final=False, last=False):
-    source = Gathered if len(weights) == 1 else Scattered
+    source = Scattered
     outs = (
         jax.ShapeDtypeStruct((ROWS, D), jnp.bfloat16),
         jax.ShapeDtypeStruct((16, SET, ROWS, D // 16), jnp.bfloat16),
@@ -369,10 +359,21 @@
     return lax.ppermute(block, axis, [((d + away) % count, d) for d in range(count)])
 
 
-def passed_round(own_part):
-    near = jnp.stack([from_ring(own_part, "zh", away) for away in (1, 2, 3)])
+def across_y(block):
+    return lax.ppermute(block, "y", [(0, 3), (3, 0), (1, 2), (2, 1)])
+
+
+def over_z(chunk_now):
+    beside = lax.ppermute(chunk_now, "zh", [(0, 1), (1, 0), (2, 3), (3, 2)])
+    return jnp.stack([beside, from_ring(chunk_now, "zh", 2)])
+
+
+def over_x_first(near):
     far = from_ring(near, "zl", 1)
-    near_up, near_down = from_ring(near, "x", 1), from_ring(near, "x", -1)
+    return near, from_ring(near, "x", 1), from_ring(near, "x", -1), far
+
+
+def over_x_rest(near, near_up, near_down, far):
     near_across = from_ring(near_up, "x", 1)
     far_up, far_down = from_ring(far, "x", 1), from_ring(far, "x", -1)
     far_across = from_ring(far_down, "x", -1)
@@ -394,22 +395,36 @@
         ]
         return jnp.stack(parts)
 
-    def gathered(own_part):
-        return lax.all_gather(own_part, ("zh",) + DP).reshape(SET, 16, 2, D // 16, R)
+    def own_half(layer_slot):
+        core = lax.axis_index("core")
+        parts = [
+            lax.dynamic_slice(w, (0, layer_slot, core * (D // 2), 0), (1, 1, D // 2, R))[0, 0]
+            for w in (w_in, w_out)
+        ]
+        return jnp.stack(parts).reshape(2, 8, D // 16, R)
 
     first_slot = jnp.where(low_half, 0, 1)
-    w_b = (gathered(own(1 - first_slot)),)
-    w_a = tuple(w[0].reshape(2, 16, D // 16, R) for w in (w_in, w_out)) + passed_round(
-        own(first_slot)
-    )
-    place_flags = jnp.stack([first_slot, zh] + [lax.axis_index(name) for name in DP])
-
-    def flag(active, reverse):
-        both = jnp.stack([active.astype(jnp.int32), reverse.astype(jnp.int32)])
-        return jnp.concatenate([both, place_flags.astype(jnp.int32)])
-
-    p_a, p_b = flag(stage_p, ~low_half), flag(stage_p, low_half)
-    q_a, q_b = flag(~stage_p, ~low_half), flag(~stage_p, low_half)
+    own_layers = tuple(w[0].reshape(2, 16, D // 16, R) for w in (w_in, w_out))
+    half_a = across_y(own_half(first_slot))
+    near_a = over_z(own(first_slot))
+    chunk_b, near_a = lax.optimization_barrier((own(1 - first_slot), near_a))
+    step_a = over_x_first(near_a)
+    near_b = over_z(chunk_b)
+    near_b, step_a = lax.optimization_barrier((near_b, step_a))
+    rest_a = over_x_rest(*step_a)
+    half_b, half_a = lax.optimization_barrier((own_half(1 - first_slot), half_a))
+    half_b = across_y(half_b)
+    w_a = own_layers + (half_a, from_ring(half_a, "core", 1)) + rest_a
+    rest_b = over_x_rest(*over_x_first(near_b))
+    w_b = own_layers + (half_b, from_ring(half_b, "core", 1)) + rest_b
+
+    def flag(active, slot_now):
+        reverse = slot_now == 1
+        here = [lax.axis_index(name) for name in ("zh",) + DP]
+        return jnp.stack([v.astype(jnp.int32) for v in [active, reverse, slot_now] + here])
+
+    p_a, p_b = flag(stage_p, first_slot), flag(stage_p, 1 - first_slot)
+    q_a, q_b = flag(~stage_p, first_slot), flag(~stage_p, 1 - first_slot)
 
     mine = jnp.where(low_half, inputs_down, inputs_up).reshape(-1, D)
     mine = lax.dynamic_slice(mine, (zh * REAL, 0), (REAL, D))
@@ -436,7 +451,7 @@
     sum_a = summed_over_zh(place, far_a, act_all, 0)
     kept = jnp.where(low_half, sum_a, sum_b)
     other = jnp.where(low_half, sum_b, sum_a)
-    received = lax.ppermute(other, "y", [(0, 3), (3, 0), (1, 2), (2, 1)])
+    received = across_y(other)
     return (kept.astype(jnp.float32) + received.astype(jnp.float32))[None]
 
 

time: 368 us -> 396 us (1.076)
  starting transfers between devices: 99.4 us -> 116 us
  local copies, waits for them, and re-layouts: 1.66 us -> 7.3 us
    ppermute x18 -> x34, waiting for transfers between devices: 138 us -> 97.7 us  [from_ring(): lax.ppermute(block, axis, [((d + away) % count, d) for d in range(count)])]
    ppermute x1 -> x5, waiting for transfers between devices: 4.29 us -> 39.2 us  [the longest x2 32.5 us: over_z(): beside = lax.ppermute(chunk_now, 'zh', [(0, 1), (1, 0), (2, 3), (3, 2)])]
    ppermute x18 -> x34, starting transfers between devices: 20.4 us -> 30.1 us  [from_ring(): lax.ppermute(block, axis, [((d + away) % count, d) for d in range(count)])]
    ppermute x4, starting transfers between devices: 47.9 us -> 56.5 us  [hop(): return lax.ppermute(rows, 'y', [(0, 1), (1, 0), (2, 3), (3, 2)])]
    ppermute x6, starting transfers between devices: 15.6 us -> 11.1 us  [summed_over_zh(): total = total + lax.ppermute(parts[k], 'zh', route).astype(jnp.float32)]
  transfers between devices with their start and end apart: 33 -> 52, of which waited for: 19 -> 23; matrix products, arithmetic and copies ran while one was open for 0% -> 1% of each run, Pallas kernels for 8% -> 8%
where the time goes in v5:
time: 396 us; the launch traced here: 392 us
  waiting for transfers between devices  193 us (49%)
  starting transfers between devices  116 us (29%)
  Pallas kernels  56.6 us (14%)
  between operations  14.1 us (4%)
  local copies, waits for them, and re-layouts  7.3 us (2%)
  other arithmetic  4.74 us (1%)
    ppermute x34, waiting for transfers between devices, from_ring(): lax.ppermute(block, axis, [((d + away) % count, d) for d in range(count)])  97.7 us
    ppermute x4, starting transfers between devices, hop(): return lax.ppermute(rows, 'y', [(0, 1), (1, 0), (2, 3), (3, 2)])  56.5 us
    ppermute x2, waiting for transfers between devices, over_z(): beside = lax.ppermute(chunk_now, 'zh', [(0, 1), (1, 0), (2, 3), (3, 2)])  32.5 us
    ppermute x34, starting transfers between devices, from_ring(): lax.ppermute(block, axis, [((d + away) % count, d) for d in range(count)])  30.1 us
    ppermute x4, waiting for transfers between devices, hop(): return lax.ppermute(rows, 'y', [(0, 1), (1, 0), (2, 3), (3, 2)])  27.6 us
    pallas_call x4, Pallas kernels, run_backward(): pl.pallas_call(lambda *refs: backward_kernel(*refs, source=source, aliase...  26.7 us
    pallas_call x4, Pallas kernels, run_forward(): pl.pallas_call(lambda *refs: forward_kernel(*refs, source=source, aliased...  25.9 us
    ppermute x6, waiting for transfers between devices, summed_over_zh(): total = total + lax.ppermute(parts[k], 'zh', route).astype(jnp.float32)  17.5 us
  transfers between devices with their start and end apart: 52, of which 23 were waited for; matrix products, arithmetic and copies ran while one was open for 1% of the time, Pallas kernels for 8%

profile of v5, /device:TPU:2, one launch (start us, length us, event | category | flops | bytes accessed | tf_op | source)
XLA Modules:
  0.0 391.8 jit_solution(6475749822384031681)
XLA Ops:
  6.5 3.9 constant_dynamic-slice_fusion
  12.1 3.0 collective-permute-start
  16.4 7.3 %collective-permute-start.3 = (bf16[2,320,256]{2,1,0:T(8,128)(2,1)S(1)}, bf16[2,320,256]{2,1,0:T(8,128)(2,1)S(1)}, u32[]{:S(2)}, u32[]{:S(2)}) collective-permute-start(bf16[2,320,256]{2,1,0:T(8,128)(2,1)S(1)} %pad_maximum_fusion.5), channel_id=1, source_target_pairs={{32,0},{48,16},{0,32},{16,48},{33,1},{49,17},{1,33},{17,49},{34,2}... | collective-permute-start | bytes 983048 | tf_op jit(solution)/shard_map/ppermute | solution.py:359
  25.2 13.1 %collective-permute-done.3 = bf16[2,320,256]{2,1,0:T(8,128)(2,1)S(1)} collective-permute-done((bf16[2,320,256]{2,1,0:T(8,128)(2,1)S(1)}, bf16[2,320,256]{2,1,0:T(8,128)(2,1)S(1)}, u32[]{:S(2)}, u32[]{:S(2)}) %collective-permute-start.3) | collective-permute-done | bytes 327712 | tf_op jit(solution)/shard_map/ppermute | solution.py:359
  38.2 14.5 %collective-permute-done.2 = bf16[2,320,256]{2,1,0:T(8,128)(2,1)S(1)} collective-permute-done((bf16[2,320,256]{2,1,0:T(8,128)(2,1)S(1)}, bf16[2,320,256]{2,1,0:T(8,128)(2,1)S(1)}, u32[]{:S(2)}, u32[]{:S(2)}) %collective-permute-start.2) | collective-permute-done | bytes 327712 | tf_op jit(solution)/shard_map/ppermute | solution.py:367
  57.2 14.8 %collective-permute-done.5 = bf16[2,320,256]{2,1,0:T(8,128)(2,1)S(1)} collective-permute-done((bf16[2,320,256]{2,1,0:T(8,128)(2,1)S(1)}, bf16[2,320,256]{2,1,0:T(8,128)(2,1)S(1)}, u32[]{:S(2)}, u32[]{:S(2)}) %collective-permute-start.5) | collective-permute-done | bytes 327712 | tf_op jit(solution)/shard_map/ppermute | solution.py:359
  72.0 18.1 %collective-permute-done.4 = bf16[2,320,256]{2,1,0:T(8,128)(2,1)S(1)} collective-permute-done((bf16[2,320,256]{2,1,0:T(8,128)(2,1)S(1)}, bf16[2,320,256]{2,1,0:T(8,128)(2,1)S(1)}, u32[]{:S(2)}, u32[]{:S(2)}) %collective-permute-start.4) | collective-permute-done | bytes 327712 | tf_op jit(solution)/shard_map/ppermute | solution.py:367
  95.5 12.9 %collective-permute-done.11.refs_10_.refs_12_ = bf16[2,2,320,256]{3,2,1,0:T(8,128)(2,1)S(1)} collective-permute-done((bf16[2,2,320,256]{3,2,1,0:T(8,128)(2,1)S(1)}, bf16[2,2,320,256]{3,2,1,0:T(8,128)(2,1)S(1)}, u32[]{:S(2)}, u32[]{:S(2)}) %collective-permute-start.11) | collective-permute-done | bytes 655392 | tf_op jit(solution)/shard_map/ppermute | solution.py:359
  109.9 12.6 %collective-permute-done.15.refs_16_.refs_18_ = bf16[2,2,320,256]{3,2,1,0:T(8,128)(2,1)S(1)} collective-permute-done((bf16[2,2,320,256]{3,2,1,0:T(8,128)(2,1)S(1)}, bf16[2,2,320,256]{3,2,1,0:T(8,128)(2,1)S(1)}, u32[]{:S(2)}, u32[]{:S(2)}) %collective-permute-start.15) | collective-permute-done | bytes 655392 | tf_op jit(solution)/shard_map/ppermute | solution.py:359
  123.9 2.5 collective-permute-start.31
  126.5 9.2 %collective-permute-done.25.refs_8_.refs_10_ = bf16[2,2,320,256]{3,2,1,0:T(8,128)(2,1)S(1)} collective-permute-done((bf16[2,2,320,256]{3,2,1,0:T(8,128)(2,1)S(1)}, bf16[2,2,320,256]{3,2,1,0:T(8,128)(2,1)S(1)}, u32[]{:S(2)}, u32[]{:S(2)}) %collective-permute-start.25) | collective-permute-done | bytes 655392 | tf_op jit(solution)/shard_map/ppermute | solution.py:359
  142.9 13.0 %collective-permute-done.18.refs_18_.refs_20_ = bf16[2,2,320,256]{3,2,1,0:T(8,128)(2,1)S(1)} collective-permute-done((bf16[2,2,320,256]{3,2,1,0:T(8,128)(2,1)S(1)}, bf16[2,2,320,256]{3,2,1,0:T(8,128)(2,1)S(1)}, u32[]{:S(2)}, u32[]{:S(2)}) %collective-permute-start.18) | collective-permute-done | bytes 655392 | tf_op jit(solution)/shard_map/ppermute | solution.py:359
  155.9 3.0 collective-permute-start.27
  159.7 13.0 %collective-permute-done.27.refs_10_.refs_12_ = bf16[2,2,320,256]{3,2,1,0:T(8,128)(2,1)} collective-permute-done((bf16[2,2,320,256]{3,2,1,0:T(8,128)(2,1)S(1)}, bf16[2,2,320,256]{3,2,1,0:T(8,128)(2,1)}, u32[]{:S(2)}, u32[]{:S(2)}) %collective-permute-start.27) | collective-permute-done | bytes 655392 | tf_op jit(solution)/shard_map/ppermute | solution.py:359
  179.7 12.3 %forward_set.4 = (bf16[24,5120]{1,0:T(8,128)(2,1)S(1)}, bf16[4,24,5120]{2,1,0:T(8,128)(2,1)}, f32[4,24,256]{2,1,0:T(8,128)S(1)}, bf16[4,24,256]{2,1,0:T(8,128)(2,1)S(1)}) custom-call(s32[7]{0:T(128)S(1)} %stack.116.refs_0_, bf16[24,5120]{1,0:T(8,128)(2,1)S(1)} %pad.4.refs_1_, bf16[2,16,320,256]{3,2,1,0:T(8,128)(2,1)} %bitcast.32, ...), custom_call_target="tpu_custom_call" | custom-call | flops 125829120 | bytes 5242880 | tf_op jit(solution)/shard_map/forward_set/pallas_call | solution.py:170
  192.1 9.2 %collective-permute-start.21 = (bf16[24,5120]{1,0:T(8,128)(2,1)S(1)}, bf16[24,5120]{1,0:T(8,128)(2,1)S(1)}, u32[]{:S(2)}, u32[]{:S(2)}) collective-permute-start(bf16[24,5120]{1,0:T(8,128)(2,1)S(1)} %get-tuple-element.54), channel_id=1, source_target_pairs={{0,64},{64,0},{128,192},{192,128},{1,65},{65,1},{129,193},{193,129... | collective-permute-start | bytes 737288 | tf_op jit(solution)/shard_map/ppermute | solution.py:350
  202.0 7.1 %collective-permute-done.21.refs_1_ = bf16[24,5120]{1,0:T(8,128)(2,1)S(1)} collective-permute-done((bf16[24,5120]{1,0:T(8,128)(2,1)S(1)}, bf16[24,5120]{1,0:T(8,128)(2,1)S(1)}, u32[]{:S(2)}, u32[]{:S(2)}) %collective-permute-start.21) | collective-permute-done | bytes 245792 | tf_op jit(solution)/shard_map/ppermute | solution.py:350
  212.2 22.2 %collective-permute-start.39 = (bf16[24,5120]{1,0:T(8,128)(2,1)S(1)}, bf16[24,5120]{1,0:T(8,128)(2,1)S(1)}, u32[]{:S(2)}, u32[]{:S(2)}) collective-permute-start(bf16[24,5120]{1,0:T(8,128)(2,1)S(1)} %get-tuple-element.61), channel_id=1, source_target_pairs={{0,64},{64,0},{128,192},{192,128},{1,65},{65,1},{129,193},{193,129... | collective-permute-start | bytes 737288 | tf_op jit(solution)/shard_map/ppermute | solution.py:350
  234.5 6.5 %collective-permute-done.39.refs_1_ = bf16[24,5120]{1,0:T(8,128)(2,1)S(1)} collective-permute-done((bf16[24,5120]{1,0:T(8,128)(2,1)S(1)}, bf16[24,5120]{1,0:T(8,128)(2,1)S(1)}, u32[]{:S(2)}, u32[]{:S(2)}) %collective-permute-start.39) | collective-permute-done | bytes 245792 | tf_op jit(solution)/shard_map/ppermute | solution.py:350
  241.0 12.3 %forward_set.7 = (bf16[24,5120]{1,0:T(8,128)(2,1)S(1)}, bf16[4,24,5120]{2,1,0:T(8,128)(2,1)}, f32[4,24,256]{2,1,0:T(8,128)S(1)}, bf16[4,24,256]{2,1,0:T(8,128)(2,1)S(1)}) custom-call(s32[7]{0:T(128)S(1)} %stack.124.refs_0_, bf16[24,5120]{1,0:T(8,128)(2,1)S(1)} %collective-permute-done.39.refs_1_, ...), custom_call_target="tpu_custom_call", output_to_operand_aliasing={{1}: (22, {}), {2}: (23, {}), {3}: (24, {})} | custom-call | flops 125829120 | bytes 5242880 | tf_op jit(solution)/shard_map/forward_set/pallas_call | solution.py:170
  253.3 13.0 %backward_set.4 = (bf16[24,5120]{1,0:T(8,128)(2,1)S(1)}, bf16[16,4,24,320]{3,2,1,0:T(8,128)(2,1)}) custom-call(s32[7]{0:T(128)S(1)} %stack.124.refs_0_, bf16[24,5120]{1,0:T(8,128)(2,1)S(1)} %get-tuple-element.65.refs_1_, bf16[4,24,5120]{2,1,0:T(8,128)(2,1)} %get-tuple-element.66.refs_2_, f32[4,24,256]{2,1,0:T(8,128)S(1)} %get-tuple-element.67.refs_3_, ...), custom_call_target="tpu_custom_call" | custom-call | flops 125829120 | bytes 5242880 | tf_op jit(solution)/shard_map/backward_set/pallas_call | solution.py:291
  266.5 7.8 %collective-permute-done.40.refs_1_ = bf16[24,5120]{1,0:T(8,128)(2,1)S(1)} collective-permute-done((bf16[24,5120]{1,0:T(8,128)(2,1)S(1)}, bf16[24,5120]{1,0:T(8,128)(2,1)S(1)}, u32[]{:S(2)}, u32[]{:S(2)}) %collective-permute-start.40) | collective-permute-done | bytes 245792 | tf_op jit(solution)/shard_map/ppermute | solution.py:350
  274.9 7.1 %all-to-all-start = ((bf16[16,4,24,320]{3,2,1,0:T(8,128)(2,1)}), bf16[16,4,24,320]{3,2,1,0:T(8,128)(2,1)S(1)}, u32[]{:S(2)}, u32[]{:S(2)}) async-start(bf16[16,4,24,320]{3,2,1,0:T(8,128)(2,1)} %get-tuple-element.76), calls=%async_computation | async-start | bytes 2359296 | tf_op jit(solution)/shard_map/all_to_all | solution.py:354
  283.6 25.0 %collective-permute-start.41 = (bf16[24,5120]{1,0:T(8,128)(2,1)S(1)}, bf16[24,5120]{1,0:T(8,128)(2,1)S(1)}, u32[]{:S(2)}, u32[]{:S(2)}) collective-permute-start(bf16[24,5120]{1,0:T(8,128)(2,1)S(1)} %get-tuple-element.73), channel_id=1, source_target_pairs={{0,64},{64,0},{128,192},{192,128},{1,65},{65,1},{129,193},{193,129... | collective-permute-start | bytes 737288 | tf_op jit(solution)/shard_map/ppermute | solution.py:350
  308.6 6.3 %collective-permute-done.41.refs_1_ = bf16[24,5120]{1,0:T(8,128)(2,1)S(1)} collective-permute-done((bf16[24,5120]{1,0:T(8,128)(2,1)S(1)}, bf16[24,5120]{1,0:T(8,128)(2,1)S(1)}, u32[]{:S(2)}, u32[]{:S(2)}) %collective-permute-start.41) | collective-permute-done | bytes 245792 | tf_op jit(solution)/shard_map/ppermute | solution.py:350
  314.9 12.2 %backward_set.7 = (bf16[24,5120]{1,0:T(8,128)(2,1)}, bf16[16,4,24,320]{3,2,1,0:T(8,128)(2,1)}) custom-call(s32[7]{0:T(128)S(1)} %stack.116.refs_0_, bf16[24,5120]{1,0:T(8,128)(2,1)S(1)} %collective-permute-done.41.refs_1_, bf16[4,24,5120]{2,1,0:T(8,128)(2,1)} %get-tuple-element.71.refs_2_, ...), custom_call_target="tpu_custom_call", output_to_operand_aliasing={{1}: (24, {})} | custom-call | flops 125829120 | bytes 5242880 | tf_op jit(solution)/shard_map/backward_set/pallas_call | solution.py:291
  327.1 5.7 %all-to-all-start.1 = ((bf16[16,4,24,320]{3,2,1,0:T(8,128)(2,1)}), bf16[16,4,24,320]{3,2,1,0:T(8,128)(2,1)S(1)}, u32[]{:S(2)}, u32[]{:S(2)}) async-start(bf16[16,4,24,320]{3,2,1,0:T(8,128)(2,1)} %get-tuple-element.77), calls=%async_computation.1 | async-start | bytes 2359296 | tf_op jit(solution)/shard_map/all_to_all | solution.py:354
  339.1 11.3 %all-to-all-done.1.refs_1_ = bf16[16,4,24,320]{3,2,1,0:T(8,128)(2,1)S(1)} async-done(((bf16[16,4,24,320]{3,2,1,0:T(8,128)(2,1)}), bf16[16,4,24,320]{3,2,1,0:T(8,128)(2,1)S(1)}, u32[]{:S(2)}, u32[]{:S(2)}) %all-to-all-start.1) | async-done | bytes 983072 | tf_op jit(solution)/shard_map/all_to_all | solution.py:354
  352.4 4.4 %collective-permute-start.44 = (bf16[320,256]{1,0:T(8,128)(2,1)S(1)}, bf16[320,256]{1,0:T(8,128)(2,1)S(1)}, u32[]{:S(2)}, u32[]{:S(2)}) collective-permute-start(bf16[320,256]{1,0:T(8,128)(2,1)S(1)} %get-tuple-element.83), channel_id=1, source_target_pairs={{0,48},{16,0},{32,16},{48,32},{1,49},{17,1},{33,17},{49,33},{2,50}... | collective-permute-start | bytes 491528 | tf_op jit(solution)/shard_map/ppermute | solution.py:345
  359.2 6.3 %collective-permute-done.45 = bf16[320,256]{1,0:T(8,128)(2,1)S(1)} collective-permute-done((bf16[320,256]{1,0:T(8,128)(2,1)S(1)}, bf16[320,256]{1,0:T(8,128)(2,1)S(1)}, u32[]{:S(2)}, u32[]{:S(2)}) %collective-permute-start.45) | collective-permute-done | bytes 163872 | tf_op jit(solution)/shard_map/ppermute | solution.py:345
  365.5 10.0 %collective-permute-done.44 = bf16[320,256]{1,0:T(8,128)(2,1)S(1)} collective-permute-done((bf16[320,256]{1,0:T(8,128)(2,1)S(1)}, bf16[320,256]{1,0:T(8,128)(2,1)S(1)}, u32[]{:S(2)}, u32[]{:S(2)}) %collective-permute-start.44) | collective-permute-done | bytes 163872 | tf_op jit(solution)/shard_map/ppermute | solution.py:345
  377.3 6.6 %collective-permute-done.48 = bf16[320,256]{1,0:T(8,128)(2,1)S(1)} collective-permute-done((bf16[320,256]{1,0:T(8,128)(2,1)S(1)}, bf16[320,256]{1,0:T(8,128)(2,1)S(1)}, u32[]{:S(2)}, u32[]{:S(2)}) %collective-permute-start.48) | collective-permute-done | bytes 163872 | tf_op jit(solution)/shard_map/ppermute | solution.py:363
  (141 shorter events, 51.5 us)
Async XLA Ops:
  12.1 82.8 %collective-permute-start = (bf16[2,8,320,256]{3,2,1,0:T(8,128)(2,1)}, bf16[2,8,320,256]{3,2,1,0:T(8,128)(2,1)}, u32[]{:S(2)}, u32[]{:S(2)}) collective-permute-start(bf16[2,8,320,256]{3,2,1,0:T(8,128)(2,1)} %pad_maximum_fusion.1), channel_id=1, source_target_pairs={{0,192},{192,0},{64,128},{128,64},{1,193},{193,1},{65,129},{129,65... | collective-permute-start | bytes 7864328 | tf_op jit(solution)/shard_map/ppermute | solution.py:363
  16.4 21.8 %collective-permute-start.3 = (bf16[2,320,256]{2,1,0:T(8,128)(2,1)S(1)}, bf16[2,320,256]{2,1,0:T(8,128)(2,1)S(1)}, u32[]{:S(2)}, u32[]{:S(2)}) collective-permute-start(bf16[2,320,256]{2,1,0:T(8,128)(2,1)S(1)} %pad_maximum_fusion.5), channel_id=1, source_target_pairs={{32,0},{48,16},{0,32},{16,48},{33,1},{49,17},{1,33},{17,49},{34,2}... | collective-permute-start | bytes 983048 | tf_op jit(solution)/shard_map/ppermute | solution.py:359
  23.7 29.0 %collective-permute-start.2 = (bf16[2,320,256]{2,1,0:T(8,128)(2,1)S(1)}, bf16[2,320,256]{2,1,0:T(8,128)(2,1)S(1)}, u32[]{:S(2)}, u32[]{:S(2)}) collective-permute-start(bf16[2,320,256]{2,1,0:T(8,128)(2,1)S(1)} %pad_maximum_fusion.5), channel_id=1, source_target_pairs={{0,16},{16,0},{32,48},{48,32},{1,17},{17,1},{33,49},{49,33},{2,18}... | collective-permute-start | bytes 983048 | tf_op jit(solution)/shard_map/ppermute | solution.py:367
  52.8 19.2 %collective-permute-start.5 = (bf16[2,320,256]{2,1,0:T(8,128)(2,1)S(1)}, bf16[2,320,256]{2,1,0:T(8,128)(2,1)S(1)}, u32[]{:S(2)}, u32[]{:S(2)}) collective-permute-start(bf16[2,320,256]{2,1,0:T(8,128)(2,1)S(1)} %pad_maximum_fusion.4), channel_id=1, source_target_pairs={{32,0},{48,16},{0,32},{16,48},{33,1},{49,17},{1,33},{17,49},{34,2}... | collective-permute-start | bytes 983048 | tf_op jit(solution)/shard_map/ppermute | solution.py:359
  55.2 35.0 %collective-permute-start.6 = (bf16[2,2,320,256]{3,2,1,0:T(8,128)(2,1)S(1)}, bf16[2,2,320,256]{3,2,1,0:T(8,128)(2,1)S(1)}, u32[]{:S(2)}, u32[]{:S(2)}) collective-permute-start(bf16[2,2,320,256]{3,2,1,0:T(8,128)(2,1)S(1)} %pad_maximum_fusion.2.refs_6_.refs_8_), channel_id=1, source_target_pairs={{2,0},{4,2},{6,4},{0,6},{3,1},{5,3},{7,5},{1,7},{10,8},{12,10},{14... | collective-permute-start | bytes 1966088 | tf_op jit(solution)/shard_map/ppermute | solution.py:359
  55.7 34.5 %collective-permute-start.7 = (bf16[2,2,320,256]{3,2,1,0:T(8,128)(2,1)S(1)}, bf16[2,2,320,256]{3,2,1,0:T(8,128)(2,1)S(1)}, u32[]{:S(2)}, u32[]{:S(2)}) collective-permute-start(bf16[2,2,320,256]{3,2,1,0:T(8,128)(2,1)S(1)} %pad_maximum_fusion.2.refs_6_.refs_8_), channel_id=1, source_target_pairs={{6,0},{0,2},{2,4},{4,6},{7,1},{1,3},{3,5},{5,7},{14,8},{8,10},{10,... | collective-permute-start | bytes 1966088 | tf_op jit(solution)/shard_map/ppermute | solution.py:359
  57.2 33.0 %collective-permute-start.8 = (bf16[2,2,320,256]{3,2,1,0:T(8,128)(2,1)S(1)}, bf16[2,2,320,256]{3,2,1,0:T(8,128)(2,1)S(1)}, u32[]{:S(2)}, u32[]{:S(2)}) collective-permute-start(bf16[2,2,320,256]{3,2,1,0:T(8,128)(2,1)S(1)} %pad_maximum_fusion.2.refs_6_.refs_8_), channel_id=1, source_target_pairs={{8,0},{0,8},{9,1},{1,9},{10,2},{2,10},{11,3},{3,11},{12,4},{4,12},... | collective-permute-start | bytes 1966088 | tf_op jit(solution)/shard_map/ppermute | solution.py:359
  72.0 18.1 %collective-permute-start.4 = (bf16[2,320,256]{2,1,0:T(8,128)(2,1)S(1)}, bf16[2,320,256]{2,1,0:T(8,128)(2,1)S(1)}, u32[]{:S(2)}, u32[]{:S(2)}) collective-permute-start(bf16[2,320,256]{2,1,0:T(8,128)(2,1)S(1)} %pad_maximum_fusion.4), channel_id=1, source_target_pairs={{0,16},{16,0},{32,48},{48,32},{1,17},{17,1},{33,49},{49,33},{2,18}... | collective-permute-start | bytes 983048 | tf_op jit(solution)/shard_map/ppermute | solution.py:367
  90.8 17.6 %collective-permute-start.11 = (bf16[2,2,320,256]{3,2,1,0:T(8,128)(2,1)S(1)}, bf16[2,2,320,256]{3,2,1,0:T(8,128)(2,1)S(1)}, u32[]{:S(2)}, u32[]{:S(2)}) collective-permute-start(bf16[2,2,320,256]{3,2,1,0:T(8,128)(2,1)S(1)} %collective-permute-done.6.refs_8_.refs_10_), channel_id=1, source_target_pairs={{2,0},{4,2},{6,4},{0,6},{3,1},{5,3},{7,5},{1,7},{10,8},{12,10},{14... | collective-permute-start | bytes 1966088 | tf_op jit(solution)/shard_map/ppermute | solution.py:359
  92.4 30.0 %collective-permute-start.15 = (bf16[2,2,320,256]{3,2,1,0:T(8,128)(2,1)S(1)}, bf16[2,2,320,256]{3,2,1,0:T(8,128)(2,1)S(1)}, u32[]{:S(2)}, u32[]{:S(2)}) collective-permute-start(bf16[2,2,320,256]{3,2,1,0:T(8,128)(2,1)S(1)} %collective-permute-done.8.refs_14_.refs_16_), channel_id=1, source_target_pairs={{2,0},{4,2},{6,4},{0,6},{3,1},{5,3},{7,5},{1,7},{10,8},{12,10},{14... | collective-permute-start | bytes 1966088 | tf_op jit(solution)/shard_map/ppermute | solution.py:359
  94.1 29.8 %collective-permute-start.17 = (bf16[2,2,320,256]{3,2,1,0:T(8,128)(2,1)S(1)}, bf16[2,2,320,256]{3,2,1,0:T(8,128)(2,1)S(1)}, u32[]{:S(2)}, u32[]{:S(2)}) collective-permute-start(bf16[2,2,320,256]{3,2,1,0:T(8,128)(2,1)S(1)} %collective-permute-done.8.refs_14_.refs_16_), channel_id=1, source_target_pairs={{6,0},{0,2},{2,4},{4,6},{7,1},{1,3},{3,5},{5,7},{14,8},{8,10},{10,... | collective-permute-start | bytes 1966088 | tf_op jit(solution)/shard_map/ppermute | solution.py:359
  108.4 64.4 %collective-permute-start.22 = (bf16[2,8,320,256]{3,2,1,0:T(8,128)(2,1)S(1)}, bf16[2,8,320,256]{3,2,1,0:T(8,128)(2,1)}, u32[]{:S(2)}, u32[]{:S(2)}) collective-permute-start(bf16[2,8,320,256]{3,2,1,0:T(8,128)(2,1)S(1)} %pad_maximum_fusion), channel_id=1, source_target_pairs={{0,192},{192,0},{64,128},{128,64},{1,193},{193,1},{65,129},{129,65... | collective-permute-start | bytes 7864328 | tf_op jit(solution)/shard_map/ppermute | solution.py:363
  108.7 17.8 %collective-permute-start.24 = (bf16[2,2,320,256]{3,2,1,0:T(8,128)(2,1)S(1)}, bf16[2,2,320,256]{3,2,1,0:T(8,128)(2,1)S(1)}, u32[]{:S(2)}, u32[]{:S(2)}) collective-permute-start(bf16[2,2,320,256]{3,2,1,0:T(8,128)(2,1)S(1)} %pad_maximum_fusion.3.refs_6_.refs_8_), channel_id=1, source_target_pairs={{1,0},{0,1},{3,2},{2,3},{5,4},{4,5},{7,6},{6,7},{9,8},{8,9},{11,10... | collective-permute-start | bytes 1966088 | tf_op jit(solution)/shard_map/ppermute | solution.py:359
  108.7 26.9 %collective-permute-start.25 = (bf16[2,2,320,256]{3,2,1,0:T(8,128)(2,1)S(1)}, bf16[2,2,320,256]{3,2,1,0:T(8,128)(2,1)S(1)}, u32[]{:S(2)}, u32[]{:S(2)}) collective-permute-start(bf16[2,2,320,256]{3,2,1,0:T(8,128)(2,1)S(1)} %pad_maximum_fusion.3.refs_6_.refs_8_), channel_id=1, source_target_pairs={{2,0},{4,2},{6,4},{0,6},{3,1},{5,3},{7,5},{1,7},{10,8},{12,10},{14... | collective-permute-start | bytes 1966088 | tf_op jit(solution)/shard_map/ppermute | solution.py:359
  126.5 51.8 %collective-permute-start.1 = (bf16[2,8,320,256]{3,2,1,0:T(8,128)(2,1)}, bf16[2,8,320,256]{3,2,1,0:T(8,128)(2,1)}, u32[]{:S(2)}, u32[]{:S(2)}) collective-permute-start(bf16[2,8,320,256]{3,2,1,0:T(8,128)(2,1)} %collective-permute-done.refs_4_.refs_6_), channel_id=1, source_target_pairs={{1,0},{0,1},{3,2},{2,3},{5,4},{4,5},{7,6},{6,7},{9,8},{8,9},{11,10... | collective-permute-start | bytes 7864328 | tf_op jit(solution)/shard_map/ppermute | solution.py:359
  158.9 33.2 %collective-permute-start.30 = (bf16[2,2,320,256]{3,2,1,0:T(8,128)(2,1)}, bf16[2,2,320,256]{3,2,1,0:T(8,128)(2,1)}, u32[]{:S(2)}, u32[]{:S(2)}) collective-permute-start(bf16[2,2,320,256]{3,2,1,0:T(8,128)(2,1)} %collective-permute-done.29.refs_12_.refs_14_), channel_id=1, source_target_pairs={{1,0},{0,1},{3,2},{2,3},{5,4},{4,5},{7,6},{6,7},{9,8},{8,9},{11,10... | collective-permute-start | bytes 1966088 | tf_op jit(solution)/shard_map/ppermute | solution.py:359
  159.0 17.5 %collective-permute-start.35 = (bf16[2,2,320,256]{3,2,1,0:T(8,128)(2,1)}, bf16[2,2,320,256]{3,2,1,0:T(8,128)(2,1)}, u32[]{:S(2)}, u32[]{:S(2)}) collective-permute-start(bf16[2,2,320,256]{3,2,1,0:T(8,128)(2,1)} %collective-permute-done.31.refs_14_.refs_16_), channel_id=1, source_target_pairs={{6,0},{0,2},{2,4},{4,6},{7,1},{1,3},{3,5},{5,7},{14,8},{8,10},{10,... | collective-permute-start | bytes 1966088 | tf_op jit(solution)/shard_map/ppermute | solution.py:359
  172.8 38.7 %collective-permute-start.23 = (bf16[2,8,320,256]{3,2,1,0:T(8,128)(2,1)}, bf16[2,8,320,256]{3,2,1,0:T(8,128)(2,1)}, u32[]{:S(2)}, u32[]{:S(2)}) collective-permute-start(bf16[2,8,320,256]{3,2,1,0:T(8,128)(2,1)} %collective-permute-done.22.refs_4_.refs_6_), channel_id=1, source_target_pairs={{1,0},{0,1},{3,2},{2,3},{5,4},{4,5},{7,6},{6,7},{9,8},{8,9},{11,10... | collective-permute-start | bytes 7864328 | tf_op jit(solution)/shard_map/ppermute | solution.py:359
  176.5 24.8 %collective-permute-start.32 = (bf16[2,2,320,256]{3,2,1,0:T(8,128)(2,1)}, bf16[2,2,320,256]{3,2,1,0:T(8,128)(2,1)}, u32[]{:S(2)}, u32[]{:S(2)}) collective-permute-start(bf16[2,2,320,256]{3,2,1,0:T(8,128)(2,1)} %collective-permute-done.31.refs_14_.refs_16_), channel_id=1, source_target_pairs={{1,0},{0,1},{3,2},{2,3},{5,4},{4,5},{7,6},{6,7},{9,8},{8,9},{11,10... | collective-permute-start | bytes 1966088 | tf_op jit(solution)/shard_map/ppermute | solution.py:359
  176.5 24.9 %collective-permute-start.33 = (bf16[2,2,320,256]{3,2,1,0:T(8,128)(2,1)}, bf16[2,2,320,256]{3,2,1,0:T(8,128)(2,1)}, u32[]{:S(2)}, u32[]{:S(2)}) collective-permute-start(bf16[2,2,320,256]{3,2,1,0:T(8,128)(2,1)} %collective-permute-done.31.refs_14_.refs_16_), channel_id=1, source_target_pairs={{2,0},{4,2},{6,4},{0,6},{3,1},{5,3},{7,5},{1,7},{10,8},{12,10},{14... | collective-permute-start | bytes 1966088 | tf_op jit(solution)/shard_map/ppermute | solution.py:359
  178.3 23.6 %collective-permute-start.36 = (bf16[2,2,320,256]{3,2,1,0:T(8,128)(2,1)}, bf16[2,2,320,256]{3,2,1,0:T(8,128)(2,1)}, u32[]{:S(2)}, u32[]{:S(2)}) collective-permute-start(bf16[2,2,320,256]{3,2,1,0:T(8,128)(2,1)} %collective-permute-done.35.refs_20_.refs_22_), channel_id=1, source_target_pairs={{6,0},{0,2},{2,4},{4,6},{7,1},{1,3},{3,5},{5,7},{14,8},{8,10},{10,... | collective-permute-start | bytes 1966088 | tf_op jit(solution)/shard_map/ppermute | solution.py:359
  212.2 28.8 %collective-permute-start.39 = (bf16[24,5120]{1,0:T(8,128)(2,1)S(1)}, bf16[24,5120]{1,0:T(8,128)(2,1)S(1)}, u32[]{:S(2)}, u32[]{:S(2)}) collective-permute-start(bf16[24,5120]{1,0:T(8,128)(2,1)S(1)} %get-tuple-element.61), channel_id=1, source_target_pairs={{0,64},{64,0},{128,192},{192,128},{1,65},{65,1},{129,193},{193,129... | collective-permute-start | bytes 737288 | tf_op jit(solution)/shard_map/ppermute | solution.py:350
  274.9 52.2 %all-to-all-start = ((bf16[16,4,24,320]{3,2,1,0:T(8,128)(2,1)}), bf16[16,4,24,320]{3,2,1,0:T(8,128)(2,1)S(1)}, u32[]{:S(2)}, u32[]{:S(2)}) async-start(bf16[16,4,24,320]{3,2,1,0:T(8,128)(2,1)} %get-tuple-element.76), calls=%async_computation | async-start | bytes 2359296 | tf_op jit(solution)/shard_map/all_to_all | solution.py:354
  282.0 50.8 %all-gather.3.cloned.1.call-start = ((), (), s32[]{:S(2)}) async-start(), calls=%async_computation.2 | async-start | bytes 1671168 | tf_op jit(solution)/shard_map/all_gather | solution.py:439
  283.6 31.3 %collective-permute-start.41 = (bf16[24,5120]{1,0:T(8,128)(2,1)S(1)}, bf16[24,5120]{1,0:T(8,128)(2,1)S(1)}, u32[]{:S(2)}, u32[]{:S(2)}) collective-permute-start(bf16[24,5120]{1,0:T(8,128)(2,1)S(1)} %get-tuple-element.73), channel_id=1, source_target_pairs={{0,64},{64,0},{128,192},{192,128},{1,65},{65,1},{129,193},{193,129... | collective-permute-start | bytes 737288 | tf_op jit(solution)/shard_map/ppermute | solution.py:350
  327.1 23.3 %all-to-all-start.1 = ((bf16[16,4,24,320]{3,2,1,0:T(8,128)(2,1)}), bf16[16,4,24,320]{3,2,1,0:T(8,128)(2,1)S(1)}, u32[]{:S(2)}, u32[]{:S(2)}) async-start(bf16[16,4,24,320]{3,2,1,0:T(8,128)(2,1)} %get-tuple-element.77), calls=%async_computation.1 | async-start | bytes 2359296 | tf_op jit(solution)/shard_map/all_to_all | solution.py:354
  334.8 21.9 %collective-permute-start.47 = (bf16[320,256]{1,0:T(8,128)(2,1)S(1)}, bf16[320,256]{1,0:T(8,128)(2,1)S(1)}, u32[]{:S(2)}, u32[]{:S(2)}) collective-permute-start(bf16[320,256]{1,0:T(8,128)(2,1)S(1)} %get-tuple-element.88), channel_id=1, source_target_pairs={{0,48},{16,0},{32,16},{48,32},{1,49},{17,1},{33,17},{49,33},{2,50}... | collective-permute-start | bytes 491528 | tf_op jit(solution)/shard_map/ppermute | solution.py:345
  336.7 22.5 %collective-permute-start.46 = (bf16[320,256]{1,0:T(8,128)(2,1)S(1)}, bf16[320,256]{1,0:T(8,128)(2,1)S(1)}, u32[]{:S(2)}, u32[]{:S(2)}) collective-permute-start(bf16[320,256]{1,0:T(8,128)(2,1)S(1)} %get-tuple-element.87), channel_id=1, source_target_pairs={{0,32},{16,48},{32,0},{48,16},{1,33},{17,49},{33,1},{49,17},{2,34}... | collective-permute-start | bytes 491528 | tf_op jit(solution)/shard_map/ppermute | solution.py:345
  338.3 27.2 %collective-permute-start.45 = (bf16[320,256]{1,0:T(8,128)(2,1)S(1)}, bf16[320,256]{1,0:T(8,128)(2,1)S(1)}, u32[]{:S(2)}, u32[]{:S(2)}) collective-permute-start(bf16[320,256]{1,0:T(8,128)(2,1)S(1)} %get-tuple-element.86), channel_id=1, source_target_pairs={{0,16},{16,32},{32,48},{48,0},{1,17},{17,33},{33,49},{49,1},{2,18}... | collective-permute-start | bytes 491528 | tf_op jit(solution)/shard_map/ppermute | solution.py:345
  352.4 23.2 %collective-permute-start.44 = (bf16[320,256]{1,0:T(8,128)(2,1)S(1)}, bf16[320,256]{1,0:T(8,128)(2,1)S(1)}, u32[]{:S(2)}, u32[]{:S(2)}) collective-permute-start(bf16[320,256]{1,0:T(8,128)(2,1)S(1)} %get-tuple-element.83), channel_id=1, source_target_pairs={{0,48},{16,0},{32,16},{48,32},{1,49},{17,1},{33,17},{49,33},{2,50}... | collective-permute-start | bytes 491528 | tf_op jit(solution)/shard_map/ppermute | solution.py:345
  356.7 18.8 %collective-permute-start.43 = (bf16[320,256]{1,0:T(8,128)(2,1)S(1)}, bf16[320,256]{1,0:T(8,128)(2,1)S(1)}, u32[]{:S(2)}, u32[]{:S(2)}) collective-permute-start(bf16[320,256]{1,0:T(8,128)(2,1)S(1)} %get-tuple-element.82), channel_id=1, source_target_pairs={{0,32},{16,48},{32,0},{48,16},{1,33},{17,49},{33,1},{49,17},{2,34}... | collective-permute-start | bytes 491528 | tf_op jit(solution)/shard_map/ppermute | solution.py:345
  356.7 19.9 %collective-permute-start.42 = (bf16[320,256]{1,0:T(8,128)(2,1)S(1)}, bf16[320,256]{1,0:T(8,128)(2,1)S(1)}, u32[]{:S(2)}, u32[]{:S(2)}) collective-permute-start(bf16[320,256]{1,0:T(8,128)(2,1)S(1)} %get-tuple-element.81), channel_id=1, source_target_pairs={{0,16},{16,32},{32,48},{48,0},{1,17},{17,33},{33,49},{49,1},{2,18}... | collective-permute-start | bytes 491528 | tf_op jit(solution)/shard_map/ppermute | solution.py:345
  (40 other events, 732.9 us)
Sparse Core Ops, SparseCore 0:
  284.7 42.2 all-gather.2

commit v6 on v5

--- a/solution.py
+++ b/solution.py
@@ -17,6 +17,30 @@
 ANY = pl.BlockSpec(memory_space=pl.ANY)
 VM = pl.BlockSpec(memory_space=pltpu.VMEM)
 SM = pl.BlockSpec(memory_space=pltpu.SMEM)
+
+
+class Gathered:
+    count = 1
+
+    def __init__(self, refs, flags, wbuf, sem):
+        self.w, self.flags, self.wbuf, self.sem = refs[0], flags, wbuf, sem
+
+    def copy(self, layer, slot, which):
+        held = jnp.where(self.flags[1] == 1, SET - 1 - layer, layer)
+        return pltpu.make_async_copy(
+            self.w.at[held, :, which], self.wbuf.at[slot, :, which], self.sem.at[slot, which]
+        )
+
+    def first(self, layer, order):
+        self.order = order
+        self.begin(layer, 0)
+
+    def begin(self, layer, slot):
+        for which in self.order:
+            self.copy(layer, slot, which).start()
+
+    def arrive(self, layer, slot, which):
+        self.copy(layer, slot, which).wait()
 
 
 class Scattered:
@@ -158,7 +182,7 @@
 
 
 def run_forward(flags, rows, weights, held=None):
-    source = Scattered
+    source = Gathered if len(weights) == 1 else Scattered
     first = 2 + source.count
     outs = (
         jax.ShapeDtypeStruct((ROWS, D), jnp.bfloat16),
@@ -282,7 +306,7 @@
 
 
 def run_backward(flags, g_rows, weights, h_held, pre_held, held=None, from_final=False, last=False):
-    source = Scattered
+    source = Gathered if len(weights) == 1 else Scattered
     outs = (
         jax.ShapeDtypeStruct((ROWS, D), jnp.bfloat16),
         jax.ShapeDtypeStruct((16, SET, ROWS, D // 16), jnp.bfloat16),
@@ -365,15 +389,16 @@
 
 def over_z(chunk_now):
     beside = lax.ppermute(chunk_now, "zh", [(0, 1), (1, 0), (2, 3), (3, 2)])
-    return jnp.stack([beside, from_ring(chunk_now, "zh", 2)])
-
-
-def over_x_first(near):
+    route = []
+    for y in range(4):
+        for zh in range(4):
+            route.append((y * 4 + zh, (3 - y) * 4 + (zh ^ 1)))
+    return jnp.stack([beside, lax.ppermute(chunk_now, ("y", "zh"), route)])
+
+
+def over_x(near):
     far = from_ring(near, "zl", 1)
-    return near, from_ring(near, "x", 1), from_ring(near, "x", -1), far
-
-
-def over_x_rest(near, near_up, near_down, far):
+    near_up, near_down = from_ring(near, "x", 1), from_ring(near, "x", -1)
     near_across = from_ring(near_up, "x", 1)
     far_up, far_down = from_ring(far, "x", 1), from_ring(far, "x", -1)
     far_across = from_ring(far_down, "x", -1)
@@ -395,6 +420,9 @@
         ]
         return jnp.stack(parts)
 
+    def gathered(own_part):
+        return lax.all_gather(own_part, ("zh",) + DP).reshape(SET, 16, 2, D // 16, R)
+
     def own_half(layer_slot):
         core = lax.axis_index("core")
         parts = [
@@ -405,18 +433,9 @@
 
     first_slot = jnp.where(low_half, 0, 1)
     own_layers = tuple(w[0].reshape(2, 16, D // 16, R) for w in (w_in, w_out))
+    w_b = (gathered(own(1 - first_slot)),)
     half_a = across_y(own_half(first_slot))
-    near_a = over_z(own(first_slot))
-    chunk_b, near_a = lax.optimization_barrier((own(1 - first_slot), near_a))
-    step_a = over_x_first(near_a)
-    near_b = over_z(chunk_b)
-    near_b, step_a = lax.optimization_barrier((near_b, step_a))
-    rest_a = over_x_rest(*step_a)
-    half_b, half_a = lax.optimization_barrier((own_half(1 - first_slot), half_a))
-    half_b = across_y(half_b)
-    w_a = own_layers + (half_a, from_ring(half_a, "core", 1)) + rest_a
-    rest_b = over_x_rest(*over_x_first(near_b))
-    w_b = own_layers + (half_b, from_ring(half_b, "core", 1)) + rest_b
+    w_a = own_layers + (half_a, from_ring(half_a, "core", 1)) + over_x(over_z(own(first_slot)))
 
     def flag(active, slot_now):
         reverse = slot_now == 1
@@ -441,6 +460,7 @@
     rows = hop(rows)
     rows, g_b = run_backward(q_b, rows, w_b, h_b, pre_b, held=g_b)
     rows, g_a = run_backward(q_a, rows, w_a, h_a, pre_a)
+    rows, act_all = lax.optimization_barrier((rows, act_all))
     rows = hop(rows)
     rows, g_a = run_backward(p_a, rows, w_a, h_a, pre_a, held=g_a, last=True)
     place = zh.astype(jnp.int32)[None]

time: 396 us -> 353 us (0.89)
  starting transfers between devices: 116 us -> 87.5 us
  waiting for transfers between devices: 193 us -> 188 us
    ppermute x0 -> x1, waiting for transfers between devices: none -> 30.6 us  [over_z(): return jnp.stack([beside, lax.ppermute(chunk_now, ('y', 'zh'), route)])]
    ppermute x4, starting transfers between devices: 56.5 us -> 27.1 us  [hop(): return lax.ppermute(rows, 'y', [(0, 1), (1, 0), (2, 3), (3, 2)])]
    ppermute x34 -> x16, waiting for transfers between devices: 97.7 us -> 73.7 us  [from_ring(): lax.ppermute(block, axis, [((d + away) % count, d) for d in range(count)])]
    ppermute x2 -> x1, waiting for transfers between devices: 32.5 us -> 8.84 us  [over_z(): beside = lax.ppermute(chunk_now, 'zh', [(0, 1), (1, 0), (2, 3), (3, 2)])]
    all_gather x1, waiting for transfers between devices: 0.01 us -> 20.8 us  [shards(): act_all = lax.all_gather(jnp.concatenate([act_a, act_b], axis=0), DP)]
    ppermute x34 -> x16, starting transfers between devices: 30.1 us -> 13.9 us  [from_ring(): lax.ppermute(block, axis, [((d + away) % count, d) for d in range(count)])]
    ppermute x6, starting transfers between devices: 11.1 us -> 24.1 us  [summed_over_zh(): total = total + lax.ppermute(parts[k], 'zh', route).astype(jnp.float32)]
    all_to_all x2, waiting for transfers between devices: 11.3 us -> 3.41 us  [spread(): return lax.all_to_all(g_set, DP, 0, 0)]
  transfers between devices with their start and end apart: 52 -> 34, of which waited for: 23 -> 22; matrix products, arithmetic and copies ran while one was open for 1% -> 1% of each run, Pallas kernels for 8% -> 12%
where the time goes in v6:
time: 353 us; the launch traced here: 352 us
  waiting for transfers between devices  188 us (53%)
  starting transfers between devices  87.5 us (25%)
  Pallas kernels  55.4 us (16%)
  between operations  13.7 us (4%)
  local copies, waits for them, and re-layouts  4.53 us (1%)
  other arithmetic  3.67 us (1%)
    ppermute x16, waiting for transfers between devices, from_ring(): lax.ppermute(block, axis, [((d + away) % count, d) for d in range(count)])  73.7 us
    ppermute x1, waiting for transfers between devices, over_z(): return jnp.stack([beside, lax.ppermute(chunk_now, ('y', 'zh'), route)])  30.6 us
    ppermute x4, starting transfers between devices, hop(): return lax.ppermute(rows, 'y', [(0, 1), (1, 0), (2, 3), (3, 2)])  27.1 us
    ppermute x4, waiting for transfers between devices, hop(): return lax.ppermute(rows, 'y', [(0, 1), (1, 0), (2, 3), (3, 2)])  26.9 us
    pallas_call x4, Pallas kernels, run_forward(): pl.pallas_call(lambda *refs: forward_kernel(*refs, source=source, aliased...  25.8 us
    pallas_call x4, Pallas kernels, run_backward(): pl.pallas_call(lambda *refs: backward_kernel(*refs, source=source, aliase...  25.7 us
    ppermute x6, starting transfers between devices, summed_over_zh(): total = total + lax.ppermute(parts[k], 'zh', route).astype(jnp.float32)  24.1 us
    all_gather x1, waiting for transfers between devices, shards(): act_all = lax.all_gather(jnp.concatenate([act_a, act_b], axis=0), DP)  20.8 us
  transfers between devices with their start and end apart: 34, of which 22 were waited for; matrix products, arithmetic and copies ran while one was open for 1% of the time, Pallas kernels for 12%

profile of v6, /device:TPU:2, one launch (start us, length us, event | category | flops | bytes accessed | tf_op | source)
XLA Modules:
  0.0 352.3 jit_solution(6924145233316590441)
XLA Ops:
  10.7 3.1 collective-permute-start
  17.3 30.6 %collective-permute-done.3 = bf16[2,320,256]{2,1,0:T(8,128)(2,1)S(1)} collective-permute-done((bf16[2,320,256]{2,1,0:T(8,128)(2,1)S(1)}, bf16[2,320,256]{2,1,0:T(8,128)(2,1)S(1)}, u32[]{:S(2)}, u32[]{:S(2)}) %collective-permute-start.3) | collective-permute-done | bytes 327712 | tf_op jit(solution)/shard_map/ppermute | solution.py:396
  47.9 8.8 %collective-permute-done.2 = bf16[2,320,256]{2,1,0:T(8,128)(2,1)S(1)} collective-permute-done((bf16[2,320,256]{2,1,0:T(8,128)(2,1)S(1)}, bf16[2,320,256]{2,1,0:T(8,128)(2,1)S(1)}, u32[]{:S(2)}, u32[]{:S(2)}) %collective-permute-start.2) | collective-permute-done | bytes 327712 | tf_op jit(solution)/shard_map/ppermute | solution.py:391
  60.3 10.8 %collective-permute-done.5.refs_8_.refs_10_ = bf16[2,2,320,256]{3,2,1,0:T(8,128)(2,1)S(1)} collective-permute-done((bf16[2,2,320,256]{3,2,1,0:T(8,128)(2,1)S(1)}, bf16[2,2,320,256]{3,2,1,0:T(8,128)(2,1)S(1)}, u32[]{:S(2)}, u32[]{:S(2)}) %collective-permute-start.5) | collective-permute-done | bytes 655392 | tf_op jit(solution)/shard_map/ppermute | solution.py:383
  71.1 4.2 %collective-permute-start.7 = (bf16[2,2,320,256]{3,2,1,0:T(8,128)(2,1)S(1)}, bf16[2,2,320,256]{3,2,1,0:T(8,128)(2,1)S(1)}, u32[]{:S(2)}, u32[]{:S(2)}) collective-permute-start(bf16[2,2,320,256]{3,2,1,0:T(8,128)(2,1)S(1)} %collective-permute-done.5.refs_8_.refs_10_), channel_id=1, source_target_pairs={{2,0},{4,2},{6,4},{0,6},{3,1},{5,3},{7,5},{1,7},{10,8},{12,10},{14... | collective-permute-start | bytes 1966088 | tf_op jit(solution)/shard_map/ppermute | solution.py:383
  79.3 3.9 %collective-permute-done.9.refs_12_.refs_14_ = bf16[2,2,320,256]{3,2,1,0:T(8,128)(2,1)S(1)} collective-permute-done((bf16[2,2,320,256]{3,2,1,0:T(8,128)(2,1)S(1)}, bf16[2,2,320,256]{3,2,1,0:T(8,128)(2,1)S(1)}, u32[]{:S(2)}, u32[]{:S(2)}) %collective-permute-start.9) | collective-permute-done | bytes 655392 | tf_op jit(solution)/shard_map/ppermute | solution.py:383
  83.7 20.5 %collective-permute-done.7.refs_10_.refs_12_ = bf16[2,2,320,256]{3,2,1,0:T(8,128)(2,1)S(1)} collective-permute-done((bf16[2,2,320,256]{3,2,1,0:T(8,128)(2,1)S(1)}, bf16[2,2,320,256]{3,2,1,0:T(8,128)(2,1)S(1)}, u32[]{:S(2)}, u32[]{:S(2)}) %collective-permute-start.7) | collective-permute-done | bytes 655392 | tf_op jit(solution)/shard_map/ppermute | solution.py:383
  104.2 3.7 %collective-permute-start.13 = (bf16[2,2,320,256]{3,2,1,0:T(8,128)(2,1)S(1)}, bf16[2,2,320,256]{3,2,1,0:T(8,128)(2,1)}, u32[]{:S(2)}, u32[]{:S(2)}) collective-permute-start(bf16[2,2,320,256]{3,2,1,0:T(8,128)(2,1)S(1)} %collective-permute-done.11.refs_14_.refs_16_), channel_id=1, source_target_pairs={{2,0},{4,2},{6,4},{0,6},{3,1},{5,3},{7,5},{1,7},{10,8},{12,10},{14... | collective-permute-start | bytes 1966088 | tf_op jit(solution)/shard_map/ppermute | solution.py:383
  107.9 4.0 %collective-permute-done.15.refs_20_.refs_22_ = bf16[2,2,320,256]{3,2,1,0:T(8,128)(2,1)} collective-permute-done((bf16[2,2,320,256]{3,2,1,0:T(8,128)(2,1)S(1)}, bf16[2,2,320,256]{3,2,1,0:T(8,128)(2,1)}, u32[]{:S(2)}, u32[]{:S(2)}) %collective-permute-start.15) | collective-permute-done | bytes 655392 | tf_op jit(solution)/shard_map/ppermute | solution.py:383
  112.5 24.8 %collective-permute-done.13.refs_16_.refs_18_ = bf16[2,2,320,256]{3,2,1,0:T(8,128)(2,1)} collective-permute-done((bf16[2,2,320,256]{3,2,1,0:T(8,128)(2,1)S(1)}, bf16[2,2,320,256]{3,2,1,0:T(8,128)(2,1)}, u32[]{:S(2)}, u32[]{:S(2)}) %collective-permute-start.13) | collective-permute-done | bytes 655392 | tf_op jit(solution)/shard_map/ppermute | solution.py:383
  137.3 6.9 %collective-permute-done.16.refs_18_.refs_20_ = bf16[2,2,320,256]{3,2,1,0:T(8,128)(2,1)} collective-permute-done((bf16[2,2,320,256]{3,2,1,0:T(8,128)(2,1)}, bf16[2,2,320,256]{3,2,1,0:T(8,128)(2,1)}, u32[]{:S(2)}, u32[]{:S(2)}) %collective-permute-start.16) | collective-permute-done | bytes 655392 | tf_op jit(solution)/shard_map/ppermute | solution.py:383
  146.7 12.8 %forward_set.4 = (bf16[24,5120]{1,0:T(8,128)(2,1)S(1)}, bf16[4,24,5120]{2,1,0:T(8,128)(2,1)}, f32[4,24,256]{2,1,0:T(8,128)S(1)}, bf16[4,24,256]{2,1,0:T(8,128)(2,1)S(1)}) custom-call(s32[7]{0:T(128)S(1)} %stack.100.refs_0_, bf16[24,5120]{1,0:T(8,128)(2,1)S(1)} %pad.4.refs_1_, bf16[2,16,320,256]{3,2,1,0:T(8,128)(2,1)} %bitcast.33, ...), custom_call_target="tpu_custom_call" | custom-call | flops 125829120 | bytes 5242880 | tf_op jit(solution)/shard_map/forward_set/pallas_call | solution.py:194
  159.8 7.9 %collective-permute-done.19.refs_1_ = bf16[24,5120]{1,0:T(8,128)(2,1)S(1)} collective-permute-done((bf16[24,5120]{1,0:T(8,128)(2,1)S(1)}, bf16[24,5120]{1,0:T(8,128)(2,1)S(1)}, u32[]{:S(2)}, u32[]{:S(2)}) %collective-permute-start.19) | collective-permute-done | bytes 245792 | tf_op jit(solution)/shard_map/ppermute | solution.py:374
  169.0 23.1 %collective-permute-start.20 = (bf16[24,5120]{1,0:T(8,128)(2,1)S(1)}, bf16[24,5120]{1,0:T(8,128)(2,1)S(1)}, u32[]{:S(2)}, u32[]{:S(2)}) collective-permute-start(bf16[24,5120]{1,0:T(8,128)(2,1)S(1)} %get-tuple-element.45), channel_id=1, source_target_pairs={{0,64},{64,0},{128,192},{192,128},{1,65},{65,1},{129,193},{193,129... | collective-permute-start | bytes 737288 | tf_op jit(solution)/shard_map/ppermute | solution.py:374
  192.2 5.8 %collective-permute-done.20.refs_1_ = bf16[24,5120]{1,0:T(8,128)(2,1)S(1)} collective-permute-done((bf16[24,5120]{1,0:T(8,128)(2,1)S(1)}, bf16[24,5120]{1,0:T(8,128)(2,1)S(1)}, u32[]{:S(2)}, u32[]{:S(2)}) %collective-permute-start.20) | collective-permute-done | bytes 245792 | tf_op jit(solution)/shard_map/ppermute | solution.py:374
  198.0 11.7 %forward_set.7 = (bf16[24,5120]{1,0:T(8,128)(2,1)S(1)}, bf16[4,24,5120]{2,1,0:T(8,128)(2,1)S(1)}, f32[4,24,256]{2,1,0:T(8,128)S(1)}, bf16[4,24,256]{2,1,0:T(8,128)(2,1)S(1)}) custom-call(s32[7]{0:T(128)S(1)} %stack.108.refs_0_, bf16[24,5120]{1,0:T(8,128)(2,1)S(1)} %collective-permute-done.20.refs_1_, ...), custom_call_target="tpu_custom_call", output_to_operand_aliasing={{1}: (3, {}), {2}: (4, {}), {3}: (5, {})} | custom-call | flops 125829120 | bytes 5242880 | tf_op jit(solution)/shard_map/forward_set/pallas_call | solution.py:194
  210.4 12.3 %backward_set.4 = (bf16[24,5120]{1,0:T(8,128)(2,1)S(1)}, bf16[16,4,24,320]{3,2,1,0:T(8,128)(2,1)}) custom-call(s32[7]{0:T(128)S(1)} %stack.108.refs_0_, bf16[24,5120]{1,0:T(8,128)(2,1)S(1)} %get-tuple-element.49.refs_1_, bf16[4,24,5120]{2,1,0:T(8,128)(2,1)S(1)} %get-tuple-element.50.refs_2_, f32[4,24,256]{2,1,0:T(8,128)S(1)} %get-tuple-element.51.refs_3_, ...), custom_call_target="tpu_custom_call" | custom-call | flops 125829120 | bytes 5242880 | tf_op jit(solution)/shard_map/backward_set/pallas_call | solution.py:315
  222.8 7.0 %collective-permute-done.21.refs_1_ = bf16[24,5120]{1,0:T(8,128)(2,1)S(1)} collective-permute-done((bf16[24,5120]{1,0:T(8,128)(2,1)S(1)}, bf16[24,5120]{1,0:T(8,128)(2,1)S(1)}, u32[]{:S(2)}, u32[]{:S(2)}) %collective-permute-start.21) | collective-permute-done | bytes 245792 | tf_op jit(solution)/shard_map/ppermute | solution.py:374
  230.5 6.9 %all-to-all-start = ((bf16[16,4,24,320]{3,2,1,0:T(8,128)(2,1)}), bf16[16,4,24,320]{3,2,1,0:T(8,128)(2,1)S(1)}, u32[]{:S(2)}, u32[]{:S(2)}) async-start(bf16[16,4,24,320]{3,2,1,0:T(8,128)(2,1)} %get-tuple-element.63), calls=%async_computation | async-start | bytes 2359296 | tf_op jit(solution)/shard_map/all_to_all | solution.py:378
  238.1 20.8 %all-gather.7.cloned.1.call-done = bf16[128,24,256]{2,1,0:T(8,128)(2,1)} async-done(((bf16[8,24,256]{2,1,0:T(8,128)(2,1)}), bf16[128,24,256]{2,1,0:T(8,128)(2,1)}) %all-gather.7.cloned.1.call-update) | async-done | bytes 1572880 | tf_op jit(solution)/shard_map/all_gather | solution.py:458
  258.8 3.8 %collective-permute-start.22 = (bf16[24,5120]{1,0:T(8,128)(2,1)S(1)}, bf16[24,5120]{1,0:T(8,128)(2,1)S(1)}, u32[]{:S(2)}, u32[]{:S(2)}) collective-permute-start(bf16[24,5120]{1,0:T(8,128)(2,1)S(1)} %get-tuple-element.60), channel_id=1, source_target_pairs={{0,64},{64,0},{128,192},{192,128},{1,65},{65,1},{129,193},{193,129... | collective-permute-start | bytes 737288 | tf_op jit(solution)/shard_map/ppermute | solution.py:374
  262.7 6.2 %collective-permute-done.22.refs_1_ = bf16[24,5120]{1,0:T(8,128)(2,1)S(1)} collective-permute-done((bf16[24,5120]{1,0:T(8,128)(2,1)S(1)}, bf16[24,5120]{1,0:T(8,128)(2,1)S(1)}, u32[]{:S(2)}, u32[]{:S(2)}) %collective-permute-start.22) | collective-permute-done | bytes 245792 | tf_op jit(solution)/shard_map/ppermute | solution.py:374
  268.9 12.1 %backward_set.7 = (bf16[24,5120]{1,0:T(8,128)(2,1)}, bf16[16,4,24,320]{3,2,1,0:T(8,128)(2,1)}) custom-call(s32[7]{0:T(128)S(1)} %stack.100.refs_0_, bf16[24,5120]{1,0:T(8,128)(2,1)S(1)} %collective-permute-done.22.refs_1_, bf16[4,24,5120]{2,1,0:T(8,128)(2,1)} %get-tuple-element.55.refs_2_, ...), custom_call_target="tpu_custom_call", output_to_operand_aliasing={{1}: (24, {})} | custom-call | flops 125829120 | bytes 5242880 | tf_op jit(solution)/shard_map/backward_set/pallas_call | solution.py:315
  281.0 5.7 %all-to-all-start.1 = ((bf16[16,4,24,320]{3,2,1,0:T(8,128)(2,1)}), bf16[16,4,24,320]{3,2,1,0:T(8,128)(2,1)S(1)}, u32[]{:S(2)}, u32[]{:S(2)}) async-start(bf16[16,4,24,320]{3,2,1,0:T(8,128)(2,1)} %get-tuple-element.64), calls=%async_computation.1 | async-start | bytes 2359296 | tf_op jit(solution)/shard_map/all_to_all | solution.py:378
  288.7 8.7 %collective-permute-start.28 = (bf16[320,256]{1,0:T(8,128)(2,1)S(1)}, bf16[320,256]{1,0:T(8,128)(2,1)S(1)}, u32[]{:S(2)}, u32[]{:S(2)}) collective-permute-start(bf16[320,256]{1,0:T(8,128)(2,1)S(1)} %get-tuple-element.74), channel_id=1, source_target_pairs={{0,48},{16,0},{32,16},{48,32},{1,49},{17,1},{33,17},{49,33},{2,50}... | collective-permute-start | bytes 491528 | tf_op jit(solution)/shard_map/ppermute | solution.py:369
  300.1 3.4 all-to-all-done.1.refs_1_
  305.5 10.2 %collective-permute-start.25 = (bf16[320,256]{1,0:T(8,128)(2,1)S(1)}, bf16[320,256]{1,0:T(8,128)(2,1)S(1)}, u32[]{:S(2)}, u32[]{:S(2)}) collective-permute-start(bf16[320,256]{1,0:T(8,128)(2,1)S(1)} %get-tuple-element.69), channel_id=1, source_target_pairs={{0,48},{16,0},{32,16},{48,32},{1,49},{17,1},{33,17},{49,33},{2,50}... | collective-permute-start | bytes 491528 | tf_op jit(solution)/shard_map/ppermute | solution.py:369
  320.1 3.8 %collective-permute-done.26 = bf16[320,256]{1,0:T(8,128)(2,1)S(1)} collective-permute-done((bf16[320,256]{1,0:T(8,128)(2,1)S(1)}, bf16[320,256]{1,0:T(8,128)(2,1)S(1)}, u32[]{:S(2)}, u32[]{:S(2)}) %collective-permute-start.26) | collective-permute-done | bytes 163872 | tf_op jit(solution)/shard_map/ppermute | solution.py:369
  326.7 4.1 %collective-permute-done.24 = bf16[320,256]{1,0:T(8,128)(2,1)S(1)} collective-permute-done((bf16[320,256]{1,0:T(8,128)(2,1)S(1)}, bf16[320,256]{1,0:T(8,128)(2,1)S(1)}, u32[]{:S(2)}, u32[]{:S(2)}) %collective-permute-start.24) | collective-permute-done | bytes 163872 | tf_op jit(solution)/shard_map/ppermute | solution.py:369
  330.8 6.7 %collective-permute-done.23 = bf16[320,256]{1,0:T(8,128)(2,1)S(1)} collective-permute-done((bf16[320,256]{1,0:T(8,128)(2,1)S(1)}, bf16[320,256]{1,0:T(8,128)(2,1)S(1)}, u32[]{:S(2)}, u32[]{:S(2)}) %collective-permute-start.23) | collective-permute-done | bytes 163872 | tf_op jit(solution)/shard_map/ppermute | solution.py:369
  337.6 3.1 collective-permute-start.29
  340.7 4.0 %collective-permute-done.29 = bf16[320,256]{1,0:T(8,128)(2,1)S(1)} collective-permute-done((bf16[320,256]{1,0:T(8,128)(2,1)S(1)}, bf16[320,256]{1,0:T(8,128)(2,1)S(1)}, u32[]{:S(2)}, u32[]{:S(2)}) %collective-permute-start.29) | collective-permute-done | bytes 163872 | tf_op jit(solution)/shard_map/ppermute | solution.py:387
  (82 shorter events, 37.1 us)
Async XLA Ops:
  6.5 161.8 %all-gather.5.cloned.1.call-start = ((), (), s32[]{:S(2)}) async-start(), calls=%async_computation.2 | async-start | bytes 21299200 | tf_op jit(solution)/shard_map/all_gather | solution.py:424
  8.5 250.3 %all-gather.7.cloned.1.call-start = ((), (), s32[]{:S(2)}) async-start(), calls=%async_computation.3 | async-start | bytes 1671168 | tf_op jit(solution)/shard_map/all_gather | solution.py:458
  10.7 68.5 %collective-permute-start = (bf16[2,8,320,256]{3,2,1,0:T(8,128)(2,1)S(1)}, bf16[2,8,320,256]{3,2,1,0:T(8,128)(2,1)}, u32[]{:S(2)}, u32[]{:S(2)}) collective-permute-start(bf16[2,8,320,256]{3,2,1,0:T(8,128)(2,1)S(1)} %pad_maximum_fusion), channel_id=1, source_target_pairs={{0,192},{192,0},{64,128},{128,64},{1,193},{193,1},{65,129},{129,65... | collective-permute-start | bytes 7864328 | tf_op jit(solution)/shard_map/ppermute | solution.py:387
  13.9 34.1 %collective-permute-start.3 = (bf16[2,320,256]{2,1,0:T(8,128)(2,1)S(1)}, bf16[2,320,256]{2,1,0:T(8,128)(2,1)S(1)}, u32[]{:S(2)}, u32[]{:S(2)}) collective-permute-start(bf16[2,320,256]{2,1,0:T(8,128)(2,1)S(1)} %pad_maximum_fusion.2), channel_id=1, source_target_pairs={{0,208},{16,192},{32,240},{48,224},{64,144},{80,128},{96,176},{112... | collective-permute-start | bytes 983048 | tf_op jit(solution)/shard_map/ppermute | solution.py:396
  16.9 39.9 %collective-permute-start.2 = (bf16[2,320,256]{2,1,0:T(8,128)(2,1)S(1)}, bf16[2,320,256]{2,1,0:T(8,128)(2,1)S(1)}, u32[]{:S(2)}, u32[]{:S(2)}) collective-permute-start(bf16[2,320,256]{2,1,0:T(8,128)(2,1)S(1)} %pad_maximum_fusion.2), channel_id=1, source_target_pairs={{0,16},{16,0},{32,48},{48,32},{1,17},{17,1},{33,49},{49,33},{2,18}... | collective-permute-start | bytes 983048 | tf_op jit(solution)/shard_map/ppermute | solution.py:391
  56.8 14.2 %collective-permute-start.5 = (bf16[2,2,320,256]{3,2,1,0:T(8,128)(2,1)S(1)}, bf16[2,2,320,256]{3,2,1,0:T(8,128)(2,1)S(1)}, u32[]{:S(2)}, u32[]{:S(2)}) collective-permute-start(bf16[2,2,320,256]{3,2,1,0:T(8,128)(2,1)S(1)} %pad_maximum_fusion.1.refs_6_.refs_8_), channel_id=1, source_target_pairs={{2,0},{4,2},{6,4},{0,6},{3,1},{5,3},{7,5},{1,7},{10,8},{12,10},{14... | collective-permute-start | bytes 1966088 | tf_op jit(solution)/shard_map/ppermute | solution.py:383
  57.5 13.6 %collective-permute-start.4 = (bf16[2,2,320,256]{3,2,1,0:T(8,128)(2,1)S(1)}, bf16[2,2,320,256]{3,2,1,0:T(8,128)(2,1)S(1)}, u32[]{:S(2)}, u32[]{:S(2)}) collective-permute-start(bf16[2,2,320,256]{3,2,1,0:T(8,128)(2,1)S(1)} %pad_maximum_fusion.1.refs_6_.refs_8_), channel_id=1, source_target_pairs={{1,0},{0,1},{3,2},{2,3},{5,4},{4,5},{7,6},{6,7},{9,8},{8,9},{11,10... | collective-permute-start | bytes 1966088 | tf_op jit(solution)/shard_map/ppermute | solution.py:383
  57.5 20.3 %collective-permute-start.11 = (bf16[2,2,320,256]{3,2,1,0:T(8,128)(2,1)S(1)}, bf16[2,2,320,256]{3,2,1,0:T(8,128)(2,1)S(1)}, u32[]{:S(2)}, u32[]{:S(2)}) collective-permute-start(bf16[2,2,320,256]{3,2,1,0:T(8,128)(2,1)S(1)} %pad_maximum_fusion.1.refs_6_.refs_8_), channel_id=1, source_target_pairs={{8,0},{0,8},{9,1},{1,9},{10,2},{2,10},{11,3},{3,11},{12,4},{4,12},... | collective-permute-start | bytes 1966088 | tf_op jit(solution)/shard_map/ppermute | solution.py:383
  58.8 24.3 %collective-permute-start.9 = (bf16[2,2,320,256]{3,2,1,0:T(8,128)(2,1)S(1)}, bf16[2,2,320,256]{3,2,1,0:T(8,128)(2,1)S(1)}, u32[]{:S(2)}, u32[]{:S(2)}) collective-permute-start(bf16[2,2,320,256]{3,2,1,0:T(8,128)(2,1)S(1)} %pad_maximum_fusion.1.refs_6_.refs_8_), channel_id=1, source_target_pairs={{6,0},{0,2},{2,4},{4,6},{7,1},{1,3},{3,5},{5,7},{14,8},{8,10},{10,... | collective-permute-start | bytes 1966088 | tf_op jit(solution)/shard_map/ppermute | solution.py:383
  71.1 12.1 %collective-permute-start.6 = (bf16[2,2,320,256]{3,2,1,0:T(8,128)(2,1)S(1)}, bf16[2,2,320,256]{3,2,1,0:T(8,128)(2,1)S(1)}, u32[]{:S(2)}, u32[]{:S(2)}) collective-permute-start(bf16[2,2,320,256]{3,2,1,0:T(8,128)(2,1)S(1)} %collective-permute-done.5.refs_8_.refs_10_), channel_id=1, source_target_pairs={{1,0},{0,1},{3,2},{2,3},{5,4},{4,5},{7,6},{6,7},{9,8},{8,9},{11,10... | collective-permute-start | bytes 1966088 | tf_op jit(solution)/shard_map/ppermute | solution.py:383
  71.1 33.1 %collective-permute-start.7 = (bf16[2,2,320,256]{3,2,1,0:T(8,128)(2,1)S(1)}, bf16[2,2,320,256]{3,2,1,0:T(8,128)(2,1)S(1)}, u32[]{:S(2)}, u32[]{:S(2)}) collective-permute-start(bf16[2,2,320,256]{3,2,1,0:T(8,128)(2,1)S(1)} %collective-permute-done.5.refs_8_.refs_10_), channel_id=1, source_target_pairs={{2,0},{4,2},{6,4},{0,6},{3,1},{5,3},{7,5},{1,7},{10,8},{12,10},{14... | collective-permute-start | bytes 1966088 | tf_op jit(solution)/shard_map/ppermute | solution.py:383
  77.8 34.2 %collective-permute-start.15 = (bf16[2,2,320,256]{3,2,1,0:T(8,128)(2,1)S(1)}, bf16[2,2,320,256]{3,2,1,0:T(8,128)(2,1)}, u32[]{:S(2)}, u32[]{:S(2)}) collective-permute-start(bf16[2,2,320,256]{3,2,1,0:T(8,128)(2,1)S(1)} %collective-permute-done.11.refs_14_.refs_16_), channel_id=1, source_target_pairs={{6,0},{0,2},{2,4},{4,6},{7,1},{1,3},{3,5},{5,7},{14,8},{8,10},{10,... | collective-permute-start | bytes 1966088 | tf_op jit(solution)/shard_map/ppermute | solution.py:383
  79.3 67.5 %collective-permute-start.1 = (bf16[2,8,320,256]{3,2,1,0:T(8,128)(2,1)}, bf16[2,8,320,256]{3,2,1,0:T(8,128)(2,1)}, u32[]{:S(2)}, u32[]{:S(2)}) collective-permute-start(bf16[2,8,320,256]{3,2,1,0:T(8,128)(2,1)} %collective-permute-done.refs_4_.refs_6_), channel_id=1, source_target_pairs={{1,0},{0,1},{3,2},{2,3},{5,4},{4,5},{7,6},{6,7},{9,8},{8,9},{11,10... | collective-permute-start | bytes 7864328 | tf_op jit(solution)/shard_map/ppermute | solution.py:383
  83.2 28.7 %collective-permute-start.10 = (bf16[2,2,320,256]{3,2,1,0:T(8,128)(2,1)S(1)}, bf16[2,2,320,256]{3,2,1,0:T(8,128)(2,1)S(1)}, u32[]{:S(2)}, u32[]{:S(2)}) collective-permute-start(bf16[2,2,320,256]{3,2,1,0:T(8,128)(2,1)S(1)} %collective-permute-done.9.refs_12_.refs_14_), channel_id=1, source_target_pairs={{1,0},{0,1},{3,2},{2,3},{5,4},{4,5},{7,6},{6,7},{9,8},{8,9},{11,10... | collective-permute-start | bytes 1966088 | tf_op jit(solution)/shard_map/ppermute | solution.py:383
  83.2 28.8 %collective-permute-start.12 = (bf16[2,2,320,256]{3,2,1,0:T(8,128)(2,1)S(1)}, bf16[2,2,320,256]{3,2,1,0:T(8,128)(2,1)S(1)}, u32[]{:S(2)}, u32[]{:S(2)}) collective-permute-start(bf16[2,2,320,256]{3,2,1,0:T(8,128)(2,1)S(1)} %collective-permute-done.11.refs_14_.refs_16_), channel_id=1, source_target_pairs={{1,0},{0,1},{3,2},{2,3},{5,4},{4,5},{7,6},{6,7},{9,8},{8,9},{11,10... | collective-permute-start | bytes 1966088 | tf_op jit(solution)/shard_map/ppermute | solution.py:383
  104.2 33.1 %collective-permute-start.13 = (bf16[2,2,320,256]{3,2,1,0:T(8,128)(2,1)S(1)}, bf16[2,2,320,256]{3,2,1,0:T(8,128)(2,1)}, u32[]{:S(2)}, u32[]{:S(2)}) collective-permute-start(bf16[2,2,320,256]{3,2,1,0:T(8,128)(2,1)S(1)} %collective-permute-done.11.refs_14_.refs_16_), channel_id=1, source_target_pairs={{2,0},{4,2},{6,4},{0,6},{3,1},{5,3},{7,5},{1,7},{10,8},{12,10},{14... | collective-permute-start | bytes 1966088 | tf_op jit(solution)/shard_map/ppermute | solution.py:383
  111.9 32.4 %collective-permute-start.16 = (bf16[2,2,320,256]{3,2,1,0:T(8,128)(2,1)}, bf16[2,2,320,256]{3,2,1,0:T(8,128)(2,1)}, u32[]{:S(2)}, u32[]{:S(2)}) collective-permute-start(bf16[2,2,320,256]{3,2,1,0:T(8,128)(2,1)} %collective-permute-done.15.refs_20_.refs_22_), channel_id=1, source_target_pairs={{6,0},{0,2},{2,4},{4,6},{7,1},{1,3},{3,5},{5,7},{14,8},{8,10},{10,... | collective-permute-start | bytes 1966088 | tf_op jit(solution)/shard_map/ppermute | solution.py:383
  111.9 34.5 %collective-permute-start.18 = (bf16[2,2,320,256]{3,2,1,0:T(8,128)(2,1)}, bf16[2,2,320,256]{3,2,1,0:T(8,128)(2,1)}, u32[]{:S(2)}, u32[]{:S(2)}) collective-permute-start(bf16[2,2,320,256]{3,2,1,0:T(8,128)(2,1)} %collective-permute-done.15.refs_20_.refs_22_), channel_id=1, source_target_pairs={{1,0},{0,1},{3,2},{2,3},{5,4},{4,5},{7,6},{6,7},{9,8},{8,9},{11,10... | collective-permute-start | bytes 1966088 | tf_op jit(solution)/shard_map/ppermute | solution.py:383
  112.0 34.4 %collective-permute-start.8 = (bf16[2,2,320,256]{3,2,1,0:T(8,128)(2,1)S(1)}, bf16[2,2,320,256]{3,2,1,0:T(8,128)(2,1)}, u32[]{:S(2)}, u32[]{:S(2)}) collective-permute-start(bf16[2,2,320,256]{3,2,1,0:T(8,128)(2,1)S(1)} %collective-permute-done.7.refs_10_.refs_12_), channel_id=1, source_target_pairs={{1,0},{0,1},{3,2},{2,3},{5,4},{4,5},{7,6},{6,7},{9,8},{8,9},{11,10... | collective-permute-start | bytes 1966088 | tf_op jit(solution)/shard_map/ppermute | solution.py:383
  137.3 9.1 %collective-permute-start.14 = (bf16[2,2,320,256]{3,2,1,0:T(8,128)(2,1)}, bf16[2,2,320,256]{3,2,1,0:T(8,128)(2,1)}, u32[]{:S(2)}, u32[]{:S(2)}) collective-permute-start(bf16[2,2,320,256]{3,2,1,0:T(8,128)(2,1)} %collective-permute-done.13.refs_16_.refs_18_), channel_id=1, source_target_pairs={{1,0},{0,1},{3,2},{2,3},{5,4},{4,5},{7,6},{6,7},{9,8},{8,9},{11,10... | collective-permute-start | bytes 1966088 | tf_op jit(solution)/shard_map/ppermute | solution.py:383
  159.5 8.2 %collective-permute-start.19 = (bf16[24,5120]{1,0:T(8,128)(2,1)S(1)}, bf16[24,5120]{1,0:T(8,128)(2,1)S(1)}, u32[]{:S(2)}, u32[]{:S(2)}) collective-permute-start(bf16[24,5120]{1,0:T(8,128)(2,1)S(1)} %get-tuple-element.40), channel_id=1, source_target_pairs={{0,64},{64,0},{128,192},{192,128},{1,65},{65,1},{129,193},{193,129... | collective-permute-start | bytes 737288 | tf_op jit(solution)/shard_map/ppermute | solution.py:374
  169.0 29.0 %collective-permute-start.20 = (bf16[24,5120]{1,0:T(8,128)(2,1)S(1)}, bf16[24,5120]{1,0:T(8,128)(2,1)S(1)}, u32[]{:S(2)}, u32[]{:S(2)}) collective-permute-start(bf16[24,5120]{1,0:T(8,128)(2,1)S(1)} %get-tuple-element.45), channel_id=1, source_target_pairs={{0,64},{64,0},{128,192},{192,128},{1,65},{65,1},{129,193},{193,129... | collective-permute-start | bytes 737288 | tf_op jit(solution)/shard_map/ppermute | solution.py:374
  222.7 7.1 %collective-permute-start.21 = (bf16[24,5120]{1,0:T(8,128)(2,1)S(1)}, bf16[24,5120]{1,0:T(8,128)(2,1)S(1)}, u32[]{:S(2)}, u32[]{:S(2)}) collective-permute-start(bf16[24,5120]{1,0:T(8,128)(2,1)S(1)} %get-tuple-element.52), channel_id=1, source_target_pairs={{0,64},{64,0},{128,192},{192,128},{1,65},{65,1},{129,193},{193,129... | collective-permute-start | bytes 737288 | tf_op jit(solution)/shard_map/ppermute | solution.py:374
  230.5 50.5 %all-to-all-start = ((bf16[16,4,24,320]{3,2,1,0:T(8,128)(2,1)}), bf16[16,4,24,320]{3,2,1,0:T(8,128)(2,1)S(1)}, u32[]{:S(2)}, u32[]{:S(2)}) async-start(bf16[16,4,24,320]{3,2,1,0:T(8,128)(2,1)} %get-tuple-element.63), calls=%async_computation | async-start | bytes 2359296 | tf_op jit(solution)/shard_map/all_to_all | solution.py:378
  258.8 10.1 %collective-permute-start.22 = (bf16[24,5120]{1,0:T(8,128)(2,1)S(1)}, bf16[24,5120]{1,0:T(8,128)(2,1)S(1)}, u32[]{:S(2)}, u32[]{:S(2)}) collective-permute-start(bf16[24,5120]{1,0:T(8,128)(2,1)S(1)} %get-tuple-element.60), channel_id=1, source_target_pairs={{0,64},{64,0},{128,192},{192,128},{1,65},{65,1},{129,193},{193,129... | collective-permute-start | bytes 737288 | tf_op jit(solution)/shard_map/ppermute | solution.py:374
  281.0 22.5 %all-to-all-start.1 = ((bf16[16,4,24,320]{3,2,1,0:T(8,128)(2,1)}), bf16[16,4,24,320]{3,2,1,0:T(8,128)(2,1)S(1)}, u32[]{:S(2)}, u32[]{:S(2)}) async-start(bf16[16,4,24,320]{3,2,1,0:T(8,128)(2,1)} %get-tuple-element.64), calls=%async_computation.1 | async-start | bytes 2359296 | tf_op jit(solution)/shard_map/all_to_all | solution.py:378
  288.7 27.5 %collective-permute-start.28 = (bf16[320,256]{1,0:T(8,128)(2,1)S(1)}, bf16[320,256]{1,0:T(8,128)(2,1)S(1)}, u32[]{:S(2)}, u32[]{:S(2)}) collective-permute-start(bf16[320,256]{1,0:T(8,128)(2,1)S(1)} %get-tuple-element.74), channel_id=1, source_target_pairs={{0,48},{16,0},{32,16},{48,32},{1,49},{17,1},{33,17},{49,33},{2,50}... | collective-permute-start | bytes 491528 | tf_op jit(solution)/shard_map/ppermute | solution.py:369
  297.4 22.7 %collective-permute-start.27 = (bf16[320,256]{1,0:T(8,128)(2,1)S(1)}, bf16[320,256]{1,0:T(8,128)(2,1)S(1)}, u32[]{:S(2)}, u32[]{:S(2)}) collective-permute-start(bf16[320,256]{1,0:T(8,128)(2,1)S(1)} %get-tuple-element.73), channel_id=1, source_target_pairs={{0,32},{16,48},{32,0},{48,16},{1,33},{17,49},{33,1},{49,17},{2,34}... | collective-permute-start | bytes 491528 | tf_op jit(solution)/shard_map/ppermute | solution.py:369
  297.4 26.5 %collective-permute-start.26 = (bf16[320,256]{1,0:T(8,128)(2,1)S(1)}, bf16[320,256]{1,0:T(8,128)(2,1)S(1)}, u32[]{:S(2)}, u32[]{:S(2)}) collective-permute-start(bf16[320,256]{1,0:T(8,128)(2,1)S(1)} %get-tuple-element.72), channel_id=1, source_target_pairs={{0,16},{16,32},{32,48},{48,0},{1,17},{17,33},{33,49},{49,1},{2,18}... | collective-permute-start | bytes 491528 | tf_op jit(solution)/shard_map/ppermute | solution.py:369
  305.5 21.2 %collective-permute-start.25 = (bf16[320,256]{1,0:T(8,128)(2,1)S(1)}, bf16[320,256]{1,0:T(8,128)(2,1)S(1)}, u32[]{:S(2)}, u32[]{:S(2)}) collective-permute-start(bf16[320,256]{1,0:T(8,128)(2,1)S(1)} %get-tuple-element.69), channel_id=1, source_target_pairs={{0,48},{16,0},{32,16},{48,32},{1,49},{17,1},{33,17},{49,33},{2,50}... | collective-permute-start | bytes 491528 | tf_op jit(solution)/shard_map/ppermute | solution.py:369
  315.7 15.0 %collective-permute-start.24 = (bf16[320,256]{1,0:T(8,128)(2,1)S(1)}, bf16[320,256]{1,0:T(8,128)(2,1)S(1)}, u32[]{:S(2)}, u32[]{:S(2)}) collective-permute-start(bf16[320,256]{1,0:T(8,128)(2,1)S(1)} %get-tuple-element.68), channel_id=1, source_target_pairs={{0,32},{16,48},{32,0},{48,16},{1,33},{17,49},{33,1},{49,17},{2,34}... | collective-permute-start | bytes 491528 | tf_op jit(solution)/shard_map/ppermute | solution.py:369
  316.2 21.3 %collective-permute-start.23 = (bf16[320,256]{1,0:T(8,128)(2,1)S(1)}, bf16[320,256]{1,0:T(8,128)(2,1)S(1)}, u32[]{:S(2)}, u32[]{:S(2)}) collective-permute-start(bf16[320,256]{1,0:T(8,128)(2,1)S(1)} %get-tuple-element.67), channel_id=1, source_target_pairs={{0,16},{16,32},{32,48},{48,0},{1,17},{17,33},{33,49},{49,1},{2,18}... | collective-permute-start | bytes 491528 | tf_op jit(solution)/shard_map/ppermute | solution.py:369
  (11 other events, 594.7 us)
Sparse Core Ops, SparseCore 0:
  10.1 151.1 all-gather.4
  210.5 48.2 all-gather.6

commit v7 on v5

--- a/solution.py
+++ b/solution.py
@@ -365,20 +365,27 @@
 
 def over_z(chunk_now):
     beside = lax.ppermute(chunk_now, "zh", [(0, 1), (1, 0), (2, 3), (3, 2)])
-    return jnp.stack([beside, from_ring(chunk_now, "zh", 2)])
-
-
-def over_x_first(near):
-    far = from_ring(near, "zl", 1)
-    return near, from_ring(near, "x", 1), from_ring(near, "x", -1), far
-
-
-def over_x_rest(near, near_up, near_down, far):
-    near_across = from_ring(near_up, "x", 1)
-    far_up, far_down = from_ring(far, "x", 1), from_ring(far, "x", -1)
-    far_across = from_ring(far_down, "x", -1)
+    route = []
+    for y in range(4):
+        for zh in range(4):
+            route.append((y * 4 + zh, (3 - y) * 4 + (zh ^ 1)))
+    return jnp.stack([beside, lax.ppermute(chunk_now, ("y", "zh"), route)])
+
+
+def over_x_sides(block):
+    return block, from_ring(block, "x", 1), from_ring(block, "x", -1)
+
+
+def over_x_across(near_side, far_side):
+    near, near_up, near_down = near_side
+    far, far_up, far_down = far_side
+    near_across, far_across = from_ring(near_up, "x", 1), from_ring(far_down, "x", -1)
+    return near, near_up, near_across, near_down, far, far_up, far_across, far_down
+
+
+def both_cores(blocks):
     parts = []
-    for one in (near, near_up, near_across, near_down, far, far_up, far_across, far_down):
+    for one in blocks:
         parts += [one, from_ring(one, "core", 1)]
     return tuple(parts)
 
@@ -408,15 +415,14 @@
     half_a = across_y(own_half(first_slot))
     near_a = over_z(own(first_slot))
     chunk_b, near_a = lax.optimization_barrier((own(1 - first_slot), near_a))
-    step_a = over_x_first(near_a)
     near_b = over_z(chunk_b)
-    near_b, step_a = lax.optimization_barrier((near_b, step_a))
-    rest_a = over_x_rest(*step_a)
+    blocks_a = over_x_across(over_x_sides(near_a), over_x_sides(from_ring(near_a, "zl", 1)))
+    far_b = from_ring(near_b, "zl", 1)
+    near_b, far_b, blocks_a = lax.optimization_barrier((near_b, far_b, blocks_a))
     half_b, half_a = lax.optimization_barrier((own_half(1 - first_slot), half_a))
     half_b = across_y(half_b)
-    w_a = own_layers + (half_a, from_ring(half_a, "core", 1)) + rest_a
-    rest_b = over_x_rest(*over_x_first(near_b))
-    w_b = own_layers + (half_b, from_ring(half_b, "core", 1)) + rest_b
+    w_a = own_layers + both_cores((half_a,)) + both_cores(blocks_a)
+    near_side, far_side = over_x_sides(near_b), over_x_sides(far_b)
 
     def flag(active, slot_now):
         reverse = slot_now == 1
@@ -431,8 +437,13 @@
     rows = jnp.pad(mine, ((0, ROWS - REAL), (0, 0)))
 
     rows, h_a, pre_a, act_a = run_forward(p_a, rows, w_a)
+    rows, near_side = lax.optimization_barrier((rows, near_side))
     rows = hop(rows)
+    rows, far_side = lax.optimization_barrier((rows, far_side))
+    parts_b = both_cores(over_x_across(near_side, far_side))
     rows, h_a, pre_a, act_a = run_forward(q_a, rows, w_a, (h_a, pre_a, act_a))
+    rows, half_b = lax.optimization_barrier((rows, half_b))
+    w_b = own_layers + both_cores((half_b,)) + parts_b
     rows, h_b, pre_b, act_b = run_forward(q_b, rows, w_b)
     rows = hop(rows)
     rows, h_b, pre_b, act_b = run_forward(p_b, rows, w_b, (h_b, pre_b, act_b))
@@ -441,6 +452,7 @@
     rows = hop(rows)
     rows, g_b = run_backward(q_b, rows, w_b, h_b, pre_b, held=g_b)
     rows, g_a = run_backward(q_a, rows, w_a, h_a, pre_a)
+    rows, act_all = lax.optimization_barrier((rows, act_all))
     rows = hop(rows)
     rows, g_a = run_backward(p_a, rows, w_a, h_a, pre_a, held=g_a, last=True)
     place = zh.astype(jnp.int32)[None]

time: 396 us -> 403 us (1.018)
  waiting for transfers between devices: 193 us -> 217 us
  starting transfers between devices: 116 us -> 95 us
    ppermute x0 -> x2, waiting for transfers between devices: none -> 46.6 us  [over_z(): return jnp.stack([beside, lax.ppermute(chunk_now, ('y', 'zh'), route)])]
    ppermute x4, starting transfers between devices: 56.5 us -> 24.1 us  [hop(): return lax.ppermute(rows, 'y', [(0, 1), (1, 0), (2, 3), (3, 2)])]
    ppermute x3, waiting for transfers between devices: 6.65 us -> 32.3 us  [across_y(): return lax.ppermute(block, 'y', [(0, 3), (3, 0), (1, 2), (2, 1)])]
    ppermute x2, waiting for transfers between devices: 32.5 us -> 7.2 us  [over_z(): beside = lax.ppermute(chunk_now, 'zh', [(0, 1), (1, 0), (2, 3), (3, 2)])]
    ppermute x34 -> x32, waiting for transfers between devices: 97.7 us -> 76 us  [from_ring(): lax.ppermute(block, axis, [((d + away) % count, d) for d in range(count)])]
    all_gather x1, waiting for transfers between devices: 0.01 us -> 10.4 us  [shards(): act_all = lax.all_gather(jnp.concatenate([act_a, act_b], axis=0), DP)]
    ppermute x0 -> x2, starting transfers between devices: none -> 8.54 us  [over_z(): return jnp.stack([beside, lax.ppermute(chunk_now, ('y', 'zh'), route)])]
    ppermute x4, waiting for transfers between devices: 27.6 us -> 19.8 us  [hop(): return lax.ppermute(rows, 'y', [(0, 1), (1, 0), (2, 3), (3, 2)])]
  transfers between devices with their start and end apart: 52 -> 52, of which waited for: 23 -> 30; matrix products, arithmetic and copies ran while one was open for 1% -> 1% of each run, Pallas kernels for 8% -> 11%
where the time goes in v7:
time: 403 us; the launch traced here: 397 us
  waiting for transfers between devices  217 us (54%)
  starting transfers between devices  95 us (24%)
  Pallas kernels  56.6 us (14%)
  between operations  14 us (3%)
  local copies, waits for them, and re-layouts  8.06 us (2%)
  other arithmetic  6.23 us (2%)
    ppermute x32, waiting for transfers between devices, from_ring(): lax.ppermute(block, axis, [((d + away) % count, d) for d in range(count)])  76 us
    ppermute x2, waiting for transfers between devices, over_z(): return jnp.stack([beside, lax.ppermute(chunk_now, ('y', 'zh'), route)])  46.6 us
    ppermute x3, waiting for transfers between devices, across_y(): return lax.ppermute(block, 'y', [(0, 3), (3, 0), (1, 2), (2, 1)])  32.3 us
    ppermute x32, starting transfers between devices, from_ring(): lax.ppermute(block, axis, [((d + away) % count, d) for d in range(count)])  26.9 us
    pallas_call x4, Pallas kernels, run_backward(): pl.pallas_call(lambda *refs: backward_kernel(*refs, source=source, aliase...  26.7 us
    pallas_call x4, Pallas kernels, run_forward(): pl.pallas_call(lambda *refs: forward_kernel(*refs, source=source, aliased...  25.9 us
    ppermute x4, starting transfers between devices, hop(): return lax.ppermute(rows, 'y', [(0, 1), (1, 0), (2, 3), (3, 2)])  24.1 us
    ppermute x4, waiting for transfers between devices, hop(): return lax.ppermute(rows, 'y', [(0, 1), (1, 0), (2, 3), (3, 2)])  19.8 us
  transfers between devices with their start and end apart: 52, of which 30 were waited for; matrix products, arithmetic and copies ran while one was open for 1% of the time, Pallas kernels for 11%

profile of v7, /device:TPU:2, one launch (start us, length us, event | category | flops | bytes accessed | tf_op | source)
XLA Modules:
  0.0 397.0 jit_solution(4413626604335880647)
XLA Ops:
  6.5 4.4 %constant_dynamic-slice_fusion = (bf16[1,1,2560,256]{3,2,1,0:T(8,128)(2,1)S(1)}, bf16[1,1,2560,256]{3,2,1,0:T(8,128)(2,1)}, bf16[1,1,2560,256]{3,2,1,0:T(8,128)(2,1)}, bf16[1,1,2560,256]{3,2,1,0:T(8,128)(2,1)S(1)}) fusion(bf16[1,2,5120,256]{3,2,1,0:T(8,128)(2,1)} %param.7, s32[]{:T(128)} %select_n.50, s32[]{:T(128)S(6)} %select_n.55, s32[]{:T(128)S(6)} %select_n.54, ...), kind=kLoop, calls=%fused_computation.16 | loop fusion | bytes 10485772 | tf_op jit(solution)/shard_map/dynamic_slice | solution.py:408
  20.4 24.3 %collective-permute-done.3 = bf16[2,320,256]{2,1,0:T(8,128)(2,1)S(1)} collective-permute-done((bf16[2,320,256]{2,1,0:T(8,128)(2,1)S(1)}, bf16[2,320,256]{2,1,0:T(8,128)(2,1)S(1)}, u32[]{:S(2)}, u32[]{:S(2)}) %collective-permute-start.3) | collective-permute-done | bytes 327712 | tf_op jit(solution)/shard_map/ppermute | solution.py:372
  44.7 4.1 %collective-permute-done.2 = bf16[2,320,256]{2,1,0:T(8,128)(2,1)S(1)} collective-permute-done((bf16[2,320,256]{2,1,0:T(8,128)(2,1)S(1)}, bf16[2,320,256]{2,1,0:T(8,128)(2,1)S(1)}, u32[]{:S(2)}, u32[]{:S(2)}) %collective-permute-start.2) | collective-permute-done | bytes 327712 | tf_op jit(solution)/shard_map/ppermute | solution.py:367
  49.9 14.7 %collective-permute-done.10.refs_14_.refs_16_ = bf16[2,2,320,256]{3,2,1,0:T(8,128)(2,1)S(1)} collective-permute-done((bf16[2,2,320,256]{3,2,1,0:T(8,128)(2,1)S(1)}, bf16[2,2,320,256]{3,2,1,0:T(8,128)(2,1)S(1)}, u32[]{:S(2)}, u32[]{:S(2)}) %collective-permute-start.10) | collective-permute-done | bytes 655392 | tf_op jit(solution)/shard_map/ppermute | solution.py:359
  66.1 5.5 %collective-permute-start.5 = (bf16[2,320,256]{2,1,0:T(8,128)(2,1)S(1)}, bf16[2,320,256]{2,1,0:T(8,128)(2,1)S(1)}, u32[]{:S(2)}, u32[]{:S(2)}) collective-permute-start(bf16[2,320,256]{2,1,0:T(8,128)(2,1)S(1)} %pad_maximum_fusion.4), channel_id=1, source_target_pairs={{0,208},{16,192},{32,240},{48,224},{64,144},{80,128},{96,176},{112... | collective-permute-start | bytes 983048 | tf_op jit(solution)/shard_map/ppermute | solution.py:372
  71.6 22.3 %collective-permute-done.5 = bf16[2,320,256]{2,1,0:T(8,128)(2,1)S(1)} collective-permute-done((bf16[2,320,256]{2,1,0:T(8,128)(2,1)S(1)}, bf16[2,320,256]{2,1,0:T(8,128)(2,1)S(1)}, u32[]{:S(2)}, u32[]{:S(2)}) %collective-permute-start.5) | collective-permute-done | bytes 327712 | tf_op jit(solution)/shard_map/ppermute | solution.py:372
  105.1 6.5 %collective-permute-done.9.refs_12_.refs_14_ = bf16[2,2,320,256]{3,2,1,0:T(8,128)(2,1)S(1)} collective-permute-done((bf16[2,2,320,256]{3,2,1,0:T(8,128)(2,1)S(1)}, bf16[2,2,320,256]{3,2,1,0:T(8,128)(2,1)S(1)}, u32[]{:S(2)}, u32[]{:S(2)}) %collective-permute-start.9) | collective-permute-done | bytes 655392 | tf_op jit(solution)/shard_map/ppermute | solution.py:359
  111.6 4.1 %collective-permute-done.6.refs_14_.refs_16_ = bf16[2,2,320,256]{3,2,1,0:T(8,128)(2,1)S(1)} collective-permute-done((bf16[2,2,320,256]{3,2,1,0:T(8,128)(2,1)S(1)}, bf16[2,2,320,256]{3,2,1,0:T(8,128)(2,1)S(1)}, u32[]{:S(2)}, u32[]{:S(2)}) %collective-permute-start.6) | collective-permute-done | bytes 655392 | tf_op jit(solution)/shard_map/ppermute | solution.py:359
  115.6 15.5 %collective-permute-done.8.refs_10_.refs_12_ = bf16[2,2,320,256]{3,2,1,0:T(8,128)(2,1)S(1)} collective-permute-done((bf16[2,2,320,256]{3,2,1,0:T(8,128)(2,1)S(1)}, bf16[2,2,320,256]{3,2,1,0:T(8,128)(2,1)S(1)}, u32[]{:S(2)}, u32[]{:S(2)}) %collective-permute-start.8) | collective-permute-done | bytes 655392 | tf_op jit(solution)/shard_map/ppermute | solution.py:359
  145.7 12.3 %forward_set.4 = (bf16[24,5120]{1,0:T(8,128)(2,1)S(1)}, bf16[4,24,5120]{2,1,0:T(8,128)(2,1)}, f32[4,24,256]{2,1,0:T(8,128)S(1)}, bf16[4,24,256]{2,1,0:T(8,128)(2,1)S(1)}) custom-call(s32[7]{0:T(128)S(1)} %stack.116.refs_0_, bf16[24,5120]{1,0:T(8,128)(2,1)S(1)} %pad.4.refs_1_, bf16[2,16,320,256]{3,2,1,0:T(8,128)(2,1)} %bitcast.32, ...), custom_call_target="tpu_custom_call" | custom-call | flops 125829120 | bytes 5242880 | tf_op jit(solution)/shard_map/forward_set/pallas_call | solution.py:170
  158.3 9.8 %collective-permute-done.25.refs_16_.refs_18_ = bf16[2,2,320,256]{3,2,1,0:T(8,128)(2,1)} collective-permute-done((bf16[2,2,320,256]{3,2,1,0:T(8,128)(2,1)S(1)}, bf16[2,2,320,256]{3,2,1,0:T(8,128)(2,1)}, u32[]{:S(2)}, u32[]{:S(2)}) %collective-permute-start.25) | collective-permute-done | bytes 655392 | tf_op jit(solution)/shard_map/ppermute | solution.py:359
  170.2 26.4 %collective-permute-done.27.refs_4_.refs_6_ = bf16[2,8,320,256]{3,2,1,0:T(8,128)(2,1)} collective-permute-done((bf16[2,8,320,256]{3,2,1,0:T(8,128)(2,1)}, bf16[2,8,320,256]{3,2,1,0:T(8,128)(2,1)}, u32[]{:S(2)}, u32[]{:S(2)}) %collective-permute-start.27) | collective-permute-done | bytes 2621472 | tf_op jit(solution)/shard_map/ppermute | solution.py:363
  197.7 9.0 %collective-permute-start.33 = (bf16[2,2,320,256]{3,2,1,0:T(8,128)(2,1)}, bf16[2,2,320,256]{3,2,1,0:T(8,128)(2,1)S(1)}, u32[]{:S(2)}, u32[]{:S(2)}) collective-permute-start(bf16[2,2,320,256]{3,2,1,0:T(8,128)(2,1)} %collective-permute-done.23.refs_12_.refs_14_), channel_id=1, source_target_pairs={{1,0},{0,1},{3,2},{2,3},{5,4},{4,5},{7,6},{6,7},{9,8},{8,9},{11,10... | collective-permute-start | bytes 1966088 | tf_op jit(solution)/shard_map/ppermute | solution.py:359
  208.5 6.1 %collective-permute-done.31.refs_10_.refs_12_ = bf16[2,2,320,256]{3,2,1,0:T(8,128)(2,1)} collective-permute-done((bf16[2,2,320,256]{3,2,1,0:T(8,128)(2,1)}, bf16[2,2,320,256]{3,2,1,0:T(8,128)(2,1)}, u32[]{:S(2)}, u32[]{:S(2)}) %collective-permute-start.31) | collective-permute-done | bytes 655392 | tf_op jit(solution)/shard_map/ppermute | solution.py:359
  215.4 9.9 %collective-permute-done.36.refs_18_.refs_20_ = bf16[2,2,320,256]{3,2,1,0:T(8,128)(2,1)} collective-permute-done((bf16[2,2,320,256]{3,2,1,0:T(8,128)(2,1)}, bf16[2,2,320,256]{3,2,1,0:T(8,128)(2,1)}, u32[]{:S(2)}, u32[]{:S(2)}) %collective-permute-start.36) | collective-permute-done | bytes 655392 | tf_op jit(solution)/shard_map/ppermute | solution.py:359
  228.5 9.3 %collective-permute-start.39 = (bf16[24,5120]{1,0:T(8,128)(2,1)S(1)}, bf16[24,5120]{1,0:T(8,128)(2,1)S(1)}, u32[]{:S(2)}, u32[]{:S(2)}) collective-permute-start(bf16[24,5120]{1,0:T(8,128)(2,1)S(1)} %get-tuple-element.93), channel_id=1, source_target_pairs={{0,64},{64,0},{128,192},{192,128},{1,65},{65,1},{129,193},{193,129... | collective-permute-start | bytes 737288 | tf_op jit(solution)/shard_map/ppermute | solution.py:350
  237.8 6.2 %collective-permute-done.39.refs_1_ = bf16[24,5120]{1,0:T(8,128)(2,1)S(1)} collective-permute-done((bf16[24,5120]{1,0:T(8,128)(2,1)S(1)}, bf16[24,5120]{1,0:T(8,128)(2,1)S(1)}, u32[]{:S(2)}, u32[]{:S(2)}) %collective-permute-start.39) | collective-permute-done | bytes 245792 | tf_op jit(solution)/shard_map/ppermute | solution.py:350
  244.0 12.3 %forward_set.7 = (bf16[24,5120]{1,0:T(8,128)(2,1)S(1)}, bf16[4,24,5120]{2,1,0:T(8,128)(2,1)}, f32[4,24,256]{2,1,0:T(8,128)S(1)}, bf16[4,24,256]{2,1,0:T(8,128)(2,1)S(1)}) custom-call(s32[7]{0:T(128)S(1)} %stack.124.refs_0_, bf16[24,5120]{1,0:T(8,128)(2,1)S(1)} %collective-permute-done.39.refs_1_, ...), custom_call_target="tpu_custom_call", output_to_operand_aliasing={{1}: (22, {}), {2}: (23, {}), {3}: (24, {})} | custom-call | flops 125829120 | bytes 5242880 | tf_op jit(solution)/shard_map/forward_set/pallas_call | solution.py:170
  257.0 13.1 %backward_set.4 = (bf16[24,5120]{1,0:T(8,128)(2,1)S(1)}, bf16[16,4,24,320]{3,2,1,0:T(8,128)(2,1)}) custom-call(s32[7]{0:T(128)S(1)} %stack.124.refs_0_, bf16[24,5120]{1,0:T(8,128)(2,1)S(1)} %get-tuple-element.97.refs_1_, bf16[4,24,5120]{2,1,0:T(8,128)(2,1)} %get-tuple-element.98.refs_2_, f32[4,24,256]{2,1,0:T(8,128)S(1)} %get-tuple-element.99.refs_3_, ...), custom_call_target="tpu_custom_call" | custom-call | flops 125829120 | bytes 5242880 | tf_op jit(solution)/shard_map/backward_set/pallas_call | solution.py:291
  270.2 7.4 %collective-permute-done.40.refs_1_ = bf16[24,5120]{1,0:T(8,128)(2,1)S(1)} collective-permute-done((bf16[24,5120]{1,0:T(8,128)(2,1)S(1)}, bf16[24,5120]{1,0:T(8,128)(2,1)S(1)}, u32[]{:S(2)}, u32[]{:S(2)}) %collective-permute-start.40) | collective-permute-done | bytes 245792 | tf_op jit(solution)/shard_map/ppermute | solution.py:350
  278.3 6.5 %all-to-all-start = ((bf16[16,4,24,320]{3,2,1,0:T(8,128)(2,1)}), bf16[16,4,24,320]{3,2,1,0:T(8,128)(2,1)S(1)}, u32[]{:S(2)}, u32[]{:S(2)}) async-start(bf16[16,4,24,320]{3,2,1,0:T(8,128)(2,1)} %get-tuple-element.111), calls=%async_computation | async-start | bytes 2359296 | tf_op jit(solution)/shard_map/all_to_all | solution.py:354
  285.6 10.4 %all-gather.3.cloned.1.call-done = bf16[128,24,256]{2,1,0:T(8,128)(2,1)} async-done(((bf16[8,24,256]{2,1,0:T(8,128)(2,1)}), bf16[128,24,256]{2,1,0:T(8,128)(2,1)}) %all-gather.3.cloned.1.call-update) | async-done | bytes 1572880 | tf_op jit(solution)/shard_map/all_gather | solution.py:450
  296.0 14.7 %collective-permute-start.41 = (bf16[24,5120]{1,0:T(8,128)(2,1)S(1)}, bf16[24,5120]{1,0:T(8,128)(2,1)S(1)}, u32[]{:S(2)}, u32[]{:S(2)}) collective-permute-start(bf16[24,5120]{1,0:T(8,128)(2,1)S(1)} %get-tuple-element.108), channel_id=1, source_target_pairs={{0,64},{64,0},{128,192},{192,128},{1,65},{65,1},{129,193},{193,129... | collective-permute-start | bytes 737288 | tf_op jit(solution)/shard_map/ppermute | solution.py:350
  310.7 6.3 %collective-permute-done.41.refs_1_ = bf16[24,5120]{1,0:T(8,128)(2,1)S(1)} collective-permute-done((bf16[24,5120]{1,0:T(8,128)(2,1)S(1)}, bf16[24,5120]{1,0:T(8,128)(2,1)S(1)}, u32[]{:S(2)}, u32[]{:S(2)}) %collective-permute-start.41) | collective-permute-done | bytes 245792 | tf_op jit(solution)/shard_map/ppermute | solution.py:350
  317.0 12.1 %backward_set.7 = (bf16[24,5120]{1,0:T(8,128)(2,1)}, bf16[16,4,24,320]{3,2,1,0:T(8,128)(2,1)}) custom-call(s32[7]{0:T(128)S(1)} %stack.116.refs_0_, bf16[24,5120]{1,0:T(8,128)(2,1)S(1)} %collective-permute-done.41.refs_1_, bf16[4,24,5120]{2,1,0:T(8,128)(2,1)} %get-tuple-element.103.refs_2_, ...), custom_call_target="tpu_custom_call", output_to_operand_aliasing={{1}: (24, {})} | custom-call | flops 125829120 | bytes 5242880 | tf_op jit(solution)/shard_map/backward_set/pallas_call | solution.py:291
  329.1 5.8 %all-to-all-start.1 = ((bf16[16,4,24,320]{3,2,1,0:T(8,128)(2,1)}), bf16[16,4,24,320]{3,2,1,0:T(8,128)(2,1)S(1)}, u32[]{:S(2)}, u32[]{:S(2)}) async-start(bf16[16,4,24,320]{3,2,1,0:T(8,128)(2,1)} %get-tuple-element.112), calls=%async_computation.1 | async-start | bytes 2359296 | tf_op jit(solution)/shard_map/all_to_all | solution.py:354
  336.8 5.0 %collective-permute-start.47 = (bf16[320,256]{1,0:T(8,128)(2,1)S(1)}, bf16[320,256]{1,0:T(8,128)(2,1)S(1)}, u32[]{:S(2)}, u32[]{:S(2)}) collective-permute-start(bf16[320,256]{1,0:T(8,128)(2,1)S(1)} %get-tuple-element.122), channel_id=1, source_target_pairs={{0,48},{16,0},{32,16},{48,32},{1,49},{17,1},{33,17},{49,33},{2,50}... | collective-permute-start | bytes 491528 | tf_op jit(solution)/shard_map/ppermute | solution.py:345
  344.3 8.1 %all-to-all-done.1.refs_1_ = bf16[16,4,24,320]{3,2,1,0:T(8,128)(2,1)S(1)} async-done(((bf16[16,4,24,320]{3,2,1,0:T(8,128)(2,1)}), bf16[16,4,24,320]{3,2,1,0:T(8,128)(2,1)S(1)}, u32[]{:S(2)}, u32[]{:S(2)}) %all-to-all-start.1) | async-done | bytes 983072 | tf_op jit(solution)/shard_map/all_to_all | solution.py:354
  354.4 8.3 %collective-permute-start.44 = (bf16[320,256]{1,0:T(8,128)(2,1)S(1)}, bf16[320,256]{1,0:T(8,128)(2,1)S(1)}, u32[]{:S(2)}, u32[]{:S(2)}) collective-permute-start(bf16[320,256]{1,0:T(8,128)(2,1)S(1)} %get-tuple-element.117), channel_id=1, source_target_pairs={{0,48},{16,0},{32,16},{48,32},{1,49},{17,1},{33,17},{49,33},{2,50}... | collective-permute-start | bytes 491528 | tf_op jit(solution)/shard_map/ppermute | solution.py:345
  365.2 5.0 %collective-permute-done.45 = bf16[320,256]{1,0:T(8,128)(2,1)S(1)} collective-permute-done((bf16[320,256]{1,0:T(8,128)(2,1)S(1)}, bf16[320,256]{1,0:T(8,128)(2,1)S(1)}, u32[]{:S(2)}, u32[]{:S(2)}) %collective-permute-start.45) | collective-permute-done | bytes 163872 | tf_op jit(solution)/shard_map/ppermute | solution.py:345
  370.2 8.3 %collective-permute-done.44 = bf16[320,256]{1,0:T(8,128)(2,1)S(1)} collective-permute-done((bf16[320,256]{1,0:T(8,128)(2,1)S(1)}, bf16[320,256]{1,0:T(8,128)(2,1)S(1)}, u32[]{:S(2)}, u32[]{:S(2)}) %collective-permute-start.44) | collective-permute-done | bytes 163872 | tf_op jit(solution)/shard_map/ppermute | solution.py:345
  383.3 5.8 %collective-permute-done.48 = bf16[320,256]{1,0:T(8,128)(2,1)S(1)} collective-permute-done((bf16[320,256]{1,0:T(8,128)(2,1)S(1)}, bf16[320,256]{1,0:T(8,128)(2,1)S(1)}, u32[]{:S(2)}, u32[]{:S(2)}) %collective-permute-start.48) | collective-permute-done | bytes 163872 | tf_op jit(solution)/shard_map/ppermute | solution.py:363
  (147 shorter events, 63.5 us)
Async XLA Ops:
  6.5 289.5 %all-gather.3.cloned.1.call-start = ((), (), s32[]{:S(2)}) async-start(), calls=%async_computation.2 | async-start | bytes 1671168 | tf_op jit(solution)/shard_map/all_gather | solution.py:450
  12.6 90.4 %collective-permute-start = (bf16[2,8,320,256]{3,2,1,0:T(8,128)(2,1)}, bf16[2,8,320,256]{3,2,1,0:T(8,128)(2,1)}, u32[]{:S(2)}, u32[]{:S(2)}) collective-permute-start(bf16[2,8,320,256]{3,2,1,0:T(8,128)(2,1)} %pad_maximum_fusion.1), channel_id=1, source_target_pairs={{0,192},{192,0},{64,128},{128,64},{1,193},{193,1},{65,129},{129,65... | collective-permute-start | bytes 7864328 | tf_op jit(solution)/shard_map/ppermute | solution.py:363
  16.9 27.8 %collective-permute-start.3 = (bf16[2,320,256]{2,1,0:T(8,128)(2,1)S(1)}, bf16[2,320,256]{2,1,0:T(8,128)(2,1)S(1)}, u32[]{:S(2)}, u32[]{:S(2)}) collective-permute-start(bf16[2,320,256]{2,1,0:T(8,128)(2,1)S(1)} %pad_maximum_fusion.5), channel_id=1, source_target_pairs={{0,208},{16,192},{32,240},{48,224},{64,144},{80,128},{96,176},{112... | collective-permute-start | bytes 983048 | tf_op jit(solution)/shard_map/ppermute | solution.py:372
  19.9 28.9 %collective-permute-start.2 = (bf16[2,320,256]{2,1,0:T(8,128)(2,1)S(1)}, bf16[2,320,256]{2,1,0:T(8,128)(2,1)S(1)}, u32[]{:S(2)}, u32[]{:S(2)}) collective-permute-start(bf16[2,320,256]{2,1,0:T(8,128)(2,1)S(1)} %pad_maximum_fusion.5), channel_id=1, source_target_pairs={{0,16},{16,0},{32,48},{48,32},{1,17},{17,1},{33,49},{49,33},{2,18}... | collective-permute-start | bytes 983048 | tf_op jit(solution)/shard_map/ppermute | solution.py:367
  49.3 51.4 %collective-permute-start.7 = (bf16[2,2,320,256]{3,2,1,0:T(8,128)(2,1)S(1)}, bf16[2,2,320,256]{3,2,1,0:T(8,128)(2,1)S(1)}, u32[]{:S(2)}, u32[]{:S(2)}) collective-permute-start(bf16[2,2,320,256]{3,2,1,0:T(8,128)(2,1)S(1)} %pad_maximum_fusion.2.refs_6_.refs_8_), channel_id=1, source_target_pairs={{2,0},{4,2},{6,4},{0,6},{3,1},{5,3},{7,5},{1,7},{10,8},{12,10},{14... | collective-permute-start | bytes 1966088 | tf_op jit(solution)/shard_map/ppermute | solution.py:359
  64.6 36.7 %collective-permute-start.12 = (bf16[2,2,320,256]{3,2,1,0:T(8,128)(2,1)S(1)}, bf16[2,2,320,256]{3,2,1,0:T(8,128)(2,1)S(1)}, u32[]{:S(2)}, u32[]{:S(2)}) collective-permute-start(bf16[2,2,320,256]{3,2,1,0:T(8,128)(2,1)S(1)} %collective-permute-done.10.refs_14_.refs_16_), channel_id=1, source_target_pairs={{6,0},{0,2},{2,4},{4,6},{7,1},{1,3},{3,5},{5,7},{14,8},{8,10},{10,... | collective-permute-start | bytes 1966088 | tf_op jit(solution)/shard_map/ppermute | solution.py:359
  66.1 27.8 %collective-permute-start.5 = (bf16[2,320,256]{2,1,0:T(8,128)(2,1)S(1)}, bf16[2,320,256]{2,1,0:T(8,128)(2,1)S(1)}, u32[]{:S(2)}, u32[]{:S(2)}) collective-permute-start(bf16[2,320,256]{2,1,0:T(8,128)(2,1)S(1)} %pad_maximum_fusion.4), channel_id=1, source_target_pairs={{0,208},{16,192},{32,240},{48,224},{64,144},{80,128},{96,176},{112... | collective-permute-start | bytes 983048 | tf_op jit(solution)/shard_map/ppermute | solution.py:372
  71.6 26.6 %collective-permute-start.4 = (bf16[2,320,256]{2,1,0:T(8,128)(2,1)S(1)}, bf16[2,320,256]{2,1,0:T(8,128)(2,1)S(1)}, u32[]{:S(2)}, u32[]{:S(2)}) collective-permute-start(bf16[2,320,256]{2,1,0:T(8,128)(2,1)S(1)} %pad_maximum_fusion.4), channel_id=1, source_target_pairs={{0,16},{16,0},{32,48},{48,32},{1,17},{17,1},{33,49},{49,33},{2,18}... | collective-permute-start | bytes 983048 | tf_op jit(solution)/shard_map/ppermute | solution.py:367
  93.9 17.7 %collective-permute-start.9 = (bf16[2,2,320,256]{3,2,1,0:T(8,128)(2,1)S(1)}, bf16[2,2,320,256]{3,2,1,0:T(8,128)(2,1)S(1)}, u32[]{:S(2)}, u32[]{:S(2)}) collective-permute-start(bf16[2,2,320,256]{3,2,1,0:T(8,128)(2,1)S(1)} %pad_maximum_fusion.2.refs_6_.refs_8_), channel_id=1, source_target_pairs={{6,0},{0,2},{2,4},{4,6},{7,1},{1,3},{3,5},{5,7},{14,8},{8,10},{10,... | collective-permute-start | bytes 1966088 | tf_op jit(solution)/shard_map/ppermute | solution.py:359
  98.3 17.4 %collective-permute-start.6 = (bf16[2,2,320,256]{3,2,1,0:T(8,128)(2,1)S(1)}, bf16[2,2,320,256]{3,2,1,0:T(8,128)(2,1)S(1)}, u32[]{:S(2)}, u32[]{:S(2)}) collective-permute-start(bf16[2,2,320,256]{3,2,1,0:T(8,128)(2,1)S(1)} %pad_maximum_fusion.3.refs_6_.refs_8_), channel_id=1, source_target_pairs={{8,0},{0,8},{9,1},{1,9},{10,2},{2,10},{11,3},{3,11},{12,4},{4,12},... | collective-permute-start | bytes 1966088 | tf_op jit(solution)/shard_map/ppermute | solution.py:359
  100.8 30.4 %collective-permute-start.11 = (bf16[2,2,320,256]{3,2,1,0:T(8,128)(2,1)S(1)}, bf16[2,2,320,256]{3,2,1,0:T(8,128)(2,1)S(1)}, u32[]{:S(2)}, u32[]{:S(2)}) collective-permute-start(bf16[2,2,320,256]{3,2,1,0:T(8,128)(2,1)S(1)} %collective-permute-done.10.refs_14_.refs_16_), channel_id=1, source_target_pairs={{2,0},{4,2},{6,4},{0,6},{3,1},{5,3},{7,5},{1,7},{10,8},{12,10},{14... | collective-permute-start | bytes 1966088 | tf_op jit(solution)/shard_map/ppermute | solution.py:359
  101.3 29.8 %collective-permute-start.8 = (bf16[2,2,320,256]{3,2,1,0:T(8,128)(2,1)S(1)}, bf16[2,2,320,256]{3,2,1,0:T(8,128)(2,1)S(1)}, u32[]{:S(2)}, u32[]{:S(2)}) collective-permute-start(bf16[2,2,320,256]{3,2,1,0:T(8,128)(2,1)S(1)} %collective-permute-done.7.refs_8_.refs_10_), channel_id=1, source_target_pairs={{2,0},{4,2},{6,4},{0,6},{3,1},{5,3},{7,5},{1,7},{10,8},{12,10},{14... | collective-permute-start | bytes 1966088 | tf_op jit(solution)/shard_map/ppermute | solution.py:359
  103.1 28.1 %collective-permute-start.13 = (bf16[2,2,320,256]{3,2,1,0:T(8,128)(2,1)S(1)}, bf16[2,2,320,256]{3,2,1,0:T(8,128)(2,1)S(1)}, u32[]{:S(2)}, u32[]{:S(2)}) collective-permute-start(bf16[2,2,320,256]{3,2,1,0:T(8,128)(2,1)S(1)} %collective-permute-done.12.refs_20_.refs_22_), channel_id=1, source_target_pairs={{6,0},{0,2},{2,4},{4,6},{7,1},{1,3},{3,5},{5,7},{14,8},{8,10},{10,... | collective-permute-start | bytes 1966088 | tf_op jit(solution)/shard_map/ppermute | solution.py:359
  111.6 33.0 %collective-permute-start.1 = (bf16[2,8,320,256]{3,2,1,0:T(8,128)(2,1)}, bf16[2,8,320,256]{3,2,1,0:T(8,128)(2,1)}, u32[]{:S(2)}, u32[]{:S(2)}) collective-permute-start(bf16[2,8,320,256]{3,2,1,0:T(8,128)(2,1)} %collective-permute-done.refs_4_.refs_6_), channel_id=1, source_target_pairs={{1,0},{0,1},{3,2},{2,3},{5,4},{4,5},{7,6},{6,7},{9,8},{8,9},{11,10... | collective-permute-start | bytes 7864328 | tf_op jit(solution)/shard_map/ppermute | solution.py:359
  136.2 60.4 %collective-permute-start.27 = (bf16[2,8,320,256]{3,2,1,0:T(8,128)(2,1)}, bf16[2,8,320,256]{3,2,1,0:T(8,128)(2,1)}, u32[]{:S(2)}, u32[]{:S(2)}) collective-permute-start(bf16[2,8,320,256]{3,2,1,0:T(8,128)(2,1)} %pad_maximum_fusion), channel_id=1, source_target_pairs={{0,192},{192,0},{64,128},{128,64},{1,193},{193,1},{65,129},{129,65... | collective-permute-start | bytes 7864328 | tf_op jit(solution)/shard_map/ppermute | solution.py:363
  137.1 21.0 %collective-permute-start.22 = (bf16[2,2,320,256]{3,2,1,0:T(8,128)(2,1)S(1)}, bf16[2,2,320,256]{3,2,1,0:T(8,128)(2,1)}, u32[]{:S(2)}, u32[]{:S(2)}) collective-permute-start(bf16[2,2,320,256]{3,2,1,0:T(8,128)(2,1)S(1)} %pad_maximum_fusion.3.refs_6_.refs_8_), channel_id=1, source_target_pairs={{2,0},{4,2},{6,4},{0,6},{3,1},{5,3},{7,5},{1,7},{10,8},{12,10},{14... | collective-permute-start | bytes 1966088 | tf_op jit(solution)/shard_map/ppermute | solution.py:359
  138.1 20.0 %collective-permute-start.23 = (bf16[2,2,320,256]{3,2,1,0:T(8,128)(2,1)S(1)}, bf16[2,2,320,256]{3,2,1,0:T(8,128)(2,1)}, u32[]{:S(2)}, u32[]{:S(2)}) collective-permute-start(bf16[2,2,320,256]{3,2,1,0:T(8,128)(2,1)S(1)} %pad_maximum_fusion.3.refs_6_.refs_8_), channel_id=1, source_target_pairs={{6,0},{0,2},{2,4},{4,6},{7,1},{1,3},{3,5},{5,7},{14,8},{8,10},{10,... | collective-permute-start | bytes 1966088 | tf_op jit(solution)/shard_map/ppermute | solution.py:359
  142.4 25.6 %collective-permute-start.25 = (bf16[2,2,320,256]{3,2,1,0:T(8,128)(2,1)S(1)}, bf16[2,2,320,256]{3,2,1,0:T(8,128)(2,1)}, u32[]{:S(2)}, u32[]{:S(2)}) collective-permute-start(bf16[2,2,320,256]{3,2,1,0:T(8,128)(2,1)S(1)} %copy-done.11), channel_id=1, source_target_pairs={{2,0},{4,2},{6,4},{0,6},{3,1},{5,3},{7,5},{1,7},{10,8},{12,10},{14... | collective-permute-start | bytes 1966088 | tf_op jit(solution)/shard_map/ppermute | solution.py:359
  144.6 24.9 %collective-permute-start.26 = (bf16[2,2,320,256]{3,2,1,0:T(8,128)(2,1)S(1)}, bf16[2,2,320,256]{3,2,1,0:T(8,128)(2,1)}, u32[]{:S(2)}, u32[]{:S(2)}) collective-permute-start(bf16[2,2,320,256]{3,2,1,0:T(8,128)(2,1)S(1)} %copy-done.11), channel_id=1, source_target_pairs={{6,0},{0,2},{2,4},{4,6},{7,1},{1,3},{3,5},{5,7},{14,8},{8,10},{10,... | collective-permute-start | bytes 1966088 | tf_op jit(solution)/shard_map/ppermute | solution.py:359
  196.6 31.2 %collective-permute-start.28 = (bf16[2,8,320,256]{3,2,1,0:T(8,128)(2,1)}, bf16[2,8,320,256]{3,2,1,0:T(8,128)(2,1)}, u32[]{:S(2)}, u32[]{:S(2)}) collective-permute-start(bf16[2,8,320,256]{3,2,1,0:T(8,128)(2,1)} %collective-permute-done.27.refs_4_.refs_6_), channel_id=1, source_target_pairs={{1,0},{0,1},{3,2},{2,3},{5,4},{4,5},{7,6},{6,7},{9,8},{8,9},{11,10... | collective-permute-start | bytes 7864328 | tf_op jit(solution)/shard_map/ppermute | solution.py:359
  197.1 17.5 %collective-permute-start.31 = (bf16[2,2,320,256]{3,2,1,0:T(8,128)(2,1)}, bf16[2,2,320,256]{3,2,1,0:T(8,128)(2,1)}, u32[]{:S(2)}, u32[]{:S(2)}) collective-permute-start(bf16[2,2,320,256]{3,2,1,0:T(8,128)(2,1)} %collective-permute-done.22.refs_8_.refs_10_), channel_id=1, source_target_pairs={{2,0},{4,2},{6,4},{0,6},{3,1},{5,3},{7,5},{1,7},{10,8},{12,10},{14... | collective-permute-start | bytes 1966088 | tf_op jit(solution)/shard_map/ppermute | solution.py:359
  197.7 16.9 %collective-permute-start.33 = (bf16[2,2,320,256]{3,2,1,0:T(8,128)(2,1)}, bf16[2,2,320,256]{3,2,1,0:T(8,128)(2,1)S(1)}, u32[]{:S(2)}, u32[]{:S(2)}) collective-permute-start(bf16[2,2,320,256]{3,2,1,0:T(8,128)(2,1)} %collective-permute-done.23.refs_12_.refs_14_), channel_id=1, source_target_pairs={{1,0},{0,1},{3,2},{2,3},{5,4},{4,5},{7,6},{6,7},{9,8},{8,9},{11,10... | collective-permute-start | bytes 1966088 | tf_op jit(solution)/shard_map/ppermute | solution.py:359
  207.0 18.4 %collective-permute-start.36 = (bf16[2,2,320,256]{3,2,1,0:T(8,128)(2,1)}, bf16[2,2,320,256]{3,2,1,0:T(8,128)(2,1)}, u32[]{:S(2)}, u32[]{:S(2)}) collective-permute-start(bf16[2,2,320,256]{3,2,1,0:T(8,128)(2,1)} %collective-permute-done.26.refs_20_.refs_22_), channel_id=1, source_target_pairs={{6,0},{0,2},{2,4},{4,6},{7,1},{1,3},{3,5},{5,7},{14,8},{8,10},{10,... | collective-permute-start | bytes 1966088 | tf_op jit(solution)/shard_map/ppermute | solution.py:359
  278.3 50.8 %all-to-all-start = ((bf16[16,4,24,320]{3,2,1,0:T(8,128)(2,1)}), bf16[16,4,24,320]{3,2,1,0:T(8,128)(2,1)S(1)}, u32[]{:S(2)}, u32[]{:S(2)}) async-start(bf16[16,4,24,320]{3,2,1,0:T(8,128)(2,1)} %get-tuple-element.111), calls=%async_computation | async-start | bytes 2359296 | tf_op jit(solution)/shard_map/all_to_all | solution.py:354
  296.0 20.9 %collective-permute-start.41 = (bf16[24,5120]{1,0:T(8,128)(2,1)S(1)}, bf16[24,5120]{1,0:T(8,128)(2,1)S(1)}, u32[]{:S(2)}, u32[]{:S(2)}) collective-permute-start(bf16[24,5120]{1,0:T(8,128)(2,1)S(1)} %get-tuple-element.108), channel_id=1, source_target_pairs={{0,64},{64,0},{128,192},{192,128},{1,65},{65,1},{129,193},{193,129... | collective-permute-start | bytes 737288 | tf_op jit(solution)/shard_map/ppermute | solution.py:350
  329.1 23.4 %all-to-all-start.1 = ((bf16[16,4,24,320]{3,2,1,0:T(8,128)(2,1)}), bf16[16,4,24,320]{3,2,1,0:T(8,128)(2,1)S(1)}, u32[]{:S(2)}, u32[]{:S(2)}) async-start(bf16[16,4,24,320]{3,2,1,0:T(8,128)(2,1)} %get-tuple-element.112), calls=%async_computation.1 | async-start | bytes 2359296 | tf_op jit(solution)/shard_map/all_to_all | solution.py:354
  336.8 25.9 %collective-permute-start.47 = (bf16[320,256]{1,0:T(8,128)(2,1)S(1)}, bf16[320,256]{1,0:T(8,128)(2,1)S(1)}, u32[]{:S(2)}, u32[]{:S(2)}) collective-permute-start(bf16[320,256]{1,0:T(8,128)(2,1)S(1)} %get-tuple-element.122), channel_id=1, source_target_pairs={{0,48},{16,0},{32,16},{48,32},{1,49},{17,1},{33,17},{49,33},{2,50}... | collective-permute-start | bytes 491528 | tf_op jit(solution)/shard_map/ppermute | solution.py:345
  341.8 23.4 %collective-permute-start.46 = (bf16[320,256]{1,0:T(8,128)(2,1)S(1)}, bf16[320,256]{1,0:T(8,128)(2,1)S(1)}, u32[]{:S(2)}, u32[]{:S(2)}) collective-permute-start(bf16[320,256]{1,0:T(8,128)(2,1)S(1)} %get-tuple-element.121), channel_id=1, source_target_pairs={{0,32},{16,48},{32,0},{48,16},{1,33},{17,49},{33,1},{49,17},{2,34}... | collective-permute-start | bytes 491528 | tf_op jit(solution)/shard_map/ppermute | solution.py:345
  342.6 27.7 %collective-permute-start.45 = (bf16[320,256]{1,0:T(8,128)(2,1)S(1)}, bf16[320,256]{1,0:T(8,128)(2,1)S(1)}, u32[]{:S(2)}, u32[]{:S(2)}) collective-permute-start(bf16[320,256]{1,0:T(8,128)(2,1)S(1)} %get-tuple-element.120), channel_id=1, source_target_pairs={{0,16},{16,32},{32,48},{48,0},{1,17},{17,33},{33,49},{49,1},{2,18}... | collective-permute-start | bytes 491528 | tf_op jit(solution)/shard_map/ppermute | solution.py:345
  354.4 24.1 %collective-permute-start.44 = (bf16[320,256]{1,0:T(8,128)(2,1)S(1)}, bf16[320,256]{1,0:T(8,128)(2,1)S(1)}, u32[]{:S(2)}, u32[]{:S(2)}) collective-permute-start(bf16[320,256]{1,0:T(8,128)(2,1)S(1)} %get-tuple-element.117), channel_id=1, source_target_pairs={{0,48},{16,0},{32,16},{48,32},{1,49},{17,1},{33,17},{49,33},{2,50}... | collective-permute-start | bytes 491528 | tf_op jit(solution)/shard_map/ppermute | solution.py:345
  362.8 15.8 %collective-permute-start.43 = (bf16[320,256]{1,0:T(8,128)(2,1)S(1)}, bf16[320,256]{1,0:T(8,128)(2,1)S(1)}, u32[]{:S(2)}, u32[]{:S(2)}) collective-permute-start(bf16[320,256]{1,0:T(8,128)(2,1)S(1)} %get-tuple-element.116), channel_id=1, source_target_pairs={{0,32},{16,48},{32,0},{48,16},{1,33},{17,49},{33,1},{49,17},{2,34}... | collective-permute-start | bytes 491528 | tf_op jit(solution)/shard_map/ppermute | solution.py:345
  362.8 19.1 %collective-permute-start.42 = (bf16[320,256]{1,0:T(8,128)(2,1)S(1)}, bf16[320,256]{1,0:T(8,128)(2,1)S(1)}, u32[]{:S(2)}, u32[]{:S(2)}) collective-permute-start(bf16[320,256]{1,0:T(8,128)(2,1)S(1)} %get-tuple-element.115), channel_id=1, source_target_pairs={{0,16},{16,32},{32,48},{48,0},{1,17},{17,33},{33,49},{49,1},{2,18}... | collective-permute-start | bytes 491528 | tf_op jit(solution)/shard_map/ppermute | solution.py:345
  (43 other events, 673.2 us)
Sparse Core Ops, SparseCore 0:
  257.1 38.8 all-gather.2

commit v8 on v6

--- a/solution.py
+++ b/solution.py
@@ -361,8 +361,7 @@
     )(place, g_all, act_all)
 
 
-def summed_over_zh(place, g_all, act_all, first):
-    parts = run_grad(place, g_all, act_all, first)
+def summed_over_zh(parts):
     total = parts[0].astype(jnp.float32)
     for k in range(1, SET):
         route = [(source, (source + k) % SET) for source in range(SET)]
@@ -434,8 +433,9 @@
     first_slot = jnp.where(low_half, 0, 1)
     own_layers = tuple(w[0].reshape(2, 16, D // 16, R) for w in (w_in, w_out))
     w_b = (gathered(own(1 - first_slot)),)
-    half_a = across_y(own_half(first_slot))
-    w_a = own_layers + (half_a, from_ring(half_a, "core", 1)) + over_x(over_z(own(first_slot)))
+    own_part, near_a = lax.optimization_barrier((own_half(first_slot), over_z(own(first_slot))))
+    half_a = across_y(own_part)
+    w_a = own_layers + (half_a, from_ring(half_a, "core", 1)) + over_x(near_a)
 
     def flag(active, slot_now):
         reverse = slot_now == 1
@@ -462,13 +462,12 @@
     rows, g_a = run_backward(q_a, rows, w_a, h_a, pre_a)
     rows, act_all = lax.optimization_barrier((rows, act_all))
     rows = hop(rows)
+    place = zh.astype(jnp.int32)[None]
+    parts_b = run_grad(place, spread(g_b), act_all, SET)
+    rows, parts_b = lax.optimization_barrier((rows, parts_b))
     rows, g_a = run_backward(p_a, rows, w_a, h_a, pre_a, held=g_a, last=True)
-    place = zh.astype(jnp.int32)[None]
-    far_b = spread(g_b)
-    g_a, far_b = lax.optimization_barrier((g_a, far_b))
-    far_a = spread(g_a)
-    sum_b = summed_over_zh(place, far_b, act_all, SET)
-    sum_a = summed_over_zh(place, far_a, act_all, 0)
+    g_a, sum_b = lax.optimization_barrier((g_a, summed_over_zh(parts_b)))
+    sum_a = summed_over_zh(run_grad(place, spread(g_a), act_all, 0))
     kept = jnp.where(low_half, sum_a, sum_b)
     other = jnp.where(low_half, sum_b, sum_a)
     received = across_y(other)

time: 353 us -> 351 us (level)
  blocking collectives: 0 us -> 22 us
  waiting for transfers between devices: 188 us -> 175 us
  starting transfers between devices: 87.5 us -> 77.3 us
    ppermute x2, waiting for transfers between devices: 4 us -> 37 us  [across_y(): return lax.ppermute(block, 'y', [(0, 3), (3, 0), (1, 2), (2, 1)])]
    ppermute x16, waiting for transfers between devices: 73.7 us -> 46.4 us  [from_ring(): lax.ppermute(block, axis, [((d + away) % count, d) for d in range(count)])]
    all_to_all x0 -> x1, blocking collectives: none -> 22 us  [spread(): return lax.all_to_all(g_set, DP, 0, 0)]
    ppermute x6, starting transfers between devices: 24.1 us -> 16.8 us  [summed_over_zh(): total = total + lax.ppermute(parts[k], 'zh', route).astype(jnp.float32)]
    ppermute x6, waiting for transfers between devices: 19.2 us -> 12 us  [summed_over_zh(): total = total + lax.ppermute(parts[k], 'zh', route).astype(jnp.float32)]
    all_to_all x2 -> x1, starting transfers between devices: 12.7 us -> 6.49 us  [spread(): return lax.all_to_all(g_set, DP, 0, 0)]
    ppermute x1, waiting for transfers between devices: 30.6 us -> 24.7 us  [over_z(): return jnp.stack([beside, lax.ppermute(chunk_now, ('y', 'zh'), route)])]
  transfers between devices with their start and end apart: 34 -> 33, of which waited for: 22 -> 19; matrix products, arithmetic and copies ran while one was open for 1% -> 1% of each run, Pallas kernels for 12% -> 12%
where the time goes in v8:
time: 351 us; the launch traced here: 349 us
  waiting for transfers between devices  175 us (50%)
  starting transfers between devices  77.3 us (22%)
  Pallas kernels  55.2 us (16%)
  blocking collectives  22 us (6%)
  between operations  13.7 us (4%)
  local copies, waits for them, and re-layouts  3.55 us (1%)
    ppermute x16, waiting for transfers between devices, from_ring(): lax.ppermute(block, axis, [((d + away) % count, d) for d in range(count)])  46.4 us
    ppermute x2, waiting for transfers between devices, across_y(): return lax.ppermute(block, 'y', [(0, 3), (3, 0), (1, 2), (2, 1)])  37 us
    ppermute x4, starting transfers between devices, hop(): return lax.ppermute(rows, 'y', [(0, 1), (1, 0), (2, 3), (3, 2)])  29.6 us
    pallas_call x4, Pallas kernels, run_backward(): pl.pallas_call(lambda *refs: backward_kernel(*refs, source=source, aliase...  25.7 us
    pallas_call x4, Pallas kernels, run_forward(): pl.pallas_call(lambda *refs: forward_kernel(*refs, source=source, aliased...  25.5 us
    ppermute x1, waiting for transfers between devices, over_z(): return jnp.stack([beside, lax.ppermute(chunk_now, ('y', 'zh'), route)])  24.7 us
    ppermute x4, waiting for transfers between devices, hop(): return lax.ppermute(rows, 'y', [(0, 1), (1, 0), (2, 3), (3, 2)])  24.6 us
    all_to_all x1, blocking collectives, spread(): return lax.all_to_all(g_set, DP, 0, 0)  22 us
  transfers between devices with their start and end apart: 33, of which 19 were waited for; matrix products, arithmetic and copies ran while one was open for 1% of the time, Pallas kernels for 12%

profile of v8, /device:TPU:2, one launch (start us, length us, event | category | flops | bytes accessed | tf_op | source)
XLA Modules:
  0.0 349.1 jit_solution(15748722768995798294)
XLA Ops:
  8.6 5.8 %collective-permute-start.1 = (bf16[2,320,256]{2,1,0:T(8,128)(2,1)S(1)}, bf16[2,320,256]{2,1,0:T(8,128)(2,1)S(1)}, u32[]{:S(2)}, u32[]{:S(2)}) collective-permute-start(bf16[2,320,256]{2,1,0:T(8,128)(2,1)S(1)} %pad_maximum_fusion.2), channel_id=1, source_target_pairs={{0,208},{16,192},{32,240},{48,224},{64,144},{80,128},{96,176},{112... | collective-permute-start | bytes 983048 | tf_op jit(solution)/shard_map/ppermute | solution.py:395
  16.6 24.7 %collective-permute-done.1 = bf16[2,320,256]{2,1,0:T(8,128)(2,1)S(1)} collective-permute-done((bf16[2,320,256]{2,1,0:T(8,128)(2,1)S(1)}, bf16[2,320,256]{2,1,0:T(8,128)(2,1)S(1)}, u32[]{:S(2)}, u32[]{:S(2)}) %collective-permute-start.1) | collective-permute-done | bytes 327712 | tf_op jit(solution)/shard_map/ppermute | solution.py:395
  41.3 11.6 %collective-permute-done = bf16[2,320,256]{2,1,0:T(8,128)(2,1)S(1)} collective-permute-done((bf16[2,320,256]{2,1,0:T(8,128)(2,1)S(1)}, bf16[2,320,256]{2,1,0:T(8,128)(2,1)S(1)}, u32[]{:S(2)}, u32[]{:S(2)}) %collective-permute-start) | collective-permute-done | bytes 327712 | tf_op jit(solution)/shard_map/ppermute | solution.py:390
  54.7 2.0 collective-permute-start.11
  58.2 13.2 %collective-permute-done.5.refs_8_.refs_10_ = bf16[2,2,320,256]{3,2,1,0:T(8,128)(2,1)S(1)} collective-permute-done((bf16[2,2,320,256]{3,2,1,0:T(8,128)(2,1)S(1)}, bf16[2,2,320,256]{3,2,1,0:T(8,128)(2,1)S(1)}, u32[]{:S(2)}, u32[]{:S(2)}) %collective-permute-start.5) | collective-permute-done | bytes 655392 | tf_op jit(solution)/shard_map/ppermute | solution.py:382
  71.4 5.3 %collective-permute-start.7 = (bf16[2,2,320,256]{3,2,1,0:T(8,128)(2,1)S(1)}, bf16[2,2,320,256]{3,2,1,0:T(8,128)(2,1)}, u32[]{:S(2)}, u32[]{:S(2)}) collective-permute-start(bf16[2,2,320,256]{3,2,1,0:T(8,128)(2,1)S(1)} %collective-permute-done.5.refs_8_.refs_10_), channel_id=1, source_target_pairs={{2,0},{4,2},{6,4},{0,6},{3,1},{5,3},{7,5},{1,7},{10,8},{12,10},{14... | collective-permute-start | bytes 1966088 | tf_op jit(solution)/shard_map/ppermute | solution.py:382
  78.4 32.8 %collective-permute-done.2.refs_4_.refs_6_ = bf16[2,8,320,256]{3,2,1,0:T(8,128)(2,1)} collective-permute-done((bf16[2,8,320,256]{3,2,1,0:T(8,128)(2,1)S(1)}, bf16[2,8,320,256]{3,2,1,0:T(8,128)(2,1)}, u32[]{:S(2)}, u32[]{:S(2)}) %collective-permute-start.2) | collective-permute-done | bytes 2621472 | tf_op jit(solution)/shard_map/ppermute | solution.py:386
  113.9 3.5 %collective-permute-done.10.refs_13_.refs_15_ = bf16[2,2,320,256]{3,2,1,0:T(8,128)(2,1)S(1)} collective-permute-done((bf16[2,2,320,256]{3,2,1,0:T(8,128)(2,1)S(1)}, bf16[2,2,320,256]{3,2,1,0:T(8,128)(2,1)S(1)}, u32[]{:S(2)}, u32[]{:S(2)}) %collective-permute-start.10) | collective-permute-done | bytes 655392 | tf_op jit(solution)/shard_map/ppermute | solution.py:382
  118.7 20.8 %collective-permute-done.13.refs_16_.refs_18_ = bf16[2,2,320,256]{3,2,1,0:T(8,128)(2,1)} collective-permute-done((bf16[2,2,320,256]{3,2,1,0:T(8,128)(2,1)S(1)}, bf16[2,2,320,256]{3,2,1,0:T(8,128)(2,1)}, u32[]{:S(2)}, u32[]{:S(2)}) %collective-permute-start.13) | collective-permute-done | bytes 655392 | tf_op jit(solution)/shard_map/ppermute | solution.py:382
  139.5 5.3 %collective-permute-done.16.refs_18_.refs_20_ = bf16[2,2,320,256]{3,2,1,0:T(8,128)(2,1)} collective-permute-done((bf16[2,2,320,256]{3,2,1,0:T(8,128)(2,1)}, bf16[2,2,320,256]{3,2,1,0:T(8,128)(2,1)}, u32[]{:S(2)}, u32[]{:S(2)}) %collective-permute-start.16) | collective-permute-done | bytes 655392 | tf_op jit(solution)/shard_map/ppermute | solution.py:382
  145.1 2.8 collective-permute-done.17.refs_19_.refs_21_
  148.0 12.5 %forward_set.4 = (bf16[24,5120]{1,0:T(8,128)(2,1)S(1)}, bf16[4,24,5120]{2,1,0:T(8,128)(2,1)}, f32[4,24,256]{2,1,0:T(8,128)S(1)}, bf16[4,24,256]{2,1,0:T(8,128)(2,1)S(1)}) custom-call(s32[7]{0:T(128)S(1)} %stack.100.refs_0_, bf16[24,5120]{1,0:T(8,128)(2,1)S(1)} %pad.4.refs_1_, bf16[2,16,320,256]{3,2,1,0:T(8,128)(2,1)} %bitcast.33, ...), custom_call_target="tpu_custom_call" | custom-call | flops 125829120 | bytes 5242880 | tf_op jit(solution)/shard_map/forward_set/pallas_call | solution.py:194
  160.8 7.8 %collective-permute-done.19.refs_1_ = bf16[24,5120]{1,0:T(8,128)(2,1)S(1)} collective-permute-done((bf16[24,5120]{1,0:T(8,128)(2,1)S(1)}, bf16[24,5120]{1,0:T(8,128)(2,1)S(1)}, u32[]{:S(2)}, u32[]{:S(2)}) %collective-permute-start.19) | collective-permute-done | bytes 245792 | tf_op jit(solution)/shard_map/ppermute | solution.py:373
  169.9 23.1 %collective-permute-start.20 = (bf16[24,5120]{1,0:T(8,128)(2,1)S(1)}, bf16[24,5120]{1,0:T(8,128)(2,1)S(1)}, u32[]{:S(2)}, u32[]{:S(2)}) collective-permute-start(bf16[24,5120]{1,0:T(8,128)(2,1)S(1)} %get-tuple-element.54), channel_id=1, source_target_pairs={{0,64},{64,0},{128,192},{192,128},{1,65},{65,1},{129,193},{193,129... | collective-permute-start | bytes 737288 | tf_op jit(solution)/shard_map/ppermute | solution.py:373
  193.1 5.7 %collective-permute-done.20.refs_1_ = bf16[24,5120]{1,0:T(8,128)(2,1)S(1)} collective-permute-done((bf16[24,5120]{1,0:T(8,128)(2,1)S(1)}, bf16[24,5120]{1,0:T(8,128)(2,1)S(1)}, u32[]{:S(2)}, u32[]{:S(2)}) %collective-permute-start.20) | collective-permute-done | bytes 245792 | tf_op jit(solution)/shard_map/ppermute | solution.py:373
  198.8 11.7 %forward_set.7 = (bf16[24,5120]{1,0:T(8,128)(2,1)S(1)}, bf16[4,24,5120]{2,1,0:T(8,128)(2,1)S(1)}, f32[4,24,256]{2,1,0:T(8,128)S(1)}, bf16[4,24,256]{2,1,0:T(8,128)(2,1)S(1)}) custom-call(s32[7]{0:T(128)S(1)} %stack.108.refs_0_, bf16[24,5120]{1,0:T(8,128)(2,1)S(1)} %collective-permute-done.20.refs_1_, ...), custom_call_target="tpu_custom_call", output_to_operand_aliasing={{1}: (3, {}), {2}: (4, {}), {3}: (5, {})} | custom-call | flops 125829120 | bytes 5242880 | tf_op jit(solution)/shard_map/forward_set/pallas_call | solution.py:194
  211.2 12.3 %backward_set.4 = (bf16[24,5120]{1,0:T(8,128)(2,1)S(1)}, bf16[16,4,24,320]{3,2,1,0:T(8,128)(2,1)}) custom-call(s32[7]{0:T(128)S(1)} %stack.108.refs_0_, bf16[24,5120]{1,0:T(8,128)(2,1)S(1)} %get-tuple-element.58.refs_1_, bf16[4,24,5120]{2,1,0:T(8,128)(2,1)S(1)} %get-tuple-element.59.refs_2_, f32[4,24,256]{2,1,0:T(8,128)S(1)} %get-tuple-element.60.refs_3_, ...), custom_call_target="tpu_custom_call" | custom-call | flops 125829120 | bytes 5242880 | tf_op jit(solution)/shard_map/backward_set/pallas_call | solution.py:315
  223.6 6.9 %collective-permute-done.21.refs_1_ = bf16[24,5120]{1,0:T(8,128)(2,1)S(1)} collective-permute-done((bf16[24,5120]{1,0:T(8,128)(2,1)S(1)}, bf16[24,5120]{1,0:T(8,128)(2,1)S(1)}, u32[]{:S(2)}, u32[]{:S(2)}) %collective-permute-start.21) | collective-permute-done | bytes 245792 | tf_op jit(solution)/shard_map/ppermute | solution.py:373
  231.1 6.5 %all-to-all-start = ((bf16[16,4,24,320]{3,2,1,0:T(8,128)(2,1)}), bf16[16,4,24,320]{3,2,1,0:T(8,128)(2,1)S(1)}, u32[]{:S(2)}, u32[]{:S(2)}) async-start(bf16[16,4,24,320]{3,2,1,0:T(8,128)(2,1)} %get-tuple-element.70), calls=%async_computation | async-start | bytes 2359296 | tf_op jit(solution)/shard_map/all_to_all | solution.py:377
  238.3 18.2 %all-gather.7.cloned.1.call-done = bf16[128,24,256]{2,1,0:T(8,128)(2,1)} async-done(((bf16[8,24,256]{2,1,0:T(8,128)(2,1)}), bf16[128,24,256]{2,1,0:T(8,128)(2,1)}) %all-gather.7.cloned.1.call-update) | async-done | bytes 1572880 | tf_op jit(solution)/shard_map/all_gather | solution.py:458
  256.5 6.3 %collective-permute-start.22 = (bf16[24,5120]{1,0:T(8,128)(2,1)S(1)}, bf16[24,5120]{1,0:T(8,128)(2,1)S(1)}, u32[]{:S(2)}, u32[]{:S(2)}) collective-permute-start(bf16[24,5120]{1,0:T(8,128)(2,1)S(1)} %get-tuple-element.69), channel_id=1, source_target_pairs={{0,64},{64,0},{128,192},{192,128},{1,65},{65,1},{129,193},{193,129... | collective-permute-start | bytes 737288 | tf_op jit(solution)/shard_map/ppermute | solution.py:373
  262.8 2.0 grad_set.2
  264.8 4.3 %collective-permute-done.22.refs_1_ = bf16[24,5120]{1,0:T(8,128)(2,1)S(1)} collective-permute-done((bf16[24,5120]{1,0:T(8,128)(2,1)S(1)}, bf16[24,5120]{1,0:T(8,128)(2,1)S(1)}, u32[]{:S(2)}, u32[]{:S(2)}) %collective-permute-start.22) | collective-permute-done | bytes 245792 | tf_op jit(solution)/shard_map/ppermute | solution.py:373
  269.1 5.9 %collective-permute-start.25 = (bf16[320,256]{1,0:T(8,128)(2,1)S(1)}, bf16[320,256]{1,0:T(8,128)(2,1)S(1)}, u32[]{:S(2)}, u32[]{:S(2)}) collective-permute-start(bf16[320,256]{1,0:T(8,128)(2,1)S(1)} %get-tuple-element.82), channel_id=1, source_target_pairs={{0,48},{16,0},{32,16},{48,32},{1,49},{17,1},{33,17},{49,33},{2,50}... | collective-permute-start | bytes 491528 | tf_op jit(solution)/shard_map/ppermute | solution.py:368
  275.0 2.4 collective-permute-start.23
  277.3 12.1 %backward_set.7 = (bf16[24,5120]{1,0:T(8,128)(2,1)}, bf16[16,4,24,320]{3,2,1,0:T(8,128)(2,1)}) custom-call(s32[7]{0:T(128)S(1)} %stack.100.refs_0_, bf16[24,5120]{1,0:T(8,128)(2,1)S(1)} %collective-permute-done.22.refs_1_, bf16[4,24,5120]{2,1,0:T(8,128)(2,1)} %get-tuple-element.64.refs_2_, ...), custom_call_target="tpu_custom_call", output_to_operand_aliasing={{1}: (24, {})} | custom-call | flops 125829120 | bytes 5242880 | tf_op jit(solution)/shard_map/backward_set/pallas_call | solution.py:315
  289.6 22.0 %all_to_all.10.refs_1_ = bf16[16,4,24,320]{3,2,1,0:T(8,128)(2,1)S(1)} all-to-all(bf16[16,4,24,320]{3,2,1,0:T(8,128)(2,1)} %get-tuple-element.83), channel_id=1, replica_groups=mesh['y'=4,'zh'=4,'zl'=2,'x'=4,'core'=2] {'zl','x','core'}, dimensions={0} | all-to-all | bytes 1966080 | tf_op jit(solution)/shard_map/all_to_all | solution.py:377
  313.5 5.6 %collective-permute-start.28 = (bf16[320,256]{1,0:T(8,128)(2,1)S(1)}, bf16[320,256]{1,0:T(8,128)(2,1)S(1)}, u32[]{:S(2)}, u32[]{:S(2)}) collective-permute-start(bf16[320,256]{1,0:T(8,128)(2,1)S(1)} %get-tuple-element.87), channel_id=1, source_target_pairs={{0,48},{16,0},{32,16},{48,32},{1,49},{17,1},{33,17},{49,33},{2,50}... | collective-permute-start | bytes 491528 | tf_op jit(solution)/shard_map/ppermute | solution.py:368
  322.0 7.4 %collective-permute-done.28 = bf16[320,256]{1,0:T(8,128)(2,1)S(1)} collective-permute-done((bf16[320,256]{1,0:T(8,128)(2,1)S(1)}, bf16[320,256]{1,0:T(8,128)(2,1)S(1)}, u32[]{:S(2)}, u32[]{:S(2)}) %collective-permute-start.28) | collective-permute-done | bytes 163872 | tf_op jit(solution)/shard_map/ppermute | solution.py:368
  329.4 4.2 %collective-permute-done.27 = bf16[320,256]{1,0:T(8,128)(2,1)S(1)} collective-permute-done((bf16[320,256]{1,0:T(8,128)(2,1)S(1)}, bf16[320,256]{1,0:T(8,128)(2,1)S(1)}, u32[]{:S(2)}, u32[]{:S(2)}) %collective-permute-start.27) | collective-permute-done | bytes 163872 | tf_op jit(solution)/shard_map/ppermute | solution.py:368
  334.1 3.1 collective-permute-start.29
  337.2 4.3 %collective-permute-done.29 = bf16[320,256]{1,0:T(8,128)(2,1)S(1)} collective-permute-done((bf16[320,256]{1,0:T(8,128)(2,1)S(1)}, bf16[320,256]{1,0:T(8,128)(2,1)S(1)}, u32[]{:S(2)}, u32[]{:S(2)}) %collective-permute-start.29) | collective-permute-done | bytes 163872 | tf_op jit(solution)/shard_map/ppermute | solution.py:386
  (80 shorter events, 23.6 us)
Async XLA Ops:
  6.5 162.7 %all-gather.5.cloned.1.call-start = ((), (), s32[]{:S(2)}) async-start(), calls=%async_computation.2 | async-start | bytes 21299200 | tf_op jit(solution)/shard_map/all_gather | solution.py:423
  8.5 248.0 %all-gather.7.cloned.1.call-start = ((), (), s32[]{:S(2)}) async-start(), calls=%async_computation.3 | async-start | bytes 1671168 | tf_op jit(solution)/shard_map/all_gather | solution.py:458
  8.6 32.7 %collective-permute-start.1 = (bf16[2,320,256]{2,1,0:T(8,128)(2,1)S(1)}, bf16[2,320,256]{2,1,0:T(8,128)(2,1)S(1)}, u32[]{:S(2)}, u32[]{:S(2)}) collective-permute-start(bf16[2,320,256]{2,1,0:T(8,128)(2,1)S(1)} %pad_maximum_fusion.2), channel_id=1, source_target_pairs={{0,208},{16,192},{32,240},{48,224},{64,144},{80,128},{96,176},{112... | collective-permute-start | bytes 983048 | tf_op jit(solution)/shard_map/ppermute | solution.py:395
  14.4 38.5 %collective-permute-start = (bf16[2,320,256]{2,1,0:T(8,128)(2,1)S(1)}, bf16[2,320,256]{2,1,0:T(8,128)(2,1)S(1)}, u32[]{:S(2)}, u32[]{:S(2)}) collective-permute-start(bf16[2,320,256]{2,1,0:T(8,128)(2,1)S(1)} %pad_maximum_fusion.2), channel_id=1, source_target_pairs={{0,16},{16,0},{32,48},{48,32},{1,17},{17,1},{33,49},{49,33},{2,18}... | collective-permute-start | bytes 983048 | tf_op jit(solution)/shard_map/ppermute | solution.py:390
  53.0 58.2 %collective-permute-start.2 = (bf16[2,8,320,256]{3,2,1,0:T(8,128)(2,1)S(1)}, bf16[2,8,320,256]{3,2,1,0:T(8,128)(2,1)}, u32[]{:S(2)}, u32[]{:S(2)}) collective-permute-start(bf16[2,8,320,256]{3,2,1,0:T(8,128)(2,1)S(1)} %pad_maximum_fusion), channel_id=1, source_target_pairs={{0,192},{192,0},{64,128},{128,64},{1,193},{193,1},{65,129},{129,65... | collective-permute-start | bytes 7864328 | tf_op jit(solution)/shard_map/ppermute | solution.py:386
  54.7 16.7 %collective-permute-start.5 = (bf16[2,2,320,256]{3,2,1,0:T(8,128)(2,1)S(1)}, bf16[2,2,320,256]{3,2,1,0:T(8,128)(2,1)S(1)}, u32[]{:S(2)}, u32[]{:S(2)}) collective-permute-start(bf16[2,2,320,256]{3,2,1,0:T(8,128)(2,1)S(1)} %pad_maximum_fusion.1.refs_6_.refs_8_), channel_id=1, source_target_pairs={{2,0},{4,2},{6,4},{0,6},{3,1},{5,3},{7,5},{1,7},{10,8},{12,10},{14... | collective-permute-start | bytes 1966088 | tf_op jit(solution)/shard_map/ppermute | solution.py:382
  54.7 16.7 %collective-permute-start.4 = (bf16[2,2,320,256]{3,2,1,0:T(8,128)(2,1)S(1)}, bf16[2,2,320,256]{3,2,1,0:T(8,128)(2,1)S(1)}, u32[]{:S(2)}, u32[]{:S(2)}) collective-permute-start(bf16[2,2,320,256]{3,2,1,0:T(8,128)(2,1)S(1)} %pad_maximum_fusion.1.refs_6_.refs_8_), channel_id=1, source_target_pairs={{1,0},{0,1},{3,2},{2,3},{5,4},{4,5},{7,6},{6,7},{9,8},{8,9},{11,10... | collective-permute-start | bytes 1966088 | tf_op jit(solution)/shard_map/ppermute | solution.py:382
  54.7 22.2 %collective-permute-start.11 = (bf16[2,2,320,256]{3,2,1,0:T(8,128)(2,1)S(1)}, bf16[2,2,320,256]{3,2,1,0:T(8,128)(2,1)S(1)}, u32[]{:S(2)}, u32[]{:S(2)}) collective-permute-start(bf16[2,2,320,256]{3,2,1,0:T(8,128)(2,1)S(1)} %pad_maximum_fusion.1.refs_6_.refs_8_), channel_id=1, source_target_pairs={{8,0},{0,8},{9,1},{1,9},{10,2},{2,10},{11,3},{3,11},{12,4},{4,12},... | collective-permute-start | bytes 1966088 | tf_op jit(solution)/shard_map/ppermute | solution.py:382
  56.7 54.5 %collective-permute-start.9 = (bf16[2,2,320,256]{3,2,1,0:T(8,128)(2,1)S(1)}, bf16[2,2,320,256]{3,2,1,0:T(8,128)(2,1)S(1)}, u32[]{:S(2)}, u32[]{:S(2)}) collective-permute-start(bf16[2,2,320,256]{3,2,1,0:T(8,128)(2,1)S(1)} %pad_maximum_fusion.1.refs_6_.refs_8_), channel_id=1, source_target_pairs={{6,0},{0,2},{2,4},{4,6},{7,1},{1,3},{3,5},{5,7},{14,8},{8,10},{10,... | collective-permute-start | bytes 1966088 | tf_op jit(solution)/shard_map/ppermute | solution.py:382
  71.4 40.3 %collective-permute-start.6 = (bf16[2,2,320,256]{3,2,1,0:T(8,128)(2,1)S(1)}, bf16[2,2,320,256]{3,2,1,0:T(8,128)(2,1)S(1)}, u32[]{:S(2)}, u32[]{:S(2)}) collective-permute-start(bf16[2,2,320,256]{3,2,1,0:T(8,128)(2,1)S(1)} %collective-permute-done.5.refs_8_.refs_10_), channel_id=1, source_target_pairs={{1,0},{0,1},{3,2},{2,3},{5,4},{4,5},{7,6},{6,7},{9,8},{8,9},{11,10... | collective-permute-start | bytes 1966088 | tf_op jit(solution)/shard_map/ppermute | solution.py:382
  71.4 40.4 %collective-permute-start.7 = (bf16[2,2,320,256]{3,2,1,0:T(8,128)(2,1)S(1)}, bf16[2,2,320,256]{3,2,1,0:T(8,128)(2,1)}, u32[]{:S(2)}, u32[]{:S(2)}) collective-permute-start(bf16[2,2,320,256]{3,2,1,0:T(8,128)(2,1)S(1)} %collective-permute-done.5.refs_8_.refs_10_), channel_id=1, source_target_pairs={{2,0},{4,2},{6,4},{0,6},{3,1},{5,3},{7,5},{1,7},{10,8},{12,10},{14... | collective-permute-start | bytes 1966088 | tf_op jit(solution)/shard_map/ppermute | solution.py:382
  76.9 35.1 %collective-permute-start.15 = (bf16[2,2,320,256]{3,2,1,0:T(8,128)(2,1)S(1)}, bf16[2,2,320,256]{3,2,1,0:T(8,128)(2,1)}, u32[]{:S(2)}, u32[]{:S(2)}) collective-permute-start(bf16[2,2,320,256]{3,2,1,0:T(8,128)(2,1)S(1)} %collective-permute-done.11.refs_14_.refs_16_), channel_id=1, source_target_pairs={{6,0},{0,2},{2,4},{4,6},{7,1},{1,3},{3,5},{5,7},{14,8},{8,10},{10,... | collective-permute-start | bytes 1966088 | tf_op jit(solution)/shard_map/ppermute | solution.py:382
  111.2 36.8 %collective-permute-start.3 = (bf16[2,8,320,256]{3,2,1,0:T(8,128)(2,1)}, bf16[2,8,320,256]{3,2,1,0:T(8,128)(2,1)}, u32[]{:S(2)}, u32[]{:S(2)}) collective-permute-start(bf16[2,8,320,256]{3,2,1,0:T(8,128)(2,1)} %collective-permute-done.2.refs_4_.refs_6_), channel_id=1, source_target_pairs={{1,0},{0,1},{3,2},{2,3},{5,4},{4,5},{7,6},{6,7},{9,8},{8,9},{11,10... | collective-permute-start | bytes 7864328 | tf_op jit(solution)/shard_map/ppermute | solution.py:382
  111.2 6.2 %collective-permute-start.10 = (bf16[2,2,320,256]{3,2,1,0:T(8,128)(2,1)S(1)}, bf16[2,2,320,256]{3,2,1,0:T(8,128)(2,1)S(1)}, u32[]{:S(2)}, u32[]{:S(2)}) collective-permute-start(bf16[2,2,320,256]{3,2,1,0:T(8,128)(2,1)S(1)} %collective-permute-done.9.refs_12_.refs_14_), channel_id=1, source_target_pairs={{1,0},{0,1},{3,2},{2,3},{5,4},{4,5},{7,6},{6,7},{9,8},{8,9},{11,10... | collective-permute-start | bytes 1966088 | tf_op jit(solution)/shard_map/ppermute | solution.py:382
  111.7 6.6 %collective-permute-start.12 = (bf16[2,2,320,256]{3,2,1,0:T(8,128)(2,1)S(1)}, bf16[2,2,320,256]{3,2,1,0:T(8,128)(2,1)S(1)}, u32[]{:S(2)}, u32[]{:S(2)}) collective-permute-start(bf16[2,2,320,256]{3,2,1,0:T(8,128)(2,1)S(1)} %collective-permute-done.11.refs_14_.refs_16_), channel_id=1, source_target_pairs={{1,0},{0,1},{3,2},{2,3},{5,4},{4,5},{7,6},{6,7},{9,8},{8,9},{11,10... | collective-permute-start | bytes 1966088 | tf_op jit(solution)/shard_map/ppermute | solution.py:382
  111.8 27.7 %collective-permute-start.13 = (bf16[2,2,320,256]{3,2,1,0:T(8,128)(2,1)S(1)}, bf16[2,2,320,256]{3,2,1,0:T(8,128)(2,1)}, u32[]{:S(2)}, u32[]{:S(2)}) collective-permute-start(bf16[2,2,320,256]{3,2,1,0:T(8,128)(2,1)S(1)} %collective-permute-done.11.refs_14_.refs_16_), channel_id=1, source_target_pairs={{2,0},{4,2},{6,4},{0,6},{3,1},{5,3},{7,5},{1,7},{10,8},{12,10},{14... | collective-permute-start | bytes 1966088 | tf_op jit(solution)/shard_map/ppermute | solution.py:382
  112.0 32.8 %collective-permute-start.16 = (bf16[2,2,320,256]{3,2,1,0:T(8,128)(2,1)}, bf16[2,2,320,256]{3,2,1,0:T(8,128)(2,1)}, u32[]{:S(2)}, u32[]{:S(2)}) collective-permute-start(bf16[2,2,320,256]{3,2,1,0:T(8,128)(2,1)} %collective-permute-done.15.refs_20_.refs_22_), channel_id=1, source_target_pairs={{6,0},{0,2},{2,4},{4,6},{7,1},{1,3},{3,5},{5,7},{14,8},{8,10},{10,... | collective-permute-start | bytes 1966088 | tf_op jit(solution)/shard_map/ppermute | solution.py:382
  117.4 27.8 %collective-permute-start.18 = (bf16[2,2,320,256]{3,2,1,0:T(8,128)(2,1)}, bf16[2,2,320,256]{3,2,1,0:T(8,128)(2,1)}, u32[]{:S(2)}, u32[]{:S(2)}) collective-permute-start(bf16[2,2,320,256]{3,2,1,0:T(8,128)(2,1)} %collective-permute-done.15.refs_20_.refs_22_), channel_id=1, source_target_pairs={{1,0},{0,1},{3,2},{2,3},{5,4},{4,5},{7,6},{6,7},{9,8},{8,9},{11,10... | collective-permute-start | bytes 1966088 | tf_op jit(solution)/shard_map/ppermute | solution.py:382
  118.3 26.8 %collective-permute-start.8 = (bf16[2,2,320,256]{3,2,1,0:T(8,128)(2,1)}, bf16[2,2,320,256]{3,2,1,0:T(8,128)(2,1)}, u32[]{:S(2)}, u32[]{:S(2)}) collective-permute-start(bf16[2,2,320,256]{3,2,1,0:T(8,128)(2,1)} %collective-permute-done.7.refs_10_.refs_12_), channel_id=1, source_target_pairs={{1,0},{0,1},{3,2},{2,3},{5,4},{4,5},{7,6},{6,7},{9,8},{8,9},{11,10... | collective-permute-start | bytes 1966088 | tf_op jit(solution)/shard_map/ppermute | solution.py:382
  139.5 5.6 %collective-permute-start.14 = (bf16[2,2,320,256]{3,2,1,0:T(8,128)(2,1)}, bf16[2,2,320,256]{3,2,1,0:T(8,128)(2,1)}, u32[]{:S(2)}, u32[]{:S(2)}) collective-permute-start(bf16[2,2,320,256]{3,2,1,0:T(8,128)(2,1)} %collective-permute-done.13.refs_16_.refs_18_), channel_id=1, source_target_pairs={{1,0},{0,1},{3,2},{2,3},{5,4},{4,5},{7,6},{6,7},{9,8},{8,9},{11,10... | collective-permute-start | bytes 1966088 | tf_op jit(solution)/shard_map/ppermute | solution.py:382
  160.5 8.1 %collective-permute-start.19 = (bf16[24,5120]{1,0:T(8,128)(2,1)S(1)}, bf16[24,5120]{1,0:T(8,128)(2,1)S(1)}, u32[]{:S(2)}, u32[]{:S(2)}) collective-permute-start(bf16[24,5120]{1,0:T(8,128)(2,1)S(1)} %get-tuple-element.49), channel_id=1, source_target_pairs={{0,64},{64,0},{128,192},{192,128},{1,65},{65,1},{129,193},{193,129... | collective-permute-start | bytes 737288 | tf_op jit(solution)/shard_map/ppermute | solution.py:373
  169.9 28.9 %collective-permute-start.20 = (bf16[24,5120]{1,0:T(8,128)(2,1)S(1)}, bf16[24,5120]{1,0:T(8,128)(2,1)S(1)}, u32[]{:S(2)}, u32[]{:S(2)}) collective-permute-start(bf16[24,5120]{1,0:T(8,128)(2,1)S(1)} %get-tuple-element.54), channel_id=1, source_target_pairs={{0,64},{64,0},{128,192},{192,128},{1,65},{65,1},{129,193},{193,129... | collective-permute-start | bytes 737288 | tf_op jit(solution)/shard_map/ppermute | solution.py:373
  223.5 7.0 %collective-permute-start.21 = (bf16[24,5120]{1,0:T(8,128)(2,1)S(1)}, bf16[24,5120]{1,0:T(8,128)(2,1)S(1)}, u32[]{:S(2)}, u32[]{:S(2)}) collective-permute-start(bf16[24,5120]{1,0:T(8,128)(2,1)S(1)} %get-tuple-element.61), channel_id=1, source_target_pairs={{0,64},{64,0},{128,192},{192,128},{1,65},{65,1},{129,193},{193,129... | collective-permute-start | bytes 737288 | tf_op jit(solution)/shard_map/ppermute | solution.py:373
  231.1 31.7 %all-to-all-start = ((bf16[16,4,24,320]{3,2,1,0:T(8,128)(2,1)}), bf16[16,4,24,320]{3,2,1,0:T(8,128)(2,1)S(1)}, u32[]{:S(2)}, u32[]{:S(2)}) async-start(bf16[16,4,24,320]{3,2,1,0:T(8,128)(2,1)} %get-tuple-element.70), calls=%async_computation | async-start | bytes 2359296 | tf_op jit(solution)/shard_map/all_to_all | solution.py:377
  256.5 12.6 %collective-permute-start.22 = (bf16[24,5120]{1,0:T(8,128)(2,1)S(1)}, bf16[24,5120]{1,0:T(8,128)(2,1)S(1)}, u32[]{:S(2)}, u32[]{:S(2)}) collective-permute-start(bf16[24,5120]{1,0:T(8,128)(2,1)S(1)} %get-tuple-element.69), channel_id=1, source_target_pairs={{0,64},{64,0},{128,192},{192,128},{1,65},{65,1},{129,193},{193,129... | collective-permute-start | bytes 737288 | tf_op jit(solution)/shard_map/ppermute | solution.py:373
  269.1 20.4 %collective-permute-start.25 = (bf16[320,256]{1,0:T(8,128)(2,1)S(1)}, bf16[320,256]{1,0:T(8,128)(2,1)S(1)}, u32[]{:S(2)}, u32[]{:S(2)}) collective-permute-start(bf16[320,256]{1,0:T(8,128)(2,1)S(1)} %get-tuple-element.82), channel_id=1, source_target_pairs={{0,48},{16,0},{32,16},{48,32},{1,49},{17,1},{33,17},{49,33},{2,50}... | collective-permute-start | bytes 491528 | tf_op jit(solution)/shard_map/ppermute | solution.py:368
  275.0 14.5 %collective-permute-start.24 = (bf16[320,256]{1,0:T(8,128)(2,1)S(1)}, bf16[320,256]{1,0:T(8,128)(2,1)S(1)}, u32[]{:S(2)}, u32[]{:S(2)}) collective-permute-start(bf16[320,256]{1,0:T(8,128)(2,1)S(1)} %get-tuple-element.81), channel_id=1, source_target_pairs={{0,32},{16,48},{32,0},{48,16},{1,33},{17,49},{33,1},{49,17},{2,34}... | collective-permute-start | bytes 491528 | tf_op jit(solution)/shard_map/ppermute | solution.py:368
  275.0 14.5 %collective-permute-start.23 = (bf16[320,256]{1,0:T(8,128)(2,1)S(1)}, bf16[320,256]{1,0:T(8,128)(2,1)S(1)}, u32[]{:S(2)}, u32[]{:S(2)}) collective-permute-start(bf16[320,256]{1,0:T(8,128)(2,1)S(1)} %get-tuple-element.80), channel_id=1, source_target_pairs={{0,16},{16,32},{32,48},{48,0},{1,17},{17,33},{33,49},{49,1},{2,18}... | collective-permute-start | bytes 491528 | tf_op jit(solution)/shard_map/ppermute | solution.py:368
  313.5 16.0 %collective-permute-start.28 = (bf16[320,256]{1,0:T(8,128)(2,1)S(1)}, bf16[320,256]{1,0:T(8,128)(2,1)S(1)}, u32[]{:S(2)}, u32[]{:S(2)}) collective-permute-start(bf16[320,256]{1,0:T(8,128)(2,1)S(1)} %get-tuple-element.87), channel_id=1, source_target_pairs={{0,48},{16,0},{32,16},{48,32},{1,49},{17,1},{33,17},{49,33},{2,50}... | collective-permute-start | bytes 491528 | tf_op jit(solution)/shard_map/ppermute | solution.py:368
  319.1 14.6 %collective-permute-start.27 = (bf16[320,256]{1,0:T(8,128)(2,1)S(1)}, bf16[320,256]{1,0:T(8,128)(2,1)S(1)}, u32[]{:S(2)}, u32[]{:S(2)}) collective-permute-start(bf16[320,256]{1,0:T(8,128)(2,1)S(1)} %get-tuple-element.86), channel_id=1, source_target_pairs={{0,32},{16,48},{32,0},{48,16},{1,33},{17,49},{33,1},{49,17},{2,34}... | collective-permute-start | bytes 491528 | tf_op jit(solution)/shard_map/ppermute | solution.py:368
  320.9 13.1 %collective-permute-start.26 = (bf16[320,256]{1,0:T(8,128)(2,1)S(1)}, bf16[320,256]{1,0:T(8,128)(2,1)S(1)}, u32[]{:S(2)}, u32[]{:S(2)}) collective-permute-start(bf16[320,256]{1,0:T(8,128)(2,1)S(1)} %get-tuple-element.85), channel_id=1, source_target_pairs={{0,16},{16,32},{32,48},{48,0},{1,17},{17,33},{33,49},{49,1},{2,18}... | collective-permute-start | bytes 491528 | tf_op jit(solution)/shard_map/ppermute | solution.py:368
  334.1 7.3 %collective-permute-start.29 = (bf16[320,256]{1,0:T(8,128)(2,1)S(1)}, bf16[320,256]{1,0:T(8,128)(2,1)S(1)}, u32[]{:S(2)}, u32[]{:S(2)}) collective-permute-start(bf16[320,256]{1,0:T(8,128)(2,1)S(1)} %get-tuple-element.89), channel_id=1, source_target_pairs={{0,192},{192,0},{64,128},{128,64},{1,193},{193,1},{65,129},{129,65... | collective-permute-start | bytes 491528 | tf_op jit(solution)/shard_map/ppermute | solution.py:386
  (9 other events, 517.8 us)
Sparse Core Ops, SparseCore 0:
  10.1 146.6 all-gather.4
  211.3 45.1 all-gather.6

commit v9 on v8

--- a/solution.py
+++ b/solution.py
@@ -398,11 +398,16 @@
 def over_x(near):
     far = from_ring(near, "zl", 1)
     near_up, near_down = from_ring(near, "x", 1), from_ring(near, "x", -1)
+    far, near_up, near_down = lax.optimization_barrier((far, near_up, near_down))
     near_across = from_ring(near_up, "x", 1)
     far_up, far_down = from_ring(far, "x", 1), from_ring(far, "x", -1)
     far_across = from_ring(far_down, "x", -1)
+    return near, near_up, near_across, near_down, far, far_up, far_across, far_down
+
+
+def both_cores(blocks):
     parts = []
-    for one in (near, near_up, near_across, near_down, far, far_up, far_across, far_down):
+    for one in blocks:
         parts += [one, from_ring(one, "core", 1)]
     return tuple(parts)
 
@@ -432,10 +437,13 @@
 
     first_slot = jnp.where(low_half, 0, 1)
     own_layers = tuple(w[0].reshape(2, 16, D // 16, R) for w in (w_in, w_out))
-    w_b = (gathered(own(1 - first_slot)),)
-    own_part, near_a = lax.optimization_barrier((own_half(first_slot), over_z(own(first_slot))))
-    half_a = across_y(own_part)
-    w_a = own_layers + (half_a, from_ring(half_a, "core", 1)) + over_x(near_a)
+    half_own, chunk_a = lax.optimization_barrier((own_half(first_slot), own(first_slot)))
+    half_a = across_y(half_own)
+    chunk_b, near_a = lax.optimization_barrier((own(1 - first_slot), over_z(chunk_a)))
+    w_b = (gathered(chunk_b),)
+    blocks = list(over_x(near_a))
+    half_a, blocks[2], *blocks[5:7] = lax.optimization_barrier((half_a, blocks[2], *blocks[5:7]))
+    w_a = own_layers + both_cores([half_a] + blocks)
 
     def flag(active, slot_now):
         reverse = slot_now == 1

time: 351 us -> 330 us (0.940)
  starting transfers between devices: 77.3 us -> 58.1 us
  waiting for transfers between devices: 175 us -> 166 us
    ppermute x2, waiting for transfers between devices: 37 us -> 5.94 us  [across_y(): return lax.ppermute(block, 'y', [(0, 3), (3, 0), (1, 2), (2, 1)])]
    all_gather x1, waiting for transfers between devices: 0.02 us -> 17 us  [gathered(): lax.all_gather(own_part, ('zh',) + DP).reshape(SET, 16, 2, D // 16, R)]
    ppermute x4, starting transfers between devices: 29.6 us -> 17.4 us  [hop(): return lax.ppermute(rows, 'y', [(0, 1), (1, 0), (2, 3), (3, 2)])]
    ppermute x16, waiting for transfers between devices: 46.4 us -> 58.4 us  [from_ring(): lax.ppermute(block, axis, [((d + away) % count, d) for d in range(count)])]
    ppermute x1, waiting for transfers between devices: 11.6 us -> 5.56 us  [over_z(): beside = lax.ppermute(chunk_now, 'zh', [(0, 1), (1, 0), (2, 3), (3, 2)])]
  transfers between devices with their start and end apart: 33 -> 33, of which waited for: 19 -> 26; matrix products, arithmetic and copies ran while one was open for 1% -> 1% of each run, Pallas kernels for 12% -> 13%
where the time goes in v9:
time: 330 us; the launch traced here: 327 us
  waiting for transfers between devices  166 us (50%)
  starting transfers between devices  58.1 us (18%)
  Pallas kernels  55.3 us (17%)
  blocking collectives  24.1 us (7%)
  between operations  13.6 us (4%)
  other arithmetic  5.47 us (2%)
  local copies, waits for them, and re-layouts  4.38 us (1%)
    ppermute x16, waiting for transfers between devices, from_ring(): lax.ppermute(block, axis, [((d + away) % count, d) for d in range(count)])  58.4 us
    ppermute x4, waiting for transfers between devices, hop(): return lax.ppermute(rows, 'y', [(0, 1), (1, 0), (2, 3), (3, 2)])  26.1 us
    pallas_call x4, Pallas kernels, run_forward(): pl.pallas_call(lambda *refs: forward_kernel(*refs, source=source, aliased...  25.7 us
    pallas_call x4, Pallas kernels, run_backward(): pl.pallas_call(lambda *refs: backward_kernel(*refs, source=source, aliase...  25.7 us
    all_to_all x1, blocking collectives, spread(): return lax.all_to_all(g_set, DP, 0, 0)  24.1 us
    ppermute x1, waiting for transfers between devices, over_z(): return jnp.stack([beside, lax.ppermute(chunk_now, ('y', 'zh'), route)])  21.8 us
    ppermute x4, starting transfers between devices, hop(): return lax.ppermute(rows, 'y', [(0, 1), (1, 0), (2, 3), (3, 2)])  17.4 us
    all_gather x1, waiting for transfers between devices, shards(): act_all = lax.all_gather(jnp.concatenate([act_a, act_b], axis=0), DP)  17 us
  transfers between devices with their start and end apart: 33, of which 26 were waited for; matrix products, arithmetic and copies ran while one was open for 1% of the time, Pallas kernels for 13%

profile of v9, /device:TPU:2, one launch (start us, length us, event | category | flops | bytes accessed | tf_op | source)
XLA Modules:
  0.0 326.5 jit_solution(12559919906274781604)
XLA Ops:
  11.4 5.8 %collective-permute-start.2 = (bf16[2,320,256]{2,1,0:T(8,128)(2,1)S(1)}, bf16[2,320,256]{2,1,0:T(8,128)(2,1)S(1)}, u32[]{:S(2)}, u32[]{:S(2)}) collective-permute-start(bf16[2,320,256]{2,1,0:T(8,128)(2,1)S(1)} %pad_maximum_fusion.2), channel_id=1, source_target_pairs={{0,208},{16,192},{32,240},{48,224},{64,144},{80,128},{96,176},{112... | collective-permute-start | bytes 983048 | tf_op jit(solution)/shard_map/ppermute | solution.py:395
  18.0 21.8 %collective-permute-done.2 = bf16[2,320,256]{2,1,0:T(8,128)(2,1)S(1)} collective-permute-done((bf16[2,320,256]{2,1,0:T(8,128)(2,1)S(1)}, bf16[2,320,256]{2,1,0:T(8,128)(2,1)S(1)}, u32[]{:S(2)}, u32[]{:S(2)}) %collective-permute-start.2) | collective-permute-done | bytes 327712 | tf_op jit(solution)/shard_map/ppermute | solution.py:395
  39.8 5.6 %collective-permute-done.1 = bf16[2,320,256]{2,1,0:T(8,128)(2,1)S(1)} collective-permute-done((bf16[2,320,256]{2,1,0:T(8,128)(2,1)S(1)}, bf16[2,320,256]{2,1,0:T(8,128)(2,1)S(1)}, u32[]{:S(2)}, u32[]{:S(2)}) %collective-permute-start.1) | collective-permute-done | bytes 327712 | tf_op jit(solution)/shard_map/ppermute | solution.py:390
  49.2 14.9 %collective-permute-done.3.refs_14_.refs_16_ = bf16[2,2,320,256]{3,2,1,0:T(8,128)(2,1)S(1)} collective-permute-done((bf16[2,2,320,256]{3,2,1,0:T(8,128)(2,1)S(1)}, bf16[2,2,320,256]{3,2,1,0:T(8,128)(2,1)S(1)}, u32[]{:S(2)}, u32[]{:S(2)}) %collective-permute-start.3) | collective-permute-done | bytes 655392 | tf_op jit(solution)/shard_map/ppermute | solution.py:382
  68.0 3.2 collective-permute-start.7
  71.2 3.2 collective-permute-start.6
  74.4 10.7 %collective-permute-done.8.refs_20_.refs_22_ = bf16[2,2,320,256]{3,2,1,0:T(8,128)(2,1)} collective-permute-done((bf16[2,2,320,256]{3,2,1,0:T(8,128)(2,1)S(1)}, bf16[2,2,320,256]{3,2,1,0:T(8,128)(2,1)}, u32[]{:S(2)}, u32[]{:S(2)}) %collective-permute-start.8) | collective-permute-done | bytes 655392 | tf_op jit(solution)/shard_map/ppermute | solution.py:382
  85.1 13.8 %collective-permute-done.6.refs_10_.refs_12_ = bf16[2,2,320,256]{3,2,1,0:T(8,128)(2,1)} collective-permute-done((bf16[2,2,320,256]{3,2,1,0:T(8,128)(2,1)S(1)}, bf16[2,2,320,256]{3,2,1,0:T(8,128)(2,1)}, u32[]{:S(2)}, u32[]{:S(2)}) %collective-permute-start.6) | collective-permute-done | bytes 655392 | tf_op jit(solution)/shard_map/ppermute | solution.py:382
  98.9 4.6 %collective-permute-done.9.refs_18_.refs_20_ = bf16[2,2,320,256]{3,2,1,0:T(8,128)(2,1)} collective-permute-done((bf16[2,2,320,256]{3,2,1,0:T(8,128)(2,1)}, bf16[2,2,320,256]{3,2,1,0:T(8,128)(2,1)}, u32[]{:S(2)}, u32[]{:S(2)}) %collective-permute-start.9) | collective-permute-done | bytes 655392 | tf_op jit(solution)/shard_map/ppermute | solution.py:382
  108.5 2.3 collective-permute-done.12.refs_9_.refs_11_
  120.4 12.7 %forward_set.4 = (bf16[24,5120]{1,0:T(8,128)(2,1)S(1)}, bf16[4,24,5120]{2,1,0:T(8,128)(2,1)}, f32[4,24,256]{2,1,0:T(8,128)S(1)}, bf16[4,24,256]{2,1,0:T(8,128)(2,1)S(1)}) custom-call(s32[7]{0:T(128)S(1)} %stack.100.refs_0_, bf16[24,5120]{1,0:T(8,128)(2,1)S(1)} %pad.4.refs_1_, bf16[2,16,320,256]{3,2,1,0:T(8,128)(2,1)} %bitcast.33, ...), custom_call_target="tpu_custom_call" | custom-call | flops 125829120 | bytes 5242880 | tf_op jit(solution)/shard_map/forward_set/pallas_call | solution.py:194
  133.5 8.0 %collective-permute-done.19.refs_1_ = bf16[24,5120]{1,0:T(8,128)(2,1)S(1)} collective-permute-done((bf16[24,5120]{1,0:T(8,128)(2,1)S(1)}, bf16[24,5120]{1,0:T(8,128)(2,1)S(1)}, u32[]{:S(2)}, u32[]{:S(2)}) %collective-permute-start.19) | collective-permute-done | bytes 245792 | tf_op jit(solution)/shard_map/ppermute | solution.py:373
  142.1 17.0 %all-gather.5.cloned.1.call-done = bf16[128,320,256]{2,1,0:T(8,128)(2,1)} async-done(((bf16[2,320,256]{2,1,0:T(8,128)(2,1)}), bf16[128,320,256]{2,1,0:T(8,128)(2,1)}) %all-gather.5.cloned.1.call-update) | async-done | bytes 20971536 | tf_op jit(solution)/shard_map/all_gather | solution.py:428
  159.7 9.6 %collective-permute-start.20 = (bf16[24,5120]{1,0:T(8,128)(2,1)S(1)}, bf16[24,5120]{1,0:T(8,128)(2,1)S(1)}, u32[]{:S(2)}, u32[]{:S(2)}) collective-permute-start(bf16[24,5120]{1,0:T(8,128)(2,1)S(1)} %get-tuple-element.72), channel_id=1, source_target_pairs={{0,64},{64,0},{128,192},{192,128},{1,65},{65,1},{129,193},{193,129... | collective-permute-start | bytes 737288 | tf_op jit(solution)/shard_map/ppermute | solution.py:373
  169.4 6.3 %collective-permute-done.20.refs_1_ = bf16[24,5120]{1,0:T(8,128)(2,1)S(1)} collective-permute-done((bf16[24,5120]{1,0:T(8,128)(2,1)S(1)}, bf16[24,5120]{1,0:T(8,128)(2,1)S(1)}, u32[]{:S(2)}, u32[]{:S(2)}) %collective-permute-start.20) | collective-permute-done | bytes 245792 | tf_op jit(solution)/shard_map/ppermute | solution.py:373
  175.7 11.7 %forward_set.7 = (bf16[24,5120]{1,0:T(8,128)(2,1)S(1)}, bf16[4,24,5120]{2,1,0:T(8,128)(2,1)S(1)}, f32[4,24,256]{2,1,0:T(8,128)S(1)}, bf16[4,24,256]{2,1,0:T(8,128)(2,1)S(1)}) custom-call(s32[7]{0:T(128)S(1)} %stack.108.refs_0_, bf16[24,5120]{1,0:T(8,128)(2,1)S(1)} %collective-permute-done.20.refs_1_, ...), custom_call_target="tpu_custom_call", output_to_operand_aliasing={{1}: (3, {}), {2}: (4, {}), {3}: (5, {})} | custom-call | flops 125829120 | bytes 5242880 | tf_op jit(solution)/shard_map/forward_set/pallas_call | solution.py:194
  188.1 12.3 %backward_set.4 = (bf16[24,5120]{1,0:T(8,128)(2,1)S(1)}, bf16[16,4,24,320]{3,2,1,0:T(8,128)(2,1)}) custom-call(s32[7]{0:T(128)S(1)} %stack.108.refs_0_, bf16[24,5120]{1,0:T(8,128)(2,1)S(1)} %get-tuple-element.76.refs_1_, bf16[4,24,5120]{2,1,0:T(8,128)(2,1)S(1)} %get-tuple-element.77.refs_2_, f32[4,24,256]{2,1,0:T(8,128)S(1)} %get-tuple-element.78.refs_3_, ...), custom_call_target="tpu_custom_call" | custom-call | flops 125829120 | bytes 5242880 | tf_op jit(solution)/shard_map/backward_set/pallas_call | solution.py:315
  200.5 7.6 %collective-permute-done.21.refs_1_ = bf16[24,5120]{1,0:T(8,128)(2,1)S(1)} collective-permute-done((bf16[24,5120]{1,0:T(8,128)(2,1)S(1)}, bf16[24,5120]{1,0:T(8,128)(2,1)S(1)}, u32[]{:S(2)}, u32[]{:S(2)}) %collective-permute-start.21) | collective-permute-done | bytes 245792 | tf_op jit(solution)/shard_map/ppermute | solution.py:373
  208.7 6.5 %all-to-all-start = ((bf16[16,4,24,320]{3,2,1,0:T(8,128)(2,1)}), bf16[16,4,24,320]{3,2,1,0:T(8,128)(2,1)S(1)}, u32[]{:S(2)}, u32[]{:S(2)}) async-start(bf16[16,4,24,320]{3,2,1,0:T(8,128)(2,1)} %get-tuple-element.88), calls=%async_computation | async-start | bytes 2359296 | tf_op jit(solution)/shard_map/all_to_all | solution.py:377
  215.9 17.0 %all-gather.7.cloned.1.call-done = bf16[128,24,256]{2,1,0:T(8,128)(2,1)} async-done(((bf16[8,24,256]{2,1,0:T(8,128)(2,1)}), bf16[128,24,256]{2,1,0:T(8,128)(2,1)}) %all-gather.7.cloned.1.call-update) | async-done | bytes 1572880 | tf_op jit(solution)/shard_map/all_gather | solution.py:466
  232.9 7.6 %collective-permute-start.22 = (bf16[24,5120]{1,0:T(8,128)(2,1)S(1)}, bf16[24,5120]{1,0:T(8,128)(2,1)S(1)}, u32[]{:S(2)}, u32[]{:S(2)}) collective-permute-start(bf16[24,5120]{1,0:T(8,128)(2,1)S(1)} %get-tuple-element.87), channel_id=1, source_target_pairs={{0,64},{64,0},{128,192},{192,128},{1,65},{65,1},{129,193},{193,129... | collective-permute-start | bytes 737288 | tf_op jit(solution)/shard_map/ppermute | solution.py:373
  242.4 4.3 %collective-permute-done.22.refs_1_ = bf16[24,5120]{1,0:T(8,128)(2,1)S(1)} collective-permute-done((bf16[24,5120]{1,0:T(8,128)(2,1)S(1)}, bf16[24,5120]{1,0:T(8,128)(2,1)S(1)}, u32[]{:S(2)}, u32[]{:S(2)}) %collective-permute-start.22) | collective-permute-done | bytes 245792 | tf_op jit(solution)/shard_map/ppermute | solution.py:373
  246.7 3.7 %collective-permute-start.25 = (bf16[320,256]{1,0:T(8,128)(2,1)S(1)}, bf16[320,256]{1,0:T(8,128)(2,1)S(1)}, u32[]{:S(2)}, u32[]{:S(2)}) collective-permute-start(bf16[320,256]{1,0:T(8,128)(2,1)S(1)} %get-tuple-element.100), channel_id=1, source_target_pairs={{0,48},{16,0},{32,16},{48,32},{1,49},{17,1},{33,17},{49,33},{2,50}... | collective-permute-start | bytes 491528 | tf_op jit(solution)/shard_map/ppermute | solution.py:368
  250.4 3.7 %collective-permute-start.24 = (bf16[320,256]{1,0:T(8,128)(2,1)S(1)}, bf16[320,256]{1,0:T(8,128)(2,1)S(1)}, u32[]{:S(2)}, u32[]{:S(2)}) collective-permute-start(bf16[320,256]{1,0:T(8,128)(2,1)S(1)} %get-tuple-element.99), channel_id=1, source_target_pairs={{0,32},{16,48},{32,0},{48,16},{1,33},{17,49},{33,1},{49,17},{2,34}... | collective-permute-start | bytes 491528 | tf_op jit(solution)/shard_map/ppermute | solution.py:368
  254.1 12.1 %backward_set.7 = (bf16[24,5120]{1,0:T(8,128)(2,1)}, bf16[16,4,24,320]{3,2,1,0:T(8,128)(2,1)}) custom-call(s32[7]{0:T(128)S(1)} %stack.100.refs_0_, bf16[24,5120]{1,0:T(8,128)(2,1)S(1)} %collective-permute-done.22.refs_1_, bf16[4,24,5120]{2,1,0:T(8,128)(2,1)} %get-tuple-element.82.refs_2_, ...), custom_call_target="tpu_custom_call", output_to_operand_aliasing={{1}: (24, {})} | custom-call | flops 125829120 | bytes 5242880 | tf_op jit(solution)/shard_map/backward_set/pallas_call | solution.py:315
  266.3 24.1 %all_to_all.10.refs_1_ = bf16[16,4,24,320]{3,2,1,0:T(8,128)(2,1)S(1)} all-to-all(bf16[16,4,24,320]{3,2,1,0:T(8,128)(2,1)} %get-tuple-element.101), channel_id=1, replica_groups=mesh['y'=4,'zh'=4,'zl'=2,'x'=4,'core'=2] {'zl','x','core'}, dimensions={0} | all-to-all | bytes 1966080 | tf_op jit(solution)/shard_map/all_to_all | solution.py:377
  292.3 2.2 collective-permute-start.28
  294.6 3.7 %collective-permute-start.27 = (bf16[320,256]{1,0:T(8,128)(2,1)S(1)}, bf16[320,256]{1,0:T(8,128)(2,1)S(1)}, u32[]{:S(2)}, u32[]{:S(2)}) collective-permute-start(bf16[320,256]{1,0:T(8,128)(2,1)S(1)} %get-tuple-element.104), channel_id=1, source_target_pairs={{0,32},{16,48},{32,0},{48,16},{1,33},{17,49},{33,1},{49,17},{2,34}... | collective-permute-start | bytes 491528 | tf_op jit(solution)/shard_map/ppermute | solution.py:368
  298.3 8.4 %collective-permute-done.28 = bf16[320,256]{1,0:T(8,128)(2,1)S(1)} collective-permute-done((bf16[320,256]{1,0:T(8,128)(2,1)S(1)}, bf16[320,256]{1,0:T(8,128)(2,1)S(1)}, u32[]{:S(2)}, u32[]{:S(2)}) %collective-permute-start.28) | collective-permute-done | bytes 163872 | tf_op jit(solution)/shard_map/ppermute | solution.py:368
  306.7 3.2 collective-permute-done.27
  312.2 2.2 collective-permute-start.29
  314.4 4.6 %collective-permute-done.29 = bf16[320,256]{1,0:T(8,128)(2,1)S(1)} collective-permute-done((bf16[320,256]{1,0:T(8,128)(2,1)S(1)}, bf16[320,256]{1,0:T(8,128)(2,1)S(1)}, u32[]{:S(2)}, u32[]{:S(2)}) %collective-permute-start.29) | collective-permute-done | bytes 163872 | tf_op jit(solution)/shard_map/ppermute | solution.py:386
  (76 shorter events, 38.7 us)
Async XLA Ops:
  6.5 152.5 %all-gather.5.cloned.1.call-start = ((), (), s32[]{:S(2)}) async-start(), calls=%async_computation.2 | async-start | bytes 21299200 | tf_op jit(solution)/shard_map/all_gather | solution.py:428
  11.4 28.4 %collective-permute-start.2 = (bf16[2,320,256]{2,1,0:T(8,128)(2,1)S(1)}, bf16[2,320,256]{2,1,0:T(8,128)(2,1)S(1)}, u32[]{:S(2)}, u32[]{:S(2)}) collective-permute-start(bf16[2,320,256]{2,1,0:T(8,128)(2,1)S(1)} %pad_maximum_fusion.2), channel_id=1, source_target_pairs={{0,208},{16,192},{32,240},{48,224},{64,144},{80,128},{96,176},{112... | collective-permute-start | bytes 983048 | tf_op jit(solution)/shard_map/ppermute | solution.py:395
  17.2 28.1 %collective-permute-start.1 = (bf16[2,320,256]{2,1,0:T(8,128)(2,1)S(1)}, bf16[2,320,256]{2,1,0:T(8,128)(2,1)S(1)}, u32[]{:S(2)}, u32[]{:S(2)}) collective-permute-start(bf16[2,320,256]{2,1,0:T(8,128)(2,1)S(1)} %pad_maximum_fusion.2), channel_id=1, source_target_pairs={{0,16},{16,0},{32,48},{48,32},{1,17},{17,1},{33,49},{49,33},{2,18}... | collective-permute-start | bytes 983048 | tf_op jit(solution)/shard_map/ppermute | solution.py:390
  45.5 187.4 %all-gather.7.cloned.1.call-start = ((), (), s32[]{:S(2)}) async-start(), calls=%async_computation.3 | async-start | bytes 1671168 | tf_op jit(solution)/shard_map/all_gather | solution.py:466
  45.5 59.3 %collective-permute-start = (bf16[2,8,320,256]{3,2,1,0:T(8,128)(2,1)}, bf16[2,8,320,256]{3,2,1,0:T(8,128)(2,1)}, u32[]{:S(2)}, u32[]{:S(2)}) collective-permute-start(bf16[2,8,320,256]{3,2,1,0:T(8,128)(2,1)} %pad_maximum_fusion), channel_id=1, source_target_pairs={{0,192},{192,0},{64,128},{128,64},{1,193},{193,1},{65,129},{129,65... | collective-permute-start | bytes 7864328 | tf_op jit(solution)/shard_map/ppermute | solution.py:386
  46.8 17.3 %collective-permute-start.3 = (bf16[2,2,320,256]{3,2,1,0:T(8,128)(2,1)S(1)}, bf16[2,2,320,256]{3,2,1,0:T(8,128)(2,1)S(1)}, u32[]{:S(2)}, u32[]{:S(2)}) collective-permute-start(bf16[2,2,320,256]{3,2,1,0:T(8,128)(2,1)S(1)} %pad_maximum_fusion.1.refs_6_.refs_8_), channel_id=1, source_target_pairs={{8,0},{0,8},{9,1},{1,9},{10,2},{2,10},{11,3},{3,11},{12,4},{4,12},... | collective-permute-start | bytes 1966088 | tf_op jit(solution)/shard_map/ppermute | solution.py:382
  47.2 18.2 %collective-permute-start.4 = (bf16[2,2,320,256]{3,2,1,0:T(8,128)(2,1)S(1)}, bf16[2,2,320,256]{3,2,1,0:T(8,128)(2,1)S(1)}, u32[]{:S(2)}, u32[]{:S(2)}) collective-permute-start(bf16[2,2,320,256]{3,2,1,0:T(8,128)(2,1)S(1)} %pad_maximum_fusion.1.refs_6_.refs_8_), channel_id=1, source_target_pairs={{2,0},{4,2},{6,4},{0,6},{3,1},{5,3},{7,5},{1,7},{10,8},{12,10},{14... | collective-permute-start | bytes 1966088 | tf_op jit(solution)/shard_map/ppermute | solution.py:382
  47.7 19.8 %collective-permute-start.5 = (bf16[2,2,320,256]{3,2,1,0:T(8,128)(2,1)S(1)}, bf16[2,2,320,256]{3,2,1,0:T(8,128)(2,1)S(1)}, u32[]{:S(2)}, u32[]{:S(2)}) collective-permute-start(bf16[2,2,320,256]{3,2,1,0:T(8,128)(2,1)S(1)} %pad_maximum_fusion.1.refs_6_.refs_8_), channel_id=1, source_target_pairs={{6,0},{0,2},{2,4},{4,6},{7,1},{1,3},{3,5},{5,7},{14,8},{8,10},{10,... | collective-permute-start | bytes 1966088 | tf_op jit(solution)/shard_map/ppermute | solution.py:382
  67.6 17.6 %collective-permute-start.8 = (bf16[2,2,320,256]{3,2,1,0:T(8,128)(2,1)S(1)}, bf16[2,2,320,256]{3,2,1,0:T(8,128)(2,1)}, u32[]{:S(2)}, u32[]{:S(2)}) collective-permute-start(bf16[2,2,320,256]{3,2,1,0:T(8,128)(2,1)S(1)} %collective-permute-done.3.refs_14_.refs_16_), channel_id=1, source_target_pairs={{6,0},{0,2},{2,4},{4,6},{7,1},{1,3},{3,5},{5,7},{14,8},{8,10},{10,... | collective-permute-start | bytes 1966088 | tf_op jit(solution)/shard_map/ppermute | solution.py:382
  68.0 30.9 %collective-permute-start.7 = (bf16[2,2,320,256]{3,2,1,0:T(8,128)(2,1)S(1)}, bf16[2,2,320,256]{3,2,1,0:T(8,128)(2,1)}, u32[]{:S(2)}, u32[]{:S(2)}) collective-permute-start(bf16[2,2,320,256]{3,2,1,0:T(8,128)(2,1)S(1)} %collective-permute-done.3.refs_14_.refs_16_), channel_id=1, source_target_pairs={{2,0},{4,2},{6,4},{0,6},{3,1},{5,3},{7,5},{1,7},{10,8},{12,10},{14... | collective-permute-start | bytes 1966088 | tf_op jit(solution)/shard_map/ppermute | solution.py:382
  71.2 27.7 %collective-permute-start.6 = (bf16[2,2,320,256]{3,2,1,0:T(8,128)(2,1)S(1)}, bf16[2,2,320,256]{3,2,1,0:T(8,128)(2,1)}, u32[]{:S(2)}, u32[]{:S(2)}) collective-permute-start(bf16[2,2,320,256]{3,2,1,0:T(8,128)(2,1)S(1)} %collective-permute-done.4.refs_8_.refs_10_), channel_id=1, source_target_pairs={{2,0},{4,2},{6,4},{0,6},{3,1},{5,3},{7,5},{1,7},{10,8},{12,10},{14... | collective-permute-start | bytes 1966088 | tf_op jit(solution)/shard_map/ppermute | solution.py:382
  85.1 18.4 %collective-permute-start.9 = (bf16[2,2,320,256]{3,2,1,0:T(8,128)(2,1)}, bf16[2,2,320,256]{3,2,1,0:T(8,128)(2,1)}, u32[]{:S(2)}, u32[]{:S(2)}) collective-permute-start(bf16[2,2,320,256]{3,2,1,0:T(8,128)(2,1)} %collective-permute-done.8.refs_20_.refs_22_), channel_id=1, source_target_pairs={{6,0},{0,2},{2,4},{4,6},{7,1},{1,3},{3,5},{5,7},{14,8},{8,10},{10,... | collective-permute-start | bytes 1966088 | tf_op jit(solution)/shard_map/ppermute | solution.py:382
  104.9 15.6 %collective-permute-start.10 = (bf16[2,8,320,256]{3,2,1,0:T(8,128)(2,1)}, bf16[2,8,320,256]{3,2,1,0:T(8,128)(2,1)}, u32[]{:S(2)}, u32[]{:S(2)}) collective-permute-start(bf16[2,8,320,256]{3,2,1,0:T(8,128)(2,1)} %collective-permute-done.refs_4_.refs_6_), channel_id=1, source_target_pairs={{1,0},{0,1},{3,2},{2,3},{5,4},{4,5},{7,6},{6,7},{9,8},{8,9},{11,10... | collective-permute-start | bytes 7864328 | tf_op jit(solution)/shard_map/ppermute | solution.py:382
  105.4 5.4 %collective-permute-start.12 = (bf16[2,2,320,256]{3,2,1,0:T(8,128)(2,1)S(1)}, bf16[2,2,320,256]{3,2,1,0:T(8,128)(2,1)S(1)}, u32[]{:S(2)}, u32[]{:S(2)}) collective-permute-start(bf16[2,2,320,256]{3,2,1,0:T(8,128)(2,1)S(1)} %collective-permute-done.4.refs_8_.refs_10_), channel_id=1, source_target_pairs={{1,0},{0,1},{3,2},{2,3},{5,4},{4,5},{7,6},{6,7},{9,8},{8,9},{11,10... | collective-permute-start | bytes 1966088 | tf_op jit(solution)/shard_map/ppermute | solution.py:382
  105.4 7.4 %collective-permute-start.14 = (bf16[2,2,320,256]{3,2,1,0:T(8,128)(2,1)S(1)}, bf16[2,2,320,256]{3,2,1,0:T(8,128)(2,1)S(1)}, u32[]{:S(2)}, u32[]{:S(2)}) collective-permute-start(bf16[2,2,320,256]{3,2,1,0:T(8,128)(2,1)S(1)} %collective-permute-done.5.refs_12_.refs_14_), channel_id=1, source_target_pairs={{1,0},{0,1},{3,2},{2,3},{5,4},{4,5},{7,6},{6,7},{9,8},{8,9},{11,10... | collective-permute-start | bytes 1966088 | tf_op jit(solution)/shard_map/ppermute | solution.py:382
  105.9 9.4 %collective-permute-start.15 = (bf16[2,2,320,256]{3,2,1,0:T(8,128)(2,1)S(1)}, bf16[2,2,320,256]{3,2,1,0:T(8,128)(2,1)S(1)}, u32[]{:S(2)}, u32[]{:S(2)}) collective-permute-start(bf16[2,2,320,256]{3,2,1,0:T(8,128)(2,1)S(1)} %collective-permute-done.3.refs_14_.refs_16_), channel_id=1, source_target_pairs={{1,0},{0,1},{3,2},{2,3},{5,4},{4,5},{7,6},{6,7},{9,8},{8,9},{11,10... | collective-permute-start | bytes 1966088 | tf_op jit(solution)/shard_map/ppermute | solution.py:382
  108.1 9.9 %collective-permute-start.18 = (bf16[2,2,320,256]{3,2,1,0:T(8,128)(2,1)}, bf16[2,2,320,256]{3,2,1,0:T(8,128)(2,1)}, u32[]{:S(2)}, u32[]{:S(2)}) collective-permute-start(bf16[2,2,320,256]{3,2,1,0:T(8,128)(2,1)} %collective-permute-done.8.refs_20_.refs_22_), channel_id=1, source_target_pairs={{1,0},{0,1},{3,2},{2,3},{5,4},{4,5},{7,6},{6,7},{9,8},{8,9},{11,10... | collective-permute-start | bytes 1966088 | tf_op jit(solution)/shard_map/ppermute | solution.py:382
  110.8 7.6 %collective-permute-start.13 = (bf16[2,2,320,256]{3,2,1,0:T(8,128)(2,1)}, bf16[2,2,320,256]{3,2,1,0:T(8,128)(2,1)}, u32[]{:S(2)}, u32[]{:S(2)}) collective-permute-start(bf16[2,2,320,256]{3,2,1,0:T(8,128)(2,1)} %collective-permute-done.6.refs_10_.refs_12_), channel_id=1, source_target_pairs={{1,0},{0,1},{3,2},{2,3},{5,4},{4,5},{7,6},{6,7},{9,8},{8,9},{11,10... | collective-permute-start | bytes 1966088 | tf_op jit(solution)/shard_map/ppermute | solution.py:382
  112.8 6.7 %collective-permute-start.16 = (bf16[2,2,320,256]{3,2,1,0:T(8,128)(2,1)}, bf16[2,2,320,256]{3,2,1,0:T(8,128)(2,1)}, u32[]{:S(2)}, u32[]{:S(2)}) collective-permute-start(bf16[2,2,320,256]{3,2,1,0:T(8,128)(2,1)} %collective-permute-done.7.refs_16_.refs_18_), channel_id=1, source_target_pairs={{1,0},{0,1},{3,2},{2,3},{5,4},{4,5},{7,6},{6,7},{9,8},{8,9},{11,10... | collective-permute-start | bytes 1966088 | tf_op jit(solution)/shard_map/ppermute | solution.py:382
  116.2 4.2 %collective-permute-start.17 = (bf16[2,2,320,256]{3,2,1,0:T(8,128)(2,1)}, bf16[2,2,320,256]{3,2,1,0:T(8,128)(2,1)}, u32[]{:S(2)}, u32[]{:S(2)}) collective-permute-start(bf16[2,2,320,256]{3,2,1,0:T(8,128)(2,1)} %collective-permute-done.9.refs_18_.refs_20_), channel_id=1, source_target_pairs={{1,0},{0,1},{3,2},{2,3},{5,4},{4,5},{7,6},{6,7},{9,8},{8,9},{11,10... | collective-permute-start | bytes 1966088 | tf_op jit(solution)/shard_map/ppermute | solution.py:382
  133.2 8.2 %collective-permute-start.19 = (bf16[24,5120]{1,0:T(8,128)(2,1)S(1)}, bf16[24,5120]{1,0:T(8,128)(2,1)S(1)}, u32[]{:S(2)}, u32[]{:S(2)}) collective-permute-start(bf16[24,5120]{1,0:T(8,128)(2,1)S(1)} %get-tuple-element.66), channel_id=1, source_target_pairs={{0,64},{64,0},{128,192},{192,128},{1,65},{65,1},{129,193},{193,129... | collective-permute-start | bytes 737288 | tf_op jit(solution)/shard_map/ppermute | solution.py:373
  159.7 16.0 %collective-permute-start.20 = (bf16[24,5120]{1,0:T(8,128)(2,1)S(1)}, bf16[24,5120]{1,0:T(8,128)(2,1)S(1)}, u32[]{:S(2)}, u32[]{:S(2)}) collective-permute-start(bf16[24,5120]{1,0:T(8,128)(2,1)S(1)} %get-tuple-element.72), channel_id=1, source_target_pairs={{0,64},{64,0},{128,192},{192,128},{1,65},{65,1},{129,193},{193,129... | collective-permute-start | bytes 737288 | tf_op jit(solution)/shard_map/ppermute | solution.py:373
  200.4 7.7 %collective-permute-start.21 = (bf16[24,5120]{1,0:T(8,128)(2,1)S(1)}, bf16[24,5120]{1,0:T(8,128)(2,1)S(1)}, u32[]{:S(2)}, u32[]{:S(2)}) collective-permute-start(bf16[24,5120]{1,0:T(8,128)(2,1)S(1)} %get-tuple-element.79), channel_id=1, source_target_pairs={{0,64},{64,0},{128,192},{192,128},{1,65},{65,1},{129,193},{193,129... | collective-permute-start | bytes 737288 | tf_op jit(solution)/shard_map/ppermute | solution.py:373
  208.7 31.7 %all-to-all-start = ((bf16[16,4,24,320]{3,2,1,0:T(8,128)(2,1)}), bf16[16,4,24,320]{3,2,1,0:T(8,128)(2,1)S(1)}, u32[]{:S(2)}, u32[]{:S(2)}) async-start(bf16[16,4,24,320]{3,2,1,0:T(8,128)(2,1)} %get-tuple-element.88), calls=%async_computation | async-start | bytes 2359296 | tf_op jit(solution)/shard_map/all_to_all | solution.py:377
  232.9 13.8 %collective-permute-start.22 = (bf16[24,5120]{1,0:T(8,128)(2,1)S(1)}, bf16[24,5120]{1,0:T(8,128)(2,1)S(1)}, u32[]{:S(2)}, u32[]{:S(2)}) collective-permute-start(bf16[24,5120]{1,0:T(8,128)(2,1)S(1)} %get-tuple-element.87), channel_id=1, source_target_pairs={{0,64},{64,0},{128,192},{192,128},{1,65},{65,1},{129,193},{193,129... | collective-permute-start | bytes 737288 | tf_op jit(solution)/shard_map/ppermute | solution.py:373
  246.7 19.5 %collective-permute-start.25 = (bf16[320,256]{1,0:T(8,128)(2,1)S(1)}, bf16[320,256]{1,0:T(8,128)(2,1)S(1)}, u32[]{:S(2)}, u32[]{:S(2)}) collective-permute-start(bf16[320,256]{1,0:T(8,128)(2,1)S(1)} %get-tuple-element.100), channel_id=1, source_target_pairs={{0,48},{16,0},{32,16},{48,32},{1,49},{17,1},{33,17},{49,33},{2,50}... | collective-permute-start | bytes 491528 | tf_op jit(solution)/shard_map/ppermute | solution.py:368
  250.4 15.8 %collective-permute-start.24 = (bf16[320,256]{1,0:T(8,128)(2,1)S(1)}, bf16[320,256]{1,0:T(8,128)(2,1)S(1)}, u32[]{:S(2)}, u32[]{:S(2)}) collective-permute-start(bf16[320,256]{1,0:T(8,128)(2,1)S(1)} %get-tuple-element.99), channel_id=1, source_target_pairs={{0,32},{16,48},{32,0},{48,16},{1,33},{17,49},{33,1},{49,17},{2,34}... | collective-permute-start | bytes 491528 | tf_op jit(solution)/shard_map/ppermute | solution.py:368
  254.1 12.1 %collective-permute-start.23 = (bf16[320,256]{1,0:T(8,128)(2,1)S(1)}, bf16[320,256]{1,0:T(8,128)(2,1)S(1)}, u32[]{:S(2)}, u32[]{:S(2)}) collective-permute-start(bf16[320,256]{1,0:T(8,128)(2,1)S(1)} %get-tuple-element.98), channel_id=1, source_target_pairs={{0,16},{16,32},{32,48},{48,0},{1,17},{17,33},{33,49},{49,1},{2,18}... | collective-permute-start | bytes 491528 | tf_op jit(solution)/shard_map/ppermute | solution.py:368
  292.3 14.4 %collective-permute-start.28 = (bf16[320,256]{1,0:T(8,128)(2,1)S(1)}, bf16[320,256]{1,0:T(8,128)(2,1)S(1)}, u32[]{:S(2)}, u32[]{:S(2)}) collective-permute-start(bf16[320,256]{1,0:T(8,128)(2,1)S(1)} %get-tuple-element.105), channel_id=1, source_target_pairs={{0,48},{16,0},{32,16},{48,32},{1,49},{17,1},{33,17},{49,33},{2,50}... | collective-permute-start | bytes 491528 | tf_op jit(solution)/shard_map/ppermute | solution.py:368
  294.6 15.4 %collective-permute-start.27 = (bf16[320,256]{1,0:T(8,128)(2,1)S(1)}, bf16[320,256]{1,0:T(8,128)(2,1)S(1)}, u32[]{:S(2)}, u32[]{:S(2)}) collective-permute-start(bf16[320,256]{1,0:T(8,128)(2,1)S(1)} %get-tuple-element.104), channel_id=1, source_target_pairs={{0,32},{16,48},{32,0},{48,16},{1,33},{17,49},{33,1},{49,17},{2,34}... | collective-permute-start | bytes 491528 | tf_op jit(solution)/shard_map/ppermute | solution.py:368
  298.3 13.8 %collective-permute-start.26 = (bf16[320,256]{1,0:T(8,128)(2,1)S(1)}, bf16[320,256]{1,0:T(8,128)(2,1)S(1)}, u32[]{:S(2)}, u32[]{:S(2)}) collective-permute-start(bf16[320,256]{1,0:T(8,128)(2,1)S(1)} %get-tuple-element.103), channel_id=1, source_target_pairs={{0,16},{16,32},{32,48},{48,0},{1,17},{17,33},{33,49},{49,1},{2,18}... | collective-permute-start | bytes 491528 | tf_op jit(solution)/shard_map/ppermute | solution.py:368
  312.2 6.8 %collective-permute-start.29 = (bf16[320,256]{1,0:T(8,128)(2,1)S(1)}, bf16[320,256]{1,0:T(8,128)(2,1)S(1)}, u32[]{:S(2)}, u32[]{:S(2)}) collective-permute-start(bf16[320,256]{1,0:T(8,128)(2,1)S(1)} %get-tuple-element.107), channel_id=1, source_target_pairs={{0,192},{192,0},{64,128},{128,64},{1,193},{193,1},{65,129},{129,65... | collective-permute-start | bytes 491528 | tf_op jit(solution)/shard_map/ppermute | solution.py:386
  (7 other events, 170.4 us)
Sparse Core Ops, SparseCore 0:
  45.6 113.3 all-gather.4
  188.2 44.6 all-gather.6

commit v10 on v9

--- a/solution.py
+++ b/solution.py
@@ -442,8 +442,12 @@
     chunk_b, near_a = lax.optimization_barrier((own(1 - first_slot), over_z(chunk_a)))
     w_b = (gathered(chunk_b),)
     blocks = list(over_x(near_a))
-    half_a, blocks[2], *blocks[5:7] = lax.optimization_barrier((half_a, blocks[2], *blocks[5:7]))
-    w_a = own_layers + both_cores([half_a] + blocks)
+    early = both_cores([blocks[0], blocks[1], blocks[3], blocks[4]])
+    half_a, early, blocks[2], *blocks[5:7] = lax.optimization_barrier(
+        (half_a, early, blocks[2], *blocks[5:7])
+    )
+    late = both_cores([half_a, blocks[2]] + blocks[5:])
+    w_a = own_layers + late[:2] + early[:4] + late[2:4] + early[4:] + late[4:]
 
     def flag(active, slot_now):
         reverse = slot_now == 1

time: 330 us -> 333 us (level)
  starting transfers between devices: 58.1 us -> 62.5 us
    ppermute x4, starting transfers between devices: 17.4 us -> 25.7 us  [hop(): return lax.ppermute(rows, 'y', [(0, 1), (1, 0), (2, 3), (3, 2)])]
    ppermute x16, waiting for transfers between devices: 58.4 us -> 66.2 us  [from_ring(): lax.ppermute(block, axis, [((d + away) % count, d) for d in range(count)])]
    all_gather x1, waiting for transfers between devices: 17 us -> 10.5 us  [shards(): act_all = lax.all_gather(jnp.concatenate([act_a, act_b], axis=0), DP)]
  transfers between devices with their start and end apart: 33 -> 33, of which waited for: 26 -> 23; matrix products, arithmetic and copies ran while one was open for 1% -> 1% of each run, Pallas kernels for 13% -> 12%
where the time goes in v10:
time: 333 us; the launch traced here: 328 us
  waiting for transfers between devices  163 us (49%)
  starting transfers between devices  62.5 us (19%)
  Pallas kernels  55.1 us (17%)
  blocking collectives  24.7 us (7%)
  between operations  13.7 us (4%)
  other arithmetic  5.47 us (2%)
  local copies, waits for them, and re-layouts  3.53 us (1%)
    ppermute x16, waiting for transfers between devices, from_ring(): lax.ppermute(block, axis, [((d + away) % count, d) for d in range(count)])  66.2 us
    ppermute x4, waiting for transfers between devices, hop(): return lax.ppermute(rows, 'y', [(0, 1), (1, 0), (2, 3), (3, 2)])  26.1 us
    ppermute x4, starting transfers between devices, hop(): return lax.ppermute(rows, 'y', [(0, 1), (1, 0), (2, 3), (3, 2)])  25.7 us
    pallas_call x4, Pallas kernels, run_backward(): pl.pallas_call(lambda *refs: backward_kernel(*refs, source=source, aliase...  25.7 us
    pallas_call x4, Pallas kernels, run_forward(): pl.pallas_call(lambda *refs: forward_kernel(*refs, source=source, aliased...  25.5 us
    all_to_all x1, blocking collectives, spread(): return lax.all_to_all(g_set, DP, 0, 0)  24.7 us
    ppermute x1, waiting for transfers between devices, over_z(): return jnp.stack([beside, lax.ppermute(chunk_now, ('y', 'zh'), route)])  21.8 us
    all_gather x1, waiting for transfers between devices, gathered(): lax.all_gather(own_part, ('zh',) + DP).reshape(SET, 16, 2, D // 16, R)  16 us
  transfers between devices with their start and end apart: 33, of which 23 were waited for; matrix products, arithmetic and copies ran while one was open for 1% of the time, Pallas kernels for 12%

profile of v10, /device:TPU:2, one launch (start us, length us, event | category | flops | bytes accessed | tf_op | source)
XLA Modules:
  0.0 328.2 jit_solution(781127887645380886)
XLA Ops:
  6.5 1.9 constant_dynamic-slice_fusion
  11.4 5.8 %collective-permute-start.2 = (bf16[2,320,256]{2,1,0:T(8,128)(2,1)S(1)}, bf16[2,320,256]{2,1,0:T(8,128)(2,1)S(1)}, u32[]{:S(2)}, u32[]{:S(2)}) collective-permute-start(bf16[2,320,256]{2,1,0:T(8,128)(2,1)S(1)} %pad_maximum_fusion.2), channel_id=1, source_target_pairs={{0,208},{16,192},{32,240},{48,224},{64,144},{80,128},{96,176},{112... | collective-permute-start | bytes 983048 | tf_op jit(solution)/shard_map/ppermute | solution.py:395
  18.0 21.8 %collective-permute-done.2 = bf16[2,320,256]{2,1,0:T(8,128)(2,1)S(1)} collective-permute-done((bf16[2,320,256]{2,1,0:T(8,128)(2,1)S(1)}, bf16[2,320,256]{2,1,0:T(8,128)(2,1)S(1)}, u32[]{:S(2)}, u32[]{:S(2)}) %collective-permute-start.2) | collective-permute-done | bytes 327712 | tf_op jit(solution)/shard_map/ppermute | solution.py:395
  39.8 5.6 %collective-permute-done.1 = bf16[2,320,256]{2,1,0:T(8,128)(2,1)S(1)} collective-permute-done((bf16[2,320,256]{2,1,0:T(8,128)(2,1)S(1)}, bf16[2,320,256]{2,1,0:T(8,128)(2,1)S(1)}, u32[]{:S(2)}, u32[]{:S(2)}) %collective-permute-start.1) | collective-permute-done | bytes 327712 | tf_op jit(solution)/shard_map/ppermute | solution.py:390
  49.2 14.9 %collective-permute-done.4.refs_14_.refs_16_ = bf16[2,2,320,256]{3,2,1,0:T(8,128)(2,1)S(1)} collective-permute-done((bf16[2,2,320,256]{3,2,1,0:T(8,128)(2,1)S(1)}, bf16[2,2,320,256]{3,2,1,0:T(8,128)(2,1)S(1)}, u32[]{:S(2)}, u32[]{:S(2)}) %collective-permute-start.4) | collective-permute-done | bytes 655392 | tf_op jit(solution)/shard_map/ppermute | solution.py:382
  65.4 2.1 collective-permute-done.6.refs_12_.refs_14_
  69.7 3.6 %collective-permute-start.10 = (bf16[2,2,320,256]{3,2,1,0:T(8,128)(2,1)S(1)}, bf16[2,2,320,256]{3,2,1,0:T(8,128)(2,1)}, u32[]{:S(2)}, u32[]{:S(2)}) collective-permute-start(bf16[2,2,320,256]{3,2,1,0:T(8,128)(2,1)S(1)} %collective-permute-done.5.refs_8_.refs_10_), channel_id=1, source_target_pairs={{2,0},{4,2},{6,4},{0,6},{3,1},{5,3},{7,5},{1,7},{10,8},{12,10},{14... | collective-permute-start | bytes 1966088 | tf_op jit(solution)/shard_map/ppermute | solution.py:382
  75.0 13.4 %collective-permute-done.12.refs_20_.refs_22_ = bf16[2,2,320,256]{3,2,1,0:T(8,128)(2,1)} collective-permute-done((bf16[2,2,320,256]{3,2,1,0:T(8,128)(2,1)S(1)}, bf16[2,2,320,256]{3,2,1,0:T(8,128)(2,1)}, u32[]{:S(2)}, u32[]{:S(2)}) %collective-permute-start.12) | collective-permute-done | bytes 655392 | tf_op jit(solution)/shard_map/ppermute | solution.py:382
  88.8 17.9 %collective-permute-done.11.refs_16_.refs_18_ = bf16[2,2,320,256]{3,2,1,0:T(8,128)(2,1)} collective-permute-done((bf16[2,2,320,256]{3,2,1,0:T(8,128)(2,1)S(1)}, bf16[2,2,320,256]{3,2,1,0:T(8,128)(2,1)}, u32[]{:S(2)}, u32[]{:S(2)}) %collective-permute-start.11) | collective-permute-done | bytes 655392 | tf_op jit(solution)/shard_map/ppermute | solution.py:382
  106.7 6.7 %collective-permute-done.13.refs_18_.refs_20_ = bf16[2,2,320,256]{3,2,1,0:T(8,128)(2,1)} collective-permute-done((bf16[2,2,320,256]{3,2,1,0:T(8,128)(2,1)}, bf16[2,2,320,256]{3,2,1,0:T(8,128)(2,1)}, u32[]{:S(2)}, u32[]{:S(2)}) %collective-permute-start.13) | collective-permute-done | bytes 655392 | tf_op jit(solution)/shard_map/ppermute | solution.py:382
  116.1 4.3 %collective-permute-done.18.refs_21_.refs_23_ = bf16[2,2,320,256]{3,2,1,0:T(8,128)(2,1)} collective-permute-done((bf16[2,2,320,256]{3,2,1,0:T(8,128)(2,1)}, bf16[2,2,320,256]{3,2,1,0:T(8,128)(2,1)}, u32[]{:S(2)}, u32[]{:S(2)}) %collective-permute-start.18) | collective-permute-done | bytes 655392 | tf_op jit(solution)/shard_map/ppermute | solution.py:382
  124.4 12.5 %forward_set.4 = (bf16[24,5120]{1,0:T(8,128)(2,1)S(1)}, bf16[4,24,5120]{2,1,0:T(8,128)(2,1)}, f32[4,24,256]{2,1,0:T(8,128)S(1)}, bf16[4,24,256]{2,1,0:T(8,128)(2,1)S(1)}) custom-call(s32[7]{0:T(128)S(1)} %stack.100.refs_0_, bf16[24,5120]{1,0:T(8,128)(2,1)S(1)} %pad.4.refs_1_, bf16[2,16,320,256]{3,2,1,0:T(8,128)(2,1)} %bitcast.33, ...), custom_call_target="tpu_custom_call" | custom-call | flops 125829120 | bytes 5242880 | tf_op jit(solution)/shard_map/forward_set/pallas_call | solution.py:194
  137.2 7.9 %collective-permute-done.19.refs_1_ = bf16[24,5120]{1,0:T(8,128)(2,1)S(1)} collective-permute-done((bf16[24,5120]{1,0:T(8,128)(2,1)S(1)}, bf16[24,5120]{1,0:T(8,128)(2,1)S(1)}, u32[]{:S(2)}, u32[]{:S(2)}) %collective-permute-start.19) | collective-permute-done | bytes 245792 | tf_op jit(solution)/shard_map/ppermute | solution.py:373
  145.8 16.0 %all-gather.5.cloned.1.call-done = bf16[128,320,256]{2,1,0:T(8,128)(2,1)} async-done(((bf16[2,320,256]{2,1,0:T(8,128)(2,1)}), bf16[128,320,256]{2,1,0:T(8,128)(2,1)}) %all-gather.5.cloned.1.call-update) | async-done | bytes 20971536 | tf_op jit(solution)/shard_map/all_gather | solution.py:428
  162.4 11.5 %collective-permute-start.20 = (bf16[24,5120]{1,0:T(8,128)(2,1)S(1)}, bf16[24,5120]{1,0:T(8,128)(2,1)S(1)}, u32[]{:S(2)}, u32[]{:S(2)}) collective-permute-start(bf16[24,5120]{1,0:T(8,128)(2,1)S(1)} %get-tuple-element.88), channel_id=1, source_target_pairs={{0,64},{64,0},{128,192},{192,128},{1,65},{65,1},{129,193},{193,129... | collective-permute-start | bytes 737288 | tf_op jit(solution)/shard_map/ppermute | solution.py:373
  173.9 6.3 %collective-permute-done.20.refs_1_ = bf16[24,5120]{1,0:T(8,128)(2,1)S(1)} collective-permute-done((bf16[24,5120]{1,0:T(8,128)(2,1)S(1)}, bf16[24,5120]{1,0:T(8,128)(2,1)S(1)}, u32[]{:S(2)}, u32[]{:S(2)}) %collective-permute-start.20) | collective-permute-done | bytes 245792 | tf_op jit(solution)/shard_map/ppermute | solution.py:373
  180.2 11.7 %forward_set.7 = (bf16[24,5120]{1,0:T(8,128)(2,1)S(1)}, bf16[4,24,5120]{2,1,0:T(8,128)(2,1)S(1)}, f32[4,24,256]{2,1,0:T(8,128)S(1)}, bf16[4,24,256]{2,1,0:T(8,128)(2,1)S(1)}) custom-call(s32[7]{0:T(128)S(1)} %stack.108.refs_0_, bf16[24,5120]{1,0:T(8,128)(2,1)S(1)} %collective-permute-done.20.refs_1_, ...), custom_call_target="tpu_custom_call", output_to_operand_aliasing={{1}: (3, {}), {2}: (4, {}), {3}: (5, {})} | custom-call | flops 125829120 | bytes 5242880 | tf_op jit(solution)/shard_map/forward_set/pallas_call | solution.py:194
  192.6 12.3 %backward_set.4 = (bf16[24,5120]{1,0:T(8,128)(2,1)S(1)}, bf16[16,4,24,320]{3,2,1,0:T(8,128)(2,1)}) custom-call(s32[7]{0:T(128)S(1)} %stack.108.refs_0_, bf16[24,5120]{1,0:T(8,128)(2,1)S(1)} %get-tuple-element.92.refs_1_, bf16[4,24,5120]{2,1,0:T(8,128)(2,1)S(1)} %get-tuple-element.93.refs_2_, f32[4,24,256]{2,1,0:T(8,128)S(1)} %get-tuple-element.94.refs_3_, ...), custom_call_target="tpu_custom_call" | custom-call | flops 125829120 | bytes 5242880 | tf_op jit(solution)/shard_map/backward_set/pallas_call | solution.py:315
  205.0 7.6 %collective-permute-done.21.refs_1_ = bf16[24,5120]{1,0:T(8,128)(2,1)S(1)} collective-permute-done((bf16[24,5120]{1,0:T(8,128)(2,1)S(1)}, bf16[24,5120]{1,0:T(8,128)(2,1)S(1)}, u32[]{:S(2)}, u32[]{:S(2)}) %collective-permute-start.21) | collective-permute-done | bytes 245792 | tf_op jit(solution)/shard_map/ppermute | solution.py:373
  213.3 6.5 %all-to-all-start = ((bf16[16,4,24,320]{3,2,1,0:T(8,128)(2,1)}), bf16[16,4,24,320]{3,2,1,0:T(8,128)(2,1)S(1)}, u32[]{:S(2)}, u32[]{:S(2)}) async-start(bf16[16,4,24,320]{3,2,1,0:T(8,128)(2,1)} %get-tuple-element.104), calls=%async_computation | async-start | bytes 2359296 | tf_op jit(solution)/shard_map/all_to_all | solution.py:377
  220.4 10.5 %all-gather.7.cloned.1.call-done = bf16[128,24,256]{2,1,0:T(8,128)(2,1)} async-done(((bf16[8,24,256]{2,1,0:T(8,128)(2,1)}), bf16[128,24,256]{2,1,0:T(8,128)(2,1)}) %all-gather.7.cloned.1.call-update) | async-done | bytes 1572880 | tf_op jit(solution)/shard_map/all_gather | solution.py:470
  230.9 14.1 %collective-permute-start.22 = (bf16[24,5120]{1,0:T(8,128)(2,1)S(1)}, bf16[24,5120]{1,0:T(8,128)(2,1)S(1)}, u32[]{:S(2)}, u32[]{:S(2)}) collective-permute-start(bf16[24,5120]{1,0:T(8,128)(2,1)S(1)} %get-tuple-element.103), channel_id=1, source_target_pairs={{0,64},{64,0},{128,192},{192,128},{1,65},{65,1},{129,193},{193,129... | collective-permute-start | bytes 737288 | tf_op jit(solution)/shard_map/ppermute | solution.py:373
  245.0 2.0 grad_set.2
  247.0 4.3 %collective-permute-done.22.refs_1_ = bf16[24,5120]{1,0:T(8,128)(2,1)S(1)} collective-permute-done((bf16[24,5120]{1,0:T(8,128)(2,1)S(1)}, bf16[24,5120]{1,0:T(8,128)(2,1)S(1)}, u32[]{:S(2)}, u32[]{:S(2)}) %collective-permute-start.22) | collective-permute-done | bytes 245792 | tf_op jit(solution)/shard_map/ppermute | solution.py:373
  252.9 2.0 collective-permute-start.24
  256.7 12.1 %backward_set.7 = (bf16[24,5120]{1,0:T(8,128)(2,1)}, bf16[16,4,24,320]{3,2,1,0:T(8,128)(2,1)}) custom-call(s32[7]{0:T(128)S(1)} %stack.100.refs_0_, bf16[24,5120]{1,0:T(8,128)(2,1)S(1)} %collective-permute-done.22.refs_1_, bf16[4,24,5120]{2,1,0:T(8,128)(2,1)} %get-tuple-element.98.refs_2_, ...), custom_call_target="tpu_custom_call", output_to_operand_aliasing={{1}: (24, {})} | custom-call | flops 125829120 | bytes 5242880 | tf_op jit(solution)/shard_map/backward_set/pallas_call | solution.py:315
  268.9 24.7 %all_to_all.10.refs_1_ = bf16[16,4,24,320]{3,2,1,0:T(8,128)(2,1)S(1)} all-to-all(bf16[16,4,24,320]{3,2,1,0:T(8,128)(2,1)} %get-tuple-element.117), channel_id=1, replica_groups=mesh['y'=4,'zh'=4,'zl'=2,'x'=4,'core'=2] {'zl','x','core'}, dimensions={0} | all-to-all | bytes 1966080 | tf_op jit(solution)/shard_map/all_to_all | solution.py:377
  293.6 2.0 grad_set.3
  297.3 2.0 collective-permute-start.27
  301.2 12.1 %collective-permute-done.28 = bf16[320,256]{1,0:T(8,128)(2,1)S(1)} collective-permute-done((bf16[320,256]{1,0:T(8,128)(2,1)S(1)}, bf16[320,256]{1,0:T(8,128)(2,1)S(1)}, u32[]{:S(2)}, u32[]{:S(2)}) %collective-permute-start.28) | collective-permute-done | bytes 163872 | tf_op jit(solution)/shard_map/ppermute | solution.py:368
  313.5 2.2 collective-permute-start.29
  315.8 4.8 %collective-permute-done.29 = bf16[320,256]{1,0:T(8,128)(2,1)S(1)} collective-permute-done((bf16[320,256]{1,0:T(8,128)(2,1)S(1)}, bf16[320,256]{1,0:T(8,128)(2,1)S(1)}, u32[]{:S(2)}, u32[]{:S(2)}) %collective-permute-start.29) | collective-permute-done | bytes 163872 | tf_op jit(solution)/shard_map/ppermute | solution.py:386
  (76 shorter events, 31.6 us)
Async XLA Ops:
  6.5 155.2 %all-gather.5.cloned.1.call-start = ((), (), s32[]{:S(2)}) async-start(), calls=%async_computation.2 | async-start | bytes 21299200 | tf_op jit(solution)/shard_map/all_gather | solution.py:428
  11.4 28.4 %collective-permute-start.2 = (bf16[2,320,256]{2,1,0:T(8,128)(2,1)S(1)}, bf16[2,320,256]{2,1,0:T(8,128)(2,1)S(1)}, u32[]{:S(2)}, u32[]{:S(2)}) collective-permute-start(bf16[2,320,256]{2,1,0:T(8,128)(2,1)S(1)} %pad_maximum_fusion.2), channel_id=1, source_target_pairs={{0,208},{16,192},{32,240},{48,224},{64,144},{80,128},{96,176},{112... | collective-permute-start | bytes 983048 | tf_op jit(solution)/shard_map/ppermute | solution.py:395
  17.2 28.1 %collective-permute-start.1 = (bf16[2,320,256]{2,1,0:T(8,128)(2,1)S(1)}, bf16[2,320,256]{2,1,0:T(8,128)(2,1)S(1)}, u32[]{:S(2)}, u32[]{:S(2)}) collective-permute-start(bf16[2,320,256]{2,1,0:T(8,128)(2,1)S(1)} %pad_maximum_fusion.2), channel_id=1, source_target_pairs={{0,16},{16,0},{32,48},{48,32},{1,17},{17,1},{33,49},{49,33},{2,18}... | collective-permute-start | bytes 983048 | tf_op jit(solution)/shard_map/ppermute | solution.py:390
  45.5 185.4 %all-gather.7.cloned.1.call-start = ((), (), s32[]{:S(2)}) async-start(), calls=%async_computation.3 | async-start | bytes 1671168 | tf_op jit(solution)/shard_map/all_gather | solution.py:470
  45.5 67.9 %collective-permute-start = (bf16[2,8,320,256]{3,2,1,0:T(8,128)(2,1)}, bf16[2,8,320,256]{3,2,1,0:T(8,128)(2,1)}, u32[]{:S(2)}, u32[]{:S(2)}) collective-permute-start(bf16[2,8,320,256]{3,2,1,0:T(8,128)(2,1)} %pad_maximum_fusion), channel_id=1, source_target_pairs={{0,192},{192,0},{64,128},{128,64},{1,193},{193,1},{65,129},{129,65... | collective-permute-start | bytes 7864328 | tf_op jit(solution)/shard_map/ppermute | solution.py:386
  46.8 17.3 %collective-permute-start.4 = (bf16[2,2,320,256]{3,2,1,0:T(8,128)(2,1)S(1)}, bf16[2,2,320,256]{3,2,1,0:T(8,128)(2,1)S(1)}, u32[]{:S(2)}, u32[]{:S(2)}) collective-permute-start(bf16[2,2,320,256]{3,2,1,0:T(8,128)(2,1)S(1)} %pad_maximum_fusion.1.refs_6_.refs_8_), channel_id=1, source_target_pairs={{8,0},{0,8},{9,1},{1,9},{10,2},{2,10},{11,3},{3,11},{12,4},{4,12},... | collective-permute-start | bytes 1966088 | tf_op jit(solution)/shard_map/ppermute | solution.py:382
  47.2 18.2 %collective-permute-start.5 = (bf16[2,2,320,256]{3,2,1,0:T(8,128)(2,1)S(1)}, bf16[2,2,320,256]{3,2,1,0:T(8,128)(2,1)S(1)}, u32[]{:S(2)}, u32[]{:S(2)}) collective-permute-start(bf16[2,2,320,256]{3,2,1,0:T(8,128)(2,1)S(1)} %pad_maximum_fusion.1.refs_6_.refs_8_), channel_id=1, source_target_pairs={{2,0},{4,2},{6,4},{0,6},{3,1},{5,3},{7,5},{1,7},{10,8},{12,10},{14... | collective-permute-start | bytes 1966088 | tf_op jit(solution)/shard_map/ppermute | solution.py:382
  47.7 19.8 %collective-permute-start.6 = (bf16[2,2,320,256]{3,2,1,0:T(8,128)(2,1)S(1)}, bf16[2,2,320,256]{3,2,1,0:T(8,128)(2,1)S(1)}, u32[]{:S(2)}, u32[]{:S(2)}) collective-permute-start(bf16[2,2,320,256]{3,2,1,0:T(8,128)(2,1)S(1)} %pad_maximum_fusion.1.refs_6_.refs_8_), channel_id=1, source_target_pairs={{6,0},{0,2},{2,4},{4,6},{7,1},{1,3},{3,5},{5,7},{14,8},{8,10},{10,... | collective-permute-start | bytes 1966088 | tf_op jit(solution)/shard_map/ppermute | solution.py:382
  49.2 19.3 %collective-permute-start.3 = (bf16[2,2,320,256]{3,2,1,0:T(8,128)(2,1)S(1)}, bf16[2,2,320,256]{3,2,1,0:T(8,128)(2,1)S(1)}, u32[]{:S(2)}, u32[]{:S(2)}) collective-permute-start(bf16[2,2,320,256]{3,2,1,0:T(8,128)(2,1)S(1)} %pad_maximum_fusion.1.refs_6_.refs_8_), channel_id=1, source_target_pairs={{1,0},{0,1},{3,2},{2,3},{5,4},{4,5},{7,6},{6,7},{9,8},{8,9},{11,10... | collective-permute-start | bytes 1966088 | tf_op jit(solution)/shard_map/ppermute | solution.py:382
  67.6 5.7 %collective-permute-start.8 = (bf16[2,2,320,256]{3,2,1,0:T(8,128)(2,1)S(1)}, bf16[2,2,320,256]{3,2,1,0:T(8,128)(2,1)S(1)}, u32[]{:S(2)}, u32[]{:S(2)}) collective-permute-start(bf16[2,2,320,256]{3,2,1,0:T(8,128)(2,1)S(1)} %collective-permute-done.6.refs_12_.refs_14_), channel_id=1, source_target_pairs={{1,0},{0,1},{3,2},{2,3},{5,4},{4,5},{7,6},{6,7},{9,8},{8,9},{11,10... | collective-permute-start | bytes 1966088 | tf_op jit(solution)/shard_map/ppermute | solution.py:382
  68.1 20.4 %collective-permute-start.12 = (bf16[2,2,320,256]{3,2,1,0:T(8,128)(2,1)S(1)}, bf16[2,2,320,256]{3,2,1,0:T(8,128)(2,1)}, u32[]{:S(2)}, u32[]{:S(2)}) collective-permute-start(bf16[2,2,320,256]{3,2,1,0:T(8,128)(2,1)S(1)} %collective-permute-done.4.refs_14_.refs_16_), channel_id=1, source_target_pairs={{6,0},{0,2},{2,4},{4,6},{7,1},{1,3},{3,5},{5,7},{14,8},{8,10},{10,... | collective-permute-start | bytes 1966088 | tf_op jit(solution)/shard_map/ppermute | solution.py:382
  68.5 19.9 %collective-permute-start.9 = (bf16[2,2,320,256]{3,2,1,0:T(8,128)(2,1)S(1)}, bf16[2,2,320,256]{3,2,1,0:T(8,128)(2,1)S(1)}, u32[]{:S(2)}, u32[]{:S(2)}) collective-permute-start(bf16[2,2,320,256]{3,2,1,0:T(8,128)(2,1)S(1)} %collective-permute-done.4.refs_14_.refs_16_), channel_id=1, source_target_pairs={{1,0},{0,1},{3,2},{2,3},{5,4},{4,5},{7,6},{6,7},{9,8},{8,9},{11,10... | collective-permute-start | bytes 1966088 | tf_op jit(solution)/shard_map/ppermute | solution.py:382
  69.7 19.1 %collective-permute-start.10 = (bf16[2,2,320,256]{3,2,1,0:T(8,128)(2,1)S(1)}, bf16[2,2,320,256]{3,2,1,0:T(8,128)(2,1)}, u32[]{:S(2)}, u32[]{:S(2)}) collective-permute-start(bf16[2,2,320,256]{3,2,1,0:T(8,128)(2,1)S(1)} %collective-permute-done.5.refs_8_.refs_10_), channel_id=1, source_target_pairs={{2,0},{4,2},{6,4},{0,6},{3,1},{5,3},{7,5},{1,7},{10,8},{12,10},{14... | collective-permute-start | bytes 1966088 | tf_op jit(solution)/shard_map/ppermute | solution.py:382
  73.3 33.4 %collective-permute-start.11 = (bf16[2,2,320,256]{3,2,1,0:T(8,128)(2,1)S(1)}, bf16[2,2,320,256]{3,2,1,0:T(8,128)(2,1)}, u32[]{:S(2)}, u32[]{:S(2)}) collective-permute-start(bf16[2,2,320,256]{3,2,1,0:T(8,128)(2,1)S(1)} %collective-permute-done.4.refs_14_.refs_16_), channel_id=1, source_target_pairs={{2,0},{4,2},{6,4},{0,6},{3,1},{5,3},{7,5},{1,7},{10,8},{12,10},{14... | collective-permute-start | bytes 1966088 | tf_op jit(solution)/shard_map/ppermute | solution.py:382
  88.4 25.0 %collective-permute-start.13 = (bf16[2,2,320,256]{3,2,1,0:T(8,128)(2,1)}, bf16[2,2,320,256]{3,2,1,0:T(8,128)(2,1)}, u32[]{:S(2)}, u32[]{:S(2)}) collective-permute-start(bf16[2,2,320,256]{3,2,1,0:T(8,128)(2,1)} %collective-permute-done.12.refs_20_.refs_22_), channel_id=1, source_target_pairs={{6,0},{0,2},{2,4},{4,6},{7,1},{1,3},{3,5},{5,7},{14,8},{8,10},{10,... | collective-permute-start | bytes 1966088 | tf_op jit(solution)/shard_map/ppermute | solution.py:382
  113.4 11.0 %collective-permute-start.14 = (bf16[2,8,320,256]{3,2,1,0:T(8,128)(2,1)}, bf16[2,8,320,256]{3,2,1,0:T(8,128)(2,1)}, u32[]{:S(2)}, u32[]{:S(2)}) collective-permute-start(bf16[2,8,320,256]{3,2,1,0:T(8,128)(2,1)} %collective-permute-done.refs_4_.refs_6_), channel_id=1, source_target_pairs={{1,0},{0,1},{3,2},{2,3},{5,4},{4,5},{7,6},{6,7},{9,8},{8,9},{11,10... | collective-permute-start | bytes 7864328 | tf_op jit(solution)/shard_map/ppermute | solution.py:382
  113.5 6.9 %collective-permute-start.18 = (bf16[2,2,320,256]{3,2,1,0:T(8,128)(2,1)}, bf16[2,2,320,256]{3,2,1,0:T(8,128)(2,1)}, u32[]{:S(2)}, u32[]{:S(2)}) collective-permute-start(bf16[2,2,320,256]{3,2,1,0:T(8,128)(2,1)} %collective-permute-done.12.refs_20_.refs_22_), channel_id=1, source_target_pairs={{1,0},{0,1},{3,2},{2,3},{5,4},{4,5},{7,6},{6,7},{9,8},{8,9},{11,10... | collective-permute-start | bytes 1966088 | tf_op jit(solution)/shard_map/ppermute | solution.py:382
  114.0 7.3 %collective-permute-start.15 = (bf16[2,2,320,256]{3,2,1,0:T(8,128)(2,1)}, bf16[2,2,320,256]{3,2,1,0:T(8,128)(2,1)}, u32[]{:S(2)}, u32[]{:S(2)}) collective-permute-start(bf16[2,2,320,256]{3,2,1,0:T(8,128)(2,1)} %collective-permute-done.10.refs_10_.refs_12_), channel_id=1, source_target_pairs={{1,0},{0,1},{3,2},{2,3},{5,4},{4,5},{7,6},{6,7},{9,8},{8,9},{11,10... | collective-permute-start | bytes 1966088 | tf_op jit(solution)/shard_map/ppermute | solution.py:382
  114.1 9.1 %collective-permute-start.16 = (bf16[2,2,320,256]{3,2,1,0:T(8,128)(2,1)}, bf16[2,2,320,256]{3,2,1,0:T(8,128)(2,1)}, u32[]{:S(2)}, u32[]{:S(2)}) collective-permute-start(bf16[2,2,320,256]{3,2,1,0:T(8,128)(2,1)} %collective-permute-done.11.refs_16_.refs_18_), channel_id=1, source_target_pairs={{1,0},{0,1},{3,2},{2,3},{5,4},{4,5},{7,6},{6,7},{9,8},{8,9},{11,10... | collective-permute-start | bytes 1966088 | tf_op jit(solution)/shard_map/ppermute | solution.py:382
  114.5 9.9 %collective-permute-start.17 = (bf16[2,2,320,256]{3,2,1,0:T(8,128)(2,1)}, bf16[2,2,320,256]{3,2,1,0:T(8,128)(2,1)}, u32[]{:S(2)}, u32[]{:S(2)}) collective-permute-start(bf16[2,2,320,256]{3,2,1,0:T(8,128)(2,1)} %collective-permute-done.13.refs_18_.refs_20_), channel_id=1, source_target_pairs={{1,0},{0,1},{3,2},{2,3},{5,4},{4,5},{7,6},{6,7},{9,8},{8,9},{11,10... | collective-permute-start | bytes 1966088 | tf_op jit(solution)/shard_map/ppermute | solution.py:382
  136.9 8.2 %collective-permute-start.19 = (bf16[24,5120]{1,0:T(8,128)(2,1)S(1)}, bf16[24,5120]{1,0:T(8,128)(2,1)S(1)}, u32[]{:S(2)}, u32[]{:S(2)}) collective-permute-start(bf16[24,5120]{1,0:T(8,128)(2,1)S(1)} %get-tuple-element.82), channel_id=1, source_target_pairs={{0,64},{64,0},{128,192},{192,128},{1,65},{65,1},{129,193},{193,129... | collective-permute-start | bytes 737288 | tf_op jit(solution)/shard_map/ppermute | solution.py:373
  162.4 17.8 %collective-permute-start.20 = (bf16[24,5120]{1,0:T(8,128)(2,1)S(1)}, bf16[24,5120]{1,0:T(8,128)(2,1)S(1)}, u32[]{:S(2)}, u32[]{:S(2)}) collective-permute-start(bf16[24,5120]{1,0:T(8,128)(2,1)S(1)} %get-tuple-element.88), channel_id=1, source_target_pairs={{0,64},{64,0},{128,192},{192,128},{1,65},{65,1},{129,193},{193,129... | collective-permute-start | bytes 737288 | tf_op jit(solution)/shard_map/ppermute | solution.py:373
  204.9 7.7 %collective-permute-start.21 = (bf16[24,5120]{1,0:T(8,128)(2,1)S(1)}, bf16[24,5120]{1,0:T(8,128)(2,1)S(1)}, u32[]{:S(2)}, u32[]{:S(2)}) collective-permute-start(bf16[24,5120]{1,0:T(8,128)(2,1)S(1)} %get-tuple-element.95), channel_id=1, source_target_pairs={{0,64},{64,0},{128,192},{192,128},{1,65},{65,1},{129,193},{193,129... | collective-permute-start | bytes 737288 | tf_op jit(solution)/shard_map/ppermute | solution.py:373
  213.3 31.7 %all-to-all-start = ((bf16[16,4,24,320]{3,2,1,0:T(8,128)(2,1)}), bf16[16,4,24,320]{3,2,1,0:T(8,128)(2,1)S(1)}, u32[]{:S(2)}, u32[]{:S(2)}) async-start(bf16[16,4,24,320]{3,2,1,0:T(8,128)(2,1)} %get-tuple-element.104), calls=%async_computation | async-start | bytes 2359296 | tf_op jit(solution)/shard_map/all_to_all | solution.py:377
  230.9 20.4 %collective-permute-start.22 = (bf16[24,5120]{1,0:T(8,128)(2,1)S(1)}, bf16[24,5120]{1,0:T(8,128)(2,1)S(1)}, u32[]{:S(2)}, u32[]{:S(2)}) collective-permute-start(bf16[24,5120]{1,0:T(8,128)(2,1)S(1)} %get-tuple-element.103), channel_id=1, source_target_pairs={{0,64},{64,0},{128,192},{192,128},{1,65},{65,1},{129,193},{193,129... | collective-permute-start | bytes 737288 | tf_op jit(solution)/shard_map/ppermute | solution.py:373
  251.2 17.5 %collective-permute-start.25 = (bf16[320,256]{1,0:T(8,128)(2,1)S(1)}, bf16[320,256]{1,0:T(8,128)(2,1)S(1)}, u32[]{:S(2)}, u32[]{:S(2)}) collective-permute-start(bf16[320,256]{1,0:T(8,128)(2,1)S(1)} %get-tuple-element.116), channel_id=1, source_target_pairs={{0,48},{16,0},{32,16},{48,32},{1,49},{17,1},{33,17},{49,33},{2,50}... | collective-permute-start | bytes 491528 | tf_op jit(solution)/shard_map/ppermute | solution.py:368
  252.9 15.9 %collective-permute-start.24 = (bf16[320,256]{1,0:T(8,128)(2,1)S(1)}, bf16[320,256]{1,0:T(8,128)(2,1)S(1)}, u32[]{:S(2)}, u32[]{:S(2)}) collective-permute-start(bf16[320,256]{1,0:T(8,128)(2,1)S(1)} %get-tuple-element.115), channel_id=1, source_target_pairs={{0,32},{16,48},{32,0},{48,16},{1,33},{17,49},{33,1},{49,17},{2,34}... | collective-permute-start | bytes 491528 | tf_op jit(solution)/shard_map/ppermute | solution.py:368
  254.8 14.0 %collective-permute-start.23 = (bf16[320,256]{1,0:T(8,128)(2,1)S(1)}, bf16[320,256]{1,0:T(8,128)(2,1)S(1)}, u32[]{:S(2)}, u32[]{:S(2)}) collective-permute-start(bf16[320,256]{1,0:T(8,128)(2,1)S(1)} %get-tuple-element.114), channel_id=1, source_target_pairs={{0,16},{16,32},{32,48},{48,0},{1,17},{17,33},{33,49},{49,1},{2,18}... | collective-permute-start | bytes 491528 | tf_op jit(solution)/shard_map/ppermute | solution.py:368
  295.6 17.6 %collective-permute-start.28 = (bf16[320,256]{1,0:T(8,128)(2,1)S(1)}, bf16[320,256]{1,0:T(8,128)(2,1)S(1)}, u32[]{:S(2)}, u32[]{:S(2)}) collective-permute-start(bf16[320,256]{1,0:T(8,128)(2,1)S(1)} %get-tuple-element.121), channel_id=1, source_target_pairs={{0,48},{16,0},{32,16},{48,32},{1,49},{17,1},{33,17},{49,33},{2,50}... | collective-permute-start | bytes 491528 | tf_op jit(solution)/shard_map/ppermute | solution.py:368
  297.3 15.9 %collective-permute-start.27 = (bf16[320,256]{1,0:T(8,128)(2,1)S(1)}, bf16[320,256]{1,0:T(8,128)(2,1)S(1)}, u32[]{:S(2)}, u32[]{:S(2)}) collective-permute-start(bf16[320,256]{1,0:T(8,128)(2,1)S(1)} %get-tuple-element.120), channel_id=1, source_target_pairs={{0,32},{16,48},{32,0},{48,16},{1,33},{17,49},{33,1},{49,17},{2,34}... | collective-permute-start | bytes 491528 | tf_op jit(solution)/shard_map/ppermute | solution.py:368
  299.3 14.1 %collective-permute-start.26 = (bf16[320,256]{1,0:T(8,128)(2,1)S(1)}, bf16[320,256]{1,0:T(8,128)(2,1)S(1)}, u32[]{:S(2)}, u32[]{:S(2)}) collective-permute-start(bf16[320,256]{1,0:T(8,128)(2,1)S(1)} %get-tuple-element.119), channel_id=1, source_target_pairs={{0,16},{16,32},{32,48},{48,0},{1,17},{17,33},{33,49},{49,1},{2,18}... | collective-permute-start | bytes 491528 | tf_op jit(solution)/shard_map/ppermute | solution.py:368
  313.5 7.0 %collective-permute-start.29 = (bf16[320,256]{1,0:T(8,128)(2,1)S(1)}, bf16[320,256]{1,0:T(8,128)(2,1)S(1)}, u32[]{:S(2)}, u32[]{:S(2)}) collective-permute-start(bf16[320,256]{1,0:T(8,128)(2,1)S(1)} %get-tuple-element.123), channel_id=1, source_target_pairs={{0,192},{192,0},{64,128},{128,64},{1,193},{193,1},{65,129},{129,65... | collective-permute-start | bytes 491528 | tf_op jit(solution)/shard_map/ppermute | solution.py:386
  (7 other events, 269.4 us)
Sparse Core Ops, SparseCore 0:
  45.6 116.1 all-gather.4
  192.7 38.0 all-gather.6

commit v11 on v9

--- a/solution.py
+++ b/solution.py
@@ -474,7 +474,8 @@
     parts_b = run_grad(place, spread(g_b), act_all, SET)
     rows, parts_b = lax.optimization_barrier((rows, parts_b))
     rows, g_a = run_backward(p_a, rows, w_a, h_a, pre_a, held=g_a, last=True)
-    g_a, sum_b = lax.optimization_barrier((g_a, summed_over_zh(parts_b)))
+    g_a, parts_b = lax.optimization_barrier((g_a, parts_b))
+    sum_b = summed_over_zh(parts_b)
     sum_a = summed_over_zh(run_grad(place, spread(g_a), act_all, 0))
     kept = jnp.where(low_half, sum_a, sum_b)
     other = jnp.where(low_half, sum_b, sum_a)

time: 330 us -> 327 us (level)
  blocking collectives: 24.1 us -> 0 us
  waiting for transfers between devices: 166 us -> 178 us
  starting transfers between devices: 58.1 us -> 68.1 us
    all_to_all x1 -> x0, blocking collectives: 24.1 us -> none  [spread(): return lax.all_to_all(g_set, DP, 0, 0)]
    all_to_all x1 -> x2, waiting for transfers between devices: 0.01 us -> 10.5 us  [spread(): return lax.all_to_all(g_set, DP, 0, 0)]
    all_to_all x1 -> x2, starting transfers between devices: 6.46 us -> 12.3 us  [spread(): return lax.all_to_all(g_set, DP, 0, 0)]
    ppermute x6, starting transfers between devices: 13.3 us -> 17.6 us  [summed_over_zh(): total = total + lax.ppermute(parts[k], 'zh', route).astype(jnp.float32)]
  transfers between devices with their start and end apart: 33 -> 34, of which waited for: 26 -> 27; matrix products, arithmetic and copies ran while one was open for 1% -> 1% of each run, Pallas kernels for 13% -> 10%
where the time goes in v11:
time: 327 us; the launch traced here: 325 us
  waiting for transfers between devices  178 us (54%)
  starting transfers between devices  68.1 us (21%)
  Pallas kernels  55.4 us (17%)
  between operations  13.7 us (4%)
  other arithmetic  5.47 us (2%)
  local copies, waits for them, and re-layouts  4.39 us (1%)
    ppermute x16, waiting for transfers between devices, from_ring(): lax.ppermute(block, axis, [((d + away) % count, d) for d in range(count)])  58.4 us
    ppermute x4, waiting for transfers between devices, hop(): return lax.ppermute(rows, 'y', [(0, 1), (1, 0), (2, 3), (3, 2)])  26.1 us
    pallas_call x4, Pallas kernels, run_backward(): pl.pallas_call(lambda *refs: backward_kernel(*refs, source=source, aliase...  25.7 us
    pallas_call x4, Pallas kernels, run_forward(): pl.pallas_call(lambda *refs: forward_kernel(*refs, source=source, aliased...  25.7 us
    ppermute x1, waiting for transfers between devices, over_z(): return jnp.stack([beside, lax.ppermute(chunk_now, ('y', 'zh'), route)])  21.8 us
    ppermute x6, starting transfers between devices, summed_over_zh(): total = total + lax.ppermute(parts[k], 'zh', route).astype(jnp.float32)  17.6 us
    ppermute x4, starting transfers between devices, hop(): return lax.ppermute(rows, 'y', [(0, 1), (1, 0), (2, 3), (3, 2)])  17.4 us
    all_gather x1, waiting for transfers between devices, shards(): act_all = lax.all_gather(jnp.concatenate([act_a, act_b], axis=0), DP)  17 us
  transfers between devices with their start and end apart: 34, of which 27 were waited for; matrix products, arithmetic and copies ran while one was open for 1% of the time, Pallas kernels for 10%

profile of v11, /device:TPU:2, one launch (start us, length us, event | category | flops | bytes accessed | tf_op | source)
XLA Modules:
  0.0 325.2 jit_solution(17887986741451398775)
XLA Ops:
  11.4 5.8 %collective-permute-start.2 = (bf16[2,320,256]{2,1,0:T(8,128)(2,1)S(1)}, bf16[2,320,256]{2,1,0:T(8,128)(2,1)S(1)}, u32[]{:S(2)}, u32[]{:S(2)}) collective-permute-start(bf16[2,320,256]{2,1,0:T(8,128)(2,1)S(1)} %pad_maximum_fusion.2), channel_id=1, source_target_pairs={{0,208},{16,192},{32,240},{48,224},{64,144},{80,128},{96,176},{112... | collective-permute-start | bytes 983048 | tf_op jit(solution)/shard_map/ppermute | solution.py:395
  18.0 21.8 %collective-permute-done.2 = bf16[2,320,256]{2,1,0:T(8,128)(2,1)S(1)} collective-permute-done((bf16[2,320,256]{2,1,0:T(8,128)(2,1)S(1)}, bf16[2,320,256]{2,1,0:T(8,128)(2,1)S(1)}, u32[]{:S(2)}, u32[]{:S(2)}) %collective-permute-start.2) | collective-permute-done | bytes 327712 | tf_op jit(solution)/shard_map/ppermute | solution.py:395
  39.8 5.6 %collective-permute-done.1 = bf16[2,320,256]{2,1,0:T(8,128)(2,1)S(1)} collective-permute-done((bf16[2,320,256]{2,1,0:T(8,128)(2,1)S(1)}, bf16[2,320,256]{2,1,0:T(8,128)(2,1)S(1)}, u32[]{:S(2)}, u32[]{:S(2)}) %collective-permute-start.1) | collective-permute-done | bytes 327712 | tf_op jit(solution)/shard_map/ppermute | solution.py:390
  49.2 14.9 %collective-permute-done.3.refs_14_.refs_16_ = bf16[2,2,320,256]{3,2,1,0:T(8,128)(2,1)S(1)} collective-permute-done((bf16[2,2,320,256]{3,2,1,0:T(8,128)(2,1)S(1)}, bf16[2,2,320,256]{3,2,1,0:T(8,128)(2,1)S(1)}, u32[]{:S(2)}, u32[]{:S(2)}) %collective-permute-start.3) | collective-permute-done | bytes 655392 | tf_op jit(solution)/shard_map/ppermute | solution.py:382
  68.0 3.2 collective-permute-start.7
  71.2 3.2 collective-permute-start.6
  74.4 10.7 %collective-permute-done.8.refs_20_.refs_22_ = bf16[2,2,320,256]{3,2,1,0:T(8,128)(2,1)} collective-permute-done((bf16[2,2,320,256]{3,2,1,0:T(8,128)(2,1)S(1)}, bf16[2,2,320,256]{3,2,1,0:T(8,128)(2,1)}, u32[]{:S(2)}, u32[]{:S(2)}) %collective-permute-start.8) | collective-permute-done | bytes 655392 | tf_op jit(solution)/shard_map/ppermute | solution.py:382
  85.2 13.8 %collective-permute-done.6.refs_10_.refs_12_ = bf16[2,2,320,256]{3,2,1,0:T(8,128)(2,1)} collective-permute-done((bf16[2,2,320,256]{3,2,1,0:T(8,128)(2,1)S(1)}, bf16[2,2,320,256]{3,2,1,0:T(8,128)(2,1)}, u32[]{:S(2)}, u32[]{:S(2)}) %collective-permute-start.6) | collective-permute-done | bytes 655392 | tf_op jit(solution)/shard_map/ppermute | solution.py:382
  98.9 4.6 %collective-permute-done.9.refs_18_.refs_20_ = bf16[2,2,320,256]{3,2,1,0:T(8,128)(2,1)} collective-permute-done((bf16[2,2,320,256]{3,2,1,0:T(8,128)(2,1)}, bf16[2,2,320,256]{3,2,1,0:T(8,128)(2,1)}, u32[]{:S(2)}, u32[]{:S(2)}) %collective-permute-start.9) | collective-permute-done | bytes 655392 | tf_op jit(solution)/shard_map/ppermute | solution.py:382
  120.5 12.7 %forward_set.4 = (bf16[24,5120]{1,0:T(8,128)(2,1)S(1)}, bf16[4,24,5120]{2,1,0:T(8,128)(2,1)}, f32[4,24,256]{2,1,0:T(8,128)S(1)}, bf16[4,24,256]{2,1,0:T(8,128)(2,1)S(1)}) custom-call(s32[7]{0:T(128)S(1)} %stack.100.refs_0_, bf16[24,5120]{1,0:T(8,128)(2,1)S(1)} %pad.4.refs_1_, bf16[2,16,320,256]{3,2,1,0:T(8,128)(2,1)} %bitcast.33, ...), custom_call_target="tpu_custom_call" | custom-call | flops 125829120 | bytes 5242880 | tf_op jit(solution)/shard_map/forward_set/pallas_call | solution.py:194
  133.5 8.0 %collective-permute-done.19.refs_1_ = bf16[24,5120]{1,0:T(8,128)(2,1)S(1)} collective-permute-done((bf16[24,5120]{1,0:T(8,128)(2,1)S(1)}, bf16[24,5120]{1,0:T(8,128)(2,1)S(1)}, u32[]{:S(2)}, u32[]{:S(2)}) %collective-permute-start.19) | collective-permute-done | bytes 245792 | tf_op jit(solution)/shard_map/ppermute | solution.py:373
  142.1 17.0 %all-gather.5.cloned.1.call-done = bf16[128,320,256]{2,1,0:T(8,128)(2,1)} async-done(((bf16[2,320,256]{2,1,0:T(8,128)(2,1)}), bf16[128,320,256]{2,1,0:T(8,128)(2,1)}) %all-gather.5.cloned.1.call-update) | async-done | bytes 20971536 | tf_op jit(solution)/shard_map/all_gather | solution.py:428
  159.7 9.6 %collective-permute-start.20 = (bf16[24,5120]{1,0:T(8,128)(2,1)S(1)}, bf16[24,5120]{1,0:T(8,128)(2,1)S(1)}, u32[]{:S(2)}, u32[]{:S(2)}) collective-permute-start(bf16[24,5120]{1,0:T(8,128)(2,1)S(1)} %get-tuple-element.75), channel_id=1, source_target_pairs={{0,64},{64,0},{128,192},{192,128},{1,65},{65,1},{129,193},{193,129... | collective-permute-start | bytes 737288 | tf_op jit(solution)/shard_map/ppermute | solution.py:373
  169.4 6.3 %collective-permute-done.20.refs_1_ = bf16[24,5120]{1,0:T(8,128)(2,1)S(1)} collective-permute-done((bf16[24,5120]{1,0:T(8,128)(2,1)S(1)}, bf16[24,5120]{1,0:T(8,128)(2,1)S(1)}, u32[]{:S(2)}, u32[]{:S(2)}) %collective-permute-start.20) | collective-permute-done | bytes 245792 | tf_op jit(solution)/shard_map/ppermute | solution.py:373
  175.7 11.7 %forward_set.7 = (bf16[24,5120]{1,0:T(8,128)(2,1)S(1)}, bf16[4,24,5120]{2,1,0:T(8,128)(2,1)S(1)}, f32[4,24,256]{2,1,0:T(8,128)S(1)}, bf16[4,24,256]{2,1,0:T(8,128)(2,1)S(1)}) custom-call(s32[7]{0:T(128)S(1)} %stack.108.refs_0_, bf16[24,5120]{1,0:T(8,128)(2,1)S(1)} %collective-permute-done.20.refs_1_, ...), custom_call_target="tpu_custom_call", output_to_operand_aliasing={{1}: (3, {}), {2}: (4, {}), {3}: (5, {})} | custom-call | flops 125829120 | bytes 5242880 | tf_op jit(solution)/shard_map/forward_set/pallas_call | solution.py:194
  188.1 12.3 %backward_set.4 = (bf16[24,5120]{1,0:T(8,128)(2,1)S(1)}, bf16[16,4,24,320]{3,2,1,0:T(8,128)(2,1)}) custom-call(s32[7]{0:T(128)S(1)} %stack.108.refs_0_, bf16[24,5120]{1,0:T(8,128)(2,1)S(1)} %get-tuple-element.79.refs_1_, bf16[4,24,5120]{2,1,0:T(8,128)(2,1)S(1)} %get-tuple-element.80.refs_2_, f32[4,24,256]{2,1,0:T(8,128)S(1)} %get-tuple-element.81.refs_3_, ...), custom_call_target="tpu_custom_call" | custom-call | flops 125829120 | bytes 5242880 | tf_op jit(solution)/shard_map/backward_set/pallas_call | solution.py:315
  200.5 7.6 %collective-permute-done.21.refs_1_ = bf16[24,5120]{1,0:T(8,128)(2,1)S(1)} collective-permute-done((bf16[24,5120]{1,0:T(8,128)(2,1)S(1)}, bf16[24,5120]{1,0:T(8,128)(2,1)S(1)}, u32[]{:S(2)}, u32[]{:S(2)}) %collective-permute-start.21) | collective-permute-done | bytes 245792 | tf_op jit(solution)/shard_map/ppermute | solution.py:373
  208.8 6.5 %all-to-all-start = ((bf16[16,4,24,320]{3,2,1,0:T(8,128)(2,1)}), bf16[16,4,24,320]{3,2,1,0:T(8,128)(2,1)S(1)}, u32[]{:S(2)}, u32[]{:S(2)}) async-start(bf16[16,4,24,320]{3,2,1,0:T(8,128)(2,1)} %get-tuple-element.91), calls=%async_computation | async-start | bytes 2359296 | tf_op jit(solution)/shard_map/all_to_all | solution.py:377
  215.9 17.0 %all-gather.7.cloned.1.call-done = bf16[128,24,256]{2,1,0:T(8,128)(2,1)} async-done(((bf16[8,24,256]{2,1,0:T(8,128)(2,1)}), bf16[128,24,256]{2,1,0:T(8,128)(2,1)}) %all-gather.7.cloned.1.call-update) | async-done | bytes 1572880 | tf_op jit(solution)/shard_map/all_gather | solution.py:466
  232.9 7.6 %collective-permute-start.22 = (bf16[24,5120]{1,0:T(8,128)(2,1)S(1)}, bf16[24,5120]{1,0:T(8,128)(2,1)S(1)}, u32[]{:S(2)}, u32[]{:S(2)}) collective-permute-start(bf16[24,5120]{1,0:T(8,128)(2,1)S(1)} %get-tuple-element.90), channel_id=1, source_target_pairs={{0,64},{64,0},{128,192},{192,128},{1,65},{65,1},{129,193},{193,129... | collective-permute-start | bytes 737288 | tf_op jit(solution)/shard_map/ppermute | solution.py:373
  242.4 4.3 %collective-permute-done.22.refs_1_ = bf16[24,5120]{1,0:T(8,128)(2,1)S(1)} collective-permute-done((bf16[24,5120]{1,0:T(8,128)(2,1)S(1)}, bf16[24,5120]{1,0:T(8,128)(2,1)S(1)}, u32[]{:S(2)}, u32[]{:S(2)}) %collective-permute-start.22) | collective-permute-done | bytes 245792 | tf_op jit(solution)/shard_map/ppermute | solution.py:373
  246.7 12.1 %backward_set.7 = (bf16[24,5120]{1,0:T(8,128)(2,1)}, bf16[16,4,24,320]{3,2,1,0:T(8,128)(2,1)}) custom-call(s32[7]{0:T(128)S(1)} %stack.100.refs_0_, bf16[24,5120]{1,0:T(8,128)(2,1)S(1)} %collective-permute-done.22.refs_1_, bf16[4,24,5120]{2,1,0:T(8,128)(2,1)} %get-tuple-element.85.refs_2_, ...), custom_call_target="tpu_custom_call", output_to_operand_aliasing={{1}: (24, {})} | custom-call | flops 125829120 | bytes 5242880 | tf_op jit(solution)/shard_map/backward_set/pallas_call | solution.py:315
  258.9 5.8 %all-to-all-start.1 = ((bf16[16,4,24,320]{3,2,1,0:T(8,128)(2,1)}), bf16[16,4,24,320]{3,2,1,0:T(8,128)(2,1)S(1)}, u32[]{:S(2)}, u32[]{:S(2)}) async-start(bf16[16,4,24,320]{3,2,1,0:T(8,128)(2,1)} %get-tuple-element.104), calls=%async_computation.1 | async-start | bytes 2359296 | tf_op jit(solution)/shard_map/all_to_all | solution.py:377
  264.7 3.7 %collective-permute-start.28 = (bf16[320,256]{1,0:T(8,128)(2,1)}, bf16[320,256]{1,0:T(8,128)(2,1)S(1)}, u32[]{:S(2)}, u32[]{:S(2)}) collective-permute-start(bf16[320,256]{1,0:T(8,128)(2,1)} %copy-done.1), channel_id=1, source_target_pairs={{0,48},{16,0},{32,16},{48,32},{1,49},{17,1},{33,17},{49,33},{2,50}... | collective-permute-start | bytes 491528 | tf_op jit(solution)/shard_map/ppermute | solution.py:368
  268.4 3.4 %collective-permute-start.27 = (bf16[320,256]{1,0:T(8,128)(2,1)}, bf16[320,256]{1,0:T(8,128)(2,1)S(1)}, u32[]{:S(2)}, u32[]{:S(2)}) collective-permute-start(bf16[320,256]{1,0:T(8,128)(2,1)} %copy-done), channel_id=1, source_target_pairs={{0,32},{16,48},{32,0},{48,16},{1,33},{17,49},{33,1},{49,17},{2,34}... | collective-permute-start | bytes 491528 | tf_op jit(solution)/shard_map/ppermute | solution.py:368
  271.7 10.5 %all-to-all-done.1.refs_1_ = bf16[16,4,24,320]{3,2,1,0:T(8,128)(2,1)S(1)} async-done(((bf16[16,4,24,320]{3,2,1,0:T(8,128)(2,1)}), bf16[16,4,24,320]{3,2,1,0:T(8,128)(2,1)S(1)}, u32[]{:S(2)}, u32[]{:S(2)}) %all-to-all-start.1) | async-done | bytes 983072 | tf_op jit(solution)/shard_map/all_to_all | solution.py:377
  284.2 7.2 %collective-permute-start.25 = (bf16[320,256]{1,0:T(8,128)(2,1)S(1)}, bf16[320,256]{1,0:T(8,128)(2,1)S(1)}, u32[]{:S(2)}, u32[]{:S(2)}) collective-permute-start(bf16[320,256]{1,0:T(8,128)(2,1)S(1)} %get-tuple-element.108), channel_id=1, source_target_pairs={{0,48},{16,0},{32,16},{48,32},{1,49},{17,1},{33,17},{49,33},{2,50}... | collective-permute-start | bytes 491528 | tf_op jit(solution)/shard_map/ppermute | solution.py:368
  291.4 3.4 %collective-permute-start.24 = (bf16[320,256]{1,0:T(8,128)(2,1)S(1)}, bf16[320,256]{1,0:T(8,128)(2,1)S(1)}, u32[]{:S(2)}, u32[]{:S(2)}) collective-permute-start(bf16[320,256]{1,0:T(8,128)(2,1)S(1)} %get-tuple-element.107), channel_id=1, source_target_pairs={{0,32},{16,48},{32,0},{48,16},{1,33},{17,49},{33,1},{49,17},{2,34}... | collective-permute-start | bytes 491528 | tf_op jit(solution)/shard_map/ppermute | solution.py:368
  294.8 6.5 %collective-permute-done.26 = bf16[320,256]{1,0:T(8,128)(2,1)S(1)} collective-permute-done((bf16[320,256]{1,0:T(8,128)(2,1)S(1)}, bf16[320,256]{1,0:T(8,128)(2,1)S(1)}, u32[]{:S(2)}, u32[]{:S(2)}) %collective-permute-start.26) | collective-permute-done | bytes 163872 | tf_op jit(solution)/shard_map/ppermute | solution.py:368
  301.3 5.0 %collective-permute-done.25 = bf16[320,256]{1,0:T(8,128)(2,1)S(1)} collective-permute-done((bf16[320,256]{1,0:T(8,128)(2,1)S(1)}, bf16[320,256]{1,0:T(8,128)(2,1)S(1)}, u32[]{:S(2)}, u32[]{:S(2)}) %collective-permute-start.25) | collective-permute-done | bytes 163872 | tf_op jit(solution)/shard_map/ppermute | solution.py:368
  306.3 4.0 %collective-permute-done.23 = bf16[320,256]{1,0:T(8,128)(2,1)S(1)} collective-permute-done((bf16[320,256]{1,0:T(8,128)(2,1)S(1)}, bf16[320,256]{1,0:T(8,128)(2,1)S(1)}, u32[]{:S(2)}, u32[]{:S(2)}) %collective-permute-start.23) | collective-permute-done | bytes 163872 | tf_op jit(solution)/shard_map/ppermute | solution.py:368
  312.7 4.9 %collective-permute-done.29 = bf16[320,256]{1,0:T(8,128)(2,1)S(1)} collective-permute-done((bf16[320,256]{1,0:T(8,128)(2,1)S(1)}, bf16[320,256]{1,0:T(8,128)(2,1)S(1)}, u32[]{:S(2)}, u32[]{:S(2)}) %collective-permute-start.29) | collective-permute-done | bytes 163872 | tf_op jit(solution)/shard_map/ppermute | solution.py:386
  (80 shorter events, 41.1 us)
Async XLA Ops:
  6.5 152.5 %all-gather.5.cloned.1.call-start = ((), (), s32[]{:S(2)}) async-start(), calls=%async_computation.2 | async-start | bytes 21299200 | tf_op jit(solution)/shard_map/all_gather | solution.py:428
  11.4 28.4 %collective-permute-start.2 = (bf16[2,320,256]{2,1,0:T(8,128)(2,1)S(1)}, bf16[2,320,256]{2,1,0:T(8,128)(2,1)S(1)}, u32[]{:S(2)}, u32[]{:S(2)}) collective-permute-start(bf16[2,320,256]{2,1,0:T(8,128)(2,1)S(1)} %pad_maximum_fusion.2), channel_id=1, source_target_pairs={{0,208},{16,192},{32,240},{48,224},{64,144},{80,128},{96,176},{112... | collective-permute-start | bytes 983048 | tf_op jit(solution)/shard_map/ppermute | solution.py:395
  17.3 28.1 %collective-permute-start.1 = (bf16[2,320,256]{2,1,0:T(8,128)(2,1)S(1)}, bf16[2,320,256]{2,1,0:T(8,128)(2,1)S(1)}, u32[]{:S(2)}, u32[]{:S(2)}) collective-permute-start(bf16[2,320,256]{2,1,0:T(8,128)(2,1)S(1)} %pad_maximum_fusion.2), channel_id=1, source_target_pairs={{0,16},{16,0},{32,48},{48,32},{1,17},{17,1},{33,49},{49,33},{2,18}... | collective-permute-start | bytes 983048 | tf_op jit(solution)/shard_map/ppermute | solution.py:390
  45.5 187.4 %all-gather.7.cloned.1.call-start = ((), (), s32[]{:S(2)}) async-start(), calls=%async_computation.3 | async-start | bytes 1671168 | tf_op jit(solution)/shard_map/all_gather | solution.py:466
  45.5 59.3 %collective-permute-start = (bf16[2,8,320,256]{3,2,1,0:T(8,128)(2,1)}, bf16[2,8,320,256]{3,2,1,0:T(8,128)(2,1)}, u32[]{:S(2)}, u32[]{:S(2)}) collective-permute-start(bf16[2,8,320,256]{3,2,1,0:T(8,128)(2,1)} %pad_maximum_fusion), channel_id=1, source_target_pairs={{0,192},{192,0},{64,128},{128,64},{1,193},{193,1},{65,129},{129,65... | collective-permute-start | bytes 7864328 | tf_op jit(solution)/shard_map/ppermute | solution.py:386
  46.8 17.3 %collective-permute-start.3 = (bf16[2,2,320,256]{3,2,1,0:T(8,128)(2,1)S(1)}, bf16[2,2,320,256]{3,2,1,0:T(8,128)(2,1)S(1)}, u32[]{:S(2)}, u32[]{:S(2)}) collective-permute-start(bf16[2,2,320,256]{3,2,1,0:T(8,128)(2,1)S(1)} %pad_maximum_fusion.1.refs_6_.refs_8_), channel_id=1, source_target_pairs={{8,0},{0,8},{9,1},{1,9},{10,2},{2,10},{11,3},{3,11},{12,4},{4,12},... | collective-permute-start | bytes 1966088 | tf_op jit(solution)/shard_map/ppermute | solution.py:382
  47.2 18.2 %collective-permute-start.4 = (bf16[2,2,320,256]{3,2,1,0:T(8,128)(2,1)S(1)}, bf16[2,2,320,256]{3,2,1,0:T(8,128)(2,1)S(1)}, u32[]{:S(2)}, u32[]{:S(2)}) collective-permute-start(bf16[2,2,320,256]{3,2,1,0:T(8,128)(2,1)S(1)} %pad_maximum_fusion.1.refs_6_.refs_8_), channel_id=1, source_target_pairs={{2,0},{4,2},{6,4},{0,6},{3,1},{5,3},{7,5},{1,7},{10,8},{12,10},{14... | collective-permute-start | bytes 1966088 | tf_op jit(solution)/shard_map/ppermute | solution.py:382
  47.7 19.8 %collective-permute-start.5 = (bf16[2,2,320,256]{3,2,1,0:T(8,128)(2,1)S(1)}, bf16[2,2,320,256]{3,2,1,0:T(8,128)(2,1)S(1)}, u32[]{:S(2)}, u32[]{:S(2)}) collective-permute-start(bf16[2,2,320,256]{3,2,1,0:T(8,128)(2,1)S(1)} %pad_maximum_fusion.1.refs_6_.refs_8_), channel_id=1, source_target_pairs={{6,0},{0,2},{2,4},{4,6},{7,1},{1,3},{3,5},{5,7},{14,8},{8,10},{10,... | collective-permute-start | bytes 1966088 | tf_op jit(solution)/shard_map/ppermute | solution.py:382
  67.6 17.6 %collective-permute-start.8 = (bf16[2,2,320,256]{3,2,1,0:T(8,128)(2,1)S(1)}, bf16[2,2,320,256]{3,2,1,0:T(8,128)(2,1)}, u32[]{:S(2)}, u32[]{:S(2)}) collective-permute-start(bf16[2,2,320,256]{3,2,1,0:T(8,128)(2,1)S(1)} %collective-permute-done.3.refs_14_.refs_16_), channel_id=1, source_target_pairs={{6,0},{0,2},{2,4},{4,6},{7,1},{1,3},{3,5},{5,7},{14,8},{8,10},{10,... | collective-permute-start | bytes 1966088 | tf_op jit(solution)/shard_map/ppermute | solution.py:382
  68.0 30.9 %collective-permute-start.7 = (bf16[2,2,320,256]{3,2,1,0:T(8,128)(2,1)S(1)}, bf16[2,2,320,256]{3,2,1,0:T(8,128)(2,1)}, u32[]{:S(2)}, u32[]{:S(2)}) collective-permute-start(bf16[2,2,320,256]{3,2,1,0:T(8,128)(2,1)S(1)} %collective-permute-done.3.refs_14_.refs_16_), channel_id=1, source_target_pairs={{2,0},{4,2},{6,4},{0,6},{3,1},{5,3},{7,5},{1,7},{10,8},{12,10},{14... | collective-permute-start | bytes 1966088 | tf_op jit(solution)/shard_map/ppermute | solution.py:382
  71.2 27.7 %collective-permute-start.6 = (bf16[2,2,320,256]{3,2,1,0:T(8,128)(2,1)S(1)}, bf16[2,2,320,256]{3,2,1,0:T(8,128)(2,1)}, u32[]{:S(2)}, u32[]{:S(2)}) collective-permute-start(bf16[2,2,320,256]{3,2,1,0:T(8,128)(2,1)S(1)} %collective-permute-done.4.refs_8_.refs_10_), channel_id=1, source_target_pairs={{2,0},{4,2},{6,4},{0,6},{3,1},{5,3},{7,5},{1,7},{10,8},{12,10},{14... | collective-permute-start | bytes 1966088 | tf_op jit(solution)/shard_map/ppermute | solution.py:382
  85.2 18.4 %collective-permute-start.9 = (bf16[2,2,320,256]{3,2,1,0:T(8,128)(2,1)}, bf16[2,2,320,256]{3,2,1,0:T(8,128)(2,1)}, u32[]{:S(2)}, u32[]{:S(2)}) collective-permute-start(bf16[2,2,320,256]{3,2,1,0:T(8,128)(2,1)} %collective-permute-done.8.refs_20_.refs_22_), channel_id=1, source_target_pairs={{6,0},{0,2},{2,4},{4,6},{7,1},{1,3},{3,5},{5,7},{14,8},{8,10},{10,... | collective-permute-start | bytes 1966088 | tf_op jit(solution)/shard_map/ppermute | solution.py:382
  104.9 15.6 %collective-permute-start.10 = (bf16[2,8,320,256]{3,2,1,0:T(8,128)(2,1)}, bf16[2,8,320,256]{3,2,1,0:T(8,128)(2,1)}, u32[]{:S(2)}, u32[]{:S(2)}) collective-permute-start(bf16[2,8,320,256]{3,2,1,0:T(8,128)(2,1)} %collective-permute-done.refs_4_.refs_6_), channel_id=1, source_target_pairs={{1,0},{0,1},{3,2},{2,3},{5,4},{4,5},{7,6},{6,7},{9,8},{8,9},{11,10... | collective-permute-start | bytes 7864328 | tf_op jit(solution)/shard_map/ppermute | solution.py:382
  105.4 5.4 %collective-permute-start.12 = (bf16[2,2,320,256]{3,2,1,0:T(8,128)(2,1)S(1)}, bf16[2,2,320,256]{3,2,1,0:T(8,128)(2,1)S(1)}, u32[]{:S(2)}, u32[]{:S(2)}) collective-permute-start(bf16[2,2,320,256]{3,2,1,0:T(8,128)(2,1)S(1)} %collective-permute-done.4.refs_8_.refs_10_), channel_id=1, source_target_pairs={{1,0},{0,1},{3,2},{2,3},{5,4},{4,5},{7,6},{6,7},{9,8},{8,9},{11,10... | collective-permute-start | bytes 1966088 | tf_op jit(solution)/shard_map/ppermute | solution.py:382
  105.4 7.4 %collective-permute-start.14 = (bf16[2,2,320,256]{3,2,1,0:T(8,128)(2,1)S(1)}, bf16[2,2,320,256]{3,2,1,0:T(8,128)(2,1)S(1)}, u32[]{:S(2)}, u32[]{:S(2)}) collective-permute-start(bf16[2,2,320,256]{3,2,1,0:T(8,128)(2,1)S(1)} %collective-permute-done.5.refs_12_.refs_14_), channel_id=1, source_target_pairs={{1,0},{0,1},{3,2},{2,3},{5,4},{4,5},{7,6},{6,7},{9,8},{8,9},{11,10... | collective-permute-start | bytes 1966088 | tf_op jit(solution)/shard_map/ppermute | solution.py:382
  105.9 9.4 %collective-permute-start.15 = (bf16[2,2,320,256]{3,2,1,0:T(8,128)(2,1)S(1)}, bf16[2,2,320,256]{3,2,1,0:T(8,128)(2,1)S(1)}, u32[]{:S(2)}, u32[]{:S(2)}) collective-permute-start(bf16[2,2,320,256]{3,2,1,0:T(8,128)(2,1)S(1)} %collective-permute-done.3.refs_14_.refs_16_), channel_id=1, source_target_pairs={{1,0},{0,1},{3,2},{2,3},{5,4},{4,5},{7,6},{6,7},{9,8},{8,9},{11,10... | collective-permute-start | bytes 1966088 | tf_op jit(solution)/shard_map/ppermute | solution.py:382
  108.1 9.9 %collective-permute-start.18 = (bf16[2,2,320,256]{3,2,1,0:T(8,128)(2,1)}, bf16[2,2,320,256]{3,2,1,0:T(8,128)(2,1)}, u32[]{:S(2)}, u32[]{:S(2)}) collective-permute-start(bf16[2,2,320,256]{3,2,1,0:T(8,128)(2,1)} %collective-permute-done.8.refs_20_.refs_22_), channel_id=1, source_target_pairs={{1,0},{0,1},{3,2},{2,3},{5,4},{4,5},{7,6},{6,7},{9,8},{8,9},{11,10... | collective-permute-start | bytes 1966088 | tf_op jit(solution)/shard_map/ppermute | solution.py:382
  110.8 7.6 %collective-permute-start.13 = (bf16[2,2,320,256]{3,2,1,0:T(8,128)(2,1)}, bf16[2,2,320,256]{3,2,1,0:T(8,128)(2,1)}, u32[]{:S(2)}, u32[]{:S(2)}) collective-permute-start(bf16[2,2,320,256]{3,2,1,0:T(8,128)(2,1)} %collective-permute-done.6.refs_10_.refs_12_), channel_id=1, source_target_pairs={{1,0},{0,1},{3,2},{2,3},{5,4},{4,5},{7,6},{6,7},{9,8},{8,9},{11,10... | collective-permute-start | bytes 1966088 | tf_op jit(solution)/shard_map/ppermute | solution.py:382
  112.8 6.7 %collective-permute-start.16 = (bf16[2,2,320,256]{3,2,1,0:T(8,128)(2,1)}, bf16[2,2,320,256]{3,2,1,0:T(8,128)(2,1)}, u32[]{:S(2)}, u32[]{:S(2)}) collective-permute-start(bf16[2,2,320,256]{3,2,1,0:T(8,128)(2,1)} %collective-permute-done.7.refs_16_.refs_18_), channel_id=1, source_target_pairs={{1,0},{0,1},{3,2},{2,3},{5,4},{4,5},{7,6},{6,7},{9,8},{8,9},{11,10... | collective-permute-start | bytes 1966088 | tf_op jit(solution)/shard_map/ppermute | solution.py:382
  133.2 8.2 %collective-permute-start.19 = (bf16[24,5120]{1,0:T(8,128)(2,1)S(1)}, bf16[24,5120]{1,0:T(8,128)(2,1)S(1)}, u32[]{:S(2)}, u32[]{:S(2)}) collective-permute-start(bf16[24,5120]{1,0:T(8,128)(2,1)S(1)} %get-tuple-element.69), channel_id=1, source_target_pairs={{0,64},{64,0},{128,192},{192,128},{1,65},{65,1},{129,193},{193,129... | collective-permute-start | bytes 737288 | tf_op jit(solution)/shard_map/ppermute | solution.py:373
  159.7 16.0 %collective-permute-start.20 = (bf16[24,5120]{1,0:T(8,128)(2,1)S(1)}, bf16[24,5120]{1,0:T(8,128)(2,1)S(1)}, u32[]{:S(2)}, u32[]{:S(2)}) collective-permute-start(bf16[24,5120]{1,0:T(8,128)(2,1)S(1)} %get-tuple-element.75), channel_id=1, source_target_pairs={{0,64},{64,0},{128,192},{192,128},{1,65},{65,1},{129,193},{193,129... | collective-permute-start | bytes 737288 | tf_op jit(solution)/shard_map/ppermute | solution.py:373
  200.4 7.7 %collective-permute-start.21 = (bf16[24,5120]{1,0:T(8,128)(2,1)S(1)}, bf16[24,5120]{1,0:T(8,128)(2,1)S(1)}, u32[]{:S(2)}, u32[]{:S(2)}) collective-permute-start(bf16[24,5120]{1,0:T(8,128)(2,1)S(1)} %get-tuple-element.82), channel_id=1, source_target_pairs={{0,64},{64,0},{128,192},{192,128},{1,65},{65,1},{129,193},{193,129... | collective-permute-start | bytes 737288 | tf_op jit(solution)/shard_map/ppermute | solution.py:373
  208.8 31.7 %all-to-all-start = ((bf16[16,4,24,320]{3,2,1,0:T(8,128)(2,1)}), bf16[16,4,24,320]{3,2,1,0:T(8,128)(2,1)S(1)}, u32[]{:S(2)}, u32[]{:S(2)}) async-start(bf16[16,4,24,320]{3,2,1,0:T(8,128)(2,1)} %get-tuple-element.91), calls=%async_computation | async-start | bytes 2359296 | tf_op jit(solution)/shard_map/all_to_all | solution.py:377
  232.9 13.8 %collective-permute-start.22 = (bf16[24,5120]{1,0:T(8,128)(2,1)S(1)}, bf16[24,5120]{1,0:T(8,128)(2,1)S(1)}, u32[]{:S(2)}, u32[]{:S(2)}) collective-permute-start(bf16[24,5120]{1,0:T(8,128)(2,1)S(1)} %get-tuple-element.90), channel_id=1, source_target_pairs={{0,64},{64,0},{128,192},{192,128},{1,65},{65,1},{129,193},{193,129... | collective-permute-start | bytes 737288 | tf_op jit(solution)/shard_map/ppermute | solution.py:373
  258.9 23.4 %all-to-all-start.1 = ((bf16[16,4,24,320]{3,2,1,0:T(8,128)(2,1)}), bf16[16,4,24,320]{3,2,1,0:T(8,128)(2,1)S(1)}, u32[]{:S(2)}, u32[]{:S(2)}) async-start(bf16[16,4,24,320]{3,2,1,0:T(8,128)(2,1)} %get-tuple-element.104), calls=%async_computation.1 | async-start | bytes 2359296 | tf_op jit(solution)/shard_map/all_to_all | solution.py:377
  264.7 30.1 %collective-permute-start.28 = (bf16[320,256]{1,0:T(8,128)(2,1)}, bf16[320,256]{1,0:T(8,128)(2,1)S(1)}, u32[]{:S(2)}, u32[]{:S(2)}) collective-permute-start(bf16[320,256]{1,0:T(8,128)(2,1)} %copy-done.1), channel_id=1, source_target_pairs={{0,48},{16,0},{32,16},{48,32},{1,49},{17,1},{33,17},{49,33},{2,50}... | collective-permute-start | bytes 491528 | tf_op jit(solution)/shard_map/ppermute | solution.py:368
  268.4 26.4 %collective-permute-start.27 = (bf16[320,256]{1,0:T(8,128)(2,1)}, bf16[320,256]{1,0:T(8,128)(2,1)S(1)}, u32[]{:S(2)}, u32[]{:S(2)}) collective-permute-start(bf16[320,256]{1,0:T(8,128)(2,1)} %copy-done), channel_id=1, source_target_pairs={{0,32},{16,48},{32,0},{48,16},{1,33},{17,49},{33,1},{49,17},{2,34}... | collective-permute-start | bytes 491528 | tf_op jit(solution)/shard_map/ppermute | solution.py:368
  271.7 29.6 %collective-permute-start.26 = (bf16[320,256]{1,0:T(8,128)(2,1)S(1)}, bf16[320,256]{1,0:T(8,128)(2,1)S(1)}, u32[]{:S(2)}, u32[]{:S(2)}) collective-permute-start(bf16[320,256]{1,0:T(8,128)(2,1)S(1)} %get-tuple-element.110), channel_id=1, source_target_pairs={{0,16},{16,32},{32,48},{48,0},{1,17},{17,33},{33,49},{49,1},{2,18}... | collective-permute-start | bytes 491528 | tf_op jit(solution)/shard_map/ppermute | solution.py:368
  284.2 22.1 %collective-permute-start.25 = (bf16[320,256]{1,0:T(8,128)(2,1)S(1)}, bf16[320,256]{1,0:T(8,128)(2,1)S(1)}, u32[]{:S(2)}, u32[]{:S(2)}) collective-permute-start(bf16[320,256]{1,0:T(8,128)(2,1)S(1)} %get-tuple-element.108), channel_id=1, source_target_pairs={{0,48},{16,0},{32,16},{48,32},{1,49},{17,1},{33,17},{49,33},{2,50}... | collective-permute-start | bytes 491528 | tf_op jit(solution)/shard_map/ppermute | solution.py:368
  291.4 15.0 %collective-permute-start.24 = (bf16[320,256]{1,0:T(8,128)(2,1)S(1)}, bf16[320,256]{1,0:T(8,128)(2,1)S(1)}, u32[]{:S(2)}, u32[]{:S(2)}) collective-permute-start(bf16[320,256]{1,0:T(8,128)(2,1)S(1)} %get-tuple-element.107), channel_id=1, source_target_pairs={{0,32},{16,48},{32,0},{48,16},{1,33},{17,49},{33,1},{49,17},{2,34}... | collective-permute-start | bytes 491528 | tf_op jit(solution)/shard_map/ppermute | solution.py:368
  294.8 15.5 %collective-permute-start.23 = (bf16[320,256]{1,0:T(8,128)(2,1)S(1)}, bf16[320,256]{1,0:T(8,128)(2,1)S(1)}, u32[]{:S(2)}, u32[]{:S(2)}) collective-permute-start(bf16[320,256]{1,0:T(8,128)(2,1)S(1)} %get-tuple-element.106), channel_id=1, source_target_pairs={{0,16},{16,32},{32,48},{48,0},{1,17},{17,33},{33,49},{49,1},{2,18}... | collective-permute-start | bytes 491528 | tf_op jit(solution)/shard_map/ppermute | solution.py:368
  310.5 7.0 %collective-permute-start.29 = (bf16[320,256]{1,0:T(8,128)(2,1)S(1)}, bf16[320,256]{1,0:T(8,128)(2,1)S(1)}, u32[]{:S(2)}, u32[]{:S(2)}) collective-permute-start(bf16[320,256]{1,0:T(8,128)(2,1)S(1)} %get-tuple-element.113), channel_id=1, source_target_pairs={{0,192},{192,0},{64,128},{128,64},{1,193},{193,1},{65,129},{129,65... | collective-permute-start | bytes 491528 | tf_op jit(solution)/shard_map/ppermute | solution.py:386
  (10 other events, 207.5 us)
Sparse Core Ops, SparseCore 0:
  45.6 113.3 all-gather.4
  188.2 44.6 all-gather.6
